TPU v7x, 256 devices: a whole 4x4x8 slice. The times are simulated.
256 devices in a mesh: phase: 4 (over x), dp: 64 (over z, y, core).
Axes of the slice: x: 4, y: 4, z: 8, core: 2. Of those that a mesh axis runs over, the one named last changes fastest.
Arguments:
- query_states: bfloat16 [4096, 2048], P('dp', 'phase'), may hold values from -25 to 25
- doc_states: bfloat16 [8192, 4096], P('dp', 'phase'), may hold values from -8.7 to 8.7
- query_proj: bfloat16 [2048, 2048], P('phase'), may hold values from -0.75 to 2.75
- doc_proj: bfloat16 [4096, 2048], P('phase'), may hold values from -0.75 to 2.75
- document_requests: int32 [64, 64, 16], P('dp'), may hold values from 0 to 127, as said below
- slot_valid: int32 [64, 1024], P('dp'), may hold values from 0 to 1
- neg_slot: int32 [4096, 7], P('dp'), may hold values from 0 to 1023, as said below
- query_weight: float32 [4096], P('dp'), may hold values from 0.5 to 2
Outputs:
- loss_rows: float32 [4096], P('dp')
- grad_query: bfloat16 [4096, 2048], P('dp', 'phase')
- grad_doc: bfloat16 [8192, 4096], P('dp', 'phase')
Inputs may be any that keep to these rules, and one draw needn't show every extreme that they name: `document_requests`: rows may repeat within and across slots. `neg_slot`: slots index the rows received by the query's own dp index.
All inputs are finite; a program needn't handle non-finite values.
Results may differ from a plain program's by a relative error of at most 0.0067.
Values may be sent and summed in bfloat16 or wider, within the bound.
No kernel may reach another device: no remote copies, remote signals or barrier semaphores. Data moves between devices by JAX's collectives and lax.ppermute only.
A program may use at most 128 MiB of HBM per device.

v0:
```python
import jax
import jax.numpy as jnp
from jax import lax
from jax.sharding import PartitionSpec as P

logit_scale = 20.0
epsilon = 1e-06


def softmax_terms(inner_scores, slot_scores, negatives, validity, weights):
    count_slots = slot_scores.shape[1]
    hard_scores = jnp.take_along_axis(slot_scores, negatives, axis=1)
    kept_mask = jnp.take(validity, negatives).astype(jnp.float32)
    inner_exp = jnp.exp(inner_scores)
    hard_exp = jnp.exp(hard_scores) * kept_mask
    row_total = jnp.sum(inner_exp, axis=1) + jnp.sum(hard_exp, axis=1)
    row_ids = lax.broadcasted_iota(jnp.int32, inner_scores.shape, 0)
    col_ids = lax.broadcasted_iota(jnp.int32, inner_scores.shape, 1)
    is_positive = (row_ids == col_ids).astype(jnp.float32)
    positive = jnp.sum(inner_scores * is_positive, axis=1)
    loss_rows = jnp.log(row_total) - positive
    factor = (logit_scale * weights / row_total)[:, None]
    grad_inner = factor * inner_exp - (logit_scale * weights)[:, None] * is_positive
    hard_grad = factor * hard_exp
    slot_ids = lax.broadcasted_iota(jnp.int32, (1, 1, count_slots), 2)
    slot_onehot = (negatives[:, :, None] == slot_ids).astype(jnp.float32)
    grad_slots = jnp.sum(slot_onehot * hard_grad[:, :, None], axis=1)
    return (loss_rows, grad_inner.astype(jnp.bfloat16), grad_slots.astype(jnp.bfloat16))


def local(
    query_states,
    doc_states,
    query_proj,
    doc_proj,
    document_requests,
    slot_valid,
    neg_slot,
    query_weight,
):
    q_part = jnp.dot(query_states, query_proj, preferred_element_type=jnp.float32)
    d_part = jnp.dot(doc_states, doc_proj, preferred_element_type=jnp.float32)
    q_raw, d_raw = lax.psum((q_part, d_part), "phase")
    q_square = jnp.sum(q_raw * q_raw, axis=1)
    d_square = jnp.sum(d_raw * d_raw, axis=1)
    q_scale = lax.rsqrt(q_square + epsilon)[:, None]
    d_scale = lax.rsqrt(d_square + epsilon)[:, None]
    q_unit = q_raw * q_scale
    d_unit = d_raw * d_scale
    q_low = q_unit.astype(jnp.bfloat16)
    d_low = d_unit.astype(jnp.bfloat16)
    requested = document_requests[0]
    outgoing = d_low[requested]
    received = lax.all_to_all(outgoing, "dp", split_axis=0, concat_axis=0, tiled=True)
    received = received.reshape(-1, received.shape[2])
    inner_part = jnp.dot(q_low, d_low.T, preferred_element_type=jnp.float32)
    slot_part = jnp.dot(q_low, received.T, preferred_element_type=jnp.float32)
    loss_rows, grad_inner, grad_slots = softmax_terms(
        logit_scale * inner_part, logit_scale * slot_part, neg_slot, slot_valid[0], query_weight
    )
    g_query = jnp.dot(grad_inner, d_low, preferred_element_type=jnp.float32) + jnp.dot(
        grad_slots, received, preferred_element_type=jnp.float32
    )
    grad_local = jnp.dot(grad_inner.T, q_low, preferred_element_type=jnp.float32)
    grad_received = jnp.dot(grad_slots.T, q_low, preferred_element_type=jnp.float32)
    returned = lax.all_to_all(
        grad_received.reshape(outgoing.shape), "dp", split_axis=0, concat_axis=0, tiled=True
    )
    hard_total = jax.ops.segment_sum(
        returned.reshape(-1, returned.shape[2]), requested.reshape(-1), num_segments=d_low.shape[0]
    )
    g_docs = grad_local + hard_total
    q_inner = jnp.sum(q_unit * g_query, axis=1)
    d_inner = jnp.sum(d_unit * g_docs, axis=1)
    u_query = (q_scale * (g_query - q_unit * q_inner[:, None])).astype(jnp.bfloat16)
    u_docs = (d_scale * (g_docs - d_unit * d_inner[:, None])).astype(jnp.bfloat16)
    grad_query = jnp.dot(u_query, query_proj.T, preferred_element_type=jnp.float32).astype(
        jnp.bfloat16
    )
    grad_doc = jnp.dot(u_docs, doc_proj.T, preferred_element_type=jnp.float32).astype(jnp.bfloat16)
    return (loss_rows, grad_query, grad_doc)


def solution(mesh):
    in_specs = (
        P("dp", "phase"),
        P("dp", "phase"),
        P("phase", None),
        P("phase", None),
        P("dp", None, None),
        P("dp", None),
        P("dp", None),
        P("dp"),
    )
    out_specs = (P("dp"), P("dp", "phase"), P("dp", "phase"))
    return jax.shard_map(local, mesh=mesh, in_specs=in_specs, out_specs=out_specs, check_vma=False)
```

profile of v0, /device:TPU:1, one launch (start us, length us, event | category | flops | bytes accessed | tf_op | source)
XLA Modules:
  0.0 420.7 jit_solution(12044016468349338662)
XLA Ops:
  7.2 1.5 copy-done
  8.8 2.1 fusion.10
  10.9 4.0 fusion.11
  15.1 59.3 %all-reduce.3.cloned.1.call-done = (f32[64,2048]{1,0:T(8,128)}, f32[128,2048]{1,0:T(8,128)}) async-done(((f32[64,2048]{1,0:T(8,128)}, f32[128,2048]{1,0:T(8,128)}), (f32[64,2048]{1,0:T(8,128)}, f32[128,2048]{1,0:T(8,128)})) %all-reduce.3.cloned.1.call-update) | async-done | bytes 1572880 | tf_op jit(solution)/shard_map/psum | solution.py:43
  74.5 1.4 multiply_reduce_fusion.1
  75.9 1.3 multiply_convert_fusion.1
  77.2 6.0 %gather_fusion = bf16[1024,2048]{1,0:T(8,128)(2,1)} fusion(bf16[128,2048]{1,0:T(8,128)(2,1)S(1)} %multiply_convert_fusion.1, s32[1024]{0:T(1024)S(1)} %broadcast_clamp_fusion), kind=kCustom, calls=%fused_computation | custom fusion | bytes 8392704 | tf_op jit(solution)/shard_map/gather | solution.py:53
  83.2 11.2 %all-to-all-start = ((bf16[64,16,2048]{2,1,0:T(8,128)(2,1)}), bf16[64,16,2048]{2,1,0:T(8,128)(2,1)}, u32[]{:S(2)}, u32[]{:S(2)}) async-start(bf16[64,16,2048]{2,1,0:T(8,128)(2,1)} %bitcast.31), calls=%async_computation | async-start | bytes 8388608 | tf_op jit(solution)/shard_map/all_to_all | solution.py:54
  94.5 0.1 reshape.93
  94.7 0.1 copy.30
  94.8 0.1 reshape.99
  95.0 2.1 gather_fusion.1
  97.1 0.1 reshape.92
  97.3 0.2 multiply_reduce_fusion.3
  97.4 0.1 multiply_convert_fusion.4
  97.6 0.4 exponential_reduce_fusion
  98.0 90.9 %all-to-all-done = bf16[64,16,2048]{2,1,0:T(8,128)(2,1)} async-done(((bf16[64,16,2048]{2,1,0:T(8,128)(2,1)}), bf16[64,16,2048]{2,1,0:T(8,128)(2,1)}, u32[]{:S(2)}, u32[]{:S(2)}) %all-to-all-start) | async-done | bytes 4194336 | tf_op jit(solution)/shard_map/all_to_all | solution.py:54
  188.8 3.7 convolution_multiply_fusion
  192.5 3.9 gather_fusion.2
  196.5 0.1 reshape.102
  196.7 0.5 add_divide_fusion
  197.3 0.3 select_reduce_fusion
  197.5 4.5 %fusion.12 = f32[1024,2048]{1,0:T(8,128)} fusion(bf16[64,1024]{1,0:T(8,128)(2,1)S(1)} %select_reduce_fusion, bf16[64,2048]{1,0:T(8,128)(2,1)S(1)} %copy-done.5), kind=kOutput, calls=%fused_computation.47 | convolution fusion | flops 268435456 | bytes 8781824 | tf_op jit(solution)/shard_map/dot_general | solution.py:65
  202.0 7.5 %all-to-all-start.1 = ((f32[64,16,2048]{2,1,0:T(8,128)}), f32[64,16,2048]{2,1,0:T(8,128)}, u32[]{:S(2)}, u32[]{:S(2)}) async-start(f32[64,16,2048]{2,1,0:T(8,128)} %bitcast.30), calls=%async_computation.1 | async-start | bytes 16777216 | tf_op jit(solution)/shard_map/all_to_all | solution.py:66
  209.7 0.3 fusion.9
  209.9 1.2 fusion.8
  211.1 3.3 multiply_reduce_fusion.2
  214.5 1.4 convolution_convert_fusion.1
  215.9 176.5 %all-to-all-done.1 = f32[64,16,2048]{2,1,0:T(8,128)} async-done(((f32[64,16,2048]{2,1,0:T(8,128)}), f32[64,16,2048]{2,1,0:T(8,128)}, u32[]{:S(2)}, u32[]{:S(2)}) %all-to-all-start.1) | async-done | bytes 8388640 | tf_op jit(solution)/shard_map/all_to_all | solution.py:66
  392.4 15.3 %scatter_fusion = f32[128,2048]{1,0:T(8,128)S(1)} fusion(f32[128,2048]{1,0:T(8,128)S(1)} %fusion.8, s32[1024]{0:T(1024)S(1)} %reshape.107, f32[1024,2048]{1,0:T(8,128)} %bitcast.6), kind=kCustom, calls=%fused_computation.3 | custom fusion | flops 2097152 | bytes 25169920 | tf_op jit(solution)/shard_map/scatter-add | solution.py:69
  407.7 1.5 multiply_reduce_fusion
  409.1 4.7 %convolution_convert_fusion = bf16[128,1024]{1,0:T(8,128)(2,1)} fusion(bf16[1024,2048]{1,0:T(8,128)(2,1)} %param.11, f32[128,2048]{1,0:T(8,128)S(1)} %scatter_fusion, f32[128,2048]{1,0:T(8,128)} %get-tuple-element.6, f32[128]{0:T(128)S(1)} %multiply_reduce_fusion, f32[128]{0:T(128)S(1)} %copy-done.13), kind=kOutput, calls=%fused_computation.7 | convolution fusion | flops 538312704 | bytes 6554624 | tf_op jit(solution)/shard_map/dot_general | solution.py:80
  (47 shorter events, 0.8 us)
Async XLA Ops:
  7.2 1.6 copy-start
  7.2 67.3 %all-reduce.3.cloned.1.call-start = ((), (), s32[]{:S(2)}) async-start(), calls=%async_computation.2 | async-start | bytes 3145728 | tf_op jit(solution)/shard_map/psum | solution.py:43
  10.9 4.0 copy-start.8
  75.8 7.4 %copy-start.12 = (f32[128]{0:T(128)}, f32[128]{0:T(128)S(1)}, u32[]{:S(2)}) copy-start(f32[128]{0:T(128)S(1)} %add_rsqrt_fusion) | copy-start | bytes 1540
  83.2 11.2 %copy-start.7 = (s32[64,7]{0,1:T(8,128)S(1)}, s32[64,7]{0,1:T(8,128)}, u32[]{:S(2)}) copy-start(s32[64,7]{0,1:T(8,128)} %param.14) | copy-start | bytes 5380
  83.2 11.7 %copy-start.1 = (s32[1,1024]{1,0:T(1,128)S(1)}, s32[1,1024]{1,0:T(1,128)}, u32[]{:S(2)}) copy-start(s32[1,1024]{1,0:T(1,128)} %param.13) | copy-start | bytes 12292
  83.2 105.6 %all-to-all-start = ((bf16[64,16,2048]{2,1,0:T(8,128)(2,1)}), bf16[64,16,2048]{2,1,0:T(8,128)(2,1)}, u32[]{:S(2)}, u32[]{:S(2)}) async-start(bf16[64,16,2048]{2,1,0:T(8,128)(2,1)} %bitcast.31), calls=%async_computation | async-start | bytes 8388608 | tf_op jit(solution)/shard_map/all_to_all | solution.py:54
  95.0 2.3 copy-start.2
  97.4 99.0 %copy-start.10 = (f32[64]{0:T(128)}, f32[64]{0:T(128)S(1)}, u32[]{:S(2)}) copy-start(f32[64]{0:T(128)S(1)} %add_rsqrt_fusion.1) | copy-start | bytes 772
  97.6 91.3 %copy-start.4 = (bf16[64,2048]{1,0:T(8,128)(2,1)}, bf16[64,2048]{1,0:T(8,128)(2,1)S(1)}, u32[]{:S(2)}) copy-start(bf16[64,2048]{1,0:T(8,128)(2,1)S(1)} %multiply_convert_fusion.4) | copy-start | bytes 786436
  98.0 111.7 %copy-start.6 = (f32[64,128]{1,0:T(8,128)}, f32[64,128]{1,0:T(8,128)S(1)}, u32[]{:S(2)}) copy-start(f32[64,128]{1,0:T(8,128)S(1)} %get-tuple-element.10) | copy-start | bytes 98308
  192.5 4.2 copy-start.14
  192.5 5.0 %copy-start.5 = (bf16[64,2048]{1,0:T(8,128)(2,1)S(1)}, bf16[64,2048]{1,0:T(8,128)(2,1)}, u32[]{:S(2)}) copy-start(bf16[64,2048]{1,0:T(8,128)(2,1)} %copy-done.4) | copy-start | bytes 786436
  197.2 12.4 %copy-start.9 = (f32[64]{0:T(128)}, f32[64]{0:T(128)S(1)}, u32[]{:S(2)}) copy-start(f32[64]{0:T(128)S(1)} %get-tuple-element.9) | copy-start | bytes 772
  202.0 190.4 %all-to-all-start.1 = ((f32[64,16,2048]{2,1,0:T(8,128)}), f32[64,16,2048]{2,1,0:T(8,128)}, u32[]{:S(2)}, u32[]{:S(2)}) async-start(f32[64,16,2048]{2,1,0:T(8,128)} %bitcast.30), calls=%async_computation.1 | async-start | bytes 16777216 | tf_op jit(solution)/shard_map/all_to_all | solution.py:66
  209.6 4.9 %copy-start.11 = (f32[64]{0:T(128)S(1)}, f32[64]{0:T(128)}, u32[]{:S(2)}) copy-start(f32[64]{0:T(128)} %copy-done.10) | copy-start | bytes 772
  209.7 4.8 %copy-start.3 = (f32[64,2048]{1,0:T(8,128)S(1)}, f32[64,2048]{1,0:T(8,128)}, u32[]{:S(2)}) copy-start(f32[64,2048]{1,0:T(8,128)} %get-tuple-element.5) | copy-start | bytes 1572868
  392.4 15.3 %copy-start.13 = (f32[128]{0:T(128)S(1)}, f32[128]{0:T(128)}, u32[]{:S(2)}) copy-start(f32[128]{0:T(128)} %copy-done.12) | copy-start | bytes 1540
Sparse Core Ops, SparseCore 0:
  15.0 59.3 all-reduce.2
where the time goes:
time: 424 us; the launch traced here: 421 us
  waiting for transfers between devices  327 us (77%)
  matrix products  25.6 us (6%)
  other arithmetic  20.6 us (5%)
  starting transfers between devices  18.7 us (4%)
  local copies, waits for them, and re-layouts  14.8 us (3%)
  between operations  14.3 us (3%)
    all_to_all x1, waiting for transfers between devices, local(): lax.all_to_all(grad_received.reshape(outgoing.shape), 'dp', split_axis=0,...  176 us
    all_to_all x1, waiting for transfers between devices, local(): lax.all_to_all(outgoing, 'dp', split_axis=0, concat_axis=0, tiled=True)  90.9 us
    psum x1, waiting for transfers between devices, local(): q_raw, d_raw = lax.psum((q_part, d_part), 'phase')  59.3 us
    scatter-add x1, other arithmetic, local(): jax.ops.segment_sum(returned.reshape(-1, returned.shape[2]), requested.re...  15.3 us
    all_to_all x1, starting transfers between devices, local(): lax.all_to_all(outgoing, 'dp', split_axis=0, concat_axis=0, tiled=True)  11.2 us
  transfers between devices with their start and end apart: 3, of which 3 were waited for; matrix products, arithmetic and copies ran while one was open for 2% of the time, Pallas kernels for 0%

commit v1 on v0

v1 whole, which is shorter than its diff:
```python
import jax
import jax.numpy as jnp
from jax import lax
from jax.experimental import pallas as pl
from jax.experimental.pallas import tpu as pltpu
from jax.sharding import PartitionSpec as P

scale20 = 20.0
epsilon = 1e-06
f32 = jnp.float32
bf16 = jnp.bfloat16
NT = (((1,), (1,)), ((), ()))
TN = (((0,), (0,)), ((), ()))
N_PHASE = 4


def dot(a, b, dims=(((1,), (0,)), ((), ()))):
    return lax.dot_general(a, b, dims, preferred_element_type=f32)


def params():
    return pltpu.CompilerParams(vmem_limit_bytes=48 * 1024 * 1024)


def call(body, outs, *args):
    return pl.pallas_call(
        body,
        out_shape=[jax.ShapeDtypeStruct(s, t) for s, t in outs],
        compiler_params=params(),
    )(*args)


def iota(shape, dim):
    return lax.broadcasted_iota(jnp.int32, shape, dim)


def split_bf16(x):
    hi = x.astype(bf16)
    return hi, (x - hi.astype(f32)).astype(bf16)


def project(x, w, k):
    rows, depth = x.shape
    cols = w.shape[1] // N_PHASE

    def body(k_ref, x_ref, w_ref, own_ref, *send_refs):
        y = dot(x_ref[...], w_ref[...])
        step = pl.program_id(0)

        @pl.when(step == 0)
        def _():
            own_ref[...] = y

        for s in range(1, N_PHASE):

            @pl.when(step == s)
            def _():
                send_refs[s - 1][...] = y.astype(bf16)

    whole = pl.BlockSpec((rows, cols), lambda s, k_ref: (0, 0))
    return pl.pallas_call(
        body,
        grid_spec=pltpu.PrefetchScalarGridSpec(
            num_scalar_prefetch=1,
            grid=(N_PHASE,),
            in_specs=[
                pl.BlockSpec((rows, depth), lambda s, k_ref: (0, 0)),
                pl.BlockSpec((depth, cols), lambda s, k_ref: (0, lax.rem(k_ref[0] + s, N_PHASE))),
            ],
            out_specs=[whole] * N_PHASE,
        ),
        out_shape=[jax.ShapeDtypeStruct((rows, cols), f32)]
        + [jax.ShapeDtypeStruct((rows, cols), bf16)] * (N_PHASE - 1),
        compiler_params=params(),
    )(k, x, w)


def project_back(blocks, w, k):
    rows, cols = blocks[0].shape
    depth = w.shape[0]

    def body(k_ref, *refs):
        block_refs, w_ref, out_ref, acc_ref = refs[:N_PHASE], refs[N_PHASE], refs[N_PHASE + 1], refs[N_PHASE + 2]
        step = pl.program_id(0)

        @pl.when(step == 0)
        def _():
            acc_ref[...] = dot(block_refs[0][...], w_ref[...], NT)

        for s in range(1, N_PHASE):

            @pl.when(step == s)
            def _():
                acc_ref[...] += dot(block_refs[s][...], w_ref[...], NT)

        @pl.when(step == N_PHASE - 1)
        def _():
            out_ref[...] = acc_ref[...].astype(bf16)

    whole = pl.BlockSpec((rows, cols), lambda s, k_ref: (0, 0))
    return pl.pallas_call(
        body,
        grid_spec=pltpu.PrefetchScalarGridSpec(
            num_scalar_prefetch=1,
            grid=(N_PHASE,),
            in_specs=[whole] * N_PHASE
            + [pl.BlockSpec((depth, cols), lambda s, k_ref: (0, lax.rem(k_ref[0] + s, N_PHASE)))],
            out_specs=pl.BlockSpec((rows, depth), lambda s, k_ref: (0, 0)),
            scratch_shapes=[pltpu.VMEM((rows, depth), f32)],
        ),
        out_shape=jax.ShapeDtypeStruct((rows, depth), bf16),
        compiler_params=params(),
    )(k, *blocks, w)


def shift_sends(blocks):
    return [
        lax.ppermute(b, "phase", [(i, (i + s) % N_PHASE) for i in range(N_PHASE)])
        for s, b in enumerate(blocks, start=1)
    ]


def gather_blocks(x):
    return [x] + [
        lax.ppermute(x, "phase", [((i + s) % N_PHASE, i) for i in range(N_PHASE)]) for s in range(1, N_PHASE)
    ]


def sum_refs(refs):
    total = refs[0][...].astype(f32)
    for r in refs[1:]:
        total = total + r[...].astype(f32)
    return total


def sum_queries(own, a, b, c, total_ref, low_ref):
    total = sum_refs((own, a, b, c))
    total_ref[...] = total
    low_ref[...] = total.astype(bf16)


def sum_docs(own, a, b, c, request_ref, total_ref, rows_ref):
    total = sum_refs((own, a, b, c))
    total_ref[...] = total
    slots = rows_ref.shape[0]
    onehot = (iota((total.shape[0], slots), 0) == request_ref[...]).astype(f32).astype(bf16)
    rows_ref[...] = dot(onehot, total.astype(bf16), TN).astype(bf16)


def ones_row_sums(x):
    hi, lo = split_bf16(x)
    ones = jnp.ones((8, x.shape[1]), bf16)
    return dot(ones, hi, NT) + dot(ones, lo, NT)


def inner_partials(q_ref, d_ref, out_ref):
    q = q_ref[...]
    d = d_ref[...]
    q2 = jnp.concatenate([q, q], axis=0)
    docs = d.shape[0]
    out_ref[0:docs, :] = dot(d.astype(bf16), q2.astype(bf16), NT)
    out_ref[docs : docs + 8, :] = ones_row_sums(q2 * q2)
    out_ref[docs + 8 : docs + 16, :] = ones_row_sums(d * d)


def hard_partials(rows_ref, q_ref, neg_ref, out_ref):
    rows = rows_ref[...]
    q = q_ref[...]
    scores = dot(rows, jnp.concatenate([q, q], axis=0), NT)
    wide = rows.astype(f32)
    square = wide * wide
    lanes = scores.shape[1]
    folded = square[:, 0:lanes]
    for s in range(lanes, square.shape[1], lanes):
        folded = folded + square[:, s : s + lanes]
    hi, lo = split_bf16(folded)
    ones = jnp.ones((lanes, lanes), bf16)
    squares = dot(hi, ones) + dot(lo, ones)
    slot = iota(scores.shape, 0)
    for j in range(8):
        hit = slot == neg_ref[j : j + 1, :]
        out_ref[j : j + 1, :] = jnp.sum(jnp.where(hit, scores, 0.0), axis=0, keepdims=True)
        out_ref[8 + j : 9 + j, :] = jnp.sum(jnp.where(hit, squares, 0.0), axis=0, keepdims=True)


def softmax_terms(*refs):
    inner_refs, hard_refs = refs[0:4], refs[4:8]
    small_ref, neg_ref, coef_ref, local_ref, grad_ref, row_ref, col_ref = refs[8:]
    sums = sum_refs(inner_refs)
    picks = sum_refs(hard_refs)
    docs = grad_ref.shape[0]
    q_scale = lax.rsqrt(sums[docs : docs + 1, :] + epsilon)
    d_scale_row = lax.rsqrt(sums[docs + 8 : docs + 9, :] + epsilon)
    row = iota((docs, 128), 0)
    lane = iota((docs, 128), 1)
    d_scale = jnp.sum(jnp.where(row == lane, d_scale_row, 0.0), axis=1, keepdims=True)
    inner = scale20 * (sums[0:docs, :] * q_scale * d_scale)
    hard_scale = lax.rsqrt(picks[8:16, :] + epsilon)
    hard = scale20 * (picks[0:8, :] * q_scale * hard_scale)
    valid = small_ref[0:8, :]
    weight = scale20 * small_ref[8:9, :]
    hard_exp = jnp.exp(hard) * valid
    inner_exp = jnp.exp(inner)
    total = jnp.sum(inner_exp, axis=0, keepdims=True) + jnp.sum(hard_exp, axis=0, keepdims=True)
    own = row == lax.bitwise_and(lane, 63)
    positive = jnp.sum(jnp.where(own, inner, 0.0), axis=0, keepdims=True)
    factor = weight / total
    grad = (factor * inner_exp - jnp.where(own, weight, 0.0)).astype(bf16)
    grad_ref[...] = grad
    grad = grad.astype(f32)
    hard_grad = factor * hard_exp
    hard_dot = hard_grad * hard * (1.0 / scale20)
    products = grad * inner * (1.0 / scale20)
    row_ref[...] = jnp.zeros_like(row_ref)
    row_ref[0:1, :] = jnp.log(total) - positive
    row_ref[1:2, :] = q_scale
    row_ref[2:3, :] = jnp.sum(products, axis=0, keepdims=True) + jnp.sum(hard_dot, axis=0, keepdims=True)
    doc_dot = jnp.sum(jnp.where(lane < 64, products, 0.0), axis=1, keepdims=True)
    col_ref[...] = jnp.where(lane == 0, d_scale, doc_dot)
    sent = jnp.where(iota((8, 128), 1) < 64, hard_grad * q_scale, hard_dot)
    kept = hard_grad * hard_scale
    slots = coef_ref.shape[0]
    slot = iota((slots, 128), 0)
    coef = jnp.zeros((slots, 128), f32)
    local = jnp.zeros((slots, 128), f32)
    for j in range(7):
        hit = slot == neg_ref[j : j + 1, :]
        coef = coef + jnp.where(hit, sent[j : j + 1, :], 0.0)
        local = local + jnp.where(hit, kept[j : j + 1, :], 0.0)
    coef_ref[...] = coef.astype(bf16)
    local_ref[...] = local.astype(bf16)


def local_grads(grad_ref, local_ref, rows_ref, d_ref, q_ref, row_ref, col_ref, u_ref, g_ref):
    queries = q_ref.shape[0]
    d_low = (d_ref[...] * col_ref[:, 0:1]).astype(bf16)
    eye = iota((queries, 128), 0) == iota((queries, 128), 1)
    q_scale = jnp.sum(jnp.where(eye, row_ref[1:2, :], 0.0), axis=1, keepdims=True)
    q_dot = jnp.sum(jnp.where(eye, row_ref[2:3, :], 0.0), axis=1, keepdims=True)
    q_unit = q_ref[...] * q_scale
    q_low = q_unit.astype(bf16)
    grad = grad_ref[...]
    g = dot(grad, d_low, TN) + dot(local_ref[...], rows_ref[...], TN)
    u_ref[...] = (q_scale * (g[0:queries, :] - q_unit * q_dot)).astype(bf16)
    half = jnp.where(iota(grad.shape, 1) < 64, grad.astype(f32), 0.0).astype(bf16)
    g_ref[...] = dot(half, jnp.concatenate([q_low, q_low], axis=0))


def doc_grads(coef, requests, q_all, g_local, d_total, col):
    docs, cols = g_local.shape
    steps = 8
    slots = coef.shape[0] // steps
    queries = q_all.shape[0] // steps

    def body(coef_ref, request_ref, q_ref, g_ref, d_ref, col_ref, u_ref, acc_ref, dot_ref):
        step = pl.program_id(0)

        @pl.when(step == 0)
        def _():
            acc_ref[...] = g_ref[...]
            dot_ref[...] = jnp.zeros_like(dot_ref)

        onehot = (iota((docs, slots), 0) == request_ref[...]).astype(f32).astype(bf16)
        block = coef_ref[...]
        dot_ref[...] += dot(onehot, block)
        wide = block.astype(f32)
        lane = iota((slots, 128), 1)
        twice = jnp.where(lane < 64, wide, pltpu.roll(wide, 64, 1))
        source = lax.shift_right_logical(iota((slots, 128), 0), 4)
        part = lax.shift_right_logical(lane, 6)
        spread = jnp.concatenate(
            [jnp.where(source == part + 2 * s, twice, 0.0).astype(bf16) for s in range(queries // 128)], axis=1
        )
        mixed = dot(onehot, spread).astype(bf16)
        acc_ref[...] += dot(mixed, q_ref[...])

        @pl.when(step == steps - 1)
        def _():
            d_scale = col_ref[:, 0:1]
            far = jnp.where(iota((docs, 128), 1) < 64, 0.0, dot_ref[...])
            total = col_ref[:, 1:2] + jnp.sum(far, axis=1, keepdims=True)
            d_unit = d_ref[...] * d_scale
            u_ref[...] = (d_scale * (acc_ref[...] - d_unit * total)).astype(bf16)

    const = lambda shape: pl.BlockSpec(shape, lambda s: (0, 0))
    return pl.pallas_call(
        body,
        grid=(steps,),
        in_specs=[
            pl.BlockSpec((slots, 128), lambda s: (s, 0)),
            pl.BlockSpec((1, slots), lambda s: (0, s)),
            pl.BlockSpec((queries, cols), lambda s: (s, 0)),
            const((docs, cols)),
            const((docs, cols)),
            const((docs, 128)),
        ],
        out_specs=const((docs, cols)),
        out_shape=jax.ShapeDtypeStruct((docs, cols), bf16),
        scratch_shapes=[pltpu.VMEM((docs, cols), f32), pltpu.VMEM((docs, 128), f32)],
        compiler_params=params(),
    )(coef, requests, q_all, g_local, d_total, col)


def local(
    query_states,
    doc_states,
    query_proj,
    doc_proj,
    document_requests,
    slot_valid,
    neg_slot,
    query_weight,
):
    k = lax.axis_index("phase").astype(jnp.int32).reshape(1)
    queries, docs = query_states.shape[0], doc_states.shape[0]
    cols = query_proj.shape[1] // N_PHASE
    n_dp, cap = document_requests.shape[1:]
    slots = n_dp * cap

    negatives = neg_slot.T
    requests = document_requests.reshape(1, slots)
    neg_rows = jnp.pad(jnp.concatenate([negatives, negatives], axis=1), ((0, 1), (0, 0)), constant_values=-1)

    q_own, *q_send = project(query_states, query_proj, k)
    q_parts = shift_sends(q_send)
    d_own, *d_send = project(doc_states, doc_proj, k)
    d_parts = shift_sends(d_send)

    q_total, q_low = call(sum_queries, [((queries, cols), f32), ((queries, cols), bf16)], q_own, *q_parts)
    q_all = lax.all_gather(q_low, "dp", axis=0, tiled=True)

    d_total, outgoing = call(
        sum_docs, [((docs, cols), f32), ((slots, cols), bf16)], d_own, *d_parts, requests
    )
    received = lax.all_to_all(
        outgoing.reshape(n_dp, cap, cols), "dp", split_axis=0, concat_axis=0, tiled=True
    ).reshape(slots, cols)

    (inner,) = call(inner_partials, [((docs + 16, 128), f32)], q_total, d_total)
    inner_all = gather_blocks(inner)
    valid = jnp.take(slot_valid[0], negatives).astype(f32)
    weight = query_weight[None, :]
    small = jnp.pad(
        jnp.concatenate([valid, jnp.zeros_like(weight), weight], axis=0), ((0, 7), (0, 0))
    )
    small = jnp.concatenate([small, small], axis=1)

    (hard,) = call(hard_partials, [((16, 128), f32)], received, q_low, neg_rows)
    hard_all = gather_blocks(hard)
    coef, kept, grad, rows, columns = call(
        softmax_terms,
        [((slots, 128), bf16), ((slots, 128), bf16), ((docs, 128), bf16), ((8, 128), f32), ((docs, 128), f32)],
        *inner_all,
        *hard_all,
        small,
        neg_rows,
    )
    arrived = lax.all_to_all(
        coef.reshape(n_dp, cap, 128), "dp", split_axis=0, concat_axis=0, tiled=True
    ).reshape(slots, 128)

    u_query, g_local = call(
        local_grads,
        [((queries, cols), bf16), ((docs, cols), f32)],
        grad,
        kept,
        received,
        d_total,
        q_total,
        rows,
        columns,
    )
    grad_query = project_back(gather_blocks(u_query), query_proj, k)

    u_docs = doc_grads(arrived, requests, q_all, g_local, d_total, columns)
    grad_doc = project_back(gather_blocks(u_docs), doc_proj, k)
    return (rows[0, :queries], grad_query, grad_doc)


def solution(mesh):
    in_specs = (
        P("dp", "phase"),
        P("dp", "phase"),
        P("phase", None),
        P("phase", None),
        P("dp", None, None),
        P("dp", None),
        P("dp", None),
        P("dp"),
    )
    out_specs = (P("dp"), P("dp", "phase"), P("dp", "phase"))
    return jax.shard_map(local, mesh=mesh, in_specs=in_specs, out_specs=out_specs, check_vma=False)
```

time: 424 us -> 144 us (0.34)
  waiting for transfers between devices: 327 us -> 41.5 us
  matrix products: 25.6 us -> 0 us
  starting transfers between devices: 18.7 us -> 43.5 us
  Pallas kernels: 0 us -> 22.8 us
  other arithmetic: 20.6 us -> 1.01 us
  local copies, waits for them, and re-layouts: 14.8 us -> 19.4 us
    all_to_all x2, waiting for transfers between devices: 267 us -> 28.2 us  [the longest x1 21.9 us: local(): lax.all_to_all(outgoing.reshape(n_dp, cap, cols), 'dp', split_axis=0, con...]
    psum x1 -> x0, waiting for transfers between devices: 59.3 us -> none  [local(): q_raw, d_raw = lax.psum((q_part, d_part), 'phase')]
    dot_general x10 -> x0, matrix products: 25.6 us -> none  [the longest x1 4.75 us: local(): jnp.dot(u_docs, doc_proj.T, preferred_element_type=jnp.float32)]
    pallas_call x0 -> x11, Pallas kernels: none -> 22.8 us  [the longest x6 8.69 us: call(): pl.pallas_call(body, out_shape=[jax.ShapeDtypeStruct(s, t) for s, t in ou...]
    ppermute x0 -> x18, starting transfers between devices: none -> 19.9 us  [the longest x12 10.7 us: gather_blocks(): lax.ppermute(x, 'phase', [((i + s) % N_PHASE, i) for i in range(N_PHASE)])]
    scatter-add x1 -> x0, other arithmetic: 15.3 us -> none  [local(): jax.ops.segment_sum(returned.reshape(-1, returned.shape[2]), requested.re...]
    unnamed x31 -> x43, local copies, waits for them, and re-layouts: 1.69 us -> 15.8 us
    ppermute x0 -> x18, waiting for transfers between devices: none -> 13.3 us  [the longest x12 7.22 us: gather_blocks(): lax.ppermute(x, 'phase', [((i + s) % N_PHASE, i) for i in range(N_PHASE)])]
  transfers between devices with their start and end apart: 3 -> 21, of which waited for: 3 -> 11; matrix products, arithmetic and copies ran while one was open for 2% -> 3% of each run, Pallas kernels for 0% -> 13%
where the time goes in v1:
time: 144 us; the launch traced here: 142 us
  starting transfers between devices  43.5 us (30%)
  waiting for transfers between devices  41.5 us (29%)
  Pallas kernels  22.8 us (16%)
  local copies, waits for them, and re-layouts  19.4 us (13%)
  between operations  14.3 us (10%)
    all_to_all x1, waiting for transfers between devices, local(): lax.all_to_all(outgoing.reshape(n_dp, cap, cols), 'dp', split_axis=0, con...  21.9 us
    unnamed x43, local copies, waits for them, and re-layouts  15.8 us
    all_to_all x1, starting transfers between devices, local(): lax.all_to_all(outgoing.reshape(n_dp, cap, cols), 'dp', split_axis=0, con...  15.5 us
    ppermute x12, starting transfers between devices, gather_blocks(): lax.ppermute(x, 'phase', [((i + s) % N_PHASE, i) for i in range(N_PHASE)])  10.7 us
    ppermute x6, starting transfers between devices, shift_sends(): lax.ppermute(b, 'phase', [(i, (i + s) % N_PHASE) for i in range(N_PHASE)])  9.14 us
    pallas_call x6, Pallas kernels, call(): pl.pallas_call(body, out_shape=[jax.ShapeDtypeStruct(s, t) for s, t in ou...  8.69 us
    all_to_all x1, starting transfers between devices, local(): lax.all_to_all(coef.reshape(n_dp, cap, 128), 'dp', split_axis=0, concat_a...  8.12 us
    ppermute x12, waiting for transfers between devices, gather_blocks(): lax.ppermute(x, 'phase', [((i + s) % N_PHASE, i) for i in range(N_PHASE)])  7.22 us
  transfers between devices with their start and end apart: 21, of which 11 were waited for; matrix products, arithmetic and copies ran while one was open for 3% of the time, Pallas kernels for 13%

profile of v1, /device:TPU:1, one launch (start us, length us, event | category | flops | bytes accessed | tf_op | source)
XLA Modules:
  0.0 142.4 jit_solution(644026816751287909)
XLA Ops:
  7.3 1.6 %copy-done.3 = bf16[512,2048]{1,0:T(8,128)(2,1)S(1)} copy-done((bf16[512,2048]{1,0:T(8,128)(2,1)S(1)}, bf16[512,2048]{1,0:T(8,128)(2,1)}, u32[]{:S(2)}) %copy-start.3) | copy-done | bytes 2097176
  9.7 1.1 shard_map.103
  10.8 2.1 %collective-permute-start = (bf16[64,512]{1,0:T(8,128)(2,1)S(1)}, bf16[64,512]{1,0:T(8,128)(2,1)S(1)}, u32[]{:S(2)}, u32[]{:S(2)}) collective-permute-start(bf16[64,512]{1,0:T(8,128)(2,1)S(1)} %get-tuple-element.23), channel_id=1, source_target_pairs={{0,64},{64,128},{128,192},{192,0},{1,65},{65,129},{129,193},{193,1... | collective-permute-start | bytes 196616 | tf_op jit(solution)/shard_map/ppermute | solution.py:118
  12.9 2.5 %collective-permute-start.1 = (bf16[64,512]{1,0:T(8,128)(2,1)S(1)}, bf16[64,512]{1,0:T(8,128)(2,1)S(1)}, u32[]{:S(2)}, u32[]{:S(2)}) collective-permute-start(bf16[64,512]{1,0:T(8,128)(2,1)S(1)} %get-tuple-element.24), channel_id=1, source_target_pairs={{0,128},{64,192},{128,0},{192,64},{1,129},{65,193},{129,1},{193,65... | collective-permute-start | bytes 196616 | tf_op jit(solution)/shard_map/ppermute | solution.py:118
  15.4 1.2 collective-permute-start.2
  16.5 1.4 %collective-permute-done.1.b = bf16[64,512]{1,0:T(8,128)(2,1)S(1)} collective-permute-done((bf16[64,512]{1,0:T(8,128)(2,1)S(1)}, bf16[64,512]{1,0:T(8,128)(2,1)S(1)}, u32[]{:S(2)}, u32[]{:S(2)}) %collective-permute-start.1) | collective-permute-done | bytes 65568 | tf_op jit(solution)/shard_map/ppermute | solution.py:118
  19.5 2.2 %copy-done.1 = bf16[1024,2048]{1,0:T(8,128)(2,1)S(1)} copy-done((bf16[1024,2048]{1,0:T(8,128)(2,1)S(1)}, bf16[1024,2048]{1,0:T(8,128)(2,1)}, u32[]{:S(2)}) %copy-start.1) | copy-done | bytes 4194328
  22.6 1.7 %shard_map.105 = (f32[128,512]{1,0:T(8,128)S(1)}, bf16[128,512]{1,0:T(8,128)(2,1)S(1)}, bf16[128,512]{1,0:T(8,128)(2,1)S(1)}, bf16[128,512]{1,0:T(8,128)(2,1)S(1)}) custom-call(s32[1]{0:T(128)} %bitcast.k_ref, bf16[128,1024]{1,0:T(8,128)(2,1)S(1)} %copy-done.9, bf16[1024,2048]{1,0:T(8,128)(2,1)S(1)} %copy-done.1), custom_call_target="tpu_custom_call" | custom-call | tf_op jit(solution)/shard_map/pallas_call | solution.py:61
  24.5 3.2 %collective-permute-start.4 = (bf16[128,512]{1,0:T(8,128)(2,1)S(1)}, bf16[128,512]{1,0:T(8,128)(2,1)S(1)}, u32[]{:S(2)}, u32[]{:S(2)}) collective-permute-start(bf16[128,512]{1,0:T(8,128)(2,1)S(1)} %get-tuple-element.29), channel_id=1, source_target_pairs={{0,128},{64,192},{128,0},{192,64},{1,129},{65,193},{129,1},{193,65... | collective-permute-start | bytes 393224 | tf_op jit(solution)/shard_map/ppermute | solution.py:118
  28.0 1.5 %collective-permute-done.3.a = bf16[128,512]{1,0:T(8,128)(2,1)S(1)} collective-permute-done((bf16[128,512]{1,0:T(8,128)(2,1)S(1)}, bf16[128,512]{1,0:T(8,128)(2,1)S(1)}, u32[]{:S(2)}, u32[]{:S(2)}) %collective-permute-start.3) | collective-permute-done | bytes 131104 | tf_op jit(solution)/shard_map/ppermute | solution.py:118
  29.5 2.0 %collective-permute-done.4.b = bf16[128,512]{1,0:T(8,128)(2,1)S(1)} collective-permute-done((bf16[128,512]{1,0:T(8,128)(2,1)S(1)}, bf16[128,512]{1,0:T(8,128)(2,1)S(1)}, u32[]{:S(2)}, u32[]{:S(2)}) %collective-permute-start.4) | collective-permute-done | bytes 131104 | tf_op jit(solution)/shard_map/ppermute | solution.py:118
  31.8 1.5 %shard_map.106 = (f32[128,512]{1,0:T(8,128)S(1)}, bf16[1024,512]{1,0:T(8,128)(2,1)}) custom-call(f32[128,512]{1,0:T(8,128)S(1)} %get-tuple-element.27.own, bf16[128,512]{1,0:T(8,128)(2,1)S(1)} %collective-permute-done.3.a, bf16[128,512]{1,0:T(8,128)(2,1)S(1)} %collective-permute-done.4.b, bf16[128,512]{1,0:T(8,128)(2,1)S(1)} %collective-permute-done.5.c, ...), custom_call_target="tpu_custom_call" | custom-call | tf_op jit(solution)/shard_map/pallas_call | solution.py:26
  33.3 15.5 %all-to-all-start = ((bf16[64,16,512]{2,1,0:T(8,128)(2,1)}), bf16[64,16,512]{2,1,0:T(8,128)(2,1)S(1)}, u32[]{:S(2)}, u32[]{:S(2)}) async-start(bf16[64,16,512]{2,1,0:T(8,128)(2,1)} %bitcast.1), calls=%async_computation | async-start | bytes 2097152 | tf_op jit(solution)/shard_map/all_to_all | solution.py:335
  48.9 2.1 %gather_fusion = s32[448]{0:T(512)S(1)} fusion(s32[1024]{0:T(1024)S(1)} %bitcast.14, s32[1024]{0:T(1024)S(1)} %pad_clamp_fusion), kind=kCustom, calls=%fused_computation | custom fusion | bytes 5376 | tf_op jit(solution)/shard_map/jit(_take)/gather | solution.py:341
  52.7 2.1 %collective-permute-start.6 = (f32[144,128]{1,0:T(8,128)}, f32[144,128]{1,0:T(8,128)}, u32[]{:S(2)}, u32[]{:S(2)}) collective-permute-start(f32[144,128]{1,0:T(8,128)} %shard_map.107.refs_0_), channel_id=1, source_target_pairs={{64,0},{128,64},{192,128},{0,192},{65,1},{129,65},{193,129},{1,193... | collective-permute-start | bytes 221192 | tf_op jit(solution)/shard_map/ppermute | solution.py:125
  55.5 21.9 %all-to-all-done = bf16[64,16,512]{2,1,0:T(8,128)(2,1)S(1)} async-done(((bf16[64,16,512]{2,1,0:T(8,128)(2,1)}), bf16[64,16,512]{2,1,0:T(8,128)(2,1)S(1)}, u32[]{:S(2)}, u32[]{:S(2)}) %all-to-all-start) | async-done | bytes 1048608 | tf_op jit(solution)/shard_map/all_to_all | solution.py:335
  77.4 2.2 %shard_map.108.refs_4_ = f32[16,128]{1,0:T(8,128)S(1)} custom-call(bf16[1024,512]{1,0:T(8,128)(2,1)S(1)} %bitcast.15, bf16[64,512]{1,0:T(8,128)(2,1)} %get-tuple-element.33.q_ref, s32[8,128]{1,0:T(8,128)S(1)} %pad.8.neg_ref.refs_9_), custom_call_target="tpu_custom_call" | custom-call | tf_op jit(solution)/shard_map/pallas_call | solution.py:26
  79.6 2.1 %collective-permute-start.9 = (f32[16,128]{1,0:T(8,128)S(1)}, f32[16,128]{1,0:T(8,128)S(1)}, u32[]{:S(2)}, u32[]{:S(2)}) collective-permute-start(f32[16,128]{1,0:T(8,128)S(1)} %shard_map.108.refs_4_), channel_id=1, source_target_pairs={{64,0},{128,64},{192,128},{0,192},{65,1},{129,65},{193,129},{1,193... | collective-permute-start | bytes 24584 | tf_op jit(solution)/shard_map/ppermute | solution.py:125
  83.3 2.5 %collective-permute-done.10.refs_6_ = f32[16,128]{1,0:T(8,128)S(1)} collective-permute-done((f32[16,128]{1,0:T(8,128)S(1)}, f32[16,128]{1,0:T(8,128)S(1)}, u32[]{:S(2)}, u32[]{:S(2)}) %collective-permute-start.10) | collective-permute-done | bytes 8224 | tf_op jit(solution)/shard_map/ppermute | solution.py:125
  86.0 2.4 %shard_map.109 = (bf16[1024,128]{1,0:T(8,128)(2,1)S(1)}, bf16[1024,128]{1,0:T(8,128)(2,1)S(1)}, bf16[128,128]{1,0:T(8,128)(2,1)S(1)}, f32[8,128]{1,0:T(8,128)S(1)}, f32[128,128]{1,0:T(8,128)S(1)}) custom-call(f32[144,128]{1,0:T(8,128)} %shard_map.107.refs_0_, f32[144,128]{1,0:T(8,128)} %collective-permute-done.6.refs_1_, ...), custom_call_target="tpu_custom_call" | custom-call | tf_op jit(solution)/shard_map/pallas_call | solution.py:26
  91.1 8.1 %all-to-all-start.1 = ((bf16[64,16,128]{2,1,0:T(8,128)(2,1)}), bf16[64,16,128]{2,1,0:T(8,128)(2,1)}, u32[]{:S(2)}, u32[]{:S(2)}) async-start(bf16[64,16,128]{2,1,0:T(8,128)(2,1)} %bitcast.17), calls=%async_computation.1 | async-start | bytes 524288 | tf_op jit(solution)/shard_map/all_to_all | solution.py:358
  100.0 1.0 copy-done.13
  101.7 1.0 shard_map.110
  103.9 1.3 collective-permute-start.13
  106.0 6.2 %all-to-all-done.1 = bf16[64,16,128]{2,1,0:T(8,128)(2,1)} async-done(((bf16[64,16,128]{2,1,0:T(8,128)(2,1)}), bf16[64,16,128]{2,1,0:T(8,128)(2,1)}, u32[]{:S(2)}, u32[]{:S(2)}) %all-to-all-start.1) | async-done | bytes 262176 | tf_op jit(solution)/shard_map/all_to_all | solution.py:358
  112.3 2.3 %copy-done.5 = bf16[4096,512]{1,0:T(8,128)(2,1)S(1)} copy-done((bf16[4096,512]{1,0:T(8,128)(2,1)S(1)}, bf16[4096,512]{1,0:T(8,128)(2,1)}, u32[]{:S(2)}) %copy-start.5) | copy-done | bytes 4194328
  114.6 1.0 copy-done.8
  116.6 5.4 %shard_map.112.refs_0_ = bf16[128,512]{1,0:T(8,128)(2,1)S(1)} custom-call(bf16[1024,128]{1,0:T(8,128)(2,1)} %bitcast.8.coef_ref, s32[1,1024]{1,0:T(1,128)S(1)} %reshape.30.request_ref, bf16[4096,512]{1,0:T(8,128)(2,1)S(1)} %copy-done.5, f32[128,512]{1,0:T(8,128)S(1)} %copy-done.11, f32[128,512]{1,0:T(8,128)S(1)} %get-tuple-element.31.d_ref, ...), custom_call_target="tpu_custom_call" | custom-call | tf_op jit(solution)/shard_map/pallas_call | solution.py:286
  122.8 1.0 collective-permute-start.16
  125.1 2.9 %shard_map.111 = bf16[64,512]{1,0:T(8,128)(2,1)} custom-call(s32[1]{0:T(128)} %bitcast.k_ref, bf16[64,512]{1,0:T(8,128)(2,1)} %get-tuple-element.38.refs_0_, bf16[64,512]{1,0:T(8,128)(2,1)S(1)} %collective-permute-done.12.refs_1_, bf16[64,512]{1,0:T(8,128)(2,1)S(1)} %collective-permute-done.13.refs_2_, bf16[64,512]{1,0:T(8,128)(2,1)S(1)} %collective-permute-done.14.refs_3_, ...), custom_call_target="tpu_custom_call" | custom-call | tf_op jit(solution)/shard_map/pallas_call | solution.py:101
  128.7 3.8 %collective-permute-done.17.refs_3_ = bf16[128,512]{1,0:T(8,128)(2,1)S(1)} collective-permute-done((bf16[128,512]{1,0:T(8,128)(2,1)S(1)}, bf16[128,512]{1,0:T(8,128)(2,1)S(1)}, u32[]{:S(2)}, u32[]{:S(2)}) %collective-permute-start.17) | collective-permute-done | bytes 131104 | tf_op jit(solution)/shard_map/ppermute | solution.py:125
  132.5 3.1 %shard_map.113 = bf16[128,1024]{1,0:T(8,128)(2,1)} custom-call(s32[1]{0:T(128)} %bitcast.k_ref, bf16[128,512]{1,0:T(8,128)(2,1)S(1)} %shard_map.112.refs_0_, bf16[128,512]{1,0:T(8,128)(2,1)S(1)} %collective-permute-done.15.refs_1_, bf16[128,512]{1,0:T(8,128)(2,1)S(1)} %collective-permute-done.16.refs_2_, ...), custom_call_target="tpu_custom_call" | custom-call | tf_op jit(solution)/shard_map/pallas_call | solution.py:101
  (79 shorter events, 18.2 us)
Async XLA Ops:
  7.2 41.7 %copy-start = (s32[1,1024]{1,0:T(1,128)S(1)}, s32[1,1024]{1,0:T(1,128)}, u32[]{:S(2)}) copy-start(s32[1,1024]{1,0:T(1,128)} %param.13) | copy-start | bytes 12292
  7.2 20.6 %copy-start.19 = (s32[1,64,16]{1,2,0:T(8,128)S(1)}, s32[1,64,16]{1,2,0:T(8,128)}, u32[]{:S(2)}) copy-start(s32[1,64,16]{1,2,0:T(8,128)} %param.12) | copy-start | bytes 12292
  7.2 105.1 %all-gather.2.cloned.1.call-start = ((), (), s32[]{:S(2)}) async-start(), calls=%async_computation.2 | async-start | bytes 4259840 | tf_op jit(solution)/shard_map/all_gather | solution.py:330
  7.2 1.6 %copy-start.3 = (bf16[512,2048]{1,0:T(8,128)(2,1)S(1)}, bf16[512,2048]{1,0:T(8,128)(2,1)}, u32[]{:S(2)}) copy-start(bf16[512,2048]{1,0:T(8,128)(2,1)} %refs_4_.2) | copy-start | bytes 6291460
  10.8 38.0 %copy-start.18 = (s32[64,7]{0,1:T(8,128)S(1)}, s32[64,7]{0,1:T(8,128)}, u32[]{:S(2)}) copy-start(s32[64,7]{0,1:T(8,128)} %param.14) | copy-start | bytes 5380
  10.8 5.7 %collective-permute-start = (bf16[64,512]{1,0:T(8,128)(2,1)S(1)}, bf16[64,512]{1,0:T(8,128)(2,1)S(1)}, u32[]{:S(2)}, u32[]{:S(2)}) collective-permute-start(bf16[64,512]{1,0:T(8,128)(2,1)S(1)} %get-tuple-element.23), channel_id=1, source_target_pairs={{0,64},{64,128},{128,192},{192,0},{1,65},{65,129},{129,193},{193,1... | collective-permute-start | bytes 196616 | tf_op jit(solution)/shard_map/ppermute | solution.py:118
  12.9 5.1 %collective-permute-start.1 = (bf16[64,512]{1,0:T(8,128)(2,1)S(1)}, bf16[64,512]{1,0:T(8,128)(2,1)S(1)}, u32[]{:S(2)}, u32[]{:S(2)}) collective-permute-start(bf16[64,512]{1,0:T(8,128)(2,1)S(1)} %get-tuple-element.24), channel_id=1, source_target_pairs={{0,128},{64,192},{128,0},{192,64},{1,129},{65,193},{129,1},{193,65... | collective-permute-start | bytes 196616 | tf_op jit(solution)/shard_map/ppermute | solution.py:118
  15.4 3.4 %collective-permute-start.2 = (bf16[64,512]{1,0:T(8,128)(2,1)S(1)}, bf16[64,512]{1,0:T(8,128)(2,1)S(1)}, u32[]{:S(2)}, u32[]{:S(2)}) collective-permute-start(bf16[64,512]{1,0:T(8,128)(2,1)S(1)} %get-tuple-element.25), channel_id=1, source_target_pairs={{0,192},{64,0},{128,64},{192,128},{1,193},{65,1},{129,65},{193,129... | collective-permute-start | bytes 196616 | tf_op jit(solution)/shard_map/ppermute | solution.py:118
  19.5 2.2 %copy-start.1 = (bf16[1024,2048]{1,0:T(8,128)(2,1)S(1)}, bf16[1024,2048]{1,0:T(8,128)(2,1)}, u32[]{:S(2)}) copy-start(bf16[1024,2048]{1,0:T(8,128)(2,1)} %refs_4_.3) | copy-start | bytes 12582916
  24.4 26.8 %copy-start.20 = (f32[64]{0:T(128)S(1)}, f32[64]{0:T(128)}, u32[]{:S(2)}) copy-start(f32[64]{0:T(128)} %param.15) | copy-start | bytes 772
  24.4 5.1 %collective-permute-start.3 = (bf16[128,512]{1,0:T(8,128)(2,1)S(1)}, bf16[128,512]{1,0:T(8,128)(2,1)S(1)}, u32[]{:S(2)}, u32[]{:S(2)}) collective-permute-start(bf16[128,512]{1,0:T(8,128)(2,1)S(1)} %get-tuple-element.28), channel_id=1, source_target_pairs={{0,64},{64,128},{128,192},{192,0},{1,65},{65,129},{129,193},{193,1... | collective-permute-start | bytes 393224 | tf_op jit(solution)/shard_map/ppermute | solution.py:118
  24.5 7.1 %collective-permute-start.4 = (bf16[128,512]{1,0:T(8,128)(2,1)S(1)}, bf16[128,512]{1,0:T(8,128)(2,1)S(1)}, u32[]{:S(2)}, u32[]{:S(2)}) collective-permute-start(bf16[128,512]{1,0:T(8,128)(2,1)S(1)} %get-tuple-element.29), channel_id=1, source_target_pairs={{0,128},{64,192},{128,0},{192,64},{1,129},{65,193},{129,1},{193,65... | collective-permute-start | bytes 393224 | tf_op jit(solution)/shard_map/ppermute | solution.py:118
  27.7 4.1 %collective-permute-start.5 = (bf16[128,512]{1,0:T(8,128)(2,1)S(1)}, bf16[128,512]{1,0:T(8,128)(2,1)S(1)}, u32[]{:S(2)}, u32[]{:S(2)}) collective-permute-start(bf16[128,512]{1,0:T(8,128)(2,1)S(1)} %get-tuple-element.30), channel_id=1, source_target_pairs={{0,192},{64,0},{128,64},{192,128},{1,193},{65,1},{129,65},{193,129... | collective-permute-start | bytes 393224 | tf_op jit(solution)/shard_map/ppermute | solution.py:118
  33.3 44.1 %all-to-all-start = ((bf16[64,16,512]{2,1,0:T(8,128)(2,1)}), bf16[64,16,512]{2,1,0:T(8,128)(2,1)S(1)}, u32[]{:S(2)}, u32[]{:S(2)}) async-start(bf16[64,16,512]{2,1,0:T(8,128)(2,1)} %bitcast.1), calls=%async_computation | async-start | bytes 2097152 | tf_op jit(solution)/shard_map/all_to_all | solution.py:335
  52.7 29.1 %collective-permute-start.6 = (f32[144,128]{1,0:T(8,128)}, f32[144,128]{1,0:T(8,128)}, u32[]{:S(2)}, u32[]{:S(2)}) collective-permute-start(f32[144,128]{1,0:T(8,128)} %shard_map.107.refs_0_), channel_id=1, source_target_pairs={{64,0},{128,64},{192,128},{0,192},{65,1},{129,65},{193,129},{1,193... | collective-permute-start | bytes 221192 | tf_op jit(solution)/shard_map/ppermute | solution.py:125
  54.9 28.4 %collective-permute-start.7 = (f32[144,128]{1,0:T(8,128)}, f32[144,128]{1,0:T(8,128)}, u32[]{:S(2)}, u32[]{:S(2)}) collective-permute-start(f32[144,128]{1,0:T(8,128)} %shard_map.107.refs_0_), channel_id=1, source_target_pairs={{128,0},{192,64},{0,128},{64,192},{129,1},{193,65},{1,129},{65,193... | collective-permute-start | bytes 221192 | tf_op jit(solution)/shard_map/ppermute | solution.py:125
  54.9 28.4 %collective-permute-start.8 = (f32[144,128]{1,0:T(8,128)}, f32[144,128]{1,0:T(8,128)}, u32[]{:S(2)}, u32[]{:S(2)}) collective-permute-start(f32[144,128]{1,0:T(8,128)} %shard_map.107.refs_0_), channel_id=1, source_target_pairs={{192,0},{0,64},{64,128},{128,192},{193,1},{1,65},{65,129},{129,193... | collective-permute-start | bytes 221192 | tf_op jit(solution)/shard_map/ppermute | solution.py:125
  79.6 45.5 %copy-start.4 = (bf16[512,2048]{1,0:T(8,128)(2,1)S(1)}, bf16[512,2048]{1,0:T(8,128)(2,1)}, u32[]{:S(2)}) copy-start(bf16[512,2048]{1,0:T(8,128)(2,1)} %refs_4_.2) | copy-start | bytes 6291460
  79.6 3.7 %collective-permute-start.9 = (f32[16,128]{1,0:T(8,128)S(1)}, f32[16,128]{1,0:T(8,128)S(1)}, u32[]{:S(2)}, u32[]{:S(2)}) collective-permute-start(f32[16,128]{1,0:T(8,128)S(1)} %shard_map.108.refs_4_), channel_id=1, source_target_pairs={{64,0},{128,64},{192,128},{0,192},{65,1},{129,65},{193,129},{1,193... | collective-permute-start | bytes 24584 | tf_op jit(solution)/shard_map/ppermute | solution.py:125
  81.8 4.1 %collective-permute-start.10 = (f32[16,128]{1,0:T(8,128)S(1)}, f32[16,128]{1,0:T(8,128)S(1)}, u32[]{:S(2)}, u32[]{:S(2)}) collective-permute-start(f32[16,128]{1,0:T(8,128)S(1)} %shard_map.108.refs_4_), channel_id=1, source_target_pairs={{128,0},{192,64},{0,128},{64,192},{129,1},{193,65},{1,129},{65,193... | collective-permute-start | bytes 24584 | tf_op jit(solution)/shard_map/ppermute | solution.py:125
  81.9 4.1 %collective-permute-start.11 = (f32[16,128]{1,0:T(8,128)S(1)}, f32[16,128]{1,0:T(8,128)S(1)}, u32[]{:S(2)}, u32[]{:S(2)}) collective-permute-start(f32[16,128]{1,0:T(8,128)S(1)} %shard_map.108.refs_4_), channel_id=1, source_target_pairs={{192,0},{0,64},{64,128},{128,192},{193,1},{1,65},{65,129},{129,193... | collective-permute-start | bytes 24584 | tf_op jit(solution)/shard_map/ppermute | solution.py:125
  91.1 21.2 %all-to-all-start.1 = ((bf16[64,16,128]{2,1,0:T(8,128)(2,1)}), bf16[64,16,128]{2,1,0:T(8,128)(2,1)}, u32[]{:S(2)}, u32[]{:S(2)}) async-start(bf16[64,16,128]{2,1,0:T(8,128)(2,1)} %bitcast.17), calls=%async_computation.1 | async-start | bytes 524288 | tf_op jit(solution)/shard_map/all_to_all | solution.py:358
  100.0 1.0 copy-start.13
  103.4 20.4 %collective-permute-start.12 = (bf16[64,512]{1,0:T(8,128)(2,1)}, bf16[64,512]{1,0:T(8,128)(2,1)S(1)}, u32[]{:S(2)}, u32[]{:S(2)}) collective-permute-start(bf16[64,512]{1,0:T(8,128)(2,1)} %get-tuple-element.38.refs_0_), channel_id=1, source_target_pairs={{64,0},{128,64},{192,128},{0,192},{65,1},{129,65},{193,129},{1,193... | collective-permute-start | bytes 196616 | tf_op jit(solution)/shard_map/ppermute | solution.py:125
  103.9 21.2 %collective-permute-start.13 = (bf16[64,512]{1,0:T(8,128)(2,1)}, bf16[64,512]{1,0:T(8,128)(2,1)S(1)}, u32[]{:S(2)}, u32[]{:S(2)}) collective-permute-start(bf16[64,512]{1,0:T(8,128)(2,1)} %get-tuple-element.38.refs_0_), channel_id=1, source_target_pairs={{128,0},{192,64},{0,128},{64,192},{129,1},{193,65},{1,129},{65,193... | collective-permute-start | bytes 196616 | tf_op jit(solution)/shard_map/ppermute | solution.py:125
  105.2 20.0 %collective-permute-start.14 = (bf16[64,512]{1,0:T(8,128)(2,1)}, bf16[64,512]{1,0:T(8,128)(2,1)S(1)}, u32[]{:S(2)}, u32[]{:S(2)}) collective-permute-start(bf16[64,512]{1,0:T(8,128)(2,1)} %get-tuple-element.38.refs_0_), channel_id=1, source_target_pairs={{192,0},{0,64},{64,128},{128,192},{193,1},{1,65},{65,129},{129,193... | collective-permute-start | bytes 196616 | tf_op jit(solution)/shard_map/ppermute | solution.py:125
  112.3 20.2 %copy-start.2 = (bf16[1024,2048]{1,0:T(8,128)(2,1)S(1)}, bf16[1024,2048]{1,0:T(8,128)(2,1)}, u32[]{:S(2)}) copy-start(bf16[1024,2048]{1,0:T(8,128)(2,1)} %refs_4_.3) | copy-start | bytes 12582916
  112.3 2.3 %copy-start.5 = (bf16[4096,512]{1,0:T(8,128)(2,1)S(1)}, bf16[4096,512]{1,0:T(8,128)(2,1)}, u32[]{:S(2)}) copy-start(bf16[4096,512]{1,0:T(8,128)(2,1)} %all-gather.2.cloned.1.call-done.q_ref) | copy-start | bytes 12582916
  114.6 1.0 copy-start.8
  122.0 6.0 %collective-permute-start.15 = (bf16[128,512]{1,0:T(8,128)(2,1)S(1)}, bf16[128,512]{1,0:T(8,128)(2,1)S(1)}, u32[]{:S(2)}, u32[]{:S(2)}) collective-permute-start(bf16[128,512]{1,0:T(8,128)(2,1)S(1)} %shard_map.112.refs_0_), channel_id=1, source_target_pairs={{64,0},{128,64},{192,128},{0,192},{65,1},{129,65},{193,129},{1,193... | collective-permute-start | bytes 393224 | tf_op jit(solution)/shard_map/ppermute | solution.py:125
  122.8 5.9 %collective-permute-start.16 = (bf16[128,512]{1,0:T(8,128)(2,1)S(1)}, bf16[128,512]{1,0:T(8,128)(2,1)S(1)}, u32[]{:S(2)}, u32[]{:S(2)}) collective-permute-start(bf16[128,512]{1,0:T(8,128)(2,1)S(1)} %shard_map.112.refs_0_), channel_id=1, source_target_pairs={{128,0},{192,64},{0,128},{64,192},{129,1},{193,65},{1,129},{65,193... | collective-permute-start | bytes 393224 | tf_op jit(solution)/shard_map/ppermute | solution.py:125
  123.9 8.7 %collective-permute-start.17 = (bf16[128,512]{1,0:T(8,128)(2,1)S(1)}, bf16[128,512]{1,0:T(8,128)(2,1)S(1)}, u32[]{:S(2)}, u32[]{:S(2)}) collective-permute-start(bf16[128,512]{1,0:T(8,128)(2,1)S(1)} %shard_map.112.refs_0_), channel_id=1, source_target_pairs={{192,0},{0,64},{64,128},{128,192},{193,1},{1,65},{65,129},{129,193... | collective-permute-start | bytes 393224 | tf_op jit(solution)/shard_map/ppermute | solution.py:125
  (10 other events, 7.7 us)
Sparse Core Ops, SparseCore 0:
  19.6 87.6 all-gather.1

commit v2 on v1

v2 whole, which is shorter than its diff:
```python
import jax
import jax.numpy as jnp
from jax import lax
from jax.experimental import pallas as pl
from jax.experimental.pallas import tpu as pltpu
from jax.sharding import PartitionSpec as P

scale20 = 20.0
epsilon = 1e-06
f32 = jnp.float32
bf16 = jnp.bfloat16
NT = (((1,), (1,)), ((), ()))
TN = (((0,), (0,)), ((), ()))
N_PHASE = 4
cost = pl.CostEstimate(flops=10**9, bytes_accessed=10**5, transcendentals=0)


def dot(a, b, dims=(((1,), (0,)), ((), ()))):
    return lax.dot_general(a, b, dims, preferred_element_type=f32)


def params():
    return pltpu.CompilerParams(vmem_limit_bytes=48 * 1024 * 1024)


def call(body, outs, *args):
    return pl.pallas_call(
        body,
        out_shape=[jax.ShapeDtypeStruct(s, t) for s, t in outs],
        compiler_params=params(),
        cost_estimate=cost,
    )(*args)


def iota(shape, dim):
    return lax.broadcasted_iota(jnp.int32, shape, dim)


def split_bf16(x):
    hi = x.astype(bf16)
    return hi, (x - hi.astype(f32)).astype(bf16)


def project(x, w, k):
    rows, depth = x.shape
    cols = w.shape[1] // N_PHASE

    def body(k_ref, x_ref, w_ref, own_ref, *refs):
        send_refs, buf_ref, sem_ref = refs[: N_PHASE - 1], refs[N_PHASE - 1], refs[N_PHASE]

        def copy(s):
            start = pl.multiple_of(lax.rem(k_ref[0] + s, N_PHASE) * cols, cols)
            return pltpu.make_async_copy(w_ref.at[:, pl.ds(start, cols)], buf_ref.at[s], sem_ref.at[s])

        for s in range(N_PHASE):
            copy(s).start()
        for s in range(N_PHASE):
            copy(s).wait()
            y = dot(x_ref[...], buf_ref[s])
            if s == 0:
                own_ref[...] = y
            else:
                send_refs[s - 1][...] = y.astype(bf16)

    vmem = pl.BlockSpec(memory_space=pltpu.VMEM)
    return pl.pallas_call(
        body,
        in_specs=[pl.BlockSpec(memory_space=pltpu.SMEM), vmem, pl.BlockSpec(memory_space=pltpu.HBM)],
        out_specs=[vmem] * N_PHASE,
        out_shape=[jax.ShapeDtypeStruct((rows, cols), f32)]
        + [jax.ShapeDtypeStruct((rows, cols), bf16)] * (N_PHASE - 1),
        scratch_shapes=[pltpu.VMEM((N_PHASE, depth, cols), bf16), pltpu.SemaphoreType.DMA((N_PHASE,))],
        compiler_params=params(),
        cost_estimate=cost,
    )(k, x, w)


def project_back_own(block, w, k):
    rows, cols = block.shape
    depth = w.shape[0]

    def body(k_ref, u_ref, w_ref, acc_ref):
        acc_ref[...] = dot(u_ref[...], w_ref[...], NT)

    return pl.pallas_call(
        body,
        grid_spec=pltpu.PrefetchScalarGridSpec(
            num_scalar_prefetch=1,
            grid=(1,),
            in_specs=[
                pl.BlockSpec((rows, cols), lambda s, k_ref: (0, 0)),
                pl.BlockSpec((depth, cols), lambda s, k_ref: (0, k_ref[0])),
            ],
            out_specs=pl.BlockSpec((rows, depth), lambda s, k_ref: (0, 0)),
        ),
        out_shape=jax.ShapeDtypeStruct((rows, depth), f32),
        compiler_params=params(),
        cost_estimate=cost,
    )(k, block, w)


def project_back_rest(acc, blocks, w, k):
    rows, cols = blocks[0].shape
    depth = w.shape[0]

    def body(k_ref, in_ref, *refs):
        block_refs, w_ref, out_ref, acc_ref = refs[:3], refs[3], refs[4], refs[5]
        step = pl.program_id(0)
        for s in range(N_PHASE - 1):

            @pl.when(step == s)
            def _():
                before = in_ref if s == 0 else acc_ref
                total = before[...] + dot(block_refs[s][...], w_ref[...], NT)
                if s == N_PHASE - 2:
                    out_ref[...] = total.astype(bf16)
                else:
                    acc_ref[...] = total

    const = lambda shape: pl.BlockSpec(shape, lambda s, k_ref: (0, 0))
    return pl.pallas_call(
        body,
        grid_spec=pltpu.PrefetchScalarGridSpec(
            num_scalar_prefetch=1,
            grid=(N_PHASE - 1,),
            in_specs=[const((rows, depth))]
            + [const((rows, cols))] * (N_PHASE - 1)
            + [pl.BlockSpec((depth, cols), lambda s, k_ref: (0, lax.rem(k_ref[0] + s + 1, N_PHASE)))],
            out_specs=const((rows, depth)),
            scratch_shapes=[pltpu.VMEM((rows, depth), f32)],
        ),
        out_shape=jax.ShapeDtypeStruct((rows, depth), bf16),
        compiler_params=params(),
        cost_estimate=cost,
    )(k, acc, *blocks, w)


def project_back(u, w, k):
    return project_back_rest(project_back_own(u, w, k), gather_blocks(u)[1:], w, k)


def shift_sends(blocks):
    return [
        lax.ppermute(b, "phase", [(i, (i + s) % N_PHASE) for i in range(N_PHASE)])
        for s, b in enumerate(blocks, start=1)
    ]


def gather_blocks(x):
    return [x] + [
        lax.ppermute(x, "phase", [((i + s) % N_PHASE, i) for i in range(N_PHASE)]) for s in range(1, N_PHASE)
    ]


def sum_refs(refs):
    total = refs[0][...].astype(f32)
    for r in refs[1:]:
        total = total + r[...].astype(f32)
    return total


def sum_queries(own, a, b, c, total_ref, low_ref):
    total = sum_refs((own, a, b, c))
    total_ref[...] = total
    low_ref[...] = total.astype(bf16)


def sum_docs(own, a, b, c, request_ref, total_ref, rows_ref):
    total = sum_refs((own, a, b, c))
    total_ref[...] = total
    slots = rows_ref.shape[0]
    onehot = (iota((total.shape[0], slots), 0) == request_ref[...]).astype(f32).astype(bf16)
    rows_ref[...] = dot(onehot, total.astype(bf16), TN).astype(bf16)


def ones_row_sums(x):
    hi, lo = split_bf16(x)
    ones = jnp.ones((8, x.shape[1]), bf16)
    return dot(ones, hi, NT) + dot(ones, lo, NT)


def inner_partials(q_ref, d_ref, out_ref):
    q = q_ref[...]
    d = d_ref[...]
    q2 = jnp.concatenate([q, q], axis=0)
    docs = d.shape[0]
    out_ref[0:docs, :] = dot(d.astype(bf16), q2.astype(bf16), NT)
    out_ref[docs : docs + 8, :] = ones_row_sums(q2 * q2)
    out_ref[docs + 8 : docs + 16, :] = ones_row_sums(d * d)


def hard_partials(rows_ref, q_ref, neg_ref, out_ref):
    rows = rows_ref[...]
    q = q_ref[...]
    scores = dot(rows, jnp.concatenate([q, q], axis=0), NT)
    wide = rows.astype(f32)
    square = wide * wide
    lanes = scores.shape[1]
    folded = square[:, 0:lanes]
    for s in range(lanes, square.shape[1], lanes):
        folded = folded + square[:, s : s + lanes]
    hi, lo = split_bf16(folded)
    ones = jnp.ones((lanes, lanes), bf16)
    squares = dot(hi, ones) + dot(lo, ones)
    slot = iota(scores.shape, 0)
    for j in range(8):
        hit = slot == neg_ref[j : j + 1, :]
        out_ref[j : j + 1, :] = jnp.sum(jnp.where(hit, scores, 0.0), axis=0, keepdims=True)
        out_ref[8 + j : 9 + j, :] = jnp.sum(jnp.where(hit, squares, 0.0), axis=0, keepdims=True)


def softmax_terms(*refs):
    inner_refs, hard_refs = refs[0:4], refs[4:8]
    small_ref, neg_ref, rows_ref, d_ref, q_ref, out_ref, u_ref, g_ref, loss_ref = refs[8:]
    sums = sum_refs(inner_refs)
    picks = sum_refs(hard_refs)
    docs, queries = d_ref.shape[0], q_ref.shape[0]
    q_scale = lax.rsqrt(sums[docs : docs + 1, :] + epsilon)
    d_scale_row = lax.rsqrt(sums[docs + 8 : docs + 9, :] + epsilon)
    row = iota((docs, 128), 0)
    lane = iota((docs, 128), 1)
    d_scale = jnp.sum(jnp.where(row == lane, d_scale_row, 0.0), axis=1, keepdims=True)
    inner = scale20 * (sums[0:docs, :] * q_scale * d_scale)
    hard_scale = lax.rsqrt(picks[8:16, :] + epsilon)
    hard = scale20 * (picks[0:8, :] * q_scale * hard_scale)
    valid = small_ref[0:8, :]
    weight = scale20 * small_ref[8:9, :]
    hard_exp = jnp.exp(hard) * valid
    inner_exp = jnp.exp(inner)
    total = jnp.sum(inner_exp, axis=0, keepdims=True) + jnp.sum(hard_exp, axis=0, keepdims=True)
    own = row == lax.bitwise_and(lane, 63)
    positive = jnp.sum(jnp.where(own, inner, 0.0), axis=0, keepdims=True)
    loss_ref[...] = jnp.broadcast_to(jnp.log(total) - positive, loss_ref.shape)
    factor = weight / total
    grad = (factor * inner_exp - jnp.where(own, weight, 0.0)).astype(bf16)
    wide_grad = grad.astype(f32)
    hard_grad = factor * hard_exp
    hard_dot = hard_grad * hard * (1.0 / scale20)
    products = wide_grad * inner * (1.0 / scale20)
    q_dot = jnp.sum(products, axis=0, keepdims=True) + jnp.sum(hard_dot, axis=0, keepdims=True)
    d_dot = jnp.sum(jnp.where(lane < 64, products, 0.0), axis=1, keepdims=True)
    sent = hard_scale * jnp.where(iota((8, 128), 1) < 64, hard_grad, hard_dot * hard_scale)
    slots = out_ref.shape[0]
    slot = iota((slots, 128), 0)
    coef = jnp.zeros((slots, 128), f32)
    for j in range(7):
        coef = coef + jnp.where(slot == neg_ref[j : j + 1, :], sent[j : j + 1, :], 0.0)
    coef = coef.astype(bf16)

    eye = iota((queries, 128), 0) == iota((queries, 128), 1)
    q_scale_col = jnp.sum(jnp.where(eye, q_scale, 0.0), axis=1, keepdims=True)
    q_dot_col = jnp.sum(jnp.where(eye, q_dot, 0.0), axis=1, keepdims=True)
    q_unit = q_ref[...] * q_scale_col
    q_low = jnp.concatenate([q_unit.astype(bf16), jnp.zeros(q_ref.shape, bf16)], axis=0)
    second = (iota((128, 128), 0) >= 64).astype(f32).astype(bf16)
    along = dot(coef, second)
    mixed = dot(coef, q_low)
    for s in range(0, mixed.shape[1], 128):
        part = rows_ref[:, s : s + 128].astype(f32)
        out_ref[:, s : s + 128] = (mixed[:, s : s + 128] - along * part).astype(bf16)

    d_unit = d_ref[...] * d_scale
    g_query = dot(grad, d_unit.astype(bf16), TN) + dot(coef, rows_ref[...], TN)
    u_ref[...] = (q_scale_col * (g_query[0:queries, :] - q_unit * q_dot_col)).astype(bf16)
    g_ref[...] = d_scale * (dot(grad, q_low) - d_unit * d_dot)


def doc_grads(rows_ref, request_ref, g_ref, u_ref):
    docs, slots = g_ref.shape[0], rows_ref.shape[0]
    onehot = (iota((docs, slots), 0) == request_ref[...]).astype(f32).astype(bf16)
    u_ref[...] = (g_ref[...] + dot(onehot, rows_ref[...])).astype(bf16)


def local(
    query_states,
    doc_states,
    query_proj,
    doc_proj,
    document_requests,
    slot_valid,
    neg_slot,
    query_weight,
):
    k = lax.axis_index("phase").astype(jnp.int32).reshape(1)
    queries, docs = query_states.shape[0], doc_states.shape[0]
    cols = query_proj.shape[1] // N_PHASE
    n_dp, cap = document_requests.shape[1:]
    slots = n_dp * cap

    negatives = neg_slot.T
    requests = document_requests.reshape(1, slots)
    neg_rows = jnp.pad(jnp.concatenate([negatives, negatives], axis=1), ((0, 1), (0, 0)), constant_values=-1)

    d_own, *d_send = project(doc_states, doc_proj, k)
    d_parts = shift_sends(d_send)
    d_total, outgoing = call(
        sum_docs, [((docs, cols), f32), ((slots, cols), bf16)], d_own, *d_parts, requests
    )
    outgoing, query_states = lax.optimization_barrier((outgoing, query_states))
    received = lax.all_to_all(
        outgoing.reshape(n_dp, cap, cols), "dp", split_axis=0, concat_axis=0, tiled=True
    ).reshape(slots, cols)

    q_own, *q_send = project(query_states, query_proj, k)
    q_parts = shift_sends(q_send)
    q_total, q_low = call(sum_queries, [((queries, cols), f32), ((queries, cols), bf16)], q_own, *q_parts)
    (inner,) = call(inner_partials, [((docs + 16, 128), f32)], q_total, d_total)
    inner_all = gather_blocks(inner)
    valid = jnp.take(slot_valid[0], negatives).astype(f32)
    weight = query_weight[None, :]
    small = jnp.pad(
        jnp.concatenate([valid, jnp.zeros_like(weight), weight], axis=0), ((0, 7), (0, 0))
    )
    small = jnp.concatenate([small, small], axis=1)
    received, small, neg_rows = lax.optimization_barrier((received, small, neg_rows))

    (hard,) = call(hard_partials, [((16, 128), f32)], received, q_low, neg_rows)
    hard_all = gather_blocks(hard)
    rows, u_query, g_local, loss = call(
        softmax_terms,
        [((slots, cols), bf16), ((queries, cols), bf16), ((docs, cols), f32), ((8, 128), f32)],
        *inner_all,
        *hard_all,
        small,
        neg_rows,
        received,
        d_total,
        q_total,
    )
    arrived = lax.all_to_all(
        rows.reshape(n_dp, cap, cols), "dp", split_axis=0, concat_axis=0, tiled=True
    ).reshape(slots, cols)
    grad_query = project_back(u_query, query_proj, k)

    (u_docs,) = call(doc_grads, [((docs, cols), bf16)], arrived, requests, g_local)
    grad_doc = project_back(u_docs, doc_proj, k)
    return (loss[0, :queries], grad_query, grad_doc)


def solution(mesh):
    in_specs = (
        P("dp", "phase"),
        P("dp", "phase"),
        P("phase", None),
        P("phase", None),
        P("dp", None, None),
        P("dp", None),
        P("dp", None),
        P("dp"),
    )
    out_specs = (P("dp"), P("dp", "phase"), P("dp", "phase"))
    return jax.shard_map(local, mesh=mesh, in_specs=in_specs, out_specs=out_specs, check_vma=False)
```

time: 144 us -> 121 us (0.84)
  between operations: 14.3 us -> 0.84 us
  Pallas kernels: 22.8 us -> 13.6 us
  local copies, waits for them, and re-layouts: 19.4 us -> 12.8 us
  waiting for transfers between devices: 41.5 us -> 45.5 us
  starting transfers between devices: 43.5 us -> 47.1 us
    all_to_all x1, waiting for transfers between devices: 6.23 us -> 22.8 us  [local(): lax.all_to_all(rows.reshape(n_dp, cap, cols), 'dp', split_axis=0, concat_...]
    all_to_all x1, waiting for transfers between devices: 21.9 us -> 12.5 us  [local(): lax.all_to_all(outgoing.reshape(n_dp, cap, cols), 'dp', split_axis=0, con...]
    pallas_call x5 -> x6, Pallas kernels: 14.2 us -> 7.99 us  [the longest x2 4.15 us: project_back_rest(): pl.pallas_call(body, grid_spec=pltpu.PrefetchScalarGridSpec(num_scalar_pr...]
    unnamed x43 -> x39, local copies, waits for them, and re-layouts: 15.8 us -> 9.92 us
    ppermute x12, starting transfers between devices: 10.7 us -> 15.7 us  [gather_blocks(): lax.ppermute(x, 'phase', [((i + s) % N_PHASE, i) for i in range(N_PHASE)])]
    ppermute x12, waiting for transfers between devices: 7.22 us -> 3.31 us  [gather_blocks(): lax.ppermute(x, 'phase', [((i + s) % N_PHASE, i) for i in range(N_PHASE)])]
    pallas_call x6, Pallas kernels: 8.69 us -> 5.61 us  [call(): pl.pallas_call(body, out_shape=[jax.ShapeDtypeStruct(s, t) for s, t in ou...]
    all_to_all x1, starting transfers between devices: 15.5 us -> 13.2 us  [local(): lax.all_to_all(outgoing.reshape(n_dp, cap, cols), 'dp', split_axis=0, con...]
  transfers between devices with their start and end apart: 21 -> 20, of which waited for: 11 -> 10; matrix products, arithmetic and copies ran while one was open for 3% -> 3% of each run, Pallas kernels for 13% -> 5%
where the time goes in v2:
time: 121 us; the launch traced here: 120 us
  starting transfers between devices  47.1 us (39%)
  waiting for transfers between devices  45.5 us (38%)
  Pallas kernels  13.6 us (11%)
  local copies, waits for them, and re-layouts  12.8 us (11%)
    all_to_all x1, waiting for transfers between devices, local(): lax.all_to_all(rows.reshape(n_dp, cap, cols), 'dp', split_axis=0, concat_...  22.8 us
    ppermute x12, starting transfers between devices, gather_blocks(): lax.ppermute(x, 'phase', [((i + s) % N_PHASE, i) for i in range(N_PHASE)])  15.7 us
    all_to_all x1, starting transfers between devices, local(): lax.all_to_all(outgoing.reshape(n_dp, cap, cols), 'dp', split_axis=0, con...  13.2 us
    all_to_all x1, waiting for transfers between devices, local(): lax.all_to_all(outgoing.reshape(n_dp, cap, cols), 'dp', split_axis=0, con...  12.5 us
    ppermute x6, starting transfers between devices, shift_sends(): lax.ppermute(b, 'phase', [(i, (i + s) % N_PHASE) for i in range(N_PHASE)])  10.2 us
    unnamed x39, local copies, waits for them, and re-layouts  9.92 us
    all_to_all x1, starting transfers between devices, local(): lax.all_to_all(rows.reshape(n_dp, cap, cols), 'dp', split_axis=0, concat_...  8 us
    ppermute x6, waiting for transfers between devices, shift_sends(): lax.ppermute(b, 'phase', [(i, (i + s) % N_PHASE) for i in range(N_PHASE)])  6.96 us
  transfers between devices with their start and end apart: 20, of which 10 were waited for; matrix products, arithmetic and copies ran while one was open for 3% of the time, Pallas kernels for 5%

profile of v2, /device:TPU:1, one launch (start us, length us, event | category | flops | bytes accessed | tf_op | source)
XLA Modules:
  0.0 120.1 jit_solution(12565639112694179337)
XLA Ops:
  0.7 2.2 %copy-done.1 = bf16[1024,2048]{1,0:T(8,128)(2,1)S(1)} copy-done((bf16[1024,2048]{1,0:T(8,128)(2,1)S(1)}, bf16[1024,2048]{1,0:T(8,128)(2,1)}, u32[]{:S(2)}) %copy-start.1) | copy-done | bytes 4194328
  2.9 0.9 copy-done.3
  3.8 1.9 %shard_map.103 = (f32[128,512]{1,0:T(8,128)S(1)}, bf16[128,512]{1,0:T(8,128)(2,1)S(1)}, bf16[128,512]{1,0:T(8,128)(2,1)S(1)}, bf16[128,512]{1,0:T(8,128)(2,1)S(1)}) custom-call(s32[1]{0:T(128)} %bitcast.k_ref, bf16[128,1024]{1,0:T(8,128)(2,1)S(1)} %copy-done.3, bf16[1024,2048]{1,0:T(8,128)(2,1)S(1)} %copy-done.1), custom_call_target="tpu_custom_call" | custom-call | flops 1000000000 | bytes 100000 | tf_op jit(solution)/shard_map/pallas_call | solution.py:66
  5.7 2.1 %collective-permute-start = (bf16[128,512]{1,0:T(8,128)(2,1)S(1)}, bf16[128,512]{1,0:T(8,128)(2,1)S(1)}, u32[]{:S(2)}, u32[]{:S(2)}) collective-permute-start(bf16[128,512]{1,0:T(8,128)(2,1)S(1)} %get-tuple-element.25), channel_id=1, source_target_pairs={{0,64},{64,128},{128,192},{192,0},{1,65},{65,129},{129,193},{193,1... | collective-permute-start | bytes 393224 | tf_op jit(solution)/shard_map/ppermute | solution.py:144
  7.8 2.5 %collective-permute-start.1 = (bf16[128,512]{1,0:T(8,128)(2,1)S(1)}, bf16[128,512]{1,0:T(8,128)(2,1)S(1)}, u32[]{:S(2)}, u32[]{:S(2)}) collective-permute-start(bf16[128,512]{1,0:T(8,128)(2,1)S(1)} %get-tuple-element.26), channel_id=1, source_target_pairs={{0,128},{64,192},{128,0},{192,64},{1,129},{65,193},{129,1},{193,65... | collective-permute-start | bytes 393224 | tf_op jit(solution)/shard_map/ppermute | solution.py:144
  10.3 1.2 collective-permute-start.2
  11.6 4.4 %collective-permute-done.1.b = bf16[128,512]{1,0:T(8,128)(2,1)S(1)} collective-permute-done((bf16[128,512]{1,0:T(8,128)(2,1)S(1)}, bf16[128,512]{1,0:T(8,128)(2,1)S(1)}, u32[]{:S(2)}, u32[]{:S(2)}) %collective-permute-start.1) | collective-permute-done | bytes 131104 | tf_op jit(solution)/shard_map/ppermute | solution.py:144
  16.0 1.5 %shard_map.104 = (f32[128,512]{1,0:T(8,128)S(1)}, bf16[1024,512]{1,0:T(8,128)(2,1)}) custom-call(f32[128,512]{1,0:T(8,128)S(1)} %get-tuple-element.24.own, bf16[128,512]{1,0:T(8,128)(2,1)S(1)} %collective-permute-done.a, bf16[128,512]{1,0:T(8,128)(2,1)S(1)} %collective-permute-done.1.b, bf16[128,512]{1,0:T(8,128)(2,1)S(1)} %collective-permute-done.2.c, ...), custom_call_target="tpu_custom_call" | custom-call | flops 1000000000 | bytes 100000 | tf_op jit(solution)/shard_map/pallas_call | solution.py:27
  17.5 13.2 %all-to-all-start = ((bf16[64,16,512]{2,1,0:T(8,128)(2,1)}), bf16[64,16,512]{2,1,0:T(8,128)(2,1)S(1)}, u32[]{:S(2)}, u32[]{:S(2)}) async-start(bf16[64,16,512]{2,1,0:T(8,128)(2,1)} %bitcast.1), calls=%async_computation | async-start | bytes 2097152 | tf_op jit(solution)/shard_map/all_to_all | solution.py:300
  30.8 2.1 %gather_fusion = s32[448]{0:T(512)S(1)} fusion(s32[1024]{0:T(1024)S(1)} %bitcast.14, s32[1024]{0:T(1024)S(1)} %pad_clamp_fusion), kind=kCustom, calls=%fused_computation | custom fusion | bytes 5376 | tf_op jit(solution)/shard_map/jit(_take)/gather | solution.py:309
  33.2 1.2 shard_map.105
  34.4 1.1 collective-permute-start.3
  35.5 2.1 %collective-permute-start.4 = (bf16[64,512]{1,0:T(8,128)(2,1)S(1)}, bf16[64,512]{1,0:T(8,128)(2,1)S(1)}, u32[]{:S(2)}, u32[]{:S(2)}) collective-permute-start(bf16[64,512]{1,0:T(8,128)(2,1)S(1)} %get-tuple-element.32), channel_id=1, source_target_pairs={{0,128},{64,192},{128,0},{192,64},{1,129},{65,193},{129,1},{193,65... | collective-permute-start | bytes 196616 | tf_op jit(solution)/shard_map/ppermute | solution.py:144
  37.7 1.3 %collective-permute-start.5 = (bf16[64,512]{1,0:T(8,128)(2,1)S(1)}, bf16[64,512]{1,0:T(8,128)(2,1)S(1)}, u32[]{:S(2)}, u32[]{:S(2)}) collective-permute-start(bf16[64,512]{1,0:T(8,128)(2,1)S(1)} %get-tuple-element.33), channel_id=1, source_target_pairs={{0,192},{64,0},{128,64},{192,128},{1,193},{65,1},{129,65},{193,129... | collective-permute-start | bytes 196616 | tf_op jit(solution)/shard_map/ppermute | solution.py:144
  39.1 1.9 %collective-permute-done.4.b = bf16[64,512]{1,0:T(8,128)(2,1)S(1)} collective-permute-done((bf16[64,512]{1,0:T(8,128)(2,1)S(1)}, bf16[64,512]{1,0:T(8,128)(2,1)S(1)}, u32[]{:S(2)}, u32[]{:S(2)}) %collective-permute-start.4) | collective-permute-done | bytes 65568 | tf_op jit(solution)/shard_map/ppermute | solution.py:144
  42.9 3.4 %collective-permute-start.7 = (f32[144,128]{1,0:T(8,128)S(1)}, f32[144,128]{1,0:T(8,128)S(1)}, u32[]{:S(2)}, u32[]{:S(2)}) collective-permute-start(f32[144,128]{1,0:T(8,128)S(1)} %shard_map.107.refs_0_), channel_id=1, source_target_pairs={{128,0},{192,64},{0,128},{64,192},{129,1},{193,65},{1,129},{65,193... | collective-permute-start | bytes 221192 | tf_op jit(solution)/shard_map/ppermute | solution.py:151
  46.2 12.5 %all-to-all-done = bf16[64,16,512]{2,1,0:T(8,128)(2,1)S(1)} async-done(((bf16[64,16,512]{2,1,0:T(8,128)(2,1)}), bf16[64,16,512]{2,1,0:T(8,128)(2,1)S(1)}, u32[]{:S(2)}, u32[]{:S(2)}) %all-to-all-start) | async-done | bytes 1048608 | tf_op jit(solution)/shard_map/all_to_all | solution.py:300
  59.5 1.4 %shard_map.108.refs_4_ = f32[16,128]{1,0:T(8,128)S(1)} custom-call(bf16[1024,512]{1,0:T(8,128)(2,1)S(1)} %bitcast.15, bf16[64,512]{1,0:T(8,128)(2,1)S(1)} %copy-done.15, s32[8,128]{1,0:T(8,128)S(1)} %pad.9.neg_ref.refs_9_), custom_call_target="tpu_custom_call" | custom-call | flops 1000000000 | bytes 100000 | tf_op jit(solution)/shard_map/pallas_call | solution.py:27
  60.9 1.1 collective-permute-start.11
  62.0 2.1 %collective-permute-start.10 = (f32[16,128]{1,0:T(8,128)S(1)}, f32[16,128]{1,0:T(8,128)S(1)}, u32[]{:S(2)}, u32[]{:S(2)}) collective-permute-start(f32[16,128]{1,0:T(8,128)S(1)} %shard_map.108.refs_4_), channel_id=1, source_target_pairs={{128,0},{192,64},{0,128},{64,192},{129,1},{193,65},{1,129},{65,193... | collective-permute-start | bytes 24584 | tf_op jit(solution)/shard_map/ppermute | solution.py:151
  64.1 1.3 %collective-permute-start.9 = (f32[16,128]{1,0:T(8,128)S(1)}, f32[16,128]{1,0:T(8,128)S(1)}, u32[]{:S(2)}, u32[]{:S(2)}) collective-permute-start(f32[16,128]{1,0:T(8,128)S(1)} %shard_map.108.refs_4_), channel_id=1, source_target_pairs={{64,0},{128,64},{192,128},{0,192},{65,1},{129,65},{193,129},{1,193... | collective-permute-start | bytes 24584 | tf_op jit(solution)/shard_map/ppermute | solution.py:151
  66.8 0.9 copy-done.9
  67.7 0.9 copy-done.13
  68.6 2.1 %shard_map.109 = (bf16[1024,512]{1,0:T(8,128)(2,1)}, bf16[64,512]{1,0:T(8,128)(2,1)S(1)}, f32[128,512]{1,0:T(8,128)S(1)}, f32[8,128]{1,0:T(8,128)S(1)}) custom-call(f32[144,128]{1,0:T(8,128)S(1)} %shard_map.107.refs_0_, f32[144,128]{1,0:T(8,128)S(1)} %collective-permute-done.6.refs_1_, f32[144,128]{1,0:T(8,128)S(1)} %collective-permute-done.7.refs_2_, ...), custom_call_target="tpu_custom_call" | custom-call | flops 1000000000 | bytes 100000 | tf_op jit(solution)/shard_map/pallas_call | solution.py:27
  71.5 8.0 %all-to-all-start.1 = ((bf16[64,16,512]{2,1,0:T(8,128)(2,1)}), bf16[64,16,512]{2,1,0:T(8,128)(2,1)S(1)}, u32[]{:S(2)}, u32[]{:S(2)}) async-start(bf16[64,16,512]{2,1,0:T(8,128)(2,1)} %bitcast.7), calls=%async_computation.1 | async-start | bytes 2097152 | tf_op jit(solution)/shard_map/all_to_all | solution.py:330
  79.8 3.5 %collective-permute-start.13 = (bf16[64,512]{1,0:T(8,128)(2,1)S(1)}, bf16[64,512]{1,0:T(8,128)(2,1)S(1)}, u32[]{:S(2)}, u32[]{:S(2)}) collective-permute-start(bf16[64,512]{1,0:T(8,128)(2,1)S(1)} %get-tuple-element.42.u_ref), channel_id=1, source_target_pairs={{128,0},{192,64},{0,128},{64,192},{129,1},{193,65},{1,129},{65,193... | collective-permute-start | bytes 196616 | tf_op jit(solution)/shard_map/ppermute | solution.py:151
  84.7 22.8 %all-to-all-done.1 = bf16[64,16,512]{2,1,0:T(8,128)(2,1)S(1)} async-done(((bf16[64,16,512]{2,1,0:T(8,128)(2,1)}), bf16[64,16,512]{2,1,0:T(8,128)(2,1)S(1)}, u32[]{:S(2)}, u32[]{:S(2)}) %all-to-all-start.1) | async-done | bytes 1048608 | tf_op jit(solution)/shard_map/all_to_all | solution.py:330
  107.5 1.1 copy-done.11
  109.2 3.5 %collective-permute-start.16 = (bf16[128,512]{1,0:T(8,128)(2,1)S(1)}, bf16[128,512]{1,0:T(8,128)(2,1)S(1)}, u32[]{:S(2)}, u32[]{:S(2)}) collective-permute-start(bf16[128,512]{1,0:T(8,128)(2,1)S(1)} %shard_map.112.u_ref), channel_id=1, source_target_pairs={{128,0},{192,64},{0,128},{64,192},{129,1},{193,65},{1,129},{65,193... | collective-permute-start | bytes 393224 | tf_op jit(solution)/shard_map/ppermute | solution.py:151
  113.6 1.7 %shard_map.111 = bf16[64,512]{1,0:T(8,128)(2,1)} custom-call(s32[1]{0:T(128)} %bitcast.k_ref, f32[64,512]{1,0:T(8,128)S(1)} %copy-done.7, bf16[64,512]{1,0:T(8,128)(2,1)S(1)} %collective-permute-done.12.refs_0_, bf16[64,512]{1,0:T(8,128)(2,1)S(1)} %collective-permute-done.13.refs_1_, bf16[64,512]{1,0:T(8,128)(2,1)S(1)} %collective-permute-done.14.refs_2_, ...), custom_call_target="tpu_custom_call" | custom-call | flops 1000000000 | bytes 100000 | tf_op jit(solution)/shard_map/pallas_call | solution.py:121
  115.7 1.6 %collective-permute-done.16.refs_1_ = bf16[128,512]{1,0:T(8,128)(2,1)S(1)} collective-permute-done((bf16[128,512]{1,0:T(8,128)(2,1)S(1)}, bf16[128,512]{1,0:T(8,128)(2,1)S(1)}, u32[]{:S(2)}, u32[]{:S(2)}) %collective-permute-start.16) | collective-permute-done | bytes 131104 | tf_op jit(solution)/shard_map/ppermute | solution.py:151
  117.7 2.5 %shard_map.114 = bf16[128,1024]{1,0:T(8,128)(2,1)} custom-call(s32[1]{0:T(128)} %bitcast.k_ref, f32[128,1024]{1,0:T(8,128)S(1)} %shard_map.113.in_ref, bf16[128,512]{1,0:T(8,128)(2,1)S(1)} %collective-permute-done.15.refs_0_, bf16[128,512]{1,0:T(8,128)(2,1)S(1)} %collective-permute-done.16.refs_1_, bf16[128,512]{1,0:T(8,128)(2,1)S(1)} %collective-permute-done.17.refs_2_, ...), custom_call_target="tpu_custom_call" | custom-call | flops 1000000000 | bytes 100000 | tf_op jit(solution)/shard_map/pallas_call | solution.py:121
  (73 shorter events, 9.5 us)
Async XLA Ops:
  0.6 30.2 %copy-start = (s32[1,1024]{1,0:T(1,128)S(1)}, s32[1,1024]{1,0:T(1,128)}, u32[]{:S(2)}) copy-start(s32[1,1024]{1,0:T(1,128)} %param.13) | copy-start | bytes 12292
  0.6 10.8 %copy-start.17 = (s32[1,64,16]{1,2,0:T(8,128)S(1)}, s32[1,64,16]{1,2,0:T(8,128)}, u32[]{:S(2)}) copy-start(s32[1,64,16]{1,2,0:T(8,128)} %param.12) | copy-start | bytes 12292
  0.7 2.2 %copy-start.1 = (bf16[1024,2048]{1,0:T(8,128)(2,1)S(1)}, bf16[1024,2048]{1,0:T(8,128)(2,1)}, u32[]{:S(2)}) copy-start(bf16[1024,2048]{1,0:T(8,128)(2,1)} %refs_3_.3) | copy-start | bytes 12582916
  3.8 26.9 %copy-start.16 = (s32[64,7]{0,1:T(8,128)S(1)}, s32[64,7]{0,1:T(8,128)}, u32[]{:S(2)}) copy-start(s32[64,7]{0,1:T(8,128)} %param.14) | copy-start | bytes 5380
  5.7 5.9 %collective-permute-start = (bf16[128,512]{1,0:T(8,128)(2,1)S(1)}, bf16[128,512]{1,0:T(8,128)(2,1)S(1)}, u32[]{:S(2)}, u32[]{:S(2)}) collective-permute-start(bf16[128,512]{1,0:T(8,128)(2,1)S(1)} %get-tuple-element.25), channel_id=1, source_target_pairs={{0,64},{64,128},{128,192},{192,0},{1,65},{65,129},{129,193},{193,1... | collective-permute-start | bytes 393224 | tf_op jit(solution)/shard_map/ppermute | solution.py:144
  7.8 8.2 %collective-permute-start.1 = (bf16[128,512]{1,0:T(8,128)(2,1)S(1)}, bf16[128,512]{1,0:T(8,128)(2,1)S(1)}, u32[]{:S(2)}, u32[]{:S(2)}) collective-permute-start(bf16[128,512]{1,0:T(8,128)(2,1)S(1)} %get-tuple-element.26), channel_id=1, source_target_pairs={{0,128},{64,192},{128,0},{192,64},{1,129},{65,193},{129,1},{193,65... | collective-permute-start | bytes 393224 | tf_op jit(solution)/shard_map/ppermute | solution.py:144
  10.3 5.7 %collective-permute-start.2 = (bf16[128,512]{1,0:T(8,128)(2,1)S(1)}, bf16[128,512]{1,0:T(8,128)(2,1)S(1)}, u32[]{:S(2)}, u32[]{:S(2)}) collective-permute-start(bf16[128,512]{1,0:T(8,128)(2,1)S(1)} %get-tuple-element.27), channel_id=1, source_target_pairs={{0,192},{64,0},{128,64},{192,128},{1,193},{65,1},{129,65},{193,129... | collective-permute-start | bytes 393224 | tf_op jit(solution)/shard_map/ppermute | solution.py:144
  16.0 17.1 %copy-start.18 = (f32[64]{0:T(128)S(1)}, f32[64]{0:T(128)}, u32[]{:S(2)}) copy-start(f32[64]{0:T(128)} %param.15) | copy-start | bytes 772
  16.0 17.2 %copy-start.4 = (bf16[512,2048]{1,0:T(8,128)(2,1)S(1)}, bf16[512,2048]{1,0:T(8,128)(2,1)}, u32[]{:S(2)}) copy-start(bf16[512,2048]{1,0:T(8,128)(2,1)} %refs_3_.2) | copy-start | bytes 6291460
  16.0 17.2 %copy-start.5 = (bf16[64,512]{1,0:T(8,128)(2,1)S(1)}, bf16[64,512]{1,0:T(8,128)(2,1)}, u32[]{:S(2)}) copy-start(bf16[64,512]{1,0:T(8,128)(2,1)} %x_ref.2) | copy-start | bytes 196612
  17.5 24.8 %copy-start.8 = (f32[128,512]{1,0:T(8,128)}, f32[128,512]{1,0:T(8,128)S(1)}, u32[]{:S(2)}) copy-start(f32[128,512]{1,0:T(8,128)S(1)} %get-tuple-element.35.d_ref.refs_11_) | copy-start | bytes 786436
  17.5 41.2 %all-to-all-start = ((bf16[64,16,512]{2,1,0:T(8,128)(2,1)}), bf16[64,16,512]{2,1,0:T(8,128)(2,1)S(1)}, u32[]{:S(2)}, u32[]{:S(2)}) async-start(bf16[64,16,512]{2,1,0:T(8,128)(2,1)} %bitcast.1), calls=%async_computation | async-start | bytes 2097152 | tf_op jit(solution)/shard_map/all_to_all | solution.py:300
  34.4 4.7 %collective-permute-start.3 = (bf16[64,512]{1,0:T(8,128)(2,1)S(1)}, bf16[64,512]{1,0:T(8,128)(2,1)S(1)}, u32[]{:S(2)}, u32[]{:S(2)}) collective-permute-start(bf16[64,512]{1,0:T(8,128)(2,1)S(1)} %get-tuple-element.31), channel_id=1, source_target_pairs={{0,64},{64,128},{128,192},{192,0},{1,65},{65,129},{129,193},{193,1... | collective-permute-start | bytes 196616 | tf_op jit(solution)/shard_map/ppermute | solution.py:144
  35.5 5.5 %collective-permute-start.4 = (bf16[64,512]{1,0:T(8,128)(2,1)S(1)}, bf16[64,512]{1,0:T(8,128)(2,1)S(1)}, u32[]{:S(2)}, u32[]{:S(2)}) collective-permute-start(bf16[64,512]{1,0:T(8,128)(2,1)S(1)} %get-tuple-element.32), channel_id=1, source_target_pairs={{0,128},{64,192},{128,0},{192,64},{1,129},{65,193},{129,1},{193,65... | collective-permute-start | bytes 196616 | tf_op jit(solution)/shard_map/ppermute | solution.py:144
  37.7 3.9 %collective-permute-start.5 = (bf16[64,512]{1,0:T(8,128)(2,1)S(1)}, bf16[64,512]{1,0:T(8,128)(2,1)S(1)}, u32[]{:S(2)}, u32[]{:S(2)}) collective-permute-start(bf16[64,512]{1,0:T(8,128)(2,1)S(1)} %get-tuple-element.33), channel_id=1, source_target_pairs={{0,192},{64,0},{128,64},{192,128},{1,193},{65,1},{129,65},{193,129... | collective-permute-start | bytes 196616 | tf_op jit(solution)/shard_map/ppermute | solution.py:144
  42.3 3.9 %copy-start.12 = (f32[64,512]{1,0:T(8,128)}, f32[64,512]{1,0:T(8,128)S(1)}, u32[]{:S(2)}) copy-start(f32[64,512]{1,0:T(8,128)S(1)} %get-tuple-element.34.q_ref.refs_12_) | copy-start | bytes 393220
  42.6 21.5 %collective-permute-start.8 = (f32[144,128]{1,0:T(8,128)S(1)}, f32[144,128]{1,0:T(8,128)S(1)}, u32[]{:S(2)}, u32[]{:S(2)}) collective-permute-start(f32[144,128]{1,0:T(8,128)S(1)} %shard_map.107.refs_0_), channel_id=1, source_target_pairs={{192,0},{0,64},{64,128},{128,192},{193,1},{1,65},{65,129},{129,193... | collective-permute-start | bytes 221192 | tf_op jit(solution)/shard_map/ppermute | solution.py:151
  42.9 22.6 %collective-permute-start.7 = (f32[144,128]{1,0:T(8,128)S(1)}, f32[144,128]{1,0:T(8,128)S(1)}, u32[]{:S(2)}, u32[]{:S(2)}) collective-permute-start(f32[144,128]{1,0:T(8,128)S(1)} %shard_map.107.refs_0_), channel_id=1, source_target_pairs={{128,0},{192,64},{0,128},{64,192},{129,1},{193,65},{1,129},{65,193... | collective-permute-start | bytes 221192 | tf_op jit(solution)/shard_map/ppermute | solution.py:151
  46.2 19.2 %collective-permute-start.6 = (f32[144,128]{1,0:T(8,128)S(1)}, f32[144,128]{1,0:T(8,128)S(1)}, u32[]{:S(2)}, u32[]{:S(2)}) collective-permute-start(f32[144,128]{1,0:T(8,128)S(1)} %shard_map.107.refs_0_), channel_id=1, source_target_pairs={{64,0},{128,64},{192,128},{0,192},{65,1},{129,65},{193,129},{1,193... | collective-permute-start | bytes 221192 | tf_op jit(solution)/shard_map/ppermute | solution.py:151
  60.9 4.5 %collective-permute-start.11 = (f32[16,128]{1,0:T(8,128)S(1)}, f32[16,128]{1,0:T(8,128)S(1)}, u32[]{:S(2)}, u32[]{:S(2)}) collective-permute-start(f32[16,128]{1,0:T(8,128)S(1)} %shard_map.108.refs_4_), channel_id=1, source_target_pairs={{192,0},{0,64},{64,128},{128,192},{193,1},{1,65},{65,129},{129,193... | collective-permute-start | bytes 24584 | tf_op jit(solution)/shard_map/ppermute | solution.py:151
  62.0 4.0 %collective-permute-start.10 = (f32[16,128]{1,0:T(8,128)S(1)}, f32[16,128]{1,0:T(8,128)S(1)}, u32[]{:S(2)}, u32[]{:S(2)}) collective-permute-start(f32[16,128]{1,0:T(8,128)S(1)} %shard_map.108.refs_4_), channel_id=1, source_target_pairs={{128,0},{192,64},{0,128},{64,192},{129,1},{193,65},{1,129},{65,193... | collective-permute-start | bytes 24584 | tf_op jit(solution)/shard_map/ppermute | solution.py:151
  64.1 2.7 %collective-permute-start.9 = (f32[16,128]{1,0:T(8,128)S(1)}, f32[16,128]{1,0:T(8,128)S(1)}, u32[]{:S(2)}, u32[]{:S(2)}) collective-permute-start(f32[16,128]{1,0:T(8,128)S(1)} %shard_map.108.refs_4_), channel_id=1, source_target_pairs={{64,0},{128,64},{192,128},{0,192},{65,1},{129,65},{193,129},{1,193... | collective-permute-start | bytes 24584 | tf_op jit(solution)/shard_map/ppermute | solution.py:151
  66.8 1.0 copy-start.9
  71.5 36.0 %all-to-all-start.1 = ((bf16[64,16,512]{2,1,0:T(8,128)(2,1)}), bf16[64,16,512]{2,1,0:T(8,128)(2,1)S(1)}, u32[]{:S(2)}, u32[]{:S(2)}) async-start(bf16[64,16,512]{2,1,0:T(8,128)(2,1)} %bitcast.7), calls=%async_computation.1 | async-start | bytes 2097152 | tf_op jit(solution)/shard_map/all_to_all | solution.py:330
  79.5 33.2 %collective-permute-start.14 = (bf16[64,512]{1,0:T(8,128)(2,1)S(1)}, bf16[64,512]{1,0:T(8,128)(2,1)S(1)}, u32[]{:S(2)}, u32[]{:S(2)}) collective-permute-start(bf16[64,512]{1,0:T(8,128)(2,1)S(1)} %get-tuple-element.42.u_ref), channel_id=1, source_target_pairs={{192,0},{0,64},{64,128},{128,192},{193,1},{1,65},{65,129},{129,193... | collective-permute-start | bytes 196616 | tf_op jit(solution)/shard_map/ppermute | solution.py:151
  79.8 32.9 %collective-permute-start.13 = (bf16[64,512]{1,0:T(8,128)(2,1)S(1)}, bf16[64,512]{1,0:T(8,128)(2,1)S(1)}, u32[]{:S(2)}, u32[]{:S(2)}) collective-permute-start(bf16[64,512]{1,0:T(8,128)(2,1)S(1)} %get-tuple-element.42.u_ref), channel_id=1, source_target_pairs={{128,0},{192,64},{0,128},{64,192},{129,1},{193,65},{1,129},{65,193... | collective-permute-start | bytes 196616 | tf_op jit(solution)/shard_map/ppermute | solution.py:151
  83.2 29.4 %collective-permute-start.12 = (bf16[64,512]{1,0:T(8,128)(2,1)S(1)}, bf16[64,512]{1,0:T(8,128)(2,1)S(1)}, u32[]{:S(2)}, u32[]{:S(2)}) collective-permute-start(bf16[64,512]{1,0:T(8,128)(2,1)S(1)} %get-tuple-element.42.u_ref), channel_id=1, source_target_pairs={{64,0},{128,64},{192,128},{0,192},{65,1},{129,65},{193,129},{1,193... | collective-permute-start | bytes 196616 | tf_op jit(solution)/shard_map/ppermute | solution.py:151
  107.5 7.8 %copy-start.2 = (bf16[1024,2048]{1,0:T(8,128)(2,1)S(1)}, bf16[1024,2048]{1,0:T(8,128)(2,1)}, u32[]{:S(2)}) copy-start(bf16[1024,2048]{1,0:T(8,128)(2,1)} %refs_3_.3) | copy-start | bytes 12582916
  107.5 1.1 copy-start.11
  108.9 6.8 %collective-permute-start.17 = (bf16[128,512]{1,0:T(8,128)(2,1)S(1)}, bf16[128,512]{1,0:T(8,128)(2,1)S(1)}, u32[]{:S(2)}, u32[]{:S(2)}) collective-permute-start(bf16[128,512]{1,0:T(8,128)(2,1)S(1)} %shard_map.112.u_ref), channel_id=1, source_target_pairs={{192,0},{0,64},{64,128},{128,192},{193,1},{1,65},{65,129},{129,193... | collective-permute-start | bytes 393224 | tf_op jit(solution)/shard_map/ppermute | solution.py:151
  109.2 8.2 %collective-permute-start.16 = (bf16[128,512]{1,0:T(8,128)(2,1)S(1)}, bf16[128,512]{1,0:T(8,128)(2,1)S(1)}, u32[]{:S(2)}, u32[]{:S(2)}) collective-permute-start(bf16[128,512]{1,0:T(8,128)(2,1)S(1)} %shard_map.112.u_ref), channel_id=1, source_target_pairs={{128,0},{192,64},{0,128},{64,192},{129,1},{193,65},{1,129},{65,193... | collective-permute-start | bytes 393224 | tf_op jit(solution)/shard_map/ppermute | solution.py:151
  112.7 5.0 %collective-permute-start.15 = (bf16[128,512]{1,0:T(8,128)(2,1)S(1)}, bf16[128,512]{1,0:T(8,128)(2,1)S(1)}, u32[]{:S(2)}, u32[]{:S(2)}) collective-permute-start(bf16[128,512]{1,0:T(8,128)(2,1)S(1)} %shard_map.112.u_ref), channel_id=1, source_target_pairs={{64,0},{128,64},{192,128},{0,192},{65,1},{129,65},{193,129},{1,193... | collective-permute-start | bytes 393224 | tf_op jit(solution)/shard_map/ppermute | solution.py:151
  (7 other events, 5.6 us)

commit v3 on v2

--- a/solution.py
+++ b/solution.py
@@ -19,8 +19,8 @@
     return lax.dot_general(a, b, dims, preferred_element_type=f32)
 
 
-def params():
-    return pltpu.CompilerParams(vmem_limit_bytes=48 * 1024 * 1024)
+def params(mib=16):
+    return pltpu.CompilerParams(vmem_limit_bytes=mib * 1024 * 1024)
 
 
 def call(body, outs, *args):
@@ -44,33 +44,50 @@
 def project(x, w, k):
     rows, depth = x.shape
     cols = w.shape[1] // N_PHASE
-
-    def body(k_ref, x_ref, w_ref, own_ref, *refs):
-        send_refs, buf_ref, sem_ref = refs[: N_PHASE - 1], refs[N_PHASE - 1], refs[N_PHASE]
-
-        def copy(s):
+    order = (2, 1, 3, 0)
+
+    def body(k_ref, x_ref, w_ref, *refs):
+        outs, (x_buf, w_buf, own_buf, send_buf, sem_ref) = refs[:N_PHASE], refs[N_PHASE:]
+
+        def load(s):
             start = pl.multiple_of(lax.rem(k_ref[0] + s, N_PHASE) * cols, cols)
-            return pltpu.make_async_copy(w_ref.at[:, pl.ds(start, cols)], buf_ref.at[s], sem_ref.at[s])
-
-        for s in range(N_PHASE):
-            copy(s).start()
-        for s in range(N_PHASE):
-            copy(s).wait()
-            y = dot(x_ref[...], buf_ref[s])
+            return pltpu.make_async_copy(w_ref.at[:, pl.ds(start, cols)], w_buf.at[s], sem_ref.at[s])
+
+        def store(s):
+            source = own_buf if s == 0 else send_buf.at[s - 1]
+            return pltpu.make_async_copy(source, outs[s], sem_ref.at[N_PHASE + 1 + s])
+
+        load_x = pltpu.make_async_copy(x_ref, x_buf, sem_ref.at[N_PHASE])
+        load_x.start()
+        for s in order:
+            load(s).start()
+        load_x.wait()
+        for s in order:
+            load(s).wait()
+            y = dot(x_buf[...], w_buf[s])
             if s == 0:
-                own_ref[...] = y
+                own_buf[...] = y
             else:
-                send_refs[s - 1][...] = y.astype(bf16)
-
-    vmem = pl.BlockSpec(memory_space=pltpu.VMEM)
+                send_buf[s - 1] = y.astype(bf16)
+            store(s).start()
+        for s in order:
+            store(s).wait()
+
+    hbm = pl.BlockSpec(memory_space=pltpu.HBM)
     return pl.pallas_call(
         body,
-        in_specs=[pl.BlockSpec(memory_space=pltpu.SMEM), vmem, pl.BlockSpec(memory_space=pltpu.HBM)],
-        out_specs=[vmem] * N_PHASE,
+        in_specs=[pl.BlockSpec(memory_space=pltpu.SMEM), hbm, hbm],
+        out_specs=[hbm] * N_PHASE,
         out_shape=[jax.ShapeDtypeStruct((rows, cols), f32)]
         + [jax.ShapeDtypeStruct((rows, cols), bf16)] * (N_PHASE - 1),
-        scratch_shapes=[pltpu.VMEM((N_PHASE, depth, cols), bf16), pltpu.SemaphoreType.DMA((N_PHASE,))],
-        compiler_params=params(),
+        scratch_shapes=[
+            pltpu.VMEM((rows, depth), bf16),
+            pltpu.VMEM((N_PHASE, depth, cols), bf16),
+            pltpu.VMEM((rows, cols), f32),
+            pltpu.VMEM((N_PHASE - 1, rows, cols), bf16),
+            pltpu.SemaphoreType.DMA((2 * N_PHASE + 1,)),
+        ],
+        compiler_params=params(63),
         cost_estimate=cost,
     )(k, x, w)
 
@@ -331,10 +348,11 @@
         rows.reshape(n_dp, cap, cols), "dp", split_axis=0, concat_axis=0, tiled=True
     ).reshape(slots, cols)
     grad_query = project_back(u_query, query_proj, k)
+    arrived, grad_query, loss = lax.optimization_barrier((arrived, grad_query, loss[0, :queries]))
 
     (u_docs,) = call(doc_grads, [((docs, cols), bf16)], arrived, requests, g_local)
     grad_doc = project_back(u_docs, doc_proj, k)
-    return (loss[0, :queries], grad_query, grad_doc)
+    return (loss, grad_query, grad_doc)
 
 
 def solution(mesh):

time: 121 us -> 119 us (0.983)
  Pallas kernels: 13.6 us -> 18.9 us
  local copies, waits for them, and re-layouts: 12.8 us -> 8.66 us
  waiting for transfers between devices: 45.5 us -> 41.7 us
    unnamed x39 -> x17, local copies, waits for them, and re-layouts: 9.92 us -> 5.74 us
    all_to_all x1, waiting for transfers between devices: 22.8 us -> 19.1 us  [local(): lax.all_to_all(rows.reshape(n_dp, cap, cols), 'dp', split_axis=0, concat_...]
    pallas_call x2, Pallas kernels: 3.09 us -> 6.04 us  [project(): pl.pallas_call(body, in_specs=[pl.BlockSpec(memory_space=pltpu.SMEM), hbm...]
    pallas_call x6, Pallas kernels: 5.61 us -> 7.96 us  [call(): pl.pallas_call(body, out_shape=[jax.ShapeDtypeStruct(s, t) for s, t in ou...]
    all_to_all x1, waiting for transfers between devices: 12.5 us -> 10.3 us  [local(): lax.all_to_all(outgoing.reshape(n_dp, cap, cols), 'dp', split_axis=0, con...]
    ppermute x12, waiting for transfers between devices: 3.31 us -> 4.72 us  [gather_blocks(): lax.ppermute(x, 'phase', [((i + s) % N_PHASE, i) for i in range(N_PHASE)])]
  transfers between devices with their start and end apart: 20 -> 20, of which waited for: 10 -> 13; matrix products, arithmetic and copies ran while one was open for 3% -> 3% of each run, Pallas kernels for 5% -> 7%
where the time goes in v3:
time: 119 us; the launch traced here: 118 us
  starting transfers between devices  47.3 us (40%)
  waiting for transfers between devices  41.7 us (35%)
  Pallas kernels  18.9 us (16%)
  local copies, waits for them, and re-layouts  8.66 us (7%)
    all_to_all x1, waiting for transfers between devices, local(): lax.all_to_all(rows.reshape(n_dp, cap, cols), 'dp', split_axis=0, concat_...  19.1 us
    ppermute x12, starting transfers between devices, gather_blocks(): lax.ppermute(x, 'phase', [((i + s) % N_PHASE, i) for i in range(N_PHASE)])  15.7 us
    all_to_all x1, starting transfers between devices, local(): lax.all_to_all(outgoing.reshape(n_dp, cap, cols), 'dp', split_axis=0, con...  13.4 us
    all_to_all x1, waiting for transfers between devices, local(): lax.all_to_all(outgoing.reshape(n_dp, cap, cols), 'dp', split_axis=0, con...  10.3 us
    ppermute x6, starting transfers between devices, shift_sends(): lax.ppermute(b, 'phase', [(i, (i + s) % N_PHASE) for i in range(N_PHASE)])  10.3 us
    all_to_all x1, starting transfers between devices, local(): lax.all_to_all(rows.reshape(n_dp, cap, cols), 'dp', split_axis=0, concat_...  8.04 us
    pallas_call x6, Pallas kernels, call(): pl.pallas_call(body, out_shape=[jax.ShapeDtypeStruct(s, t) for s, t in ou...  7.96 us
    ppermute x6, waiting for transfers between devices, shift_sends(): lax.ppermute(b, 'phase', [(i, (i + s) % N_PHASE) for i in range(N_PHASE)])  7.55 us
  transfers between devices with their start and end apart: 20, of which 13 were waited for; matrix products, arithmetic and copies ran while one was open for 3% of the time, Pallas kernels for 7%

profile of v3, /device:TPU:1, one launch (start us, length us, event | category | flops | bytes accessed | tf_op | source)
XLA Modules:
  0.0 117.6 jit_solution(1523209196840172088)
XLA Ops:
  0.7 3.4 %shard_map.103 = (f32[128,512]{1,0:T(8,128)}, bf16[128,512]{1,0:T(8,128)(2,1)}, bf16[128,512]{1,0:T(8,128)(2,1)}, bf16[128,512]{1,0:T(8,128)(2,1)}) custom-call(s32[1]{0:T(128)} %bitcast.k_ref, bf16[128,1024]{1,0:T(8,128)(2,1)} %x_ref.1, bf16[1024,2048]{1,0:T(8,128)(2,1)} %refs_3_.3), custom_call_target="tpu_custom_call" | custom-call | flops 1000000000 | bytes 100000 | tf_op jit(solution)/shard_map/pallas_call | solution.py:77
  4.1 2.1 %collective-permute-start = (bf16[128,512]{1,0:T(8,128)(2,1)}, bf16[128,512]{1,0:T(8,128)(2,1)S(1)}, u32[]{:S(2)}, u32[]{:S(2)}) collective-permute-start(bf16[128,512]{1,0:T(8,128)(2,1)} %get-tuple-element.28), channel_id=1, source_target_pairs={{0,64},{64,128},{128,192},{192,0},{1,65},{65,129},{129,193},{193,1... | collective-permute-start | bytes 393224 | tf_op jit(solution)/shard_map/ppermute | solution.py:161
  6.2 2.4 %collective-permute-start.1 = (bf16[128,512]{1,0:T(8,128)(2,1)}, bf16[128,512]{1,0:T(8,128)(2,1)S(1)}, u32[]{:S(2)}, u32[]{:S(2)}) collective-permute-start(bf16[128,512]{1,0:T(8,128)(2,1)} %get-tuple-element.29), channel_id=1, source_target_pairs={{0,128},{64,192},{128,0},{192,64},{1,129},{65,193},{129,1},{193,65... | collective-permute-start | bytes 393224 | tf_op jit(solution)/shard_map/ppermute | solution.py:161
  8.6 1.2 collective-permute-start.2
  10.0 4.5 %collective-permute-done.1.b = bf16[128,512]{1,0:T(8,128)(2,1)S(1)} collective-permute-done((bf16[128,512]{1,0:T(8,128)(2,1)}, bf16[128,512]{1,0:T(8,128)(2,1)S(1)}, u32[]{:S(2)}, u32[]{:S(2)}) %collective-permute-start.1) | collective-permute-done | bytes 131104 | tf_op jit(solution)/shard_map/ppermute | solution.py:161
  14.6 0.9 copy-done.3
  15.5 1.4 %shard_map.104 = (f32[128,512]{1,0:T(8,128)S(1)}, bf16[1024,512]{1,0:T(8,128)(2,1)}) custom-call(f32[128,512]{1,0:T(8,128)S(1)} %copy-done.3, bf16[128,512]{1,0:T(8,128)(2,1)S(1)} %collective-permute-done.a, bf16[128,512]{1,0:T(8,128)(2,1)S(1)} %collective-permute-done.1.b, bf16[128,512]{1,0:T(8,128)(2,1)S(1)} %collective-permute-done.2.c, ...), custom_call_target="tpu_custom_call" | custom-call | flops 1000000000 | bytes 100000 | tf_op jit(solution)/shard_map/pallas_call | solution.py:27
  17.0 13.4 %all-to-all-start = ((bf16[64,16,512]{2,1,0:T(8,128)(2,1)}), bf16[64,16,512]{2,1,0:T(8,128)(2,1)}, u32[]{:S(2)}, u32[]{:S(2)}) async-start(bf16[64,16,512]{2,1,0:T(8,128)(2,1)} %bitcast.1), calls=%async_computation | async-start | bytes 2097152 | tf_op jit(solution)/shard_map/all_to_all | solution.py:317
  30.5 2.1 %gather_fusion = s32[448]{0:T(512)S(1)} fusion(s32[1024]{0:T(1024)S(1)} %bitcast.14, s32[1024]{0:T(1024)S(1)} %pad_clamp_fusion), kind=kCustom, calls=%fused_computation | custom fusion | bytes 5376 | tf_op jit(solution)/shard_map/jit(_take)/gather | solution.py:326
  32.9 2.6 %shard_map.105 = (f32[64,512]{1,0:T(8,128)}, bf16[64,512]{1,0:T(8,128)(2,1)}, bf16[64,512]{1,0:T(8,128)(2,1)}, bf16[64,512]{1,0:T(8,128)(2,1)}) custom-call(s32[1]{0:T(128)} %bitcast.k_ref, bf16[64,512]{1,0:T(8,128)(2,1)} %x_ref.2, bf16[512,2048]{1,0:T(8,128)(2,1)} %refs_3_.2), custom_call_target="tpu_custom_call" | custom-call | flops 1000000000 | bytes 100000 | tf_op jit(solution)/shard_map/pallas_call | solution.py:77
  35.5 1.1 collective-permute-start.3
  36.7 2.1 %collective-permute-start.4 = (bf16[64,512]{1,0:T(8,128)(2,1)}, bf16[64,512]{1,0:T(8,128)(2,1)S(1)}, u32[]{:S(2)}, u32[]{:S(2)}) collective-permute-start(bf16[64,512]{1,0:T(8,128)(2,1)} %get-tuple-element.35), channel_id=1, source_target_pairs={{0,128},{64,192},{128,0},{192,64},{1,129},{65,193},{129,1},{193,65... | collective-permute-start | bytes 196616 | tf_op jit(solution)/shard_map/ppermute | solution.py:161
  38.8 1.3 %collective-permute-start.5 = (bf16[64,512]{1,0:T(8,128)(2,1)}, bf16[64,512]{1,0:T(8,128)(2,1)S(1)}, u32[]{:S(2)}, u32[]{:S(2)}) collective-permute-start(bf16[64,512]{1,0:T(8,128)(2,1)} %get-tuple-element.36), channel_id=1, source_target_pairs={{0,192},{64,0},{128,64},{192,128},{1,193},{65,1},{129,65},{193,129... | collective-permute-start | bytes 196616 | tf_op jit(solution)/shard_map/ppermute | solution.py:161
  40.6 1.9 %collective-permute-done.4.b = bf16[64,512]{1,0:T(8,128)(2,1)S(1)} collective-permute-done((bf16[64,512]{1,0:T(8,128)(2,1)}, bf16[64,512]{1,0:T(8,128)(2,1)S(1)}, u32[]{:S(2)}, u32[]{:S(2)}) %collective-permute-start.4) | collective-permute-done | bytes 65568 | tf_op jit(solution)/shard_map/ppermute | solution.py:161
  43.1 0.9 copy-done.4
  44.5 3.4 %collective-permute-start.7 = (f32[144,128]{1,0:T(8,128)S(1)}, f32[144,128]{1,0:T(8,128)S(1)}, u32[]{:S(2)}, u32[]{:S(2)}) collective-permute-start(f32[144,128]{1,0:T(8,128)S(1)} %shard_map.107.refs_0_), channel_id=1, source_target_pairs={{128,0},{192,64},{0,128},{64,192},{129,1},{193,65},{1,129},{65,193... | collective-permute-start | bytes 221192 | tf_op jit(solution)/shard_map/ppermute | solution.py:168
  48.0 10.3 %all-to-all-done = bf16[64,16,512]{2,1,0:T(8,128)(2,1)} async-done(((bf16[64,16,512]{2,1,0:T(8,128)(2,1)}), bf16[64,16,512]{2,1,0:T(8,128)(2,1)}, u32[]{:S(2)}, u32[]{:S(2)}) %all-to-all-start) | async-done | bytes 1048608 | tf_op jit(solution)/shard_map/all_to_all | solution.py:317
  58.3 2.6 %shard_map.108.refs_4_ = f32[16,128]{1,0:T(8,128)S(1)} custom-call(bf16[1024,512]{1,0:T(8,128)(2,1)} %bitcast.2.rows_ref.refs_10_, bf16[64,512]{1,0:T(8,128)(2,1)S(1)} %get-tuple-element.41.q_ref, s32[8,128]{1,0:T(8,128)S(1)} %pad.9.neg_ref.refs_9_), custom_call_target="tpu_custom_call" | custom-call | flops 1000000000 | bytes 100000 | tf_op jit(solution)/shard_map/pallas_call | solution.py:27
  60.8 1.1 collective-permute-start.11
  62.0 2.1 %collective-permute-start.10 = (f32[16,128]{1,0:T(8,128)S(1)}, f32[16,128]{1,0:T(8,128)S(1)}, u32[]{:S(2)}, u32[]{:S(2)}) collective-permute-start(f32[16,128]{1,0:T(8,128)S(1)} %shard_map.108.refs_4_), channel_id=1, source_target_pairs={{128,0},{192,64},{0,128},{64,192},{129,1},{193,65},{1,129},{65,193... | collective-permute-start | bytes 24584 | tf_op jit(solution)/shard_map/ppermute | solution.py:168
  64.1 1.3 %collective-permute-start.9 = (f32[16,128]{1,0:T(8,128)S(1)}, f32[16,128]{1,0:T(8,128)S(1)}, u32[]{:S(2)}, u32[]{:S(2)}) collective-permute-start(f32[16,128]{1,0:T(8,128)S(1)} %shard_map.108.refs_4_), channel_id=1, source_target_pairs={{64,0},{128,64},{192,128},{0,192},{65,1},{129,65},{193,129},{1,193... | collective-permute-start | bytes 24584 | tf_op jit(solution)/shard_map/ppermute | solution.py:168
  66.0 0.8 collective-permute-done.9.refs_5_
  66.7 3.3 %shard_map.109 = (bf16[1024,512]{1,0:T(8,128)(2,1)}, bf16[64,512]{1,0:T(8,128)(2,1)S(1)}, f32[128,512]{1,0:T(8,128)S(1)}, f32[8,128]{1,0:T(8,128)S(1)}) custom-call(f32[144,128]{1,0:T(8,128)S(1)} %shard_map.107.refs_0_, f32[144,128]{1,0:T(8,128)S(1)} %collective-permute-done.6.refs_1_, f32[144,128]{1,0:T(8,128)S(1)} %collective-permute-done.7.refs_2_, ...), custom_call_target="tpu_custom_call" | custom-call | flops 1000000000 | bytes 100000 | tf_op jit(solution)/shard_map/pallas_call | solution.py:27
  70.0 8.0 %all-to-all-start.1 = ((bf16[64,16,512]{2,1,0:T(8,128)(2,1)}), bf16[64,16,512]{2,1,0:T(8,128)(2,1)S(1)}, u32[]{:S(2)}, u32[]{:S(2)}) async-start(bf16[64,16,512]{2,1,0:T(8,128)(2,1)} %bitcast.6), calls=%async_computation.1 | async-start | bytes 2097152 | tf_op jit(solution)/shard_map/all_to_all | solution.py:347
  78.3 3.5 %collective-permute-start.13 = (bf16[64,512]{1,0:T(8,128)(2,1)S(1)}, bf16[64,512]{1,0:T(8,128)(2,1)S(1)}, u32[]{:S(2)}, u32[]{:S(2)}) collective-permute-start(bf16[64,512]{1,0:T(8,128)(2,1)S(1)} %get-tuple-element.45.u_ref), channel_id=1, source_target_pairs={{128,0},{192,64},{0,128},{64,192},{129,1},{193,65},{1,129},{65,193... | collective-permute-start | bytes 196616 | tf_op jit(solution)/shard_map/ppermute | solution.py:168
  82.3 1.6 %copy-done.2 = bf16[512,2048]{1,0:T(8,128)(2,1)S(1)} copy-done((bf16[512,2048]{1,0:T(8,128)(2,1)S(1)}, bf16[512,2048]{1,0:T(8,128)(2,1)}, u32[]{:S(2)}) %copy-start.2) | copy-done | bytes 2097176
  85.2 1.7 %shard_map.111 = bf16[64,512]{1,0:T(8,128)(2,1)} custom-call(s32[1]{0:T(128)} %bitcast.k_ref, f32[64,512]{1,0:T(8,128)S(1)} %shard_map.110.in_ref, bf16[64,512]{1,0:T(8,128)(2,1)S(1)} %collective-permute-done.12.refs_0_, bf16[64,512]{1,0:T(8,128)(2,1)S(1)} %collective-permute-done.13.refs_1_, bf16[64,512]{1,0:T(8,128)(2,1)S(1)} %collective-permute-done.14.refs_2_, ...), custom_call_target="tpu_custom_call" | custom-call | flops 1000000000 | bytes 100000 | tf_op jit(solution)/shard_map/pallas_call | solution.py:138
  86.9 19.1 %all-to-all-done.1 = bf16[64,16,512]{2,1,0:T(8,128)(2,1)S(1)} async-done(((bf16[64,16,512]{2,1,0:T(8,128)(2,1)}), bf16[64,16,512]{2,1,0:T(8,128)(2,1)S(1)}, u32[]{:S(2)}, u32[]{:S(2)}) %all-to-all-start.1) | async-done | bytes 1048608 | tf_op jit(solution)/shard_map/all_to_all | solution.py:347
  106.6 3.5 %collective-permute-start.16 = (bf16[128,512]{1,0:T(8,128)(2,1)S(1)}, bf16[128,512]{1,0:T(8,128)(2,1)S(1)}, u32[]{:S(2)}, u32[]{:S(2)}) collective-permute-start(bf16[128,512]{1,0:T(8,128)(2,1)S(1)} %shard_map.112.u_ref), channel_id=1, source_target_pairs={{128,0},{192,64},{0,128},{64,192},{129,1},{193,65},{1,129},{65,193... | collective-permute-start | bytes 393224 | tf_op jit(solution)/shard_map/ppermute | solution.py:168
  110.1 2.2 %copy-done.1 = bf16[1024,2048]{1,0:T(8,128)(2,1)S(1)} copy-done((bf16[1024,2048]{1,0:T(8,128)(2,1)S(1)}, bf16[1024,2048]{1,0:T(8,128)(2,1)}, u32[]{:S(2)}) %copy-start.1) | copy-done | bytes 4194328
  112.8 2.0 %collective-permute-done.16.refs_1_ = bf16[128,512]{1,0:T(8,128)(2,1)S(1)} collective-permute-done((bf16[128,512]{1,0:T(8,128)(2,1)S(1)}, bf16[128,512]{1,0:T(8,128)(2,1)S(1)}, u32[]{:S(2)}, u32[]{:S(2)}) %collective-permute-start.16) | collective-permute-done | bytes 131104 | tf_op jit(solution)/shard_map/ppermute | solution.py:168
  115.1 2.5 %shard_map.114 = bf16[128,1024]{1,0:T(8,128)(2,1)} custom-call(s32[1]{0:T(128)} %bitcast.k_ref, f32[128,1024]{1,0:T(8,128)S(1)} %shard_map.113.in_ref, bf16[128,512]{1,0:T(8,128)(2,1)S(1)} %collective-permute-done.15.refs_0_, bf16[128,512]{1,0:T(8,128)(2,1)S(1)} %collective-permute-done.16.refs_1_, bf16[128,512]{1,0:T(8,128)(2,1)S(1)} %collective-permute-done.17.refs_2_, ...), custom_call_target="tpu_custom_call" | custom-call | flops 1000000000 | bytes 100000 | tf_op jit(solution)/shard_map/pallas_call | solution.py:138
  (51 shorter events, 6.4 us)
Async XLA Ops:
  0.6 29.8 %copy-start = (s32[1,1024]{1,0:T(1,128)S(1)}, s32[1,1024]{1,0:T(1,128)}, u32[]{:S(2)}) copy-start(s32[1,1024]{1,0:T(1,128)} %param.13) | copy-start | bytes 12292
  0.6 9.1 %copy-start.6 = (s32[1,64,16]{1,2,0:T(8,128)S(1)}, s32[1,64,16]{1,2,0:T(8,128)}, u32[]{:S(2)}) copy-start(s32[1,64,16]{1,2,0:T(8,128)} %param.12) | copy-start | bytes 12292
  0.7 29.7 %copy-start.5 = (s32[64,7]{0,1:T(8,128)S(1)}, s32[64,7]{0,1:T(8,128)}, u32[]{:S(2)}) copy-start(s32[64,7]{0,1:T(8,128)} %param.14) | copy-start | bytes 5380
  4.1 6.0 %collective-permute-start = (bf16[128,512]{1,0:T(8,128)(2,1)}, bf16[128,512]{1,0:T(8,128)(2,1)S(1)}, u32[]{:S(2)}, u32[]{:S(2)}) collective-permute-start(bf16[128,512]{1,0:T(8,128)(2,1)} %get-tuple-element.28), channel_id=1, source_target_pairs={{0,64},{64,128},{128,192},{192,0},{1,65},{65,129},{129,193},{193,1... | collective-permute-start | bytes 393224 | tf_op jit(solution)/shard_map/ppermute | solution.py:161
  6.2 8.4 %collective-permute-start.1 = (bf16[128,512]{1,0:T(8,128)(2,1)}, bf16[128,512]{1,0:T(8,128)(2,1)S(1)}, u32[]{:S(2)}, u32[]{:S(2)}) collective-permute-start(bf16[128,512]{1,0:T(8,128)(2,1)} %get-tuple-element.29), channel_id=1, source_target_pairs={{0,128},{64,192},{128,0},{192,64},{1,129},{65,193},{129,1},{193,65... | collective-permute-start | bytes 393224 | tf_op jit(solution)/shard_map/ppermute | solution.py:161
  8.6 5.9 %collective-permute-start.2 = (bf16[128,512]{1,0:T(8,128)(2,1)}, bf16[128,512]{1,0:T(8,128)(2,1)S(1)}, u32[]{:S(2)}, u32[]{:S(2)}) collective-permute-start(bf16[128,512]{1,0:T(8,128)(2,1)} %get-tuple-element.30), channel_id=1, source_target_pairs={{0,192},{64,0},{128,64},{192,128},{1,193},{65,1},{129,65},{193,129... | collective-permute-start | bytes 393224 | tf_op jit(solution)/shard_map/ppermute | solution.py:161
  14.6 1.0 copy-start.3
  15.5 17.2 %copy-start.7 = (f32[64]{0:T(128)S(1)}, f32[64]{0:T(128)}, u32[]{:S(2)}) copy-start(f32[64]{0:T(128)} %param.15) | copy-start | bytes 772
  17.0 41.3 %all-to-all-start = ((bf16[64,16,512]{2,1,0:T(8,128)(2,1)}), bf16[64,16,512]{2,1,0:T(8,128)(2,1)}, u32[]{:S(2)}, u32[]{:S(2)}) async-start(bf16[64,16,512]{2,1,0:T(8,128)(2,1)} %bitcast.1), calls=%async_computation | async-start | bytes 2097152 | tf_op jit(solution)/shard_map/all_to_all | solution.py:317
  35.5 5.0 %collective-permute-start.3 = (bf16[64,512]{1,0:T(8,128)(2,1)}, bf16[64,512]{1,0:T(8,128)(2,1)S(1)}, u32[]{:S(2)}, u32[]{:S(2)}) collective-permute-start(bf16[64,512]{1,0:T(8,128)(2,1)} %get-tuple-element.34), channel_id=1, source_target_pairs={{0,64},{64,128},{128,192},{192,0},{1,65},{65,129},{129,193},{193,1... | collective-permute-start | bytes 196616 | tf_op jit(solution)/shard_map/ppermute | solution.py:161
  36.7 5.8 %collective-permute-start.4 = (bf16[64,512]{1,0:T(8,128)(2,1)}, bf16[64,512]{1,0:T(8,128)(2,1)S(1)}, u32[]{:S(2)}, u32[]{:S(2)}) collective-permute-start(bf16[64,512]{1,0:T(8,128)(2,1)} %get-tuple-element.35), channel_id=1, source_target_pairs={{0,128},{64,192},{128,0},{192,64},{1,129},{65,193},{129,1},{193,65... | collective-permute-start | bytes 196616 | tf_op jit(solution)/shard_map/ppermute | solution.py:161
  38.8 4.3 %collective-permute-start.5 = (bf16[64,512]{1,0:T(8,128)(2,1)}, bf16[64,512]{1,0:T(8,128)(2,1)S(1)}, u32[]{:S(2)}, u32[]{:S(2)}) collective-permute-start(bf16[64,512]{1,0:T(8,128)(2,1)} %get-tuple-element.36), channel_id=1, source_target_pairs={{0,192},{64,0},{128,64},{192,128},{1,193},{65,1},{129,65},{193,129... | collective-permute-start | bytes 196616 | tf_op jit(solution)/shard_map/ppermute | solution.py:161
  43.1 0.9 copy-start.4
  44.3 19.7 %collective-permute-start.8 = (f32[144,128]{1,0:T(8,128)S(1)}, f32[144,128]{1,0:T(8,128)S(1)}, u32[]{:S(2)}, u32[]{:S(2)}) collective-permute-start(f32[144,128]{1,0:T(8,128)S(1)} %shard_map.107.refs_0_), channel_id=1, source_target_pairs={{192,0},{0,64},{64,128},{128,192},{193,1},{1,65},{65,129},{129,193... | collective-permute-start | bytes 221192 | tf_op jit(solution)/shard_map/ppermute | solution.py:168
  44.5 20.8 %collective-permute-start.7 = (f32[144,128]{1,0:T(8,128)S(1)}, f32[144,128]{1,0:T(8,128)S(1)}, u32[]{:S(2)}, u32[]{:S(2)}) collective-permute-start(f32[144,128]{1,0:T(8,128)S(1)} %shard_map.107.refs_0_), channel_id=1, source_target_pairs={{128,0},{192,64},{0,128},{64,192},{129,1},{193,65},{1,129},{65,193... | collective-permute-start | bytes 221192 | tf_op jit(solution)/shard_map/ppermute | solution.py:168
  48.0 17.4 %collective-permute-start.6 = (f32[144,128]{1,0:T(8,128)S(1)}, f32[144,128]{1,0:T(8,128)S(1)}, u32[]{:S(2)}, u32[]{:S(2)}) collective-permute-start(f32[144,128]{1,0:T(8,128)S(1)} %shard_map.107.refs_0_), channel_id=1, source_target_pairs={{64,0},{128,64},{192,128},{0,192},{65,1},{129,65},{193,129},{1,193... | collective-permute-start | bytes 221192 | tf_op jit(solution)/shard_map/ppermute | solution.py:168
  60.8 4.5 %collective-permute-start.11 = (f32[16,128]{1,0:T(8,128)S(1)}, f32[16,128]{1,0:T(8,128)S(1)}, u32[]{:S(2)}, u32[]{:S(2)}) collective-permute-start(f32[16,128]{1,0:T(8,128)S(1)} %shard_map.108.refs_4_), channel_id=1, source_target_pairs={{192,0},{0,64},{64,128},{128,192},{193,1},{1,65},{65,129},{129,193... | collective-permute-start | bytes 24584 | tf_op jit(solution)/shard_map/ppermute | solution.py:168
  62.0 4.0 %collective-permute-start.10 = (f32[16,128]{1,0:T(8,128)S(1)}, f32[16,128]{1,0:T(8,128)S(1)}, u32[]{:S(2)}, u32[]{:S(2)}) collective-permute-start(f32[16,128]{1,0:T(8,128)S(1)} %shard_map.108.refs_4_), channel_id=1, source_target_pairs={{128,0},{192,64},{0,128},{64,192},{129,1},{193,65},{1,129},{65,193... | collective-permute-start | bytes 24584 | tf_op jit(solution)/shard_map/ppermute | solution.py:168
  64.1 2.6 %collective-permute-start.9 = (f32[16,128]{1,0:T(8,128)S(1)}, f32[16,128]{1,0:T(8,128)S(1)}, u32[]{:S(2)}, u32[]{:S(2)}) collective-permute-start(f32[16,128]{1,0:T(8,128)S(1)} %shard_map.108.refs_4_), channel_id=1, source_target_pairs={{64,0},{128,64},{192,128},{0,192},{65,1},{129,65},{193,129},{1,193... | collective-permute-start | bytes 24584 | tf_op jit(solution)/shard_map/ppermute | solution.py:168
  70.0 36.0 %all-to-all-start.1 = ((bf16[64,16,512]{2,1,0:T(8,128)(2,1)}), bf16[64,16,512]{2,1,0:T(8,128)(2,1)S(1)}, u32[]{:S(2)}, u32[]{:S(2)}) async-start(bf16[64,16,512]{2,1,0:T(8,128)(2,1)} %bitcast.6), calls=%async_computation.1 | async-start | bytes 2097152 | tf_op jit(solution)/shard_map/all_to_all | solution.py:347
  78.1 6.1 %collective-permute-start.14 = (bf16[64,512]{1,0:T(8,128)(2,1)S(1)}, bf16[64,512]{1,0:T(8,128)(2,1)S(1)}, u32[]{:S(2)}, u32[]{:S(2)}) collective-permute-start(bf16[64,512]{1,0:T(8,128)(2,1)S(1)} %get-tuple-element.45.u_ref), channel_id=1, source_target_pairs={{192,0},{0,64},{64,128},{128,192},{193,1},{1,65},{65,129},{129,193... | collective-permute-start | bytes 196616 | tf_op jit(solution)/shard_map/ppermute | solution.py:168
  78.3 6.7 %collective-permute-start.13 = (bf16[64,512]{1,0:T(8,128)(2,1)S(1)}, bf16[64,512]{1,0:T(8,128)(2,1)S(1)}, u32[]{:S(2)}, u32[]{:S(2)}) collective-permute-start(bf16[64,512]{1,0:T(8,128)(2,1)S(1)} %get-tuple-element.45.u_ref), channel_id=1, source_target_pairs={{128,0},{192,64},{0,128},{64,192},{129,1},{193,65},{1,129},{65,193... | collective-permute-start | bytes 196616 | tf_op jit(solution)/shard_map/ppermute | solution.py:168
  81.8 3.4 %collective-permute-start.12 = (bf16[64,512]{1,0:T(8,128)(2,1)S(1)}, bf16[64,512]{1,0:T(8,128)(2,1)S(1)}, u32[]{:S(2)}, u32[]{:S(2)}) collective-permute-start(bf16[64,512]{1,0:T(8,128)(2,1)S(1)} %get-tuple-element.45.u_ref), channel_id=1, source_target_pairs={{64,0},{128,64},{192,128},{0,192},{65,1},{129,65},{193,129},{1,193... | collective-permute-start | bytes 196616 | tf_op jit(solution)/shard_map/ppermute | solution.py:168
  82.3 1.6 %copy-start.2 = (bf16[512,2048]{1,0:T(8,128)(2,1)S(1)}, bf16[512,2048]{1,0:T(8,128)(2,1)}, u32[]{:S(2)}) copy-start(bf16[512,2048]{1,0:T(8,128)(2,1)} %refs_3_.2) | copy-start | bytes 6291460
  106.4 6.4 %collective-permute-start.17 = (bf16[128,512]{1,0:T(8,128)(2,1)S(1)}, bf16[128,512]{1,0:T(8,128)(2,1)S(1)}, u32[]{:S(2)}, u32[]{:S(2)}) collective-permute-start(bf16[128,512]{1,0:T(8,128)(2,1)S(1)} %shard_map.112.u_ref), channel_id=1, source_target_pairs={{192,0},{0,64},{64,128},{128,192},{193,1},{1,65},{65,129},{129,193... | collective-permute-start | bytes 393224 | tf_op jit(solution)/shard_map/ppermute | solution.py:168
  106.6 8.2 %collective-permute-start.16 = (bf16[128,512]{1,0:T(8,128)(2,1)S(1)}, bf16[128,512]{1,0:T(8,128)(2,1)S(1)}, u32[]{:S(2)}, u32[]{:S(2)}) collective-permute-start(bf16[128,512]{1,0:T(8,128)(2,1)S(1)} %shard_map.112.u_ref), channel_id=1, source_target_pairs={{128,0},{192,64},{0,128},{64,192},{129,1},{193,65},{1,129},{65,193... | collective-permute-start | bytes 393224 | tf_op jit(solution)/shard_map/ppermute | solution.py:168
  110.1 5.0 %collective-permute-start.15 = (bf16[128,512]{1,0:T(8,128)(2,1)S(1)}, bf16[128,512]{1,0:T(8,128)(2,1)S(1)}, u32[]{:S(2)}, u32[]{:S(2)}) collective-permute-start(bf16[128,512]{1,0:T(8,128)(2,1)S(1)} %shard_map.112.u_ref), channel_id=1, source_target_pairs={{64,0},{128,64},{192,128},{0,192},{65,1},{129,65},{193,129},{1,193... | collective-permute-start | bytes 393224 | tf_op jit(solution)/shard_map/ppermute | solution.py:168
  110.1 2.2 %copy-start.1 = (bf16[1024,2048]{1,0:T(8,128)(2,1)S(1)}, bf16[1024,2048]{1,0:T(8,128)(2,1)}, u32[]{:S(2)}) copy-start(bf16[1024,2048]{1,0:T(8,128)(2,1)} %refs_3_.3) | copy-start | bytes 12582916

commit v4 on v3

--- a/solution.py
+++ b/solution.py
@@ -41,34 +41,29 @@
     return hi, (x - hi.astype(f32)).astype(bf16)
 
 
-def project(x, w, k):
+def project_sends(x, w, k, mib):
     rows, depth = x.shape
     cols = w.shape[1] // N_PHASE
-    order = (2, 1, 3, 0)
+    order = (2, 1, 3)
 
     def body(k_ref, x_ref, w_ref, *refs):
-        outs, (x_buf, w_buf, own_buf, send_buf, sem_ref) = refs[:N_PHASE], refs[N_PHASE:]
+        outs, (x_buf, w_buf, out_buf, sem_ref) = refs[:3], refs[3:]
 
         def load(s):
             start = pl.multiple_of(lax.rem(k_ref[0] + s, N_PHASE) * cols, cols)
-            return pltpu.make_async_copy(w_ref.at[:, pl.ds(start, cols)], w_buf.at[s], sem_ref.at[s])
+            return pltpu.make_async_copy(w_ref.at[:, pl.ds(start, cols)], w_buf.at[s - 1], sem_ref.at[s])
 
         def store(s):
-            source = own_buf if s == 0 else send_buf.at[s - 1]
-            return pltpu.make_async_copy(source, outs[s], sem_ref.at[N_PHASE + 1 + s])
-
-        load_x = pltpu.make_async_copy(x_ref, x_buf, sem_ref.at[N_PHASE])
+            return pltpu.make_async_copy(out_buf.at[s - 1], outs[s - 1], sem_ref.at[N_PHASE + s])
+
+        load_x = pltpu.make_async_copy(x_ref, x_buf, sem_ref.at[0])
         load_x.start()
         for s in order:
             load(s).start()
         load_x.wait()
         for s in order:
             load(s).wait()
-            y = dot(x_buf[...], w_buf[s])
-            if s == 0:
-                own_buf[...] = y
-            else:
-                send_buf[s - 1] = y.astype(bf16)
+            out_buf[s - 1] = dot(x_buf[...], w_buf[s - 1]).astype(bf16)
             store(s).start()
         for s in order:
             store(s).wait()
@@ -77,27 +72,25 @@
     return pl.pallas_call(
         body,
         in_specs=[pl.BlockSpec(memory_space=pltpu.SMEM), hbm, hbm],
-        out_specs=[hbm] * N_PHASE,
-        out_shape=[jax.ShapeDtypeStruct((rows, cols), f32)]
-        + [jax.ShapeDtypeStruct((rows, cols), bf16)] * (N_PHASE - 1),
+        out_specs=[hbm] * 3,
+        out_shape=[jax.ShapeDtypeStruct((rows, cols), bf16)] * 3,
         scratch_shapes=[
             pltpu.VMEM((rows, depth), bf16),
-            pltpu.VMEM((N_PHASE, depth, cols), bf16),
-            pltpu.VMEM((rows, cols), f32),
-            pltpu.VMEM((N_PHASE - 1, rows, cols), bf16),
-            pltpu.SemaphoreType.DMA((2 * N_PHASE + 1,)),
+            pltpu.VMEM((3, depth, cols), bf16),
+            pltpu.VMEM((3, rows, cols), bf16),
+            pltpu.SemaphoreType.DMA((2 * N_PHASE,)),
         ],
-        compiler_params=params(63),
+        compiler_params=params(mib),
         cost_estimate=cost,
     )(k, x, w)
 
 
-def project_back_own(block, w, k):
-    rows, cols = block.shape
-    depth = w.shape[0]
-
-    def body(k_ref, u_ref, w_ref, acc_ref):
-        acc_ref[...] = dot(u_ref[...], w_ref[...], NT)
+def project_own(x, w, k):
+    rows, depth = x.shape
+    cols = w.shape[1] // N_PHASE
+
+    def body(k_ref, x_ref, w_ref, own_ref):
+        own_ref[...] = dot(x_ref[...], w_ref[...])
 
     return pl.pallas_call(
         body,
@@ -105,55 +98,51 @@
             num_scalar_prefetch=1,
             grid=(1,),
             in_specs=[
-                pl.BlockSpec((rows, cols), lambda s, k_ref: (0, 0)),
+                pl.BlockSpec((rows, depth), lambda s, k_ref: (0, 0)),
                 pl.BlockSpec((depth, cols), lambda s, k_ref: (0, k_ref[0])),
             ],
-            out_specs=pl.BlockSpec((rows, depth), lambda s, k_ref: (0, 0)),
+            out_specs=pl.BlockSpec((rows, cols), lambda s, k_ref: (0, 0)),
         ),
-        out_shape=jax.ShapeDtypeStruct((rows, depth), f32),
+        out_shape=jax.ShapeDtypeStruct((rows, cols), f32),
         compiler_params=params(),
         cost_estimate=cost,
-    )(k, block, w)
-
-
-def project_back_rest(acc, blocks, w, k):
-    rows, cols = blocks[0].shape
+    )(k, x, w)
+
+
+def project(x, w, k, mib=16):
+    return project_own(x, w, k), shift_sends(project_sends(x, w, k, mib))
+
+
+def project_back(u, w, k):
+    rows, cols = u.shape
     depth = w.shape[0]
 
-    def body(k_ref, in_ref, *refs):
-        block_refs, w_ref, out_ref, acc_ref = refs[:3], refs[3], refs[4], refs[5]
-        step = pl.program_id(0)
-        for s in range(N_PHASE - 1):
-
-            @pl.when(step == s)
-            def _():
-                before = in_ref if s == 0 else acc_ref
-                total = before[...] + dot(block_refs[s][...], w_ref[...], NT)
-                if s == N_PHASE - 2:
-                    out_ref[...] = total.astype(bf16)
-                else:
-                    acc_ref[...] = total
-
-    const = lambda shape: pl.BlockSpec(shape, lambda s, k_ref: (0, 0))
-    return pl.pallas_call(
-        body,
-        grid_spec=pltpu.PrefetchScalarGridSpec(
-            num_scalar_prefetch=1,
-            grid=(N_PHASE - 1,),
-            in_specs=[const((rows, depth))]
-            + [const((rows, cols))] * (N_PHASE - 1)
-            + [pl.BlockSpec((depth, cols), lambda s, k_ref: (0, lax.rem(k_ref[0] + s + 1, N_PHASE)))],
-            out_specs=const((rows, depth)),
-            scratch_shapes=[pltpu.VMEM((rows, depth), f32)],
-        ),
-        out_shape=jax.ShapeDtypeStruct((rows, depth), bf16),
-        compiler_params=params(),
-        cost_estimate=cost,
-    )(k, acc, *blocks, w)
-
-
-def project_back(u, w, k):
-    return project_back_rest(project_back_own(u, w, k), gather_blocks(u)[1:], w, k)
+    def columns(w_ref, k_ref, s):
+        return w_ref[:, pl.ds(pl.multiple_of(lax.rem(k_ref[0] + s, N_PHASE) * cols, cols), cols)]
+
+    def own(k_ref, u_ref, w_ref, acc_ref):
+        acc_ref[...] = dot(u_ref[...], columns(w_ref, k_ref, 0), NT)
+
+    def rest(k_ref, acc_ref, a_ref, b_ref, c_ref, w_ref, out_ref):
+        total = acc_ref[...]
+        for s, block in enumerate((a_ref, b_ref, c_ref), start=1):
+            total = total + dot(block[...], columns(w_ref, k_ref, s), NT)
+        out_ref[...] = total.astype(bf16)
+
+    def run(body, dtype, n):
+        vmem = pl.BlockSpec(memory_space=pltpu.VMEM)
+        return pl.pallas_call(
+            body,
+            in_specs=[pl.BlockSpec(memory_space=pltpu.SMEM)] + [vmem] * n,
+            out_specs=vmem,
+            out_shape=jax.ShapeDtypeStruct((rows, depth), dtype),
+            compiler_params=params(),
+            cost_estimate=cost,
+        )
+
+    blocks = gather_blocks(u)
+    acc = run(own, f32, 2)(k, blocks[0], w)
+    return run(rest, bf16, 5)(k, acc, *blocks[1:], w)
 
 
 def shift_sends(blocks):
@@ -182,12 +171,33 @@
     low_ref[...] = total.astype(bf16)
 
 
-def sum_docs(own, a, b, c, request_ref, total_ref, rows_ref):
-    total = sum_refs((own, a, b, c))
-    total_ref[...] = total
-    slots = rows_ref.shape[0]
-    onehot = (iota((total.shape[0], slots), 0) == request_ref[...]).astype(f32).astype(bf16)
-    rows_ref[...] = dot(onehot, total.astype(bf16), TN).astype(bf16)
+def sum_docs(parts, requests):
+    docs, cols = parts[0].shape
+    slots = requests.shape[1]
+    steps = 4
+    block = slots // steps
+
+    def body(a, b, c, d, request_ref, total_ref, rows_ref, low_ref):
+        @pl.when(pl.program_id(0) == 0)
+        def _():
+            total = sum_refs((a, b, c, d))
+            total_ref[...] = total
+            low_ref[...] = total.astype(bf16)
+
+        onehot = (iota((docs, block), 0) == request_ref[...]).astype(f32).astype(bf16)
+        rows_ref[...] = dot(onehot, low_ref[...], TN).astype(bf16)
+
+    whole = pl.BlockSpec((docs, cols), lambda s: (0, 0))
+    return pl.pallas_call(
+        body,
+        grid=(steps,),
+        in_specs=[whole] * 4 + [pl.BlockSpec((1, block), lambda s: (0, s))],
+        out_specs=[whole, pl.BlockSpec((block, cols), lambda s: (s, 0))],
+        out_shape=[jax.ShapeDtypeStruct((docs, cols), f32), jax.ShapeDtypeStruct((slots, cols), bf16)],
+        scratch_shapes=[pltpu.VMEM((docs, cols), bf16)],
+        compiler_params=params(),
+        cost_estimate=cost,
+    )(*parts, requests)
 
 
 def ones_row_sums(x):
@@ -308,18 +318,14 @@
     requests = document_requests.reshape(1, slots)
     neg_rows = jnp.pad(jnp.concatenate([negatives, negatives], axis=1), ((0, 1), (0, 0)), constant_values=-1)
 
-    d_own, *d_send = project(doc_states, doc_proj, k)
-    d_parts = shift_sends(d_send)
-    d_total, outgoing = call(
-        sum_docs, [((docs, cols), f32), ((slots, cols), bf16)], d_own, *d_parts, requests
-    )
+    d_own, d_parts = project(doc_states, doc_proj, k, 63)
+    d_total, outgoing = sum_docs([d_own] + d_parts, requests)
     outgoing, query_states = lax.optimization_barrier((outgoing, query_states))
     received = lax.all_to_all(
         outgoing.reshape(n_dp, cap, cols), "dp", split_axis=0, concat_axis=0, tiled=True
     ).reshape(slots, cols)
 
-    q_own, *q_send = project(query_states, query_proj, k)
-    q_parts = shift_sends(q_send)
+    q_own, q_parts = project(query_states, query_proj, k)
     q_total, q_low = call(sum_queries, [((queries, cols), f32), ((queries, cols), bf16)], q_own, *q_parts)
     (inner,) = call(inner_partials, [((docs + 16, 128), f32)], q_total, d_total)
     inner_all = gather_blocks(inner)

time: 119 us -> 115 us (0.966)
  Pallas kernels: 18.9 us -> 15 us
  local copies, waits for them, and re-layouts: 8.66 us -> 10.6 us
  waiting for transfers between devices: 41.7 us -> 40.2 us
    pallas_call x6 -> x5, Pallas kernels: 7.96 us -> 4.06 us  [call(): pl.pallas_call(body, out_shape=[jax.ShapeDtypeStruct(s, t) for s, t in ou...]
    ppermute x6, waiting for transfers between devices: 7.55 us -> 4.47 us  [shift_sends(): lax.ppermute(b, 'phase', [(i, (i + s) % N_PHASE) for i in range(N_PHASE)])]
    unnamed x17 -> x21, local copies, waits for them, and re-layouts: 5.74 us -> 7.67 us
    pallas_call x6 -> x9, Pallas kernels: 10.9 us -> 10.9 us  [the longest x2 4.25 us: project_sends(): pl.pallas_call(body, in_specs=[pl.BlockSpec(memory_space=pltpu.SMEM), hbm...]
  transfers between devices with their start and end apart: 20 -> 20, of which waited for: 13 -> 11; matrix products, arithmetic and copies ran while one was open for 3% -> 3% of each run, Pallas kernels for 7% -> 5%
where the time goes in v4:
time: 115 us; the launch traced here: 114 us
  starting transfers between devices  47.1 us (41%)
  waiting for transfers between devices  40.2 us (35%)
  Pallas kernels  15 us (13%)
  local copies, waits for them, and re-layouts  10.6 us (9%)
    all_to_all x1, waiting for transfers between devices, local(): lax.all_to_all(rows.reshape(n_dp, cap, cols), 'dp', split_axis=0, concat_...  19.6 us
    ppermute x12, starting transfers between devices, gather_blocks(): lax.ppermute(x, 'phase', [((i + s) % N_PHASE, i) for i in range(N_PHASE)])  15.7 us
    all_to_all x1, starting transfers between devices, local(): lax.all_to_all(outgoing.reshape(n_dp, cap, cols), 'dp', split_axis=0, con...  13.2 us
    all_to_all x1, waiting for transfers between devices, local(): lax.all_to_all(outgoing.reshape(n_dp, cap, cols), 'dp', split_axis=0, con...  11.4 us
    ppermute x6, starting transfers between devices, shift_sends(): lax.ppermute(b, 'phase', [(i, (i + s) % N_PHASE) for i in range(N_PHASE)])  10.3 us
    all_to_all x1, starting transfers between devices, local(): lax.all_to_all(rows.reshape(n_dp, cap, cols), 'dp', split_axis=0, concat_...  8.04 us
    unnamed x21, local copies, waits for them, and re-layouts  7.67 us
    ppermute x12, waiting for transfers between devices, gather_blocks(): lax.ppermute(x, 'phase', [((i + s) % N_PHASE, i) for i in range(N_PHASE)])  4.71 us
  transfers between devices with their start and end apart: 20, of which 11 were waited for; matrix products, arithmetic and copies ran while one was open for 3% of the time, Pallas kernels for 5%

profile of v4, /device:TPU:1, one launch (start us, length us, event | category | flops | bytes accessed | tf_op | source)
XLA Modules:
  0.0 114.0 jit_solution(9438488543568815752)
XLA Ops:
  0.7 3.0 %shard_map.104 = (bf16[128,512]{1,0:T(8,128)(2,1)}, bf16[128,512]{1,0:T(8,128)(2,1)}, bf16[128,512]{1,0:T(8,128)(2,1)}) custom-call(s32[1]{0:T(128)} %bitcast.k_ref, bf16[128,1024]{1,0:T(8,128)(2,1)} %x_ref.3, bf16[1024,2048]{1,0:T(8,128)(2,1)} %w_ref.15), custom_call_target="tpu_custom_call" | custom-call | flops 1000000000 | bytes 100000 | tf_op jit(solution)/shard_map/pallas_call | solution.py:72
  3.7 2.1 %collective-permute-start = (bf16[128,512]{1,0:T(8,128)(2,1)}, bf16[128,512]{1,0:T(8,128)(2,1)S(1)}, u32[]{:S(2)}, u32[]{:S(2)}) collective-permute-start(bf16[128,512]{1,0:T(8,128)(2,1)} %get-tuple-element.25), channel_id=1, source_target_pairs={{0,64},{64,128},{128,192},{192,0},{1,65},{65,129},{129,193},{193,1... | collective-permute-start | bytes 393224 | tf_op jit(solution)/shard_map/ppermute | solution.py:150
  5.8 2.4 %collective-permute-start.1 = (bf16[128,512]{1,0:T(8,128)(2,1)}, bf16[128,512]{1,0:T(8,128)(2,1)S(1)}, u32[]{:S(2)}, u32[]{:S(2)}) collective-permute-start(bf16[128,512]{1,0:T(8,128)(2,1)} %get-tuple-element.26), channel_id=1, source_target_pairs={{0,128},{64,192},{128,0},{192,64},{1,129},{65,193},{129,1},{193,65... | collective-permute-start | bytes 393224 | tf_op jit(solution)/shard_map/ppermute | solution.py:150
  8.3 1.2 %collective-permute-start.2 = (bf16[128,512]{1,0:T(8,128)(2,1)}, bf16[128,512]{1,0:T(8,128)(2,1)S(1)}, u32[]{:S(2)}, u32[]{:S(2)}) collective-permute-start(bf16[128,512]{1,0:T(8,128)(2,1)} %get-tuple-element.27), channel_id=1, source_target_pairs={{0,192},{64,0},{128,64},{192,128},{1,193},{65,1},{129,65},{193,129... | collective-permute-start | bytes 393224 | tf_op jit(solution)/shard_map/ppermute | solution.py:150
  9.6 2.2 %copy-done.1 = bf16[1024,2048]{1,0:T(8,128)(2,1)S(1)} copy-done((bf16[1024,2048]{1,0:T(8,128)(2,1)S(1)}, bf16[1024,2048]{1,0:T(8,128)(2,1)}, u32[]{:S(2)}) %copy-start.1) | copy-done | bytes 4194328
  12.2 2.0 %collective-permute-done.1.c = bf16[128,512]{1,0:T(8,128)(2,1)S(1)} collective-permute-done((bf16[128,512]{1,0:T(8,128)(2,1)}, bf16[128,512]{1,0:T(8,128)(2,1)S(1)}, u32[]{:S(2)}, u32[]{:S(2)}) %collective-permute-start.1) | collective-permute-done | bytes 131104 | tf_op jit(solution)/shard_map/ppermute | solution.py:150
  14.2 2.3 %shard_map.105 = (f32[128,512]{1,0:T(8,128)S(1)}, bf16[1024,512]{1,0:T(8,128)(2,1)}) custom-call(f32[128,512]{1,0:T(8,128)S(1)} %shard_map.103.a, bf16[128,512]{1,0:T(8,128)(2,1)S(1)} %collective-permute-done.b, bf16[128,512]{1,0:T(8,128)(2,1)S(1)} %collective-permute-done.1.c, bf16[128,512]{1,0:T(8,128)(2,1)S(1)} %collective-permute-done.2.d, ...), custom_call_target="tpu_custom_call" | custom-call | flops 1000000000 | bytes 100000 | tf_op jit(solution)/shard_map/pallas_call | solution.py:191
  16.5 13.2 %all-to-all-start = ((bf16[64,16,512]{2,1,0:T(8,128)(2,1)}), bf16[64,16,512]{2,1,0:T(8,128)(2,1)S(1)}, u32[]{:S(2)}, u32[]{:S(2)}) async-start(bf16[64,16,512]{2,1,0:T(8,128)(2,1)} %bitcast.1), calls=%async_computation | async-start | bytes 2097152 | tf_op jit(solution)/shard_map/all_to_all | solution.py:324
  29.8 2.1 %gather_fusion = s32[448]{0:T(512)S(1)} fusion(s32[1024]{0:T(1024)S(1)} %bitcast.14, s32[1024]{0:T(1024)S(1)} %pad_clamp_fusion), kind=kCustom, calls=%fused_computation | custom fusion | bytes 5376 | tf_op jit(solution)/shard_map/jit(_take)/gather | solution.py:332
  32.3 1.6 %copy-done.4 = bf16[512,2048]{1,0:T(8,128)(2,1)S(1)} copy-done((bf16[512,2048]{1,0:T(8,128)(2,1)S(1)}, bf16[512,2048]{1,0:T(8,128)(2,1)}, u32[]{:S(2)}) %copy-start.4) | copy-done | bytes 2097176
  33.9 1.2 %shard_map.107 = (bf16[64,512]{1,0:T(8,128)(2,1)S(1)}, bf16[64,512]{1,0:T(8,128)(2,1)S(1)}, bf16[64,512]{1,0:T(8,128)(2,1)S(1)}) custom-call(s32[1]{0:T(128)} %bitcast.k_ref, bf16[64,512]{1,0:T(8,128)(2,1)S(1)} %copy-done.6, bf16[512,2048]{1,0:T(8,128)(2,1)S(1)} %copy-done.4), custom_call_target="tpu_custom_call" | custom-call | flops 1000000000 | bytes 100000 | tf_op jit(solution)/shard_map/pallas_call | solution.py:72
  35.1 1.1 collective-permute-start.3
  36.2 2.1 %collective-permute-start.4 = (bf16[64,512]{1,0:T(8,128)(2,1)S(1)}, bf16[64,512]{1,0:T(8,128)(2,1)S(1)}, u32[]{:S(2)}, u32[]{:S(2)}) collective-permute-start(bf16[64,512]{1,0:T(8,128)(2,1)S(1)} %get-tuple-element.31), channel_id=1, source_target_pairs={{0,128},{64,192},{128,0},{192,64},{1,129},{65,193},{129,1},{193,65... | collective-permute-start | bytes 196616 | tf_op jit(solution)/shard_map/ppermute | solution.py:150
  38.4 1.3 %collective-permute-start.5 = (bf16[64,512]{1,0:T(8,128)(2,1)S(1)}, bf16[64,512]{1,0:T(8,128)(2,1)S(1)}, u32[]{:S(2)}, u32[]{:S(2)}) collective-permute-start(bf16[64,512]{1,0:T(8,128)(2,1)S(1)} %get-tuple-element.32), channel_id=1, source_target_pairs={{0,192},{64,0},{128,64},{192,128},{1,193},{65,1},{129,65},{193,129... | collective-permute-start | bytes 196616 | tf_op jit(solution)/shard_map/ppermute | solution.py:150
  39.9 1.9 %collective-permute-done.4.b = bf16[64,512]{1,0:T(8,128)(2,1)S(1)} collective-permute-done((bf16[64,512]{1,0:T(8,128)(2,1)S(1)}, bf16[64,512]{1,0:T(8,128)(2,1)S(1)}, u32[]{:S(2)}, u32[]{:S(2)}) %collective-permute-start.4) | collective-permute-done | bytes 65568 | tf_op jit(solution)/shard_map/ppermute | solution.py:150
  42.9 3.3 %collective-permute-start.7 = (f32[144,128]{1,0:T(8,128)S(1)}, f32[144,128]{1,0:T(8,128)S(1)}, u32[]{:S(2)}, u32[]{:S(2)}) collective-permute-start(f32[144,128]{1,0:T(8,128)S(1)} %shard_map.109.refs_0_), channel_id=1, source_target_pairs={{128,0},{192,64},{0,128},{64,192},{129,1},{193,65},{1,129},{65,193... | collective-permute-start | bytes 221192 | tf_op jit(solution)/shard_map/ppermute | solution.py:157
  46.2 11.4 %all-to-all-done = bf16[64,16,512]{2,1,0:T(8,128)(2,1)S(1)} async-done(((bf16[64,16,512]{2,1,0:T(8,128)(2,1)}), bf16[64,16,512]{2,1,0:T(8,128)(2,1)S(1)}, u32[]{:S(2)}, u32[]{:S(2)}) %all-to-all-start) | async-done | bytes 1048608 | tf_op jit(solution)/shard_map/all_to_all | solution.py:324
  57.7 1.3 %shard_map.110.refs_4_ = f32[16,128]{1,0:T(8,128)S(1)} custom-call(bf16[1024,512]{1,0:T(8,128)(2,1)S(1)} %bitcast.15, bf16[64,512]{1,0:T(8,128)(2,1)S(1)} %get-tuple-element.37.q_ref, s32[8,128]{1,0:T(8,128)S(1)} %pad.9.neg_ref.refs_9_), custom_call_target="tpu_custom_call" | custom-call | flops 1000000000 | bytes 100000 | tf_op jit(solution)/shard_map/pallas_call | solution.py:27
  59.0 1.1 collective-permute-start.11
  60.1 2.1 %collective-permute-start.10 = (f32[16,128]{1,0:T(8,128)S(1)}, f32[16,128]{1,0:T(8,128)S(1)}, u32[]{:S(2)}, u32[]{:S(2)}) collective-permute-start(f32[16,128]{1,0:T(8,128)S(1)} %shard_map.110.refs_4_), channel_id=1, source_target_pairs={{128,0},{192,64},{0,128},{64,192},{129,1},{193,65},{1,129},{65,193... | collective-permute-start | bytes 24584 | tf_op jit(solution)/shard_map/ppermute | solution.py:157
  62.3 1.3 %collective-permute-start.9 = (f32[16,128]{1,0:T(8,128)S(1)}, f32[16,128]{1,0:T(8,128)S(1)}, u32[]{:S(2)}, u32[]{:S(2)}) collective-permute-start(f32[16,128]{1,0:T(8,128)S(1)} %shard_map.110.refs_4_), channel_id=1, source_target_pairs={{64,0},{128,64},{192,128},{0,192},{65,1},{129,65},{193,129},{1,193... | collective-permute-start | bytes 24584 | tf_op jit(solution)/shard_map/ppermute | solution.py:157
  64.2 0.8 collective-permute-done.9.refs_5_
  64.9 2.1 %shard_map.111 = (bf16[1024,512]{1,0:T(8,128)(2,1)}, bf16[64,512]{1,0:T(8,128)(2,1)S(1)}, f32[128,512]{1,0:T(8,128)S(1)}, f32[8,128]{1,0:T(8,128)S(1)}) custom-call(f32[144,128]{1,0:T(8,128)S(1)} %shard_map.109.refs_0_, f32[144,128]{1,0:T(8,128)S(1)} %collective-permute-done.6.refs_1_, f32[144,128]{1,0:T(8,128)S(1)} %collective-permute-done.7.refs_2_, ...), custom_call_target="tpu_custom_call" | custom-call | flops 1000000000 | bytes 100000 | tf_op jit(solution)/shard_map/pallas_call | solution.py:27
  67.0 8.0 %all-to-all-start.1 = ((bf16[64,16,512]{2,1,0:T(8,128)(2,1)}), bf16[64,16,512]{2,1,0:T(8,128)(2,1)S(1)}, u32[]{:S(2)}, u32[]{:S(2)}) async-start(bf16[64,16,512]{2,1,0:T(8,128)(2,1)} %bitcast.6), calls=%async_computation.1 | async-start | bytes 2097152 | tf_op jit(solution)/shard_map/all_to_all | solution.py:353
  75.3 3.5 %collective-permute-start.13 = (bf16[64,512]{1,0:T(8,128)(2,1)S(1)}, bf16[64,512]{1,0:T(8,128)(2,1)S(1)}, u32[]{:S(2)}, u32[]{:S(2)}) collective-permute-start(bf16[64,512]{1,0:T(8,128)(2,1)S(1)} %get-tuple-element.41.u_ref), channel_id=1, source_target_pairs={{128,0},{192,64},{0,128},{64,192},{129,1},{193,65},{1,129},{65,193... | collective-permute-start | bytes 196616 | tf_op jit(solution)/shard_map/ppermute | solution.py:157
  79.3 1.6 %copy-done.5 = bf16[512,2048]{1,0:T(8,128)(2,1)S(1)} copy-done((bf16[512,2048]{1,0:T(8,128)(2,1)S(1)}, bf16[512,2048]{1,0:T(8,128)(2,1)}, u32[]{:S(2)}) %copy-start.5) | copy-done | bytes 2097176
  82.2 1.2 %shard_map.113 = bf16[64,512]{1,0:T(8,128)(2,1)} custom-call(s32[1]{0:T(128)} %bitcast.k_ref, f32[64,512]{1,0:T(8,128)S(1)} %shard_map.112.acc_ref, bf16[64,512]{1,0:T(8,128)(2,1)S(1)} %collective-permute-done.12.a_ref, bf16[64,512]{1,0:T(8,128)(2,1)S(1)} %collective-permute-done.13.b_ref, bf16[64,512]{1,0:T(8,128)(2,1)S(1)} %collective-permute-done.14.c_ref, ...), custom_call_target="tpu_custom_call" | custom-call | flops 1000000000 | bytes 100000 | tf_op jit(solution)/shard_map/pallas_call | solution.py:145
  83.5 19.6 %all-to-all-done.1 = bf16[64,16,512]{2,1,0:T(8,128)(2,1)S(1)} async-done(((bf16[64,16,512]{2,1,0:T(8,128)(2,1)}), bf16[64,16,512]{2,1,0:T(8,128)(2,1)S(1)}, u32[]{:S(2)}, u32[]{:S(2)}) %all-to-all-start.1) | async-done | bytes 1048608 | tf_op jit(solution)/shard_map/all_to_all | solution.py:353
  103.6 3.5 %collective-permute-start.16 = (bf16[128,512]{1,0:T(8,128)(2,1)S(1)}, bf16[128,512]{1,0:T(8,128)(2,1)S(1)}, u32[]{:S(2)}, u32[]{:S(2)}) collective-permute-start(bf16[128,512]{1,0:T(8,128)(2,1)S(1)} %shard_map.114.u_ref), channel_id=1, source_target_pairs={{128,0},{192,64},{0,128},{64,192},{129,1},{193,65},{1,129},{65,193... | collective-permute-start | bytes 393224 | tf_op jit(solution)/shard_map/ppermute | solution.py:157
  107.1 2.2 %copy-done.2 = bf16[1024,2048]{1,0:T(8,128)(2,1)S(1)} copy-done((bf16[1024,2048]{1,0:T(8,128)(2,1)S(1)}, bf16[1024,2048]{1,0:T(8,128)(2,1)}, u32[]{:S(2)}) %copy-start.2) | copy-done | bytes 4194328
  109.8 2.0 %collective-permute-done.16.b_ref = bf16[128,512]{1,0:T(8,128)(2,1)S(1)} collective-permute-done((bf16[128,512]{1,0:T(8,128)(2,1)S(1)}, bf16[128,512]{1,0:T(8,128)(2,1)S(1)}, u32[]{:S(2)}, u32[]{:S(2)}) %collective-permute-start.16) | collective-permute-done | bytes 131104 | tf_op jit(solution)/shard_map/ppermute | solution.py:157
  112.1 1.9 %shard_map.116 = bf16[128,1024]{1,0:T(8,128)(2,1)} custom-call(s32[1]{0:T(128)} %bitcast.k_ref, f32[128,1024]{1,0:T(8,128)S(1)} %shard_map.115.acc_ref, bf16[128,512]{1,0:T(8,128)(2,1)S(1)} %collective-permute-done.15.a_ref, bf16[128,512]{1,0:T(8,128)(2,1)S(1)} %collective-permute-done.16.b_ref, bf16[128,512]{1,0:T(8,128)(2,1)S(1)} %collective-permute-done.17.c_ref, ...), custom_call_target="tpu_custom_call" | custom-call | flops 1000000000 | bytes 100000 | tf_op jit(solution)/shard_map/pallas_call | solution.py:145
  (57 shorter events, 6.3 us)
Async XLA Ops:
  0.6 29.2 %copy-start = (s32[1,1024]{1,0:T(1,128)S(1)}, s32[1,1024]{1,0:T(1,128)}, u32[]{:S(2)}) copy-start(s32[1,1024]{1,0:T(1,128)} %param.13) | copy-start | bytes 12292
  0.6 9.0 %copy-start.3 = (bf16[128,1024]{1,0:T(8,128)(2,1)S(1)}, bf16[128,1024]{1,0:T(8,128)(2,1)}, u32[]{:S(2)}) copy-start(bf16[128,1024]{1,0:T(8,128)(2,1)} %x_ref.3) | copy-start | bytes 786436
  0.7 8.8 %copy-start.8 = (s32[1,64,16]{1,2,0:T(8,128)S(1)}, s32[1,64,16]{1,2,0:T(8,128)}, u32[]{:S(2)}) copy-start(s32[1,64,16]{1,2,0:T(8,128)} %param.12) | copy-start | bytes 12292
  3.7 8.4 %collective-permute-start = (bf16[128,512]{1,0:T(8,128)(2,1)}, bf16[128,512]{1,0:T(8,128)(2,1)S(1)}, u32[]{:S(2)}, u32[]{:S(2)}) collective-permute-start(bf16[128,512]{1,0:T(8,128)(2,1)} %get-tuple-element.25), channel_id=1, source_target_pairs={{0,64},{64,128},{128,192},{192,0},{1,65},{65,129},{129,193},{193,1... | collective-permute-start | bytes 393224 | tf_op jit(solution)/shard_map/ppermute | solution.py:150
  5.8 8.4 %collective-permute-start.1 = (bf16[128,512]{1,0:T(8,128)(2,1)}, bf16[128,512]{1,0:T(8,128)(2,1)S(1)}, u32[]{:S(2)}, u32[]{:S(2)}) collective-permute-start(bf16[128,512]{1,0:T(8,128)(2,1)} %get-tuple-element.26), channel_id=1, source_target_pairs={{0,128},{64,192},{128,0},{192,64},{1,129},{65,193},{129,1},{193,65... | collective-permute-start | bytes 393224 | tf_op jit(solution)/shard_map/ppermute | solution.py:150
  8.3 5.9 %collective-permute-start.2 = (bf16[128,512]{1,0:T(8,128)(2,1)}, bf16[128,512]{1,0:T(8,128)(2,1)S(1)}, u32[]{:S(2)}, u32[]{:S(2)}) collective-permute-start(bf16[128,512]{1,0:T(8,128)(2,1)} %get-tuple-element.27), channel_id=1, source_target_pairs={{0,192},{64,0},{128,64},{192,128},{1,193},{65,1},{129,65},{193,129... | collective-permute-start | bytes 393224 | tf_op jit(solution)/shard_map/ppermute | solution.py:150
  9.6 2.2 %copy-start.1 = (bf16[1024,2048]{1,0:T(8,128)(2,1)S(1)}, bf16[1024,2048]{1,0:T(8,128)(2,1)}, u32[]{:S(2)}) copy-start(bf16[1024,2048]{1,0:T(8,128)(2,1)} %w_ref.15) | copy-start | bytes 12582916
  11.8 17.9 %copy-start.7 = (s32[64,7]{0,1:T(8,128)S(1)}, s32[64,7]{0,1:T(8,128)}, u32[]{:S(2)}) copy-start(s32[64,7]{0,1:T(8,128)} %param.14) | copy-start | bytes 5380
  12.1 19.9 %copy-start.9 = (f32[64]{0:T(128)S(1)}, f32[64]{0:T(128)}, u32[]{:S(2)}) copy-start(f32[64]{0:T(128)} %param.15) | copy-start | bytes 772
  12.1 20.2 %copy-start.6 = (bf16[64,512]{1,0:T(8,128)(2,1)S(1)}, bf16[64,512]{1,0:T(8,128)(2,1)}, u32[]{:S(2)}) copy-start(bf16[64,512]{1,0:T(8,128)(2,1)} %x_ref.5) | copy-start | bytes 196612
  16.5 41.2 %all-to-all-start = ((bf16[64,16,512]{2,1,0:T(8,128)(2,1)}), bf16[64,16,512]{2,1,0:T(8,128)(2,1)S(1)}, u32[]{:S(2)}, u32[]{:S(2)}) async-start(bf16[64,16,512]{2,1,0:T(8,128)(2,1)} %bitcast.1), calls=%async_computation | async-start | bytes 2097152 | tf_op jit(solution)/shard_map/all_to_all | solution.py:324
  32.3 1.6 %copy-start.4 = (bf16[512,2048]{1,0:T(8,128)(2,1)S(1)}, bf16[512,2048]{1,0:T(8,128)(2,1)}, u32[]{:S(2)}) copy-start(bf16[512,2048]{1,0:T(8,128)(2,1)} %w_ref.13) | copy-start | bytes 6291460
  35.1 4.7 %collective-permute-start.3 = (bf16[64,512]{1,0:T(8,128)(2,1)S(1)}, bf16[64,512]{1,0:T(8,128)(2,1)S(1)}, u32[]{:S(2)}, u32[]{:S(2)}) collective-permute-start(bf16[64,512]{1,0:T(8,128)(2,1)S(1)} %get-tuple-element.30), channel_id=1, source_target_pairs={{0,64},{64,128},{128,192},{192,0},{1,65},{65,129},{129,193},{193,1... | collective-permute-start | bytes 196616 | tf_op jit(solution)/shard_map/ppermute | solution.py:150
  36.2 5.5 %collective-permute-start.4 = (bf16[64,512]{1,0:T(8,128)(2,1)S(1)}, bf16[64,512]{1,0:T(8,128)(2,1)S(1)}, u32[]{:S(2)}, u32[]{:S(2)}) collective-permute-start(bf16[64,512]{1,0:T(8,128)(2,1)S(1)} %get-tuple-element.31), channel_id=1, source_target_pairs={{0,128},{64,192},{128,0},{192,64},{1,129},{65,193},{129,1},{193,65... | collective-permute-start | bytes 196616 | tf_op jit(solution)/shard_map/ppermute | solution.py:150
  38.4 3.9 %collective-permute-start.5 = (bf16[64,512]{1,0:T(8,128)(2,1)S(1)}, bf16[64,512]{1,0:T(8,128)(2,1)S(1)}, u32[]{:S(2)}, u32[]{:S(2)}) collective-permute-start(bf16[64,512]{1,0:T(8,128)(2,1)S(1)} %get-tuple-element.32), channel_id=1, source_target_pairs={{0,192},{64,0},{128,64},{192,128},{1,193},{65,1},{129,65},{193,129... | collective-permute-start | bytes 196616 | tf_op jit(solution)/shard_map/ppermute | solution.py:150
  42.6 19.7 %collective-permute-start.8 = (f32[144,128]{1,0:T(8,128)S(1)}, f32[144,128]{1,0:T(8,128)S(1)}, u32[]{:S(2)}, u32[]{:S(2)}) collective-permute-start(f32[144,128]{1,0:T(8,128)S(1)} %shard_map.109.refs_0_), channel_id=1, source_target_pairs={{192,0},{0,64},{64,128},{128,192},{193,1},{1,65},{65,129},{129,193... | collective-permute-start | bytes 221192 | tf_op jit(solution)/shard_map/ppermute | solution.py:157
  42.9 20.7 %collective-permute-start.7 = (f32[144,128]{1,0:T(8,128)S(1)}, f32[144,128]{1,0:T(8,128)S(1)}, u32[]{:S(2)}, u32[]{:S(2)}) collective-permute-start(f32[144,128]{1,0:T(8,128)S(1)} %shard_map.109.refs_0_), channel_id=1, source_target_pairs={{128,0},{192,64},{0,128},{64,192},{129,1},{193,65},{1,129},{65,193... | collective-permute-start | bytes 221192 | tf_op jit(solution)/shard_map/ppermute | solution.py:157
  46.2 17.3 %collective-permute-start.6 = (f32[144,128]{1,0:T(8,128)S(1)}, f32[144,128]{1,0:T(8,128)S(1)}, u32[]{:S(2)}, u32[]{:S(2)}) collective-permute-start(f32[144,128]{1,0:T(8,128)S(1)} %shard_map.109.refs_0_), channel_id=1, source_target_pairs={{64,0},{128,64},{192,128},{0,192},{65,1},{129,65},{193,129},{1,193... | collective-permute-start | bytes 221192 | tf_op jit(solution)/shard_map/ppermute | solution.py:157
  59.0 4.5 %collective-permute-start.11 = (f32[16,128]{1,0:T(8,128)S(1)}, f32[16,128]{1,0:T(8,128)S(1)}, u32[]{:S(2)}, u32[]{:S(2)}) collective-permute-start(f32[16,128]{1,0:T(8,128)S(1)} %shard_map.110.refs_4_), channel_id=1, source_target_pairs={{192,0},{0,64},{64,128},{128,192},{193,1},{1,65},{65,129},{129,193... | collective-permute-start | bytes 24584 | tf_op jit(solution)/shard_map/ppermute | solution.py:157
  60.1 4.0 %collective-permute-start.10 = (f32[16,128]{1,0:T(8,128)S(1)}, f32[16,128]{1,0:T(8,128)S(1)}, u32[]{:S(2)}, u32[]{:S(2)}) collective-permute-start(f32[16,128]{1,0:T(8,128)S(1)} %shard_map.110.refs_4_), channel_id=1, source_target_pairs={{128,0},{192,64},{0,128},{64,192},{129,1},{193,65},{1,129},{65,193... | collective-permute-start | bytes 24584 | tf_op jit(solution)/shard_map/ppermute | solution.py:157
  62.3 2.6 %collective-permute-start.9 = (f32[16,128]{1,0:T(8,128)S(1)}, f32[16,128]{1,0:T(8,128)S(1)}, u32[]{:S(2)}, u32[]{:S(2)}) collective-permute-start(f32[16,128]{1,0:T(8,128)S(1)} %shard_map.110.refs_4_), channel_id=1, source_target_pairs={{64,0},{128,64},{192,128},{0,192},{65,1},{129,65},{193,129},{1,193... | collective-permute-start | bytes 24584 | tf_op jit(solution)/shard_map/ppermute | solution.py:157
  67.0 36.0 %all-to-all-start.1 = ((bf16[64,16,512]{2,1,0:T(8,128)(2,1)}), bf16[64,16,512]{2,1,0:T(8,128)(2,1)S(1)}, u32[]{:S(2)}, u32[]{:S(2)}) async-start(bf16[64,16,512]{2,1,0:T(8,128)(2,1)} %bitcast.6), calls=%async_computation.1 | async-start | bytes 2097152 | tf_op jit(solution)/shard_map/all_to_all | solution.py:353
  75.0 6.1 %collective-permute-start.14 = (bf16[64,512]{1,0:T(8,128)(2,1)S(1)}, bf16[64,512]{1,0:T(8,128)(2,1)S(1)}, u32[]{:S(2)}, u32[]{:S(2)}) collective-permute-start(bf16[64,512]{1,0:T(8,128)(2,1)S(1)} %get-tuple-element.41.u_ref), channel_id=1, source_target_pairs={{192,0},{0,64},{64,128},{128,192},{193,1},{1,65},{65,129},{129,193... | collective-permute-start | bytes 196616 | tf_op jit(solution)/shard_map/ppermute | solution.py:157
  75.3 6.7 %collective-permute-start.13 = (bf16[64,512]{1,0:T(8,128)(2,1)S(1)}, bf16[64,512]{1,0:T(8,128)(2,1)S(1)}, u32[]{:S(2)}, u32[]{:S(2)}) collective-permute-start(bf16[64,512]{1,0:T(8,128)(2,1)S(1)} %get-tuple-element.41.u_ref), channel_id=1, source_target_pairs={{128,0},{192,64},{0,128},{64,192},{129,1},{193,65},{1,129},{65,193... | collective-permute-start | bytes 196616 | tf_op jit(solution)/shard_map/ppermute | solution.py:157
  78.8 3.4 %collective-permute-start.12 = (bf16[64,512]{1,0:T(8,128)(2,1)S(1)}, bf16[64,512]{1,0:T(8,128)(2,1)S(1)}, u32[]{:S(2)}, u32[]{:S(2)}) collective-permute-start(bf16[64,512]{1,0:T(8,128)(2,1)S(1)} %get-tuple-element.41.u_ref), channel_id=1, source_target_pairs={{64,0},{128,64},{192,128},{0,192},{65,1},{129,65},{193,129},{1,193... | collective-permute-start | bytes 196616 | tf_op jit(solution)/shard_map/ppermute | solution.py:157
  79.3 1.6 %copy-start.5 = (bf16[512,2048]{1,0:T(8,128)(2,1)S(1)}, bf16[512,2048]{1,0:T(8,128)(2,1)}, u32[]{:S(2)}) copy-start(bf16[512,2048]{1,0:T(8,128)(2,1)} %w_ref.13) | copy-start | bytes 6291460
  103.3 6.4 %collective-permute-start.17 = (bf16[128,512]{1,0:T(8,128)(2,1)S(1)}, bf16[128,512]{1,0:T(8,128)(2,1)S(1)}, u32[]{:S(2)}, u32[]{:S(2)}) collective-permute-start(bf16[128,512]{1,0:T(8,128)(2,1)S(1)} %shard_map.114.u_ref), channel_id=1, source_target_pairs={{192,0},{0,64},{64,128},{128,192},{193,1},{1,65},{65,129},{129,193... | collective-permute-start | bytes 393224 | tf_op jit(solution)/shard_map/ppermute | solution.py:157
  103.6 8.2 %collective-permute-start.16 = (bf16[128,512]{1,0:T(8,128)(2,1)S(1)}, bf16[128,512]{1,0:T(8,128)(2,1)S(1)}, u32[]{:S(2)}, u32[]{:S(2)}) collective-permute-start(bf16[128,512]{1,0:T(8,128)(2,1)S(1)} %shard_map.114.u_ref), channel_id=1, source_target_pairs={{128,0},{192,64},{0,128},{64,192},{129,1},{193,65},{1,129},{65,193... | collective-permute-start | bytes 393224 | tf_op jit(solution)/shard_map/ppermute | solution.py:157
  107.1 5.0 %collective-permute-start.15 = (bf16[128,512]{1,0:T(8,128)(2,1)S(1)}, bf16[128,512]{1,0:T(8,128)(2,1)S(1)}, u32[]{:S(2)}, u32[]{:S(2)}) collective-permute-start(bf16[128,512]{1,0:T(8,128)(2,1)S(1)} %shard_map.114.u_ref), channel_id=1, source_target_pairs={{64,0},{128,64},{192,128},{0,192},{65,1},{129,65},{193,129},{1,193... | collective-permute-start | bytes 393224 | tf_op jit(solution)/shard_map/ppermute | solution.py:157
  107.1 2.2 %copy-start.2 = (bf16[1024,2048]{1,0:T(8,128)(2,1)S(1)}, bf16[1024,2048]{1,0:T(8,128)(2,1)}, u32[]{:S(2)}) copy-start(bf16[1024,2048]{1,0:T(8,128)(2,1)} %w_ref.15) | copy-start | bytes 12582916

commit v5 on v4

--- a/solution.py
+++ b/solution.py
@@ -12,6 +12,7 @@
 NT = (((1,), (1,)), ((), ()))
 TN = (((0,), (0,)), ((), ()))
 N_PHASE = 4
+CHUNKS = 4
 cost = pl.CostEstimate(flops=10**9, bytes_accessed=10**5, transcendentals=0)
 
 
@@ -41,44 +42,44 @@
     return hi, (x - hi.astype(f32)).astype(bf16)
 
 
-def project_sends(x, w, k, mib):
+def project_sends(x, w, k, mib, order):
     rows, depth = x.shape
     cols = w.shape[1] // N_PHASE
-    order = (2, 1, 3)
+    n = len(order)
 
     def body(k_ref, x_ref, w_ref, *refs):
-        outs, (x_buf, w_buf, out_buf, sem_ref) = refs[:3], refs[3:]
-
-        def load(s):
-            start = pl.multiple_of(lax.rem(k_ref[0] + s, N_PHASE) * cols, cols)
-            return pltpu.make_async_copy(w_ref.at[:, pl.ds(start, cols)], w_buf.at[s - 1], sem_ref.at[s])
-
-        def store(s):
-            return pltpu.make_async_copy(out_buf.at[s - 1], outs[s - 1], sem_ref.at[N_PHASE + s])
-
-        load_x = pltpu.make_async_copy(x_ref, x_buf, sem_ref.at[0])
+        outs, (x_buf, w_buf, out_buf, sem_ref) = refs[:n], refs[n:]
+
+        def load(i):
+            start = pl.multiple_of(lax.rem(k_ref[0] + order[i], N_PHASE) * cols, cols)
+            return pltpu.make_async_copy(w_ref.at[:, pl.ds(start, cols)], w_buf.at[i], sem_ref.at[i])
+
+        def store(i):
+            return pltpu.make_async_copy(out_buf.at[i], outs[i], sem_ref.at[n + i])
+
+        load_x = pltpu.make_async_copy(x_ref, x_buf, sem_ref.at[2 * n])
         load_x.start()
-        for s in order:
-            load(s).start()
+        for i in range(n):
+            load(i).start()
         load_x.wait()
-        for s in order:
-            load(s).wait()
-            out_buf[s - 1] = dot(x_buf[...], w_buf[s - 1]).astype(bf16)
-            store(s).start()
-        for s in order:
-            store(s).wait()
+        for i in range(n):
+            load(i).wait()
+            out_buf[i] = dot(x_buf[...], w_buf[i]).astype(bf16)
+            store(i).start()
+        for i in range(n):
+            store(i).wait()
 
     hbm = pl.BlockSpec(memory_space=pltpu.HBM)
     return pl.pallas_call(
         body,
         in_specs=[pl.BlockSpec(memory_space=pltpu.SMEM), hbm, hbm],
-        out_specs=[hbm] * 3,
-        out_shape=[jax.ShapeDtypeStruct((rows, cols), bf16)] * 3,
+        out_specs=[hbm] * n,
+        out_shape=[jax.ShapeDtypeStruct((rows, cols), bf16)] * n,
         scratch_shapes=[
             pltpu.VMEM((rows, depth), bf16),
-            pltpu.VMEM((3, depth, cols), bf16),
-            pltpu.VMEM((3, rows, cols), bf16),
-            pltpu.SemaphoreType.DMA((2 * N_PHASE,)),
+            pltpu.VMEM((n, depth, cols), bf16),
+            pltpu.VMEM((n, rows, cols), bf16),
+            pltpu.SemaphoreType.DMA((2 * n + 1,)),
         ],
         compiler_params=params(mib),
         cost_estimate=cost,
@@ -109,10 +110,6 @@
     )(k, x, w)
 
 
-def project(x, w, k, mib=16):
-    return project_own(x, w, k), shift_sends(project_sends(x, w, k, mib))
-
-
 def project_back(u, w, k):
     rows, cols = u.shape
     depth = w.shape[0]
@@ -120,36 +117,35 @@
     def columns(w_ref, k_ref, s):
         return w_ref[:, pl.ds(pl.multiple_of(lax.rem(k_ref[0] + s, N_PHASE) * cols, cols), cols)]
 
-    def own(k_ref, u_ref, w_ref, acc_ref):
-        acc_ref[...] = dot(u_ref[...], columns(w_ref, k_ref, 0), NT)
-
-    def rest(k_ref, acc_ref, a_ref, b_ref, c_ref, w_ref, out_ref):
-        total = acc_ref[...]
-        for s, block in enumerate((a_ref, b_ref, c_ref), start=1):
-            total = total + dot(block[...], columns(w_ref, k_ref, s), NT)
-        out_ref[...] = total.astype(bf16)
-
-    def run(body, dtype, n):
+    def product(*shifts):
+        def body(k_ref, *refs):
+            block_refs, w_ref, out_ref = refs[-len(shifts) - 2 : -2], refs[-2], refs[-1]
+            total = sum(dot(r[...], columns(w_ref, k_ref, s), NT) for s, r in zip(shifts, block_refs))
+            if len(refs) > len(shifts) + 2:
+                total = refs[0][...] + total
+            out_ref[...] = total.astype(out_ref.dtype)
+
+        return body
+
+    def run(body, dtype, *args):
         vmem = pl.BlockSpec(memory_space=pltpu.VMEM)
         return pl.pallas_call(
             body,
-            in_specs=[pl.BlockSpec(memory_space=pltpu.SMEM)] + [vmem] * n,
+            in_specs=[pl.BlockSpec(memory_space=pltpu.SMEM)] + [vmem] * len(args),
             out_specs=vmem,
             out_shape=jax.ShapeDtypeStruct((rows, depth), dtype),
             compiler_params=params(),
             cost_estimate=cost,
-        )
+        )(k, *args)
 
     blocks = gather_blocks(u)
-    acc = run(own, f32, 2)(k, blocks[0], w)
-    return run(rest, bf16, 5)(k, acc, *blocks[1:], w)
-
-
-def shift_sends(blocks):
-    return [
-        lax.ppermute(b, "phase", [(i, (i + s) % N_PHASE) for i in range(N_PHASE)])
-        for s, b in enumerate(blocks, start=1)
-    ]
+    acc = run(product(0), f32, blocks[0], w)
+    acc = run(product(3), f32, acc, blocks[3], w)
+    return run(product(1, 2), bf16, acc, blocks[1], blocks[2], w)
+
+
+def send(block, s):
+    return lax.ppermute(block, "phase", [(i, (i + s) % N_PHASE) for i in range(N_PHASE)])
 
 
 def gather_blocks(x):
@@ -171,33 +167,45 @@
     low_ref[...] = total.astype(bf16)
 
 
-def sum_docs(parts, requests):
+def onehot_rows(request_ref, out_ref):
+    docs = out_ref.shape[1]
+    slots = out_ref.shape[0]
+    onehot = (iota((docs, slots), 0) == request_ref[...]).astype(f32).astype(bf16)
+    eye = (iota((docs, docs), 0) == iota((docs, docs), 1)).astype(f32).astype(bf16)
+    out_ref[...] = dot(onehot, eye, TN).astype(bf16)
+
+
+def sum_docs(parts, onehot):
     docs, cols = parts[0].shape
-    slots = requests.shape[1]
-    steps = 4
-    block = slots // steps
-
-    def body(a, b, c, d, request_ref, total_ref, rows_ref, low_ref):
-        @pl.when(pl.program_id(0) == 0)
-        def _():
-            total = sum_refs((a, b, c, d))
-            total_ref[...] = total
-            low_ref[...] = total.astype(bf16)
-
-        onehot = (iota((docs, block), 0) == request_ref[...]).astype(f32).astype(bf16)
-        rows_ref[...] = dot(onehot, low_ref[...], TN).astype(bf16)
-
-    whole = pl.BlockSpec((docs, cols), lambda s: (0, 0))
+    slots = onehot.shape[0]
+    block = slots // CHUNKS
+
+    def body(a, b, c, d, onehot_ref, total_ref, rows_ref, buf_ref, sem_ref):
+        total = sum_refs((a, b, c, d))
+        total_ref[...] = total
+        low = total.astype(bf16)
+
+        def store(i):
+            part = pl.ds(i * block, block)
+            return pltpu.make_async_copy(buf_ref.at[part], rows_ref.at[part], sem_ref.at[i])
+
+        for i in range(CHUNKS):
+            part = slice(i * block, (i + 1) * block)
+            buf_ref[part, :] = dot(onehot_ref[part, :], low).astype(bf16)
+            store(i).start()
+        for i in range(CHUNKS):
+            store(i).wait()
+
+    vmem = pl.BlockSpec(memory_space=pltpu.VMEM)
     return pl.pallas_call(
         body,
-        grid=(steps,),
-        in_specs=[whole] * 4 + [pl.BlockSpec((1, block), lambda s: (0, s))],
-        out_specs=[whole, pl.BlockSpec((block, cols), lambda s: (s, 0))],
+        in_specs=[vmem] * 5,
+        out_specs=[vmem, pl.BlockSpec(memory_space=pltpu.HBM)],
         out_shape=[jax.ShapeDtypeStruct((docs, cols), f32), jax.ShapeDtypeStruct((slots, cols), bf16)],
-        scratch_shapes=[pltpu.VMEM((docs, cols), bf16)],
+        scratch_shapes=[pltpu.VMEM((slots, cols), bf16), pltpu.SemaphoreType.DMA((CHUNKS,))],
         compiler_params=params(),
         cost_estimate=cost,
-    )(*parts, requests)
+    )(*parts, onehot)
 
 
 def ones_row_sums(x):
@@ -238,7 +246,7 @@
 
 def softmax_terms(*refs):
     inner_refs, hard_refs = refs[0:4], refs[4:8]
-    small_ref, neg_ref, rows_ref, d_ref, q_ref, out_ref, u_ref, g_ref, loss_ref = refs[8:]
+    small_ref, neg_ref, rows_ref, d_ref, q_ref, out_ref, u_ref, g_ref, loss_ref, buf_ref, sem_ref = refs[8:]
     sums = sum_refs(inner_refs)
     picks = sum_refs(hard_refs)
     docs, queries = d_ref.shape[0], q_ref.shape[0]
@@ -280,16 +288,27 @@
     q_unit = q_ref[...] * q_scale_col
     q_low = jnp.concatenate([q_unit.astype(bf16), jnp.zeros(q_ref.shape, bf16)], axis=0)
     second = (iota((128, 128), 0) >= 64).astype(f32).astype(bf16)
-    along = dot(coef, second)
-    mixed = dot(coef, q_low)
-    for s in range(0, mixed.shape[1], 128):
-        part = rows_ref[:, s : s + 128].astype(f32)
-        out_ref[:, s : s + 128] = (mixed[:, s : s + 128] - along * part).astype(bf16)
+    block = slots // CHUNKS
+
+    def store(i):
+        part = pl.ds(i * block, block)
+        return pltpu.make_async_copy(buf_ref.at[part], out_ref.at[part], sem_ref.at[i])
+
+    for i in range(CHUNKS):
+        part = slice(i * block, (i + 1) * block)
+        along = dot(coef[part, :], second)
+        mixed = dot(coef[part, :], q_low)
+        for c in range(0, mixed.shape[1], 128):
+            away = along * rows_ref[part, c : c + 128].astype(f32)
+            buf_ref[part, c : c + 128] = (mixed[:, c : c + 128] - away).astype(bf16)
+        store(i).start()
 
     d_unit = d_ref[...] * d_scale
     g_query = dot(grad, d_unit.astype(bf16), TN) + dot(coef, rows_ref[...], TN)
     u_ref[...] = (q_scale_col * (g_query[0:queries, :] - q_unit * q_dot_col)).astype(bf16)
     g_ref[...] = d_scale * (dot(grad, q_low) - d_unit * d_dot)
+    for i in range(CHUNKS):
+        store(i).wait()
 
 
 def doc_grads(rows_ref, request_ref, g_ref, u_ref):
@@ -318,14 +337,20 @@
     requests = document_requests.reshape(1, slots)
     neg_rows = jnp.pad(jnp.concatenate([negatives, negatives], axis=1), ((0, 1), (0, 0)), constant_values=-1)
 
-    d_own, d_parts = project(doc_states, doc_proj, k, 63)
-    d_total, outgoing = sum_docs([d_own] + d_parts, requests)
+    (d_far,) = project_sends(doc_states, doc_proj, k, 63, (2,))
+    d_next, d_last, requests = lax.optimization_barrier((*project_sends(doc_states, doc_proj, k, 63, (1, 3)), requests))
+    d_parts = [send(d_far, 2), send(d_next, 1), send(d_last, 3)]
+    d_own = project_own(doc_states, doc_proj, k)
+    (onehot,) = call(onehot_rows, [((slots, docs), bf16)], requests)
+    d_total, outgoing = sum_docs([d_own] + d_parts, onehot)
     outgoing, query_states = lax.optimization_barrier((outgoing, query_states))
     received = lax.all_to_all(
         outgoing.reshape(n_dp, cap, cols), "dp", split_axis=0, concat_axis=0, tiled=True
     ).reshape(slots, cols)
 
-    q_own, q_parts = project(query_states, query_proj, k)
+    q_own = project_own(query_states, query_proj, k)
+    q_far, q_next, q_last = project_sends(query_states, query_proj, k, 16, (2, 1, 3))
+    q_parts = [send(q_far, 2), send(q_next, 1), send(q_last, 3)]
     q_total, q_low = call(sum_queries, [((queries, cols), f32), ((queries, cols), bf16)], q_own, *q_parts)
     (inner,) = call(inner_partials, [((docs + 16, 128), f32)], q_total, d_total)
     inner_all = gather_blocks(inner)
@@ -339,17 +364,21 @@
 
     (hard,) = call(hard_partials, [((16, 128), f32)], received, q_low, neg_rows)
     hard_all = gather_blocks(hard)
-    rows, u_query, g_local, loss = call(
+    vmem = pl.BlockSpec(memory_space=pltpu.VMEM)
+    rows, u_query, g_local, loss = pl.pallas_call(
         softmax_terms,
-        [((slots, cols), bf16), ((queries, cols), bf16), ((docs, cols), f32), ((8, 128), f32)],
-        *inner_all,
-        *hard_all,
-        small,
-        neg_rows,
-        received,
-        d_total,
-        q_total,
-    )
+        in_specs=[vmem] * 13,
+        out_specs=[pl.BlockSpec(memory_space=pltpu.HBM), vmem, vmem, vmem],
+        out_shape=[
+            jax.ShapeDtypeStruct((slots, cols), bf16),
+            jax.ShapeDtypeStruct((queries, cols), bf16),
+            jax.ShapeDtypeStruct((docs, cols), f32),
+            jax.ShapeDtypeStruct((8, 128), f32),
+        ],
+        scratch_shapes=[pltpu.VMEM((slots, cols), bf16), pltpu.SemaphoreType.DMA((CHUNKS,))],
+        compiler_params=params(),
+        cost_estimate=cost,
+    )(*inner_all, *hard_all, small, neg_rows, received, d_total, q_total)
     arrived = lax.all_to_all(
         rows.reshape(n_dp, cap, cols), "dp", split_axis=0, concat_axis=0, tiled=True
     ).reshape(slots, cols)

time: 115 us -> 115 us (level)
  starting transfers between devices: 47.1 us -> 45.4 us
  Pallas kernels: 15 us -> 16.2 us
    pallas_call x2 -> x3, Pallas kernels: 4.25 us -> 6.22 us  [project_sends(): pl.pallas_call(body, in_specs=[pl.BlockSpec(memory_space=pltpu.SMEM), hbm...]
    ppermute x12, starting transfers between devices: 15.7 us -> 13.7 us  [gather_blocks(): lax.ppermute(x, 'phase', [((i + s) % N_PHASE, i) for i in range(N_PHASE)])]
    pallas_call x5, Pallas kernels: 4.06 us -> 2.29 us  [call(): pl.pallas_call(body, out_shape=[jax.ShapeDtypeStruct(s, t) for s, t in ou...]
    ppermute x6, waiting for transfers between devices: 4.47 us -> 3.03 us  [send(): lax.ppermute(block, 'phase', [(i, (i + s) % N_PHASE) for i in range(N_PHA...]
    ppermute x12, waiting for transfers between devices: 4.71 us -> 5.88 us  [gather_blocks(): lax.ppermute(x, 'phase', [((i + s) % N_PHASE, i) for i in range(N_PHASE)])]
    pallas_call x5 -> x8, Pallas kernels: 6.14 us -> 7.15 us  [the longest x6 4.12 us: run(): pl.pallas_call(body, in_specs=[pl.BlockSpec(memory_space=pltpu.SMEM)] + [...]
  transfers between devices with their start and end apart: 20 -> 20, of which waited for: 11 -> 10; matrix products, arithmetic and copies ran while one was open for 3% -> 3% of each run, Pallas kernels for 5% -> 8%
where the time goes in v5:
time: 115 us; the launch traced here: 114 us
  starting transfers between devices  45.4 us (39%)
  waiting for transfers between devices  40.5 us (35%)
  Pallas kernels  16.2 us (14%)
  local copies, waits for them, and re-layouts  10.6 us (9%)
    all_to_all x1, waiting for transfers between devices, local(): lax.all_to_all(rows.reshape(n_dp, cap, cols), 'dp', split_axis=0, concat_...  19.9 us
    ppermute x12, starting transfers between devices, gather_blocks(): lax.ppermute(x, 'phase', [((i + s) % N_PHASE, i) for i in range(N_PHASE)])  13.7 us
    all_to_all x1, starting transfers between devices, local(): lax.all_to_all(outgoing.reshape(n_dp, cap, cols), 'dp', split_axis=0, con...  13.5 us
    all_to_all x1, waiting for transfers between devices, local(): lax.all_to_all(outgoing.reshape(n_dp, cap, cols), 'dp', split_axis=0, con...  11.7 us
    ppermute x6, starting transfers between devices, send(): lax.ppermute(block, 'phase', [(i, (i + s) % N_PHASE) for i in range(N_PHA...  10.3 us
    all_to_all x1, starting transfers between devices, local(): lax.all_to_all(rows.reshape(n_dp, cap, cols), 'dp', split_axis=0, concat_...  7.82 us
    unnamed x21, local copies, waits for them, and re-layouts  7.68 us
    pallas_call x3, Pallas kernels, project_sends(): pl.pallas_call(body, in_specs=[pl.BlockSpec(memory_space=pltpu.SMEM), hbm...  6.22 us
  transfers between devices with their start and end apart: 20, of which 10 were waited for; matrix products, arithmetic and copies ran while one was open for 3% of the time, Pallas kernels for 8%

profile of v5, /device:TPU:1, one launch (start us, length us, event | category | flops | bytes accessed | tf_op | source)
XLA Modules:
  0.0 113.8 jit_solution(16145396564052292935)
XLA Ops:
  0.7 2.3 %shard_map.104 = bf16[128,512]{1,0:T(8,128)(2,1)} custom-call(s32[1]{0:T(128)} %bitcast.k_ref, bf16[128,1024]{1,0:T(8,128)(2,1)} %x_ref.5, bf16[1024,2048]{1,0:T(8,128)(2,1)} %refs_3_.3), custom_call_target="tpu_custom_call" | custom-call | flops 1000000000 | bytes 100000 | tf_op jit(solution)/shard_map/pallas_call | solution.py:73
  3.0 3.7 %collective-permute-start = (bf16[128,512]{1,0:T(8,128)(2,1)}, bf16[128,512]{1,0:T(8,128)(2,1)S(1)}, u32[]{:S(2)}, u32[]{:S(2)}) collective-permute-start(bf16[128,512]{1,0:T(8,128)(2,1)} %shard_map.104), channel_id=1, source_target_pairs={{0,128},{64,192},{128,0},{192,64},{1,129},{65,193},{129,1},{193,65... | collective-permute-start | bytes 393224 | tf_op jit(solution)/shard_map/ppermute | solution.py:148
  6.7 2.6 %shard_map.105 = (bf16[128,512]{1,0:T(8,128)(2,1)}, bf16[128,512]{1,0:T(8,128)(2,1)}) custom-call(s32[1]{0:T(128)} %bitcast.k_ref, bf16[128,1024]{1,0:T(8,128)(2,1)} %x_ref.5, bf16[1024,2048]{1,0:T(8,128)(2,1)} %refs_3_.3), custom_call_target="tpu_custom_call" | custom-call | flops 1000000000 | bytes 100000 | tf_op jit(solution)/shard_map/pallas_call | solution.py:73
  9.9 2.4 %collective-permute-start.2 = (bf16[128,512]{1,0:T(8,128)(2,1)}, bf16[128,512]{1,0:T(8,128)(2,1)S(1)}, u32[]{:S(2)}, u32[]{:S(2)}) collective-permute-start(bf16[128,512]{1,0:T(8,128)(2,1)} %get-tuple-element.30), channel_id=1, source_target_pairs={{0,192},{64,0},{128,64},{192,128},{1,193},{65,1},{129,65},{193,129... | collective-permute-start | bytes 393224 | tf_op jit(solution)/shard_map/ppermute | solution.py:148
  12.2 2.2 %copy-done.1 = bf16[1024,2048]{1,0:T(8,128)(2,1)S(1)} copy-done((bf16[1024,2048]{1,0:T(8,128)(2,1)S(1)}, bf16[1024,2048]{1,0:T(8,128)(2,1)}, u32[]{:S(2)}) %copy-start.1) | copy-done | bytes 4194328
  15.1 1.3 %shard_map.107 = (f32[128,512]{1,0:T(8,128)S(1)}, bf16[1024,512]{1,0:T(8,128)(2,1)}) custom-call(f32[128,512]{1,0:T(8,128)S(1)} %shard_map.103.a, bf16[128,512]{1,0:T(8,128)(2,1)S(1)} %collective-permute-done.b, bf16[128,512]{1,0:T(8,128)(2,1)S(1)} %collective-permute-done.1.c, bf16[128,512]{1,0:T(8,128)(2,1)S(1)} %collective-permute-done.2.d, ...), custom_call_target="tpu_custom_call" | custom-call | flops 1000000000 | bytes 100000 | tf_op jit(solution)/shard_map/pallas_call | solution.py:200
  16.4 13.5 %all-to-all-start = ((bf16[64,16,512]{2,1,0:T(8,128)(2,1)}), bf16[64,16,512]{2,1,0:T(8,128)(2,1)S(1)}, u32[]{:S(2)}, u32[]{:S(2)}) async-start(bf16[64,16,512]{2,1,0:T(8,128)(2,1)} %bitcast.1), calls=%async_computation | async-start | bytes 2097152 | tf_op jit(solution)/shard_map/all_to_all | solution.py:347
  30.0 2.1 %gather_fusion = s32[448]{0:T(512)S(1)} fusion(s32[1024]{0:T(1024)S(1)} %bitcast.14, s32[1024]{0:T(1024)S(1)} %pad_clamp_fusion), kind=kCustom, calls=%fused_computation | custom fusion | bytes 5376 | tf_op jit(solution)/shard_map/jit(_take)/gather | solution.py:357
  32.5 1.6 %copy-done.4 = bf16[512,2048]{1,0:T(8,128)(2,1)S(1)} copy-done((bf16[512,2048]{1,0:T(8,128)(2,1)S(1)}, bf16[512,2048]{1,0:T(8,128)(2,1)}, u32[]{:S(2)}) %copy-start.4) | copy-done | bytes 2097176
  34.1 1.2 %shard_map.109 = (bf16[64,512]{1,0:T(8,128)(2,1)S(1)}, bf16[64,512]{1,0:T(8,128)(2,1)S(1)}, bf16[64,512]{1,0:T(8,128)(2,1)S(1)}) custom-call(s32[1]{0:T(128)} %bitcast.k_ref, bf16[64,512]{1,0:T(8,128)(2,1)S(1)} %copy-done.6, bf16[512,2048]{1,0:T(8,128)(2,1)S(1)} %copy-done.4), custom_call_target="tpu_custom_call" | custom-call | flops 1000000000 | bytes 100000 | tf_op jit(solution)/shard_map/pallas_call | solution.py:73
  35.3 1.3 %collective-permute-start.3 = (bf16[64,512]{1,0:T(8,128)(2,1)S(1)}, bf16[64,512]{1,0:T(8,128)(2,1)S(1)}, u32[]{:S(2)}, u32[]{:S(2)}) collective-permute-start(bf16[64,512]{1,0:T(8,128)(2,1)S(1)} %get-tuple-element.34), channel_id=1, source_target_pairs={{0,128},{64,192},{128,0},{192,64},{1,129},{65,193},{129,1},{193,65... | collective-permute-start | bytes 196616 | tf_op jit(solution)/shard_map/ppermute | solution.py:148
  36.6 2.3 %collective-permute-start.4 = (bf16[64,512]{1,0:T(8,128)(2,1)S(1)}, bf16[64,512]{1,0:T(8,128)(2,1)S(1)}, u32[]{:S(2)}, u32[]{:S(2)}) collective-permute-start(bf16[64,512]{1,0:T(8,128)(2,1)S(1)} %get-tuple-element.35), channel_id=1, source_target_pairs={{0,64},{64,128},{128,192},{192,0},{1,65},{65,129},{129,193},{193,1... | collective-permute-start | bytes 196616 | tf_op jit(solution)/shard_map/ppermute | solution.py:148
  39.5 0.8 collective-permute-done.3.a
  40.3 1.8 %collective-permute-done.4.b = bf16[64,512]{1,0:T(8,128)(2,1)S(1)} collective-permute-done((bf16[64,512]{1,0:T(8,128)(2,1)S(1)}, bf16[64,512]{1,0:T(8,128)(2,1)S(1)}, u32[]{:S(2)}, u32[]{:S(2)}) %collective-permute-start.4) | collective-permute-done | bytes 65568 | tf_op jit(solution)/shard_map/ppermute | solution.py:148
  42.8 3.4 %collective-permute-start.7 = (f32[144,128]{1,0:T(8,128)S(1)}, f32[144,128]{1,0:T(8,128)S(1)}, u32[]{:S(2)}, u32[]{:S(2)}) collective-permute-start(f32[144,128]{1,0:T(8,128)S(1)} %shard_map.111.refs_0_), channel_id=1, source_target_pairs={{128,0},{192,64},{0,128},{64,192},{129,1},{193,65},{1,129},{65,193... | collective-permute-start | bytes 221192 | tf_op jit(solution)/shard_map/ppermute | solution.py:153
  46.2 11.7 %all-to-all-done = bf16[64,16,512]{2,1,0:T(8,128)(2,1)S(1)} async-done(((bf16[64,16,512]{2,1,0:T(8,128)(2,1)}), bf16[64,16,512]{2,1,0:T(8,128)(2,1)S(1)}, u32[]{:S(2)}, u32[]{:S(2)}) %all-to-all-start) | async-done | bytes 1048608 | tf_op jit(solution)/shard_map/all_to_all | solution.py:347
  57.9 1.4 %shard_map.112.refs_4_ = f32[16,128]{1,0:T(8,128)S(1)} custom-call(bf16[1024,512]{1,0:T(8,128)(2,1)S(1)} %bitcast.15, bf16[64,512]{1,0:T(8,128)(2,1)S(1)} %get-tuple-element.41.q_ref, s32[8,128]{1,0:T(8,128)S(1)} %pad.9.neg_ref.refs_9_), custom_call_target="tpu_custom_call" | custom-call | flops 1000000000 | bytes 100000 | tf_op jit(solution)/shard_map/pallas_call | solution.py:28
  59.3 4.1 %collective-permute-start.10 = (f32[16,128]{1,0:T(8,128)S(1)}, f32[16,128]{1,0:T(8,128)S(1)}, u32[]{:S(2)}, u32[]{:S(2)}) collective-permute-start(f32[16,128]{1,0:T(8,128)S(1)} %shard_map.112.refs_4_), channel_id=1, source_target_pairs={{128,0},{192,64},{0,128},{64,192},{129,1},{193,65},{1,129},{65,193... | collective-permute-start | bytes 24584 | tf_op jit(solution)/shard_map/ppermute | solution.py:153
  63.5 1.1 collective-permute-done.10.refs_6_
  64.6 1.7 %collective-permute-done.9.refs_5_ = f32[16,128]{1,0:T(8,128)S(1)} collective-permute-done((f32[16,128]{1,0:T(8,128)S(1)}, f32[16,128]{1,0:T(8,128)S(1)}, u32[]{:S(2)}, u32[]{:S(2)}) %collective-permute-start.9) | collective-permute-done | bytes 8224 | tf_op jit(solution)/shard_map/ppermute | solution.py:153
  66.3 1.8 %shard_map.113 = (bf16[1024,512]{1,0:T(8,128)(2,1)}, bf16[64,512]{1,0:T(8,128)(2,1)S(1)}, f32[128,512]{1,0:T(8,128)S(1)}, f32[8,128]{1,0:T(8,128)S(1)}) custom-call(f32[144,128]{1,0:T(8,128)S(1)} %shard_map.111.refs_0_, f32[144,128]{1,0:T(8,128)S(1)} %collective-permute-done.6.refs_1_, f32[144,128]{1,0:T(8,128)S(1)} %collective-permute-done.7.refs_2_, ...), custom_call_target="tpu_custom_call" | custom-call | flops 1000000000 | bytes 100000 | tf_op jit(solution)/shard_map/pallas_call | solution.py:368
  68.1 7.8 %all-to-all-start.1 = ((bf16[64,16,512]{2,1,0:T(8,128)(2,1)}), bf16[64,16,512]{2,1,0:T(8,128)(2,1)S(1)}, u32[]{:S(2)}, u32[]{:S(2)}) async-start(bf16[64,16,512]{2,1,0:T(8,128)(2,1)} %bitcast.6), calls=%async_computation.1 | async-start | bytes 2097152 | tf_op jit(solution)/shard_map/all_to_all | solution.py:382
  75.9 1.3 %collective-permute-start.14 = (bf16[64,512]{1,0:T(8,128)(2,1)S(1)}, bf16[64,512]{1,0:T(8,128)(2,1)S(1)}, u32[]{:S(2)}, u32[]{:S(2)}) collective-permute-start(bf16[64,512]{1,0:T(8,128)(2,1)S(1)} %get-tuple-element.45.refs_0_), channel_id=1, source_target_pairs={{128,0},{192,64},{0,128},{64,192},{129,1},{193,65},{1,129},{65,193... | collective-permute-start | bytes 196616 | tf_op jit(solution)/shard_map/ppermute | solution.py:153
  79.2 1.6 %copy-done.5 = bf16[512,2048]{1,0:T(8,128)(2,1)S(1)} copy-done((bf16[512,2048]{1,0:T(8,128)(2,1)S(1)}, bf16[512,2048]{1,0:T(8,128)(2,1)}, u32[]{:S(2)}) %copy-start.5) | copy-done | bytes 2097176
  81.1 1.5 %collective-permute-done.12.refs_1_ = bf16[64,512]{1,0:T(8,128)(2,1)S(1)} collective-permute-done((bf16[64,512]{1,0:T(8,128)(2,1)S(1)}, bf16[64,512]{1,0:T(8,128)(2,1)S(1)}, u32[]{:S(2)}, u32[]{:S(2)}) %collective-permute-start.12) | collective-permute-done | bytes 65568 | tf_op jit(solution)/shard_map/ppermute | solution.py:153
  82.9 1.1 shard_map.116
  84.0 19.9 %all-to-all-done.1 = bf16[64,16,512]{2,1,0:T(8,128)(2,1)S(1)} async-done(((bf16[64,16,512]{2,1,0:T(8,128)(2,1)}), bf16[64,16,512]{2,1,0:T(8,128)(2,1)S(1)}, u32[]{:S(2)}, u32[]{:S(2)}) %all-to-all-start.1) | async-done | bytes 1048608 | tf_op jit(solution)/shard_map/all_to_all | solution.py:382
  104.3 2.1 %collective-permute-start.17 = (bf16[128,512]{1,0:T(8,128)(2,1)S(1)}, bf16[128,512]{1,0:T(8,128)(2,1)S(1)}, u32[]{:S(2)}, u32[]{:S(2)}) collective-permute-start(bf16[128,512]{1,0:T(8,128)(2,1)S(1)} %shard_map.117.refs_0_), channel_id=1, source_target_pairs={{128,0},{192,64},{0,128},{64,192},{129,1},{193,65},{1,129},{65,193... | collective-permute-start | bytes 393224 | tf_op jit(solution)/shard_map/ppermute | solution.py:153
  106.4 1.2 %collective-permute-start.16 = (bf16[128,512]{1,0:T(8,128)(2,1)S(1)}, bf16[128,512]{1,0:T(8,128)(2,1)S(1)}, u32[]{:S(2)}, u32[]{:S(2)}) collective-permute-start(bf16[128,512]{1,0:T(8,128)(2,1)S(1)} %shard_map.117.refs_0_), channel_id=1, source_target_pairs={{64,0},{128,64},{192,128},{0,192},{65,1},{129,65},{193,129},{1,193... | collective-permute-start | bytes 393224 | tf_op jit(solution)/shard_map/ppermute | solution.py:153
  107.6 2.2 %copy-done.2 = bf16[1024,2048]{1,0:T(8,128)(2,1)S(1)} copy-done((bf16[1024,2048]{1,0:T(8,128)(2,1)S(1)}, bf16[1024,2048]{1,0:T(8,128)(2,1)}, u32[]{:S(2)}) %copy-start.2) | copy-done | bytes 4194328
  110.3 0.9 collective-permute-done.15.refs_1_
  112.3 1.5 %shard_map.120 = bf16[128,1024]{1,0:T(8,128)(2,1)} custom-call(s32[1]{0:T(128)} %bitcast.k_ref, f32[128,1024]{1,0:T(8,128)S(1)} %shard_map.119.refs_0_, bf16[128,512]{1,0:T(8,128)(2,1)S(1)} %collective-permute-done.16.refs_1_, bf16[128,512]{1,0:T(8,128)(2,1)S(1)} %collective-permute-done.17.refs_2_, bf16[1024,2048]{1,0:T(8,128)(2,1)S(1)} %copy-done.2), custom_call_target="tpu_custom_call" | custom-call | flops 1000000000 | bytes 100000 | tf_op jit(solution)/shard_map/pallas_call | solution.py:132
  (61 shorter events, 7.5 us)
Async XLA Ops:
  0.6 29.3 %copy-start = (s32[1,1024]{1,0:T(1,128)S(1)}, s32[1,1024]{1,0:T(1,128)}, u32[]{:S(2)}) copy-start(s32[1,1024]{1,0:T(1,128)} %param.13) | copy-start | bytes 12292
  0.7 8.7 %copy-start.8 = (s32[1,64,16]{1,2,0:T(8,128)S(1)}, s32[1,64,16]{1,2,0:T(8,128)}, u32[]{:S(2)}) copy-start(s32[1,64,16]{1,2,0:T(8,128)} %param.12) | copy-start | bytes 12292
  0.7 11.6 %copy-start.3 = (bf16[128,1024]{1,0:T(8,128)(2,1)S(1)}, bf16[128,1024]{1,0:T(8,128)(2,1)}, u32[]{:S(2)}) copy-start(bf16[128,1024]{1,0:T(8,128)(2,1)} %x_ref.5) | copy-start | bytes 786436
  3.0 12.0 %collective-permute-start = (bf16[128,512]{1,0:T(8,128)(2,1)}, bf16[128,512]{1,0:T(8,128)(2,1)S(1)}, u32[]{:S(2)}, u32[]{:S(2)}) collective-permute-start(bf16[128,512]{1,0:T(8,128)(2,1)} %shard_map.104), channel_id=1, source_target_pairs={{0,128},{64,192},{128,0},{192,64},{1,129},{65,193},{129,1},{193,65... | collective-permute-start | bytes 393224 | tf_op jit(solution)/shard_map/ppermute | solution.py:148
  9.5 5.6 %collective-permute-start.1 = (bf16[128,512]{1,0:T(8,128)(2,1)}, bf16[128,512]{1,0:T(8,128)(2,1)S(1)}, u32[]{:S(2)}, u32[]{:S(2)}) collective-permute-start(bf16[128,512]{1,0:T(8,128)(2,1)} %get-tuple-element.29), channel_id=1, source_target_pairs={{0,64},{64,128},{128,192},{192,0},{1,65},{65,129},{129,193},{193,1... | collective-permute-start | bytes 393224 | tf_op jit(solution)/shard_map/ppermute | solution.py:148
  9.9 5.2 %collective-permute-start.2 = (bf16[128,512]{1,0:T(8,128)(2,1)}, bf16[128,512]{1,0:T(8,128)(2,1)S(1)}, u32[]{:S(2)}, u32[]{:S(2)}) collective-permute-start(bf16[128,512]{1,0:T(8,128)(2,1)} %get-tuple-element.30), channel_id=1, source_target_pairs={{0,192},{64,0},{128,64},{192,128},{1,193},{65,1},{129,65},{193,129... | collective-permute-start | bytes 393224 | tf_op jit(solution)/shard_map/ppermute | solution.py:148
  12.2 2.2 %copy-start.1 = (bf16[1024,2048]{1,0:T(8,128)(2,1)S(1)}, bf16[1024,2048]{1,0:T(8,128)(2,1)}, u32[]{:S(2)}) copy-start(bf16[1024,2048]{1,0:T(8,128)(2,1)} %refs_3_.3) | copy-start | bytes 12582916
  14.8 15.1 %copy-start.7 = (s32[64,7]{0,1:T(8,128)S(1)}, s32[64,7]{0,1:T(8,128)}, u32[]{:S(2)}) copy-start(s32[64,7]{0,1:T(8,128)} %param.14) | copy-start | bytes 5380
  15.0 17.2 %copy-start.9 = (f32[64]{0:T(128)S(1)}, f32[64]{0:T(128)}, u32[]{:S(2)}) copy-start(f32[64]{0:T(128)} %param.15) | copy-start | bytes 772
  15.0 17.4 %copy-start.6 = (bf16[64,512]{1,0:T(8,128)(2,1)S(1)}, bf16[64,512]{1,0:T(8,128)(2,1)}, u32[]{:S(2)}) copy-start(bf16[64,512]{1,0:T(8,128)(2,1)} %x_ref.7) | copy-start | bytes 196612
  16.4 41.5 %all-to-all-start = ((bf16[64,16,512]{2,1,0:T(8,128)(2,1)}), bf16[64,16,512]{2,1,0:T(8,128)(2,1)S(1)}, u32[]{:S(2)}, u32[]{:S(2)}) async-start(bf16[64,16,512]{2,1,0:T(8,128)(2,1)} %bitcast.1), calls=%async_computation | async-start | bytes 2097152 | tf_op jit(solution)/shard_map/all_to_all | solution.py:347
  32.5 1.6 %copy-start.4 = (bf16[512,2048]{1,0:T(8,128)(2,1)S(1)}, bf16[512,2048]{1,0:T(8,128)(2,1)}, u32[]{:S(2)}) copy-start(bf16[512,2048]{1,0:T(8,128)(2,1)} %refs_3_.2) | copy-start | bytes 6291460
  35.3 5.0 %collective-permute-start.3 = (bf16[64,512]{1,0:T(8,128)(2,1)S(1)}, bf16[64,512]{1,0:T(8,128)(2,1)S(1)}, u32[]{:S(2)}, u32[]{:S(2)}) collective-permute-start(bf16[64,512]{1,0:T(8,128)(2,1)S(1)} %get-tuple-element.34), channel_id=1, source_target_pairs={{0,128},{64,192},{128,0},{192,64},{1,129},{65,193},{129,1},{193,65... | collective-permute-start | bytes 196616 | tf_op jit(solution)/shard_map/ppermute | solution.py:148
  36.6 5.5 %collective-permute-start.4 = (bf16[64,512]{1,0:T(8,128)(2,1)S(1)}, bf16[64,512]{1,0:T(8,128)(2,1)S(1)}, u32[]{:S(2)}, u32[]{:S(2)}) collective-permute-start(bf16[64,512]{1,0:T(8,128)(2,1)S(1)} %get-tuple-element.35), channel_id=1, source_target_pairs={{0,64},{64,128},{128,192},{192,0},{1,65},{65,129},{129,193},{193,1... | collective-permute-start | bytes 196616 | tf_op jit(solution)/shard_map/ppermute | solution.py:148
  38.9 3.6 %collective-permute-start.5 = (bf16[64,512]{1,0:T(8,128)(2,1)S(1)}, bf16[64,512]{1,0:T(8,128)(2,1)S(1)}, u32[]{:S(2)}, u32[]{:S(2)}) collective-permute-start(bf16[64,512]{1,0:T(8,128)(2,1)S(1)} %get-tuple-element.36), channel_id=1, source_target_pairs={{0,192},{64,0},{128,64},{192,128},{1,193},{65,1},{129,65},{193,129... | collective-permute-start | bytes 196616 | tf_op jit(solution)/shard_map/ppermute | solution.py:148
  42.8 20.6 %collective-permute-start.8 = (f32[144,128]{1,0:T(8,128)S(1)}, f32[144,128]{1,0:T(8,128)S(1)}, u32[]{:S(2)}, u32[]{:S(2)}) collective-permute-start(f32[144,128]{1,0:T(8,128)S(1)} %shard_map.111.refs_0_), channel_id=1, source_target_pairs={{192,0},{0,64},{64,128},{128,192},{193,1},{1,65},{65,129},{129,193... | collective-permute-start | bytes 221192 | tf_op jit(solution)/shard_map/ppermute | solution.py:153
  42.8 20.6 %collective-permute-start.7 = (f32[144,128]{1,0:T(8,128)S(1)}, f32[144,128]{1,0:T(8,128)S(1)}, u32[]{:S(2)}, u32[]{:S(2)}) collective-permute-start(f32[144,128]{1,0:T(8,128)S(1)} %shard_map.111.refs_0_), channel_id=1, source_target_pairs={{128,0},{192,64},{0,128},{64,192},{129,1},{193,65},{1,129},{65,193... | collective-permute-start | bytes 221192 | tf_op jit(solution)/shard_map/ppermute | solution.py:153
  46.2 17.3 %collective-permute-start.6 = (f32[144,128]{1,0:T(8,128)S(1)}, f32[144,128]{1,0:T(8,128)S(1)}, u32[]{:S(2)}, u32[]{:S(2)}) collective-permute-start(f32[144,128]{1,0:T(8,128)S(1)} %shard_map.111.refs_0_), channel_id=1, source_target_pairs={{64,0},{128,64},{192,128},{0,192},{65,1},{129,65},{193,129},{1,193... | collective-permute-start | bytes 221192 | tf_op jit(solution)/shard_map/ppermute | solution.py:153
  59.2 4.2 %collective-permute-start.11 = (f32[16,128]{1,0:T(8,128)S(1)}, f32[16,128]{1,0:T(8,128)S(1)}, u32[]{:S(2)}, u32[]{:S(2)}) collective-permute-start(f32[16,128]{1,0:T(8,128)S(1)} %shard_map.112.refs_4_), channel_id=1, source_target_pairs={{192,0},{0,64},{64,128},{128,192},{193,1},{1,65},{65,129},{129,193... | collective-permute-start | bytes 24584 | tf_op jit(solution)/shard_map/ppermute | solution.py:153
  59.3 5.2 %collective-permute-start.10 = (f32[16,128]{1,0:T(8,128)S(1)}, f32[16,128]{1,0:T(8,128)S(1)}, u32[]{:S(2)}, u32[]{:S(2)}) collective-permute-start(f32[16,128]{1,0:T(8,128)S(1)} %shard_map.112.refs_4_), channel_id=1, source_target_pairs={{128,0},{192,64},{0,128},{64,192},{129,1},{193,65},{1,129},{65,193... | collective-permute-start | bytes 24584 | tf_op jit(solution)/shard_map/ppermute | solution.py:153
  63.4 2.9 %collective-permute-start.9 = (f32[16,128]{1,0:T(8,128)S(1)}, f32[16,128]{1,0:T(8,128)S(1)}, u32[]{:S(2)}, u32[]{:S(2)}) collective-permute-start(f32[16,128]{1,0:T(8,128)S(1)} %shard_map.112.refs_4_), channel_id=1, source_target_pairs={{64,0},{128,64},{192,128},{0,192},{65,1},{129,65},{193,129},{1,193... | collective-permute-start | bytes 24584 | tf_op jit(solution)/shard_map/ppermute | solution.py:153
  68.1 35.8 %all-to-all-start.1 = ((bf16[64,16,512]{2,1,0:T(8,128)(2,1)}), bf16[64,16,512]{2,1,0:T(8,128)(2,1)S(1)}, u32[]{:S(2)}, u32[]{:S(2)}) async-start(bf16[64,16,512]{2,1,0:T(8,128)(2,1)} %bitcast.6), calls=%async_computation.1 | async-start | bytes 2097152 | tf_op jit(solution)/shard_map/all_to_all | solution.py:382
  75.9 7.0 %collective-permute-start.14 = (bf16[64,512]{1,0:T(8,128)(2,1)S(1)}, bf16[64,512]{1,0:T(8,128)(2,1)S(1)}, u32[]{:S(2)}, u32[]{:S(2)}) collective-permute-start(bf16[64,512]{1,0:T(8,128)(2,1)S(1)} %get-tuple-element.45.refs_0_), channel_id=1, source_target_pairs={{128,0},{192,64},{0,128},{64,192},{129,1},{193,65},{1,129},{65,193... | collective-permute-start | bytes 196616 | tf_op jit(solution)/shard_map/ppermute | solution.py:153
  77.2 5.7 %collective-permute-start.13 = (bf16[64,512]{1,0:T(8,128)(2,1)S(1)}, bf16[64,512]{1,0:T(8,128)(2,1)S(1)}, u32[]{:S(2)}, u32[]{:S(2)}) collective-permute-start(bf16[64,512]{1,0:T(8,128)(2,1)S(1)} %get-tuple-element.45.refs_0_), channel_id=1, source_target_pairs={{64,0},{128,64},{192,128},{0,192},{65,1},{129,65},{193,129},{1,193... | collective-permute-start | bytes 196616 | tf_op jit(solution)/shard_map/ppermute | solution.py:153
  77.8 4.8 %collective-permute-start.12 = (bf16[64,512]{1,0:T(8,128)(2,1)S(1)}, bf16[64,512]{1,0:T(8,128)(2,1)S(1)}, u32[]{:S(2)}, u32[]{:S(2)}) collective-permute-start(bf16[64,512]{1,0:T(8,128)(2,1)S(1)} %get-tuple-element.45.refs_0_), channel_id=1, source_target_pairs={{192,0},{0,64},{64,128},{128,192},{193,1},{1,65},{65,129},{129,193... | collective-permute-start | bytes 196616 | tf_op jit(solution)/shard_map/ppermute | solution.py:153
  79.2 1.6 %copy-start.5 = (bf16[512,2048]{1,0:T(8,128)(2,1)S(1)}, bf16[512,2048]{1,0:T(8,128)(2,1)}, u32[]{:S(2)}) copy-start(bf16[512,2048]{1,0:T(8,128)(2,1)} %refs_3_.2) | copy-start | bytes 6291460
  104.2 6.9 %collective-permute-start.15 = (bf16[128,512]{1,0:T(8,128)(2,1)S(1)}, bf16[128,512]{1,0:T(8,128)(2,1)S(1)}, u32[]{:S(2)}, u32[]{:S(2)}) collective-permute-start(bf16[128,512]{1,0:T(8,128)(2,1)S(1)} %shard_map.117.refs_0_), channel_id=1, source_target_pairs={{192,0},{0,64},{64,128},{128,192},{193,1},{1,65},{65,129},{129,193... | collective-permute-start | bytes 393224 | tf_op jit(solution)/shard_map/ppermute | solution.py:153
  104.3 7.3 %collective-permute-start.17 = (bf16[128,512]{1,0:T(8,128)(2,1)S(1)}, bf16[128,512]{1,0:T(8,128)(2,1)S(1)}, u32[]{:S(2)}, u32[]{:S(2)}) collective-permute-start(bf16[128,512]{1,0:T(8,128)(2,1)S(1)} %shard_map.117.refs_0_), channel_id=1, source_target_pairs={{128,0},{192,64},{0,128},{64,192},{129,1},{193,65},{1,129},{65,193... | collective-permute-start | bytes 393224 | tf_op jit(solution)/shard_map/ppermute | solution.py:153
  106.4 5.8 %collective-permute-start.16 = (bf16[128,512]{1,0:T(8,128)(2,1)S(1)}, bf16[128,512]{1,0:T(8,128)(2,1)S(1)}, u32[]{:S(2)}, u32[]{:S(2)}) collective-permute-start(bf16[128,512]{1,0:T(8,128)(2,1)S(1)} %shard_map.117.refs_0_), channel_id=1, source_target_pairs={{64,0},{128,64},{192,128},{0,192},{65,1},{129,65},{193,129},{1,193... | collective-permute-start | bytes 393224 | tf_op jit(solution)/shard_map/ppermute | solution.py:153
  107.6 2.2 %copy-start.2 = (bf16[1024,2048]{1,0:T(8,128)(2,1)S(1)}, bf16[1024,2048]{1,0:T(8,128)(2,1)}, u32[]{:S(2)}) copy-start(bf16[1024,2048]{1,0:T(8,128)(2,1)} %refs_3_.3) | copy-start | bytes 12582916

commit v6 on v5

--- a/solution.py
+++ b/solution.py
@@ -334,19 +334,27 @@
     slots = n_dp * cap
 
     negatives = neg_slot.T
-    requests = document_requests.reshape(1, slots)
-    neg_rows = jnp.pad(jnp.concatenate([negatives, negatives], axis=1), ((0, 1), (0, 0)), constant_values=-1)
-
-    (d_far,) = project_sends(doc_states, doc_proj, k, 63, (2,))
-    d_next, d_last, requests = lax.optimization_barrier((*project_sends(doc_states, doc_proj, k, 63, (1, 3)), requests))
+    held = (n_dp - 1 - negatives // cap) * cap + negatives % cap
+    neg_rows = jnp.pad(jnp.concatenate([held, held], axis=1), ((0, 1), (0, 0)), constant_values=-1)
+    order = [list(range(n_dp - 1, -1, -1))]
+
+    def exchange(rows):
+        blocks = rows.reshape(n_dp, cap, cols)
+        swapped = lax.all_to_all(
+            blocks, "dp", split_axis=0, concat_axis=0, tiled=True, axis_index_groups=order
+        )
+        return swapped.reshape(slots, cols)
+
+    d_far, d_next, d_last, document_requests = lax.optimization_barrier(
+        (*project_sends(doc_states, doc_proj, k, 63, (2, 1, 3)), document_requests)
+    )
+    requests = document_requests[0, ::-1].reshape(1, slots)
     d_parts = [send(d_far, 2), send(d_next, 1), send(d_last, 3)]
     d_own = project_own(doc_states, doc_proj, k)
     (onehot,) = call(onehot_rows, [((slots, docs), bf16)], requests)
     d_total, outgoing = sum_docs([d_own] + d_parts, onehot)
     outgoing, query_states = lax.optimization_barrier((outgoing, query_states))
-    received = lax.all_to_all(
-        outgoing.reshape(n_dp, cap, cols), "dp", split_axis=0, concat_axis=0, tiled=True
-    ).reshape(slots, cols)
+    received = exchange(outgoing)
 
     q_own = project_own(query_states, query_proj, k)
     q_far, q_next, q_last = project_sends(query_states, query_proj, k, 16, (2, 1, 3))
@@ -379,9 +387,7 @@
         compiler_params=params(),
         cost_estimate=cost,
     )(*inner_all, *hard_all, small, neg_rows, received, d_total, q_total)
-    arrived = lax.all_to_all(
-        rows.reshape(n_dp, cap, cols), "dp", split_axis=0, concat_axis=0, tiled=True
-    ).reshape(slots, cols)
+    arrived = exchange(rows)
     grad_query = project_back(u_query, query_proj, k)
     arrived, grad_query, loss = lax.optimization_barrier((arrived, grad_query, loss[0, :queries]))
 

time: 115 us -> 111 us (0.965)
  waiting for transfers between devices: 40.5 us -> 34.6 us
  starting transfers between devices: 45.4 us -> 48.4 us
  Pallas kernels: 16.2 us -> 14.1 us
    all_to_all x2, waiting for transfers between devices: 31.6 us -> 24.4 us  [exchange(): lax.all_to_all(blocks, 'dp', split_axis=0, concat_axis=0, tiled=True, axi...]
    all_to_all x2, starting transfers between devices: 21.3 us -> 24.1 us  [exchange(): lax.all_to_all(blocks, 'dp', split_axis=0, concat_axis=0, tiled=True, axi...]
    pallas_call x3 -> x2, Pallas kernels: 6.22 us -> 4.22 us  [project_sends(): pl.pallas_call(body, in_specs=[pl.BlockSpec(memory_space=pltpu.SMEM), hbm...]
    unnamed x21 -> x20, local copies, waits for them, and re-layouts: 7.68 us -> 7.59 us
  transfers between devices with their start and end apart: 20 -> 20, of which waited for: 10 -> 12; matrix products, arithmetic and copies ran while one was open for 3% -> 3% of each run, Pallas kernels for 8% -> 6%
where the time goes in v6:
time: 111 us; the launch traced here: 109 us
  starting transfers between devices  48.4 us (44%)
  waiting for transfers between devices  34.6 us (31%)
  Pallas kernels  14.1 us (13%)
  local copies, waits for them, and re-layouts  10.7 us (10%)
    all_to_all x2, waiting for transfers between devices, exchange(): lax.all_to_all(blocks, 'dp', split_axis=0, concat_axis=0, tiled=True, axi...  24.4 us
    all_to_all x2, starting transfers between devices, exchange(): lax.all_to_all(blocks, 'dp', split_axis=0, concat_axis=0, tiled=True, axi...  24.1 us
    ppermute x12, starting transfers between devices, gather_blocks(): lax.ppermute(x, 'phase', [((i + s) % N_PHASE, i) for i in range(N_PHASE)])  13.7 us
    ppermute x6, starting transfers between devices, send(): lax.ppermute(block, 'phase', [(i, (i + s) % N_PHASE) for i in range(N_PHA...  10.6 us
    unnamed x20, local copies, waits for them, and re-layouts  7.59 us
    ppermute x12, waiting for transfers between devices, gather_blocks(): lax.ppermute(x, 'phase', [((i + s) % N_PHASE, i) for i in range(N_PHASE)])  6.19 us
    pallas_call x2, Pallas kernels, project_sends(): pl.pallas_call(body, in_specs=[pl.BlockSpec(memory_space=pltpu.SMEM), hbm...  4.22 us
    pallas_call x6, Pallas kernels, run(): pl.pallas_call(body, in_specs=[pl.BlockSpec(memory_space=pltpu.SMEM)] + [...  4.13 us
  transfers between devices with their start and end apart: 20, of which 12 were waited for; matrix products, arithmetic and copies ran while one was open for 3% of the time, Pallas kernels for 6%

profile of v6, /device:TPU:1, one launch (start us, length us, event | category | flops | bytes accessed | tf_op | source)
XLA Modules:
  0.0 108.9 jit_solution(16180595642994535621)
XLA Ops:
  0.7 3.0 %shard_map.104 = (bf16[128,512]{1,0:T(8,128)(2,1)}, bf16[128,512]{1,0:T(8,128)(2,1)}, bf16[128,512]{1,0:T(8,128)(2,1)}) custom-call(s32[1]{0:T(128)} %bitcast.k_ref, bf16[128,1024]{1,0:T(8,128)(2,1)} %x_ref.3, bf16[1024,2048]{1,0:T(8,128)(2,1)} %refs_3_.3), custom_call_target="tpu_custom_call" | custom-call | flops 1000000000 | bytes 100000 | tf_op jit(solution)/shard_map/pallas_call | solution.py:73
  3.7 3.7 %collective-permute-start = (bf16[128,512]{1,0:T(8,128)(2,1)}, bf16[128,512]{1,0:T(8,128)(2,1)S(1)}, u32[]{:S(2)}, u32[]{:S(2)}) collective-permute-start(bf16[128,512]{1,0:T(8,128)(2,1)} %get-tuple-element.32), channel_id=1, source_target_pairs={{0,128},{64,192},{128,0},{192,64},{1,129},{65,193},{129,1},{193,65... | collective-permute-start | bytes 393224 | tf_op jit(solution)/shard_map/ppermute | solution.py:148
  7.7 2.4 %collective-permute-start.2 = (bf16[128,512]{1,0:T(8,128)(2,1)}, bf16[128,512]{1,0:T(8,128)(2,1)S(1)}, u32[]{:S(2)}, u32[]{:S(2)}) collective-permute-start(bf16[128,512]{1,0:T(8,128)(2,1)} %get-tuple-element.34), channel_id=1, source_target_pairs={{0,192},{64,0},{128,64},{192,128},{1,193},{65,1},{129,65},{193,129... | collective-permute-start | bytes 393224 | tf_op jit(solution)/shard_map/ppermute | solution.py:148
  10.0 2.2 %copy-done.1 = bf16[1024,2048]{1,0:T(8,128)(2,1)S(1)} copy-done((bf16[1024,2048]{1,0:T(8,128)(2,1)S(1)}, bf16[1024,2048]{1,0:T(8,128)(2,1)}, u32[]{:S(2)}) %copy-start.1) | copy-done | bytes 4194328
  13.1 1.7 %collective-permute-done.1.c = bf16[128,512]{1,0:T(8,128)(2,1)S(1)} collective-permute-done((bf16[128,512]{1,0:T(8,128)(2,1)}, bf16[128,512]{1,0:T(8,128)(2,1)S(1)}, u32[]{:S(2)}, u32[]{:S(2)}) %collective-permute-start.1) | collective-permute-done | bytes 131104 | tf_op jit(solution)/shard_map/ppermute | solution.py:148
  14.8 1.3 %shard_map.106 = (f32[128,512]{1,0:T(8,128)S(1)}, bf16[1024,512]{1,0:T(8,128)(2,1)}) custom-call(f32[128,512]{1,0:T(8,128)S(1)} %shard_map.103.a, bf16[128,512]{1,0:T(8,128)(2,1)S(1)} %collective-permute-done.b, bf16[128,512]{1,0:T(8,128)(2,1)S(1)} %collective-permute-done.1.c, bf16[128,512]{1,0:T(8,128)(2,1)S(1)} %collective-permute-done.2.d, ...), custom_call_target="tpu_custom_call" | custom-call | flops 1000000000 | bytes 100000 | tf_op jit(solution)/shard_map/pallas_call | solution.py:200
  16.0 13.0 %all-to-all-start = ((bf16[64,16,512]{2,1,0:T(8,128)(2,1)}), bf16[64,16,512]{2,1,0:T(8,128)(2,1)S(1)}, u32[]{:S(2)}, u32[]{:S(2)}) async-start(bf16[64,16,512]{2,1,0:T(8,128)(2,1)} %bitcast.1), calls=%async_computation | async-start | bytes 2097152 | tf_op jit(solution)/shard_map/all_to_all | solution.py:343
  29.1 2.1 %gather_fusion = s32[448]{0:T(512)S(1)} fusion(s32[1024]{0:T(1024)S(1)} %bitcast.35, s32[1024]{0:T(1024)S(1)} %pad_clamp_fusion), kind=kCustom, calls=%fused_computation | custom fusion | bytes 5376 | tf_op jit(solution)/shard_map/jit(_take)/gather | solution.py:365
  31.6 1.6 %copy-done.4 = bf16[512,2048]{1,0:T(8,128)(2,1)S(1)} copy-done((bf16[512,2048]{1,0:T(8,128)(2,1)S(1)}, bf16[512,2048]{1,0:T(8,128)(2,1)}, u32[]{:S(2)}) %copy-start.4) | copy-done | bytes 2097176
  33.2 1.2 %shard_map.108 = (bf16[64,512]{1,0:T(8,128)(2,1)S(1)}, bf16[64,512]{1,0:T(8,128)(2,1)S(1)}, bf16[64,512]{1,0:T(8,128)(2,1)S(1)}) custom-call(s32[1]{0:T(128)} %bitcast.k_ref, bf16[64,512]{1,0:T(8,128)(2,1)S(1)} %copy-done.6, bf16[512,2048]{1,0:T(8,128)(2,1)S(1)} %copy-done.4), custom_call_target="tpu_custom_call" | custom-call | flops 1000000000 | bytes 100000 | tf_op jit(solution)/shard_map/pallas_call | solution.py:73
  34.4 1.6 %collective-permute-start.3 = (bf16[64,512]{1,0:T(8,128)(2,1)S(1)}, bf16[64,512]{1,0:T(8,128)(2,1)S(1)}, u32[]{:S(2)}, u32[]{:S(2)}) collective-permute-start(bf16[64,512]{1,0:T(8,128)(2,1)S(1)} %get-tuple-element.38), channel_id=1, source_target_pairs={{0,128},{64,192},{128,0},{192,64},{1,129},{65,193},{129,1},{193,65... | collective-permute-start | bytes 196616 | tf_op jit(solution)/shard_map/ppermute | solution.py:148
  36.1 1.7 %collective-permute-start.4 = (bf16[64,512]{1,0:T(8,128)(2,1)S(1)}, bf16[64,512]{1,0:T(8,128)(2,1)S(1)}, u32[]{:S(2)}, u32[]{:S(2)}) collective-permute-start(bf16[64,512]{1,0:T(8,128)(2,1)S(1)} %get-tuple-element.39), channel_id=1, source_target_pairs={{0,64},{64,128},{128,192},{192,0},{1,65},{65,129},{129,193},{193,1... | collective-permute-start | bytes 196616 | tf_op jit(solution)/shard_map/ppermute | solution.py:148
  39.4 1.6 %collective-permute-done.4.b = bf16[64,512]{1,0:T(8,128)(2,1)S(1)} collective-permute-done((bf16[64,512]{1,0:T(8,128)(2,1)S(1)}, bf16[64,512]{1,0:T(8,128)(2,1)S(1)}, u32[]{:S(2)}, u32[]{:S(2)}) %collective-permute-start.4) | collective-permute-done | bytes 65568 | tf_op jit(solution)/shard_map/ppermute | solution.py:148
  42.4 2.8 %collective-permute-start.7 = (f32[144,128]{1,0:T(8,128)S(1)}, f32[144,128]{1,0:T(8,128)S(1)}, u32[]{:S(2)}, u32[]{:S(2)}) collective-permute-start(f32[144,128]{1,0:T(8,128)S(1)} %shard_map.110.refs_0_), channel_id=1, source_target_pairs={{128,0},{192,64},{0,128},{64,192},{129,1},{193,65},{1,129},{65,193... | collective-permute-start | bytes 221192 | tf_op jit(solution)/shard_map/ppermute | solution.py:153
  45.3 8.1 %all-to-all-done = bf16[64,16,512]{2,1,0:T(8,128)(2,1)S(1)} async-done(((bf16[64,16,512]{2,1,0:T(8,128)(2,1)}), bf16[64,16,512]{2,1,0:T(8,128)(2,1)S(1)}, u32[]{:S(2)}, u32[]{:S(2)}) %all-to-all-start) | async-done | bytes 1048608 | tf_op jit(solution)/shard_map/all_to_all | solution.py:343
  53.4 1.3 %shard_map.111.refs_4_ = f32[16,128]{1,0:T(8,128)S(1)} custom-call(bf16[1024,512]{1,0:T(8,128)(2,1)S(1)} %bitcast.36, bf16[64,512]{1,0:T(8,128)(2,1)S(1)} %get-tuple-element.45.q_ref, s32[8,128]{1,0:T(8,128)S(1)} %pad.9.neg_ref.refs_9_), custom_call_target="tpu_custom_call" | custom-call | flops 1000000000 | bytes 100000 | tf_op jit(solution)/shard_map/pallas_call | solution.py:28
  54.7 1.0 collective-permute-start.11
  55.7 2.9 %collective-permute-start.10 = (f32[16,128]{1,0:T(8,128)S(1)}, f32[16,128]{1,0:T(8,128)S(1)}, u32[]{:S(2)}, u32[]{:S(2)}) collective-permute-start(f32[16,128]{1,0:T(8,128)S(1)} %shard_map.111.refs_4_), channel_id=1, source_target_pairs={{128,0},{192,64},{0,128},{64,192},{129,1},{193,65},{1,129},{65,193... | collective-permute-start | bytes 24584 | tf_op jit(solution)/shard_map/ppermute | solution.py:153
  58.6 1.1 %collective-permute-done.10.refs_6_ = f32[16,128]{1,0:T(8,128)S(1)} collective-permute-done((f32[16,128]{1,0:T(8,128)S(1)}, f32[16,128]{1,0:T(8,128)S(1)}, u32[]{:S(2)}, u32[]{:S(2)}) %collective-permute-start.10) | collective-permute-done | bytes 8224 | tf_op jit(solution)/shard_map/ppermute | solution.py:153
  59.7 1.7 %collective-permute-done.9.refs_5_ = f32[16,128]{1,0:T(8,128)S(1)} collective-permute-done((f32[16,128]{1,0:T(8,128)S(1)}, f32[16,128]{1,0:T(8,128)S(1)}, u32[]{:S(2)}, u32[]{:S(2)}) %collective-permute-start.9) | collective-permute-done | bytes 8224 | tf_op jit(solution)/shard_map/ppermute | solution.py:153
  61.4 1.7 %shard_map.112 = (bf16[1024,512]{1,0:T(8,128)(2,1)}, bf16[64,512]{1,0:T(8,128)(2,1)S(1)}, f32[128,512]{1,0:T(8,128)S(1)}, f32[8,128]{1,0:T(8,128)S(1)}) custom-call(f32[144,128]{1,0:T(8,128)S(1)} %shard_map.110.refs_0_, f32[144,128]{1,0:T(8,128)S(1)} %collective-permute-done.6.refs_1_, f32[144,128]{1,0:T(8,128)S(1)} %collective-permute-done.7.refs_2_, ...), custom_call_target="tpu_custom_call" | custom-call | flops 1000000000 | bytes 100000 | tf_op jit(solution)/shard_map/pallas_call | solution.py:376
  63.1 11.1 %all-to-all-start.1 = ((bf16[64,16,512]{2,1,0:T(8,128)(2,1)}), bf16[64,16,512]{2,1,0:T(8,128)(2,1)S(1)}, u32[]{:S(2)}, u32[]{:S(2)}) async-start(bf16[64,16,512]{2,1,0:T(8,128)(2,1)} %bitcast.6), calls=%async_computation.1 | async-start | bytes 2097152 | tf_op jit(solution)/shard_map/all_to_all | solution.py:343
  74.3 1.3 %collective-permute-start.14 = (bf16[64,512]{1,0:T(8,128)(2,1)S(1)}, bf16[64,512]{1,0:T(8,128)(2,1)S(1)}, u32[]{:S(2)}, u32[]{:S(2)}) collective-permute-start(bf16[64,512]{1,0:T(8,128)(2,1)S(1)} %get-tuple-element.49.refs_0_), channel_id=1, source_target_pairs={{128,0},{192,64},{0,128},{64,192},{129,1},{193,65},{1,129},{65,193... | collective-permute-start | bytes 196616 | tf_op jit(solution)/shard_map/ppermute | solution.py:153
  77.5 1.6 %copy-done.5 = bf16[512,2048]{1,0:T(8,128)(2,1)S(1)} copy-done((bf16[512,2048]{1,0:T(8,128)(2,1)S(1)}, bf16[512,2048]{1,0:T(8,128)(2,1)}, u32[]{:S(2)}) %copy-start.5) | copy-done | bytes 2097176
  79.4 1.5 %collective-permute-done.12.refs_1_ = bf16[64,512]{1,0:T(8,128)(2,1)S(1)} collective-permute-done((bf16[64,512]{1,0:T(8,128)(2,1)S(1)}, bf16[64,512]{1,0:T(8,128)(2,1)S(1)}, u32[]{:S(2)}, u32[]{:S(2)}) %collective-permute-start.12) | collective-permute-done | bytes 65568 | tf_op jit(solution)/shard_map/ppermute | solution.py:153
  81.2 1.1 shard_map.115
  82.3 16.3 %all-to-all-done.1 = bf16[64,16,512]{2,1,0:T(8,128)(2,1)S(1)} async-done(((bf16[64,16,512]{2,1,0:T(8,128)(2,1)}), bf16[64,16,512]{2,1,0:T(8,128)(2,1)S(1)}, u32[]{:S(2)}, u32[]{:S(2)}) %all-to-all-start.1) | async-done | bytes 1048608 | tf_op jit(solution)/shard_map/all_to_all | solution.py:343
  99.0 2.2 %collective-permute-start.17 = (bf16[128,512]{1,0:T(8,128)(2,1)S(1)}, bf16[128,512]{1,0:T(8,128)(2,1)S(1)}, u32[]{:S(2)}, u32[]{:S(2)}) collective-permute-start(bf16[128,512]{1,0:T(8,128)(2,1)S(1)} %shard_map.116.refs_0_), channel_id=1, source_target_pairs={{128,0},{192,64},{0,128},{64,192},{129,1},{193,65},{1,129},{65,193... | collective-permute-start | bytes 393224 | tf_op jit(solution)/shard_map/ppermute | solution.py:153
  101.2 1.1 %collective-permute-start.16 = (bf16[128,512]{1,0:T(8,128)(2,1)S(1)}, bf16[128,512]{1,0:T(8,128)(2,1)S(1)}, u32[]{:S(2)}, u32[]{:S(2)}) collective-permute-start(bf16[128,512]{1,0:T(8,128)(2,1)S(1)} %shard_map.116.refs_0_), channel_id=1, source_target_pairs={{64,0},{128,64},{192,128},{0,192},{65,1},{129,65},{193,129},{1,193... | collective-permute-start | bytes 393224 | tf_op jit(solution)/shard_map/ppermute | solution.py:153
  102.3 2.2 %copy-done.2 = bf16[1024,2048]{1,0:T(8,128)(2,1)S(1)} copy-done((bf16[1024,2048]{1,0:T(8,128)(2,1)S(1)}, bf16[1024,2048]{1,0:T(8,128)(2,1)}, u32[]{:S(2)}) %copy-start.2) | copy-done | bytes 4194328
  106.3 1.1 collective-permute-done.16.refs_1_
  107.4 1.5 %shard_map.119 = bf16[128,1024]{1,0:T(8,128)(2,1)} custom-call(s32[1]{0:T(128)} %bitcast.k_ref, f32[128,1024]{1,0:T(8,128)S(1)} %shard_map.118.refs_0_, bf16[128,512]{1,0:T(8,128)(2,1)S(1)} %collective-permute-done.16.refs_1_, bf16[128,512]{1,0:T(8,128)(2,1)S(1)} %collective-permute-done.17.refs_2_, bf16[1024,2048]{1,0:T(8,128)(2,1)S(1)} %copy-done.2), custom_call_target="tpu_custom_call" | custom-call | flops 1000000000 | bytes 100000 | tf_op jit(solution)/shard_map/pallas_call | solution.py:132
  (61 shorter events, 9.5 us)
Async XLA Ops:
  0.6 28.5 %copy-start = (s32[1,1024]{1,0:T(1,128)S(1)}, s32[1,1024]{1,0:T(1,128)}, u32[]{:S(2)}) copy-start(s32[1,1024]{1,0:T(1,128)} %param.13) | copy-start | bytes 12292
  0.6 9.4 %copy-start.3 = (bf16[128,1024]{1,0:T(8,128)(2,1)S(1)}, bf16[128,1024]{1,0:T(8,128)(2,1)}, u32[]{:S(2)}) copy-start(bf16[128,1024]{1,0:T(8,128)(2,1)} %x_ref.3) | copy-start | bytes 786436
  0.7 11.9 %copy-start.8 = (s32[1,64,16]{1,2,0:T(8,128)S(1)}, s32[1,64,16]{1,2,0:T(8,128)}, u32[]{:S(2)}) copy-start(s32[1,64,16]{1,2,0:T(8,128)} %param.12) | copy-start | bytes 12292
  3.7 9.4 %collective-permute-start = (bf16[128,512]{1,0:T(8,128)(2,1)}, bf16[128,512]{1,0:T(8,128)(2,1)S(1)}, u32[]{:S(2)}, u32[]{:S(2)}) collective-permute-start(bf16[128,512]{1,0:T(8,128)(2,1)} %get-tuple-element.32), channel_id=1, source_target_pairs={{0,128},{64,192},{128,0},{192,64},{1,129},{65,193},{129,1},{193,65... | collective-permute-start | bytes 393224 | tf_op jit(solution)/shard_map/ppermute | solution.py:148
  7.4 7.4 %collective-permute-start.1 = (bf16[128,512]{1,0:T(8,128)(2,1)}, bf16[128,512]{1,0:T(8,128)(2,1)S(1)}, u32[]{:S(2)}, u32[]{:S(2)}) collective-permute-start(bf16[128,512]{1,0:T(8,128)(2,1)} %get-tuple-element.33), channel_id=1, source_target_pairs={{0,64},{64,128},{128,192},{192,0},{1,65},{65,129},{129,193},{193,1... | collective-permute-start | bytes 393224 | tf_op jit(solution)/shard_map/ppermute | solution.py:148
  7.7 7.1 %collective-permute-start.2 = (bf16[128,512]{1,0:T(8,128)(2,1)}, bf16[128,512]{1,0:T(8,128)(2,1)S(1)}, u32[]{:S(2)}, u32[]{:S(2)}) collective-permute-start(bf16[128,512]{1,0:T(8,128)(2,1)} %get-tuple-element.34), channel_id=1, source_target_pairs={{0,192},{64,0},{128,64},{192,128},{1,193},{65,1},{129,65},{193,129... | collective-permute-start | bytes 393224 | tf_op jit(solution)/shard_map/ppermute | solution.py:148
  10.0 2.2 %copy-start.1 = (bf16[1024,2048]{1,0:T(8,128)(2,1)S(1)}, bf16[1024,2048]{1,0:T(8,128)(2,1)}, u32[]{:S(2)}) copy-start(bf16[1024,2048]{1,0:T(8,128)(2,1)} %refs_3_.3) | copy-start | bytes 12582916
  12.8 16.2 %copy-start.7 = (s32[64,7]{0,1:T(8,128)S(1)}, s32[64,7]{0,1:T(8,128)}, u32[]{:S(2)}) copy-start(s32[64,7]{0,1:T(8,128)} %param.14) | copy-start | bytes 5380
  13.1 18.3 %copy-start.9 = (f32[64]{0:T(128)S(1)}, f32[64]{0:T(128)}, u32[]{:S(2)}) copy-start(f32[64]{0:T(128)} %param.15) | copy-start | bytes 772
  13.1 18.6 %copy-start.6 = (bf16[64,512]{1,0:T(8,128)(2,1)S(1)}, bf16[64,512]{1,0:T(8,128)(2,1)}, u32[]{:S(2)}) copy-start(bf16[64,512]{1,0:T(8,128)(2,1)} %x_ref.5) | copy-start | bytes 196612
  16.0 37.3 %all-to-all-start = ((bf16[64,16,512]{2,1,0:T(8,128)(2,1)}), bf16[64,16,512]{2,1,0:T(8,128)(2,1)S(1)}, u32[]{:S(2)}, u32[]{:S(2)}) async-start(bf16[64,16,512]{2,1,0:T(8,128)(2,1)} %bitcast.1), calls=%async_computation | async-start | bytes 2097152 | tf_op jit(solution)/shard_map/all_to_all | solution.py:343
  31.6 1.6 %copy-start.4 = (bf16[512,2048]{1,0:T(8,128)(2,1)S(1)}, bf16[512,2048]{1,0:T(8,128)(2,1)}, u32[]{:S(2)}) copy-start(bf16[512,2048]{1,0:T(8,128)(2,1)} %refs_3_.2) | copy-start | bytes 6291460
  34.4 5.0 %collective-permute-start.3 = (bf16[64,512]{1,0:T(8,128)(2,1)S(1)}, bf16[64,512]{1,0:T(8,128)(2,1)S(1)}, u32[]{:S(2)}, u32[]{:S(2)}) collective-permute-start(bf16[64,512]{1,0:T(8,128)(2,1)S(1)} %get-tuple-element.38), channel_id=1, source_target_pairs={{0,128},{64,192},{128,0},{192,64},{1,129},{65,193},{129,1},{193,65... | collective-permute-start | bytes 196616 | tf_op jit(solution)/shard_map/ppermute | solution.py:148
  36.1 5.0 %collective-permute-start.4 = (bf16[64,512]{1,0:T(8,128)(2,1)S(1)}, bf16[64,512]{1,0:T(8,128)(2,1)S(1)}, u32[]{:S(2)}, u32[]{:S(2)}) collective-permute-start(bf16[64,512]{1,0:T(8,128)(2,1)S(1)} %get-tuple-element.39), channel_id=1, source_target_pairs={{0,64},{64,128},{128,192},{192,0},{1,65},{65,129},{129,193},{193,1... | collective-permute-start | bytes 196616 | tf_op jit(solution)/shard_map/ppermute | solution.py:148
  37.7 3.5 %collective-permute-start.5 = (bf16[64,512]{1,0:T(8,128)(2,1)S(1)}, bf16[64,512]{1,0:T(8,128)(2,1)S(1)}, u32[]{:S(2)}, u32[]{:S(2)}) collective-permute-start(bf16[64,512]{1,0:T(8,128)(2,1)S(1)} %get-tuple-element.40), channel_id=1, source_target_pairs={{0,192},{64,0},{128,64},{192,128},{1,193},{65,1},{129,65},{193,129... | collective-permute-start | bytes 196616 | tf_op jit(solution)/shard_map/ppermute | solution.py:148
  41.6 17.0 %collective-permute-start.8 = (f32[144,128]{1,0:T(8,128)S(1)}, f32[144,128]{1,0:T(8,128)S(1)}, u32[]{:S(2)}, u32[]{:S(2)}) collective-permute-start(f32[144,128]{1,0:T(8,128)S(1)} %shard_map.110.refs_0_), channel_id=1, source_target_pairs={{192,0},{0,64},{64,128},{128,192},{193,1},{1,65},{65,129},{129,193... | collective-permute-start | bytes 221192 | tf_op jit(solution)/shard_map/ppermute | solution.py:153
  42.4 16.2 %collective-permute-start.7 = (f32[144,128]{1,0:T(8,128)S(1)}, f32[144,128]{1,0:T(8,128)S(1)}, u32[]{:S(2)}, u32[]{:S(2)}) collective-permute-start(f32[144,128]{1,0:T(8,128)S(1)} %shard_map.110.refs_0_), channel_id=1, source_target_pairs={{128,0},{192,64},{0,128},{64,192},{129,1},{193,65},{1,129},{65,193... | collective-permute-start | bytes 221192 | tf_op jit(solution)/shard_map/ppermute | solution.py:153
  45.2 13.4 %collective-permute-start.6 = (f32[144,128]{1,0:T(8,128)S(1)}, f32[144,128]{1,0:T(8,128)S(1)}, u32[]{:S(2)}, u32[]{:S(2)}) collective-permute-start(f32[144,128]{1,0:T(8,128)S(1)} %shard_map.110.refs_0_), channel_id=1, source_target_pairs={{64,0},{128,64},{192,128},{0,192},{65,1},{129,65},{193,129},{1,193... | collective-permute-start | bytes 221192 | tf_op jit(solution)/shard_map/ppermute | solution.py:153
  54.7 3.9 %collective-permute-start.11 = (f32[16,128]{1,0:T(8,128)S(1)}, f32[16,128]{1,0:T(8,128)S(1)}, u32[]{:S(2)}, u32[]{:S(2)}) collective-permute-start(f32[16,128]{1,0:T(8,128)S(1)} %shard_map.111.refs_4_), channel_id=1, source_target_pairs={{192,0},{0,64},{64,128},{128,192},{193,1},{1,65},{65,129},{129,193... | collective-permute-start | bytes 24584 | tf_op jit(solution)/shard_map/ppermute | solution.py:153
  55.7 4.0 %collective-permute-start.10 = (f32[16,128]{1,0:T(8,128)S(1)}, f32[16,128]{1,0:T(8,128)S(1)}, u32[]{:S(2)}, u32[]{:S(2)}) collective-permute-start(f32[16,128]{1,0:T(8,128)S(1)} %shard_map.111.refs_4_), channel_id=1, source_target_pairs={{128,0},{192,64},{0,128},{64,192},{129,1},{193,65},{1,129},{65,193... | collective-permute-start | bytes 24584 | tf_op jit(solution)/shard_map/ppermute | solution.py:153
  58.6 2.8 %collective-permute-start.9 = (f32[16,128]{1,0:T(8,128)S(1)}, f32[16,128]{1,0:T(8,128)S(1)}, u32[]{:S(2)}, u32[]{:S(2)}) collective-permute-start(f32[16,128]{1,0:T(8,128)S(1)} %shard_map.111.refs_4_), channel_id=1, source_target_pairs={{64,0},{128,64},{192,128},{0,192},{65,1},{129,65},{193,129},{1,193... | collective-permute-start | bytes 24584 | tf_op jit(solution)/shard_map/ppermute | solution.py:153
  63.1 35.5 %all-to-all-start.1 = ((bf16[64,16,512]{2,1,0:T(8,128)(2,1)}), bf16[64,16,512]{2,1,0:T(8,128)(2,1)S(1)}, u32[]{:S(2)}, u32[]{:S(2)}) async-start(bf16[64,16,512]{2,1,0:T(8,128)(2,1)} %bitcast.6), calls=%async_computation.1 | async-start | bytes 2097152 | tf_op jit(solution)/shard_map/all_to_all | solution.py:343
  74.3 7.0 %collective-permute-start.14 = (bf16[64,512]{1,0:T(8,128)(2,1)S(1)}, bf16[64,512]{1,0:T(8,128)(2,1)S(1)}, u32[]{:S(2)}, u32[]{:S(2)}) collective-permute-start(bf16[64,512]{1,0:T(8,128)(2,1)S(1)} %get-tuple-element.49.refs_0_), channel_id=1, source_target_pairs={{128,0},{192,64},{0,128},{64,192},{129,1},{193,65},{1,129},{65,193... | collective-permute-start | bytes 196616 | tf_op jit(solution)/shard_map/ppermute | solution.py:153
  75.6 5.7 %collective-permute-start.13 = (bf16[64,512]{1,0:T(8,128)(2,1)S(1)}, bf16[64,512]{1,0:T(8,128)(2,1)S(1)}, u32[]{:S(2)}, u32[]{:S(2)}) collective-permute-start(bf16[64,512]{1,0:T(8,128)(2,1)S(1)} %get-tuple-element.49.refs_0_), channel_id=1, source_target_pairs={{64,0},{128,64},{192,128},{0,192},{65,1},{129,65},{193,129},{1,193... | collective-permute-start | bytes 196616 | tf_op jit(solution)/shard_map/ppermute | solution.py:153
  76.2 4.7 %collective-permute-start.12 = (bf16[64,512]{1,0:T(8,128)(2,1)S(1)}, bf16[64,512]{1,0:T(8,128)(2,1)S(1)}, u32[]{:S(2)}, u32[]{:S(2)}) collective-permute-start(bf16[64,512]{1,0:T(8,128)(2,1)S(1)} %get-tuple-element.49.refs_0_), channel_id=1, source_target_pairs={{192,0},{0,64},{64,128},{128,192},{193,1},{1,65},{65,129},{129,193... | collective-permute-start | bytes 196616 | tf_op jit(solution)/shard_map/ppermute | solution.py:153
  77.5 1.6 %copy-start.5 = (bf16[512,2048]{1,0:T(8,128)(2,1)S(1)}, bf16[512,2048]{1,0:T(8,128)(2,1)}, u32[]{:S(2)}) copy-start(bf16[512,2048]{1,0:T(8,128)(2,1)} %refs_3_.2) | copy-start | bytes 6291460
  98.9 6.4 %collective-permute-start.15 = (bf16[128,512]{1,0:T(8,128)(2,1)S(1)}, bf16[128,512]{1,0:T(8,128)(2,1)S(1)}, u32[]{:S(2)}, u32[]{:S(2)}) collective-permute-start(bf16[128,512]{1,0:T(8,128)(2,1)S(1)} %shard_map.116.refs_0_), channel_id=1, source_target_pairs={{192,0},{0,64},{64,128},{128,192},{193,1},{1,65},{65,129},{129,193... | collective-permute-start | bytes 393224 | tf_op jit(solution)/shard_map/ppermute | solution.py:153
  99.0 7.3 %collective-permute-start.17 = (bf16[128,512]{1,0:T(8,128)(2,1)S(1)}, bf16[128,512]{1,0:T(8,128)(2,1)S(1)}, u32[]{:S(2)}, u32[]{:S(2)}) collective-permute-start(bf16[128,512]{1,0:T(8,128)(2,1)S(1)} %shard_map.116.refs_0_), channel_id=1, source_target_pairs={{128,0},{192,64},{0,128},{64,192},{129,1},{193,65},{1,129},{65,193... | collective-permute-start | bytes 393224 | tf_op jit(solution)/shard_map/ppermute | solution.py:153
  101.2 6.2 %collective-permute-start.16 = (bf16[128,512]{1,0:T(8,128)(2,1)S(1)}, bf16[128,512]{1,0:T(8,128)(2,1)S(1)}, u32[]{:S(2)}, u32[]{:S(2)}) collective-permute-start(bf16[128,512]{1,0:T(8,128)(2,1)S(1)} %shard_map.116.refs_0_), channel_id=1, source_target_pairs={{64,0},{128,64},{192,128},{0,192},{65,1},{129,65},{193,129},{1,193... | collective-permute-start | bytes 393224 | tf_op jit(solution)/shard_map/ppermute | solution.py:153
  102.3 2.2 %copy-start.2 = (bf16[1024,2048]{1,0:T(8,128)(2,1)S(1)}, bf16[1024,2048]{1,0:T(8,128)(2,1)}, u32[]{:S(2)}) copy-start(bf16[1024,2048]{1,0:T(8,128)(2,1)} %refs_3_.3) | copy-start | bytes 12582916

commit v7 on v6

--- a/solution.py
+++ b/solution.py
@@ -227,37 +227,38 @@
 def hard_partials(rows_ref, q_ref, neg_ref, out_ref):
     rows = rows_ref[...]
     q = q_ref[...]
-    scores = dot(rows, jnp.concatenate([q, q], axis=0), NT)
     wide = rows.astype(f32)
     square = wide * wide
-    lanes = scores.shape[1]
-    folded = square[:, 0:lanes]
-    for s in range(lanes, square.shape[1], lanes):
-        folded = folded + square[:, s : s + lanes]
+    folded = square[:, 0:128]
+    for s in range(128, square.shape[1], 128):
+        folded = folded + square[:, s : s + 128]
     hi, lo = split_bf16(folded)
-    ones = jnp.ones((lanes, lanes), bf16)
-    squares = dot(hi, ones) + dot(lo, ones)
-    slot = iota(scores.shape, 0)
+    upper = (iota((128, 128), 1) >= 64).astype(f32).astype(bf16)
+    both = dot(rows, jnp.concatenate([q, jnp.zeros_like(q)], axis=0), NT) + dot(hi, upper) + dot(lo, upper)
+    slot = iota(both.shape, 0)
     for j in range(8):
         hit = slot == neg_ref[j : j + 1, :]
-        out_ref[j : j + 1, :] = jnp.sum(jnp.where(hit, scores, 0.0), axis=0, keepdims=True)
-        out_ref[8 + j : 9 + j, :] = jnp.sum(jnp.where(hit, squares, 0.0), axis=0, keepdims=True)
+        out_ref[j : j + 1, :] = jnp.sum(jnp.where(hit, both, 0.0), axis=0, keepdims=True)
 
 
 def softmax_terms(*refs):
     inner_refs, hard_refs = refs[0:4], refs[4:8]
-    small_ref, neg_ref, rows_ref, d_ref, q_ref, out_ref, u_ref, g_ref, loss_ref, buf_ref, sem_ref = refs[8:]
+    small_ref, neg_ref, rows_ref, q_ref, out_ref, coef_ref, grad_ref, row_ref, col_ref, buf_ref, sem_ref = refs[8:]
     sums = sum_refs(inner_refs)
     picks = sum_refs(hard_refs)
-    docs, queries = d_ref.shape[0], q_ref.shape[0]
+    docs, queries = grad_ref.shape[0], q_ref.shape[0]
+    swapped = pltpu.roll(picks, 64, 1)
+    low_lane = iota(picks.shape, 1) < 64
+    scores = jnp.where(low_lane, picks, swapped)
+    squares = jnp.where(low_lane, swapped, picks)
     q_scale = lax.rsqrt(sums[docs : docs + 1, :] + epsilon)
     d_scale_row = lax.rsqrt(sums[docs + 8 : docs + 9, :] + epsilon)
     row = iota((docs, 128), 0)
     lane = iota((docs, 128), 1)
     d_scale = jnp.sum(jnp.where(row == lane, d_scale_row, 0.0), axis=1, keepdims=True)
     inner = scale20 * (sums[0:docs, :] * q_scale * d_scale)
-    hard_scale = lax.rsqrt(picks[8:16, :] + epsilon)
-    hard = scale20 * (picks[0:8, :] * q_scale * hard_scale)
+    hard_scale = lax.rsqrt(squares + epsilon)
+    hard = scale20 * (scores * q_scale * hard_scale)
     valid = small_ref[0:8, :]
     weight = scale20 * small_ref[8:9, :]
     hard_exp = jnp.exp(hard) * valid
@@ -265,28 +266,22 @@
     total = jnp.sum(inner_exp, axis=0, keepdims=True) + jnp.sum(hard_exp, axis=0, keepdims=True)
     own = row == lax.bitwise_and(lane, 63)
     positive = jnp.sum(jnp.where(own, inner, 0.0), axis=0, keepdims=True)
-    loss_ref[...] = jnp.broadcast_to(jnp.log(total) - positive, loss_ref.shape)
     factor = weight / total
-    grad = (factor * inner_exp - jnp.where(own, weight, 0.0)).astype(bf16)
-    wide_grad = grad.astype(f32)
     hard_grad = factor * hard_exp
     hard_dot = hard_grad * hard * (1.0 / scale20)
-    products = wide_grad * inner * (1.0 / scale20)
-    q_dot = jnp.sum(products, axis=0, keepdims=True) + jnp.sum(hard_dot, axis=0, keepdims=True)
-    d_dot = jnp.sum(jnp.where(lane < 64, products, 0.0), axis=1, keepdims=True)
-    sent = hard_scale * jnp.where(iota((8, 128), 1) < 64, hard_grad, hard_dot * hard_scale)
+    sent = hard_scale * jnp.where(low_lane, hard_grad, hard_dot * hard_scale)
     slots = out_ref.shape[0]
     slot = iota((slots, 128), 0)
     coef = jnp.zeros((slots, 128), f32)
     for j in range(7):
         coef = coef + jnp.where(slot == neg_ref[j : j + 1, :], sent[j : j + 1, :], 0.0)
     coef = coef.astype(bf16)
+    coef_ref[...] = coef
 
     eye = iota((queries, 128), 0) == iota((queries, 128), 1)
     q_scale_col = jnp.sum(jnp.where(eye, q_scale, 0.0), axis=1, keepdims=True)
-    q_dot_col = jnp.sum(jnp.where(eye, q_dot, 0.0), axis=1, keepdims=True)
-    q_unit = q_ref[...] * q_scale_col
-    q_low = jnp.concatenate([q_unit.astype(bf16), jnp.zeros(q_ref.shape, bf16)], axis=0)
+    q_low = (q_ref[...] * q_scale_col).astype(bf16)
+    q_low = jnp.concatenate([q_low, jnp.zeros_like(q_low)], axis=0)
     second = (iota((128, 128), 0) >= 64).astype(f32).astype(bf16)
     block = slots // CHUNKS
 
@@ -303,12 +298,35 @@
             buf_ref[part, c : c + 128] = (mixed[:, c : c + 128] - away).astype(bf16)
         store(i).start()
 
-    d_unit = d_ref[...] * d_scale
-    g_query = dot(grad, d_unit.astype(bf16), TN) + dot(coef, rows_ref[...], TN)
-    u_ref[...] = (q_scale_col * (g_query[0:queries, :] - q_unit * q_dot_col)).astype(bf16)
-    g_ref[...] = d_scale * (dot(grad, q_low) - d_unit * d_dot)
+    grad = (factor * inner_exp - jnp.where(own, weight, 0.0)).astype(bf16)
+    grad_ref[...] = grad
+    products = grad.astype(f32) * inner * (1.0 / scale20)
+    q_dot = jnp.sum(products, axis=0, keepdims=True) + jnp.sum(hard_dot, axis=0, keepdims=True)
+    d_dot = jnp.sum(jnp.where(lane < 64, products, 0.0), axis=1, keepdims=True)
+    row_ref[...] = jnp.zeros_like(row_ref)
+    row_ref[0:1, :] = jnp.log(total) - positive
+    row_ref[1:2, :] = q_scale
+    row_ref[2:3, :] = q_dot
+    col_ref[...] = jnp.where(lane == 0, d_scale, d_dot)
     for i in range(CHUNKS):
         store(i).wait()
+
+
+def local_grads(coef_ref, grad_ref, row_ref, col_ref, rows_ref, d_ref, q_ref, u_ref, g_ref):
+    queries = q_ref.shape[0]
+    d_scale = col_ref[:, 0:1]
+    d_dot = col_ref[:, 1:2]
+    eye = iota((queries, 128), 0) == iota((queries, 128), 1)
+    q_scale = jnp.sum(jnp.where(eye, row_ref[1:2, :], 0.0), axis=1, keepdims=True)
+    q_dot = jnp.sum(jnp.where(eye, row_ref[2:3, :], 0.0), axis=1, keepdims=True)
+    q_unit = q_ref[...] * q_scale
+    q_low = q_unit.astype(bf16)
+    q_low = jnp.concatenate([q_low, jnp.zeros_like(q_low)], axis=0)
+    d_unit = d_ref[...] * d_scale
+    grad = grad_ref[...]
+    g_query = dot(grad, d_unit.astype(bf16), TN) + dot(coef_ref[...], rows_ref[...], TN)
+    u_ref[...] = (q_scale * (g_query[0:queries, :] - q_unit * q_dot)).astype(bf16)
+    g_ref[...] = d_scale * (dot(grad, q_low) - d_unit * d_dot)
 
 
 def doc_grads(rows_ref, request_ref, g_ref, u_ref):
@@ -370,26 +388,38 @@
     small = jnp.concatenate([small, small], axis=1)
     received, small, neg_rows = lax.optimization_barrier((received, small, neg_rows))
 
-    (hard,) = call(hard_partials, [((16, 128), f32)], received, q_low, neg_rows)
+    (hard,) = call(hard_partials, [((8, 128), f32)], received, q_low, neg_rows)
     hard_all = gather_blocks(hard)
     vmem = pl.BlockSpec(memory_space=pltpu.VMEM)
-    rows, u_query, g_local, loss = pl.pallas_call(
+    rows, coef, grad, by_query, by_doc = pl.pallas_call(
         softmax_terms,
-        in_specs=[vmem] * 13,
-        out_specs=[pl.BlockSpec(memory_space=pltpu.HBM), vmem, vmem, vmem],
+        in_specs=[vmem] * 12,
+        out_specs=[pl.BlockSpec(memory_space=pltpu.HBM)] + [vmem] * 4,
         out_shape=[
             jax.ShapeDtypeStruct((slots, cols), bf16),
-            jax.ShapeDtypeStruct((queries, cols), bf16),
-            jax.ShapeDtypeStruct((docs, cols), f32),
+            jax.ShapeDtypeStruct((slots, 128), bf16),
+            jax.ShapeDtypeStruct((docs, 128), bf16),
             jax.ShapeDtypeStruct((8, 128), f32),
+            jax.ShapeDtypeStruct((docs, 128), f32),
         ],
         scratch_shapes=[pltpu.VMEM((slots, cols), bf16), pltpu.SemaphoreType.DMA((CHUNKS,))],
         compiler_params=params(),
         cost_estimate=cost,
-    )(*inner_all, *hard_all, small, neg_rows, received, d_total, q_total)
+    )(*inner_all, *hard_all, small, neg_rows, received, q_total)
     arrived = exchange(rows)
+    u_query, g_local = call(
+        local_grads,
+        [((queries, cols), bf16), ((docs, cols), f32)],
+        coef,
+        grad,
+        by_query,
+        by_doc,
+        received,
+        d_total,
+        q_total,
+    )
     grad_query = project_back(u_query, query_proj, k)
-    arrived, grad_query, loss = lax.optimization_barrier((arrived, grad_query, loss[0, :queries]))
+    arrived, grad_query, loss = lax.optimization_barrier((arrived, grad_query, by_query[0, :queries]))
 
     (u_docs,) = call(doc_grads, [((docs, cols), bf16)], arrived, requests, g_local)
     grad_doc = project_back(u_docs, doc_proj, k)

time: 111 us -> 111 us (level)
    pallas_call x5 -> x6, Pallas kernels: 2.24 us -> 2.42 us  [call(): pl.pallas_call(body, out_shape=[jax.ShapeDtypeStruct(s, t) for s, t in ou...]
where the time goes in v7:
time: 111 us; the launch traced here: 109 us
  starting transfers between devices  48.4 us (44%)
  waiting for transfers between devices  34.1 us (31%)
  Pallas kernels  14.2 us (13%)
  local copies, waits for them, and re-layouts  10.7 us (10%)
    all_to_all x2, starting transfers between devices, exchange(): lax.all_to_all(blocks, 'dp', split_axis=0, concat_axis=0, tiled=True, axi...  24.1 us
    all_to_all x2, waiting for transfers between devices, exchange(): lax.all_to_all(blocks, 'dp', split_axis=0, concat_axis=0, tiled=True, axi...  23.9 us
    ppermute x12, starting transfers between devices, gather_blocks(): lax.ppermute(x, 'phase', [((i + s) % N_PHASE, i) for i in range(N_PHASE)])  13.7 us
    ppermute x6, starting transfers between devices, send(): lax.ppermute(block, 'phase', [(i, (i + s) % N_PHASE) for i in range(N_PHA...  10.6 us
    unnamed x20, local copies, waits for them, and re-layouts  7.59 us
    ppermute x12, waiting for transfers between devices, gather_blocks(): lax.ppermute(x, 'phase', [((i + s) % N_PHASE, i) for i in range(N_PHASE)])  6.15 us
    pallas_call x2, Pallas kernels, project_sends(): pl.pallas_call(body, in_specs=[pl.BlockSpec(memory_space=pltpu.SMEM), hbm...  4.23 us
    pallas_call x6, Pallas kernels, run(): pl.pallas_call(body, in_specs=[pl.BlockSpec(memory_space=pltpu.SMEM)] + [...  4.13 us
  transfers between devices with their start and end apart: 20, of which 12 were waited for; matrix products, arithmetic and copies ran while one was open for 3% of the time, Pallas kernels for 6%

profile of v7, /device:TPU:1, one launch (start us, length us, event | category | flops | bytes accessed | tf_op | source)
XLA Modules:
  0.0 108.5 jit_solution(8067383746672010563)
XLA Ops:
  0.7 3.0 %shard_map.104 = (bf16[128,512]{1,0:T(8,128)(2,1)}, bf16[128,512]{1,0:T(8,128)(2,1)}, bf16[128,512]{1,0:T(8,128)(2,1)}) custom-call(s32[1]{0:T(128)} %bitcast.k_ref, bf16[128,1024]{1,0:T(8,128)(2,1)} %x_ref.3, bf16[1024,2048]{1,0:T(8,128)(2,1)} %refs_3_.3), custom_call_target="tpu_custom_call" | custom-call | flops 1000000000 | bytes 100000 | tf_op jit(solution)/shard_map/pallas_call | solution.py:73
  3.7 3.7 %collective-permute-start = (bf16[128,512]{1,0:T(8,128)(2,1)}, bf16[128,512]{1,0:T(8,128)(2,1)S(1)}, u32[]{:S(2)}, u32[]{:S(2)}) collective-permute-start(bf16[128,512]{1,0:T(8,128)(2,1)} %get-tuple-element.35), channel_id=1, source_target_pairs={{0,128},{64,192},{128,0},{192,64},{1,129},{65,193},{129,1},{193,65... | collective-permute-start | bytes 393224 | tf_op jit(solution)/shard_map/ppermute | solution.py:148
  7.7 2.4 %collective-permute-start.2 = (bf16[128,512]{1,0:T(8,128)(2,1)}, bf16[128,512]{1,0:T(8,128)(2,1)S(1)}, u32[]{:S(2)}, u32[]{:S(2)}) collective-permute-start(bf16[128,512]{1,0:T(8,128)(2,1)} %get-tuple-element.37), channel_id=1, source_target_pairs={{0,192},{64,0},{128,64},{192,128},{1,193},{65,1},{129,65},{193,129... | collective-permute-start | bytes 393224 | tf_op jit(solution)/shard_map/ppermute | solution.py:148
  10.0 2.2 %copy-done.1 = bf16[1024,2048]{1,0:T(8,128)(2,1)S(1)} copy-done((bf16[1024,2048]{1,0:T(8,128)(2,1)S(1)}, bf16[1024,2048]{1,0:T(8,128)(2,1)}, u32[]{:S(2)}) %copy-start.1) | copy-done | bytes 4194328
  13.1 1.7 %collective-permute-done.1.c = bf16[128,512]{1,0:T(8,128)(2,1)S(1)} collective-permute-done((bf16[128,512]{1,0:T(8,128)(2,1)}, bf16[128,512]{1,0:T(8,128)(2,1)S(1)}, u32[]{:S(2)}, u32[]{:S(2)}) %collective-permute-start.1) | collective-permute-done | bytes 131104 | tf_op jit(solution)/shard_map/ppermute | solution.py:148
  14.8 1.3 %shard_map.106 = (f32[128,512]{1,0:T(8,128)S(1)}, bf16[1024,512]{1,0:T(8,128)(2,1)}) custom-call(f32[128,512]{1,0:T(8,128)S(1)} %shard_map.103.a, bf16[128,512]{1,0:T(8,128)(2,1)S(1)} %collective-permute-done.b, bf16[128,512]{1,0:T(8,128)(2,1)S(1)} %collective-permute-done.1.c, bf16[128,512]{1,0:T(8,128)(2,1)S(1)} %collective-permute-done.2.d, ...), custom_call_target="tpu_custom_call" | custom-call | flops 1000000000 | bytes 100000 | tf_op jit(solution)/shard_map/pallas_call | solution.py:200
  16.1 13.0 %all-to-all-start = ((bf16[64,16,512]{2,1,0:T(8,128)(2,1)}), bf16[64,16,512]{2,1,0:T(8,128)(2,1)S(1)}, u32[]{:S(2)}, u32[]{:S(2)}) async-start(bf16[64,16,512]{2,1,0:T(8,128)(2,1)} %bitcast.1), calls=%async_computation | async-start | bytes 2097152 | tf_op jit(solution)/shard_map/all_to_all | solution.py:361
  29.1 2.1 %gather_fusion = s32[448]{0:T(512)S(1)} fusion(s32[1024]{0:T(1024)S(1)} %bitcast.35, s32[1024]{0:T(1024)S(1)} %pad_clamp_fusion), kind=kCustom, calls=%fused_computation | custom fusion | bytes 5376 | tf_op jit(solution)/shard_map/jit(_take)/gather | solution.py:383
  31.6 1.6 %copy-done.4 = bf16[512,2048]{1,0:T(8,128)(2,1)S(1)} copy-done((bf16[512,2048]{1,0:T(8,128)(2,1)S(1)}, bf16[512,2048]{1,0:T(8,128)(2,1)}, u32[]{:S(2)}) %copy-start.4) | copy-done | bytes 2097176
  33.2 1.2 %shard_map.108 = (bf16[64,512]{1,0:T(8,128)(2,1)S(1)}, bf16[64,512]{1,0:T(8,128)(2,1)S(1)}, bf16[64,512]{1,0:T(8,128)(2,1)S(1)}) custom-call(s32[1]{0:T(128)} %bitcast.k_ref, bf16[64,512]{1,0:T(8,128)(2,1)S(1)} %copy-done.6, bf16[512,2048]{1,0:T(8,128)(2,1)S(1)} %copy-done.4), custom_call_target="tpu_custom_call" | custom-call | flops 1000000000 | bytes 100000 | tf_op jit(solution)/shard_map/pallas_call | solution.py:73
  34.5 1.6 %collective-permute-start.3 = (bf16[64,512]{1,0:T(8,128)(2,1)S(1)}, bf16[64,512]{1,0:T(8,128)(2,1)S(1)}, u32[]{:S(2)}, u32[]{:S(2)}) collective-permute-start(bf16[64,512]{1,0:T(8,128)(2,1)S(1)} %get-tuple-element.41), channel_id=1, source_target_pairs={{0,128},{64,192},{128,0},{192,64},{1,129},{65,193},{129,1},{193,65... | collective-permute-start | bytes 196616 | tf_op jit(solution)/shard_map/ppermute | solution.py:148
  36.1 1.7 %collective-permute-start.4 = (bf16[64,512]{1,0:T(8,128)(2,1)S(1)}, bf16[64,512]{1,0:T(8,128)(2,1)S(1)}, u32[]{:S(2)}, u32[]{:S(2)}) collective-permute-start(bf16[64,512]{1,0:T(8,128)(2,1)S(1)} %get-tuple-element.42), channel_id=1, source_target_pairs={{0,64},{64,128},{128,192},{192,0},{1,65},{65,129},{129,193},{193,1... | collective-permute-start | bytes 196616 | tf_op jit(solution)/shard_map/ppermute | solution.py:148
  39.5 1.6 %collective-permute-done.4.b = bf16[64,512]{1,0:T(8,128)(2,1)S(1)} collective-permute-done((bf16[64,512]{1,0:T(8,128)(2,1)S(1)}, bf16[64,512]{1,0:T(8,128)(2,1)S(1)}, u32[]{:S(2)}, u32[]{:S(2)}) %collective-permute-start.4) | collective-permute-done | bytes 65568 | tf_op jit(solution)/shard_map/ppermute | solution.py:148
  42.4 2.8 %collective-permute-start.7 = (f32[144,128]{1,0:T(8,128)S(1)}, f32[144,128]{1,0:T(8,128)S(1)}, u32[]{:S(2)}, u32[]{:S(2)}) collective-permute-start(f32[144,128]{1,0:T(8,128)S(1)} %shard_map.110.refs_0_), channel_id=1, source_target_pairs={{128,0},{192,64},{0,128},{64,192},{129,1},{193,65},{1,129},{65,193... | collective-permute-start | bytes 221192 | tf_op jit(solution)/shard_map/ppermute | solution.py:153
  45.3 8.1 %all-to-all-done = bf16[64,16,512]{2,1,0:T(8,128)(2,1)S(1)} async-done(((bf16[64,16,512]{2,1,0:T(8,128)(2,1)}), bf16[64,16,512]{2,1,0:T(8,128)(2,1)S(1)}, u32[]{:S(2)}, u32[]{:S(2)}) %all-to-all-start) | async-done | bytes 1048608 | tf_op jit(solution)/shard_map/all_to_all | solution.py:361
  53.4 1.1 shard_map.111.refs_4_
  54.5 1.0 collective-permute-start.11
  55.5 2.9 %collective-permute-start.10 = (f32[8,128]{1,0:T(8,128)S(1)}, f32[8,128]{1,0:T(8,128)S(1)}, u32[]{:S(2)}, u32[]{:S(2)}) collective-permute-start(f32[8,128]{1,0:T(8,128)S(1)} %shard_map.111.refs_4_), channel_id=1, source_target_pairs={{128,0},{192,64},{0,128},{64,192},{129,1},{193,65},{1,129},{65,193... | collective-permute-start | bytes 12296 | tf_op jit(solution)/shard_map/ppermute | solution.py:153
  58.4 1.1 collective-permute-done.10.refs_6_
  59.4 1.7 %collective-permute-done.9.refs_5_ = f32[8,128]{1,0:T(8,128)S(1)} collective-permute-done((f32[8,128]{1,0:T(8,128)S(1)}, f32[8,128]{1,0:T(8,128)S(1)}, u32[]{:S(2)}, u32[]{:S(2)}) %collective-permute-start.9) | collective-permute-done | bytes 4128 | tf_op jit(solution)/shard_map/ppermute | solution.py:153
  61.1 1.7 %shard_map.112 = (bf16[1024,512]{1,0:T(8,128)(2,1)}, bf16[1024,128]{1,0:T(8,128)(2,1)S(1)}, bf16[128,128]{1,0:T(8,128)(2,1)S(1)}, f32[8,128]{1,0:T(8,128)S(1)}, f32[128,128]{1,0:T(8,128)S(1)}) custom-call(f32[144,128]{1,0:T(8,128)S(1)} %shard_map.110.refs_0_, f32[144,128]{1,0:T(8,128)S(1)} %collective-permute-done.6.refs_1_, ...), custom_call_target="tpu_custom_call" | custom-call | flops 1000000000 | bytes 100000 | tf_op jit(solution)/shard_map/pallas_call | solution.py:394
  62.8 11.1 %all-to-all-start.1 = ((bf16[64,16,512]{2,1,0:T(8,128)(2,1)}), bf16[64,16,512]{2,1,0:T(8,128)(2,1)S(1)}, u32[]{:S(2)}, u32[]{:S(2)}) async-start(bf16[64,16,512]{2,1,0:T(8,128)(2,1)} %bitcast.6), calls=%async_computation.1 | async-start | bytes 2097152 | tf_op jit(solution)/shard_map/all_to_all | solution.py:361
  74.3 1.3 %collective-permute-start.14 = (bf16[64,512]{1,0:T(8,128)(2,1)S(1)}, bf16[64,512]{1,0:T(8,128)(2,1)S(1)}, u32[]{:S(2)}, u32[]{:S(2)}) collective-permute-start(bf16[64,512]{1,0:T(8,128)(2,1)S(1)} %get-tuple-element.56.refs_0_), channel_id=1, source_target_pairs={{128,0},{192,64},{0,128},{64,192},{129,1},{193,65},{1,129},{65,193... | collective-permute-start | bytes 196616 | tf_op jit(solution)/shard_map/ppermute | solution.py:153
  77.6 1.6 %copy-done.5 = bf16[512,2048]{1,0:T(8,128)(2,1)S(1)} copy-done((bf16[512,2048]{1,0:T(8,128)(2,1)S(1)}, bf16[512,2048]{1,0:T(8,128)(2,1)}, u32[]{:S(2)}) %copy-start.5) | copy-done | bytes 2097176
  79.5 1.5 %collective-permute-done.12.refs_1_ = bf16[64,512]{1,0:T(8,128)(2,1)S(1)} collective-permute-done((bf16[64,512]{1,0:T(8,128)(2,1)S(1)}, bf16[64,512]{1,0:T(8,128)(2,1)S(1)}, u32[]{:S(2)}, u32[]{:S(2)}) %collective-permute-start.12) | collective-permute-done | bytes 65568 | tf_op jit(solution)/shard_map/ppermute | solution.py:153
  81.3 1.1 shard_map.116
  82.4 15.8 %all-to-all-done.1 = bf16[64,16,512]{2,1,0:T(8,128)(2,1)S(1)} async-done(((bf16[64,16,512]{2,1,0:T(8,128)(2,1)}), bf16[64,16,512]{2,1,0:T(8,128)(2,1)S(1)}, u32[]{:S(2)}, u32[]{:S(2)}) %all-to-all-start.1) | async-done | bytes 1048608 | tf_op jit(solution)/shard_map/all_to_all | solution.py:361
  98.6 2.2 %collective-permute-start.17 = (bf16[128,512]{1,0:T(8,128)(2,1)S(1)}, bf16[128,512]{1,0:T(8,128)(2,1)S(1)}, u32[]{:S(2)}, u32[]{:S(2)}) collective-permute-start(bf16[128,512]{1,0:T(8,128)(2,1)S(1)} %shard_map.117.refs_0_), channel_id=1, source_target_pairs={{128,0},{192,64},{0,128},{64,192},{129,1},{193,65},{1,129},{65,193... | collective-permute-start | bytes 393224 | tf_op jit(solution)/shard_map/ppermute | solution.py:153
  100.8 1.1 %collective-permute-start.16 = (bf16[128,512]{1,0:T(8,128)(2,1)S(1)}, bf16[128,512]{1,0:T(8,128)(2,1)S(1)}, u32[]{:S(2)}, u32[]{:S(2)}) collective-permute-start(bf16[128,512]{1,0:T(8,128)(2,1)S(1)} %shard_map.117.refs_0_), channel_id=1, source_target_pairs={{64,0},{128,64},{192,128},{0,192},{65,1},{129,65},{193,129},{1,193... | collective-permute-start | bytes 393224 | tf_op jit(solution)/shard_map/ppermute | solution.py:153
  101.9 2.2 %copy-done.2 = bf16[1024,2048]{1,0:T(8,128)(2,1)S(1)} copy-done((bf16[1024,2048]{1,0:T(8,128)(2,1)S(1)}, bf16[1024,2048]{1,0:T(8,128)(2,1)}, u32[]{:S(2)}) %copy-start.2) | copy-done | bytes 4194328
  105.9 1.1 collective-permute-done.16.refs_1_
  107.0 1.5 %shard_map.120 = bf16[128,1024]{1,0:T(8,128)(2,1)} custom-call(s32[1]{0:T(128)} %bitcast.k_ref, f32[128,1024]{1,0:T(8,128)S(1)} %shard_map.119.refs_0_, bf16[128,512]{1,0:T(8,128)(2,1)S(1)} %collective-permute-done.16.refs_1_, bf16[128,512]{1,0:T(8,128)(2,1)S(1)} %collective-permute-done.17.refs_2_, bf16[1024,2048]{1,0:T(8,128)(2,1)S(1)} %copy-done.2), custom_call_target="tpu_custom_call" | custom-call | flops 1000000000 | bytes 100000 | tf_op jit(solution)/shard_map/pallas_call | solution.py:132
  (62 shorter events, 10.0 us)
Async XLA Ops:
  0.6 28.5 %copy-start = (s32[1,1024]{1,0:T(1,128)S(1)}, s32[1,1024]{1,0:T(1,128)}, u32[]{:S(2)}) copy-start(s32[1,1024]{1,0:T(1,128)} %param.13) | copy-start | bytes 12292
  0.6 9.4 %copy-start.3 = (bf16[128,1024]{1,0:T(8,128)(2,1)S(1)}, bf16[128,1024]{1,0:T(8,128)(2,1)}, u32[]{:S(2)}) copy-start(bf16[128,1024]{1,0:T(8,128)(2,1)} %x_ref.3) | copy-start | bytes 786436
  0.7 11.9 %copy-start.8 = (s32[1,64,16]{1,2,0:T(8,128)S(1)}, s32[1,64,16]{1,2,0:T(8,128)}, u32[]{:S(2)}) copy-start(s32[1,64,16]{1,2,0:T(8,128)} %param.12) | copy-start | bytes 12292
  3.7 9.4 %collective-permute-start = (bf16[128,512]{1,0:T(8,128)(2,1)}, bf16[128,512]{1,0:T(8,128)(2,1)S(1)}, u32[]{:S(2)}, u32[]{:S(2)}) collective-permute-start(bf16[128,512]{1,0:T(8,128)(2,1)} %get-tuple-element.35), channel_id=1, source_target_pairs={{0,128},{64,192},{128,0},{192,64},{1,129},{65,193},{129,1},{193,65... | collective-permute-start | bytes 393224 | tf_op jit(solution)/shard_map/ppermute | solution.py:148
  7.4 7.4 %collective-permute-start.1 = (bf16[128,512]{1,0:T(8,128)(2,1)}, bf16[128,512]{1,0:T(8,128)(2,1)S(1)}, u32[]{:S(2)}, u32[]{:S(2)}) collective-permute-start(bf16[128,512]{1,0:T(8,128)(2,1)} %get-tuple-element.36), channel_id=1, source_target_pairs={{0,64},{64,128},{128,192},{192,0},{1,65},{65,129},{129,193},{193,1... | collective-permute-start | bytes 393224 | tf_op jit(solution)/shard_map/ppermute | solution.py:148
  7.7 7.1 %collective-permute-start.2 = (bf16[128,512]{1,0:T(8,128)(2,1)}, bf16[128,512]{1,0:T(8,128)(2,1)S(1)}, u32[]{:S(2)}, u32[]{:S(2)}) collective-permute-start(bf16[128,512]{1,0:T(8,128)(2,1)} %get-tuple-element.37), channel_id=1, source_target_pairs={{0,192},{64,0},{128,64},{192,128},{1,193},{65,1},{129,65},{193,129... | collective-permute-start | bytes 393224 | tf_op jit(solution)/shard_map/ppermute | solution.py:148
  10.0 2.2 %copy-start.1 = (bf16[1024,2048]{1,0:T(8,128)(2,1)S(1)}, bf16[1024,2048]{1,0:T(8,128)(2,1)}, u32[]{:S(2)}) copy-start(bf16[1024,2048]{1,0:T(8,128)(2,1)} %refs_3_.3) | copy-start | bytes 12582916
  12.8 16.2 %copy-start.7 = (s32[64,7]{0,1:T(8,128)S(1)}, s32[64,7]{0,1:T(8,128)}, u32[]{:S(2)}) copy-start(s32[64,7]{0,1:T(8,128)} %param.14) | copy-start | bytes 5380
  13.1 18.3 %copy-start.9 = (f32[64]{0:T(128)S(1)}, f32[64]{0:T(128)}, u32[]{:S(2)}) copy-start(f32[64]{0:T(128)} %param.15) | copy-start | bytes 772
  13.1 18.6 %copy-start.6 = (bf16[64,512]{1,0:T(8,128)(2,1)S(1)}, bf16[64,512]{1,0:T(8,128)(2,1)}, u32[]{:S(2)}) copy-start(bf16[64,512]{1,0:T(8,128)(2,1)} %x_ref.5) | copy-start | bytes 196612
  16.1 37.3 %all-to-all-start = ((bf16[64,16,512]{2,1,0:T(8,128)(2,1)}), bf16[64,16,512]{2,1,0:T(8,128)(2,1)S(1)}, u32[]{:S(2)}, u32[]{:S(2)}) async-start(bf16[64,16,512]{2,1,0:T(8,128)(2,1)} %bitcast.1), calls=%async_computation | async-start | bytes 2097152 | tf_op jit(solution)/shard_map/all_to_all | solution.py:361
  31.6 1.6 %copy-start.4 = (bf16[512,2048]{1,0:T(8,128)(2,1)S(1)}, bf16[512,2048]{1,0:T(8,128)(2,1)}, u32[]{:S(2)}) copy-start(bf16[512,2048]{1,0:T(8,128)(2,1)} %refs_3_.2) | copy-start | bytes 6291460
  34.5 5.0 %collective-permute-start.3 = (bf16[64,512]{1,0:T(8,128)(2,1)S(1)}, bf16[64,512]{1,0:T(8,128)(2,1)S(1)}, u32[]{:S(2)}, u32[]{:S(2)}) collective-permute-start(bf16[64,512]{1,0:T(8,128)(2,1)S(1)} %get-tuple-element.41), channel_id=1, source_target_pairs={{0,128},{64,192},{128,0},{192,64},{1,129},{65,193},{129,1},{193,65... | collective-permute-start | bytes 196616 | tf_op jit(solution)/shard_map/ppermute | solution.py:148
  36.1 5.0 %collective-permute-start.4 = (bf16[64,512]{1,0:T(8,128)(2,1)S(1)}, bf16[64,512]{1,0:T(8,128)(2,1)S(1)}, u32[]{:S(2)}, u32[]{:S(2)}) collective-permute-start(bf16[64,512]{1,0:T(8,128)(2,1)S(1)} %get-tuple-element.42), channel_id=1, source_target_pairs={{0,64},{64,128},{128,192},{192,0},{1,65},{65,129},{129,193},{193,1... | collective-permute-start | bytes 196616 | tf_op jit(solution)/shard_map/ppermute | solution.py:148
  37.8 3.5 %collective-permute-start.5 = (bf16[64,512]{1,0:T(8,128)(2,1)S(1)}, bf16[64,512]{1,0:T(8,128)(2,1)S(1)}, u32[]{:S(2)}, u32[]{:S(2)}) collective-permute-start(bf16[64,512]{1,0:T(8,128)(2,1)S(1)} %get-tuple-element.43), channel_id=1, source_target_pairs={{0,192},{64,0},{128,64},{192,128},{1,193},{65,1},{129,65},{193,129... | collective-permute-start | bytes 196616 | tf_op jit(solution)/shard_map/ppermute | solution.py:148
  41.6 16.7 %collective-permute-start.8 = (f32[144,128]{1,0:T(8,128)S(1)}, f32[144,128]{1,0:T(8,128)S(1)}, u32[]{:S(2)}, u32[]{:S(2)}) collective-permute-start(f32[144,128]{1,0:T(8,128)S(1)} %shard_map.110.refs_0_), channel_id=1, source_target_pairs={{192,0},{0,64},{64,128},{128,192},{193,1},{1,65},{65,129},{129,193... | collective-permute-start | bytes 221192 | tf_op jit(solution)/shard_map/ppermute | solution.py:153
  42.4 15.9 %collective-permute-start.7 = (f32[144,128]{1,0:T(8,128)S(1)}, f32[144,128]{1,0:T(8,128)S(1)}, u32[]{:S(2)}, u32[]{:S(2)}) collective-permute-start(f32[144,128]{1,0:T(8,128)S(1)} %shard_map.110.refs_0_), channel_id=1, source_target_pairs={{128,0},{192,64},{0,128},{64,192},{129,1},{193,65},{1,129},{65,193... | collective-permute-start | bytes 221192 | tf_op jit(solution)/shard_map/ppermute | solution.py:153
  45.2 13.2 %collective-permute-start.6 = (f32[144,128]{1,0:T(8,128)S(1)}, f32[144,128]{1,0:T(8,128)S(1)}, u32[]{:S(2)}, u32[]{:S(2)}) collective-permute-start(f32[144,128]{1,0:T(8,128)S(1)} %shard_map.110.refs_0_), channel_id=1, source_target_pairs={{64,0},{128,64},{192,128},{0,192},{65,1},{129,65},{193,129},{1,193... | collective-permute-start | bytes 221192 | tf_op jit(solution)/shard_map/ppermute | solution.py:153
  54.5 3.9 %collective-permute-start.11 = (f32[8,128]{1,0:T(8,128)S(1)}, f32[8,128]{1,0:T(8,128)S(1)}, u32[]{:S(2)}, u32[]{:S(2)}) collective-permute-start(f32[8,128]{1,0:T(8,128)S(1)} %shard_map.111.refs_4_), channel_id=1, source_target_pairs={{192,0},{0,64},{64,128},{128,192},{193,1},{1,65},{65,129},{129,193... | collective-permute-start | bytes 12296 | tf_op jit(solution)/shard_map/ppermute | solution.py:153
  55.5 4.0 %collective-permute-start.10 = (f32[8,128]{1,0:T(8,128)S(1)}, f32[8,128]{1,0:T(8,128)S(1)}, u32[]{:S(2)}, u32[]{:S(2)}) collective-permute-start(f32[8,128]{1,0:T(8,128)S(1)} %shard_map.111.refs_4_), channel_id=1, source_target_pairs={{128,0},{192,64},{0,128},{64,192},{129,1},{193,65},{1,129},{65,193... | collective-permute-start | bytes 12296 | tf_op jit(solution)/shard_map/ppermute | solution.py:153
  58.4 2.8 %collective-permute-start.9 = (f32[8,128]{1,0:T(8,128)S(1)}, f32[8,128]{1,0:T(8,128)S(1)}, u32[]{:S(2)}, u32[]{:S(2)}) collective-permute-start(f32[8,128]{1,0:T(8,128)S(1)} %shard_map.111.refs_4_), channel_id=1, source_target_pairs={{64,0},{128,64},{192,128},{0,192},{65,1},{129,65},{193,129},{1,193... | collective-permute-start | bytes 12296 | tf_op jit(solution)/shard_map/ppermute | solution.py:153
  62.8 35.5 %all-to-all-start.1 = ((bf16[64,16,512]{2,1,0:T(8,128)(2,1)}), bf16[64,16,512]{2,1,0:T(8,128)(2,1)S(1)}, u32[]{:S(2)}, u32[]{:S(2)}) async-start(bf16[64,16,512]{2,1,0:T(8,128)(2,1)} %bitcast.6), calls=%async_computation.1 | async-start | bytes 2097152 | tf_op jit(solution)/shard_map/all_to_all | solution.py:361
  74.3 7.0 %collective-permute-start.14 = (bf16[64,512]{1,0:T(8,128)(2,1)S(1)}, bf16[64,512]{1,0:T(8,128)(2,1)S(1)}, u32[]{:S(2)}, u32[]{:S(2)}) collective-permute-start(bf16[64,512]{1,0:T(8,128)(2,1)S(1)} %get-tuple-element.56.refs_0_), channel_id=1, source_target_pairs={{128,0},{192,64},{0,128},{64,192},{129,1},{193,65},{1,129},{65,193... | collective-permute-start | bytes 196616 | tf_op jit(solution)/shard_map/ppermute | solution.py:153
  75.7 5.7 %collective-permute-start.13 = (bf16[64,512]{1,0:T(8,128)(2,1)S(1)}, bf16[64,512]{1,0:T(8,128)(2,1)S(1)}, u32[]{:S(2)}, u32[]{:S(2)}) collective-permute-start(bf16[64,512]{1,0:T(8,128)(2,1)S(1)} %get-tuple-element.56.refs_0_), channel_id=1, source_target_pairs={{64,0},{128,64},{192,128},{0,192},{65,1},{129,65},{193,129},{1,193... | collective-permute-start | bytes 196616 | tf_op jit(solution)/shard_map/ppermute | solution.py:153
  76.3 4.7 %collective-permute-start.12 = (bf16[64,512]{1,0:T(8,128)(2,1)S(1)}, bf16[64,512]{1,0:T(8,128)(2,1)S(1)}, u32[]{:S(2)}, u32[]{:S(2)}) collective-permute-start(bf16[64,512]{1,0:T(8,128)(2,1)S(1)} %get-tuple-element.56.refs_0_), channel_id=1, source_target_pairs={{192,0},{0,64},{64,128},{128,192},{193,1},{1,65},{65,129},{129,193... | collective-permute-start | bytes 196616 | tf_op jit(solution)/shard_map/ppermute | solution.py:153
  77.6 1.6 %copy-start.5 = (bf16[512,2048]{1,0:T(8,128)(2,1)S(1)}, bf16[512,2048]{1,0:T(8,128)(2,1)}, u32[]{:S(2)}) copy-start(bf16[512,2048]{1,0:T(8,128)(2,1)} %refs_3_.2) | copy-start | bytes 6291460
  98.6 6.4 %collective-permute-start.15 = (bf16[128,512]{1,0:T(8,128)(2,1)S(1)}, bf16[128,512]{1,0:T(8,128)(2,1)S(1)}, u32[]{:S(2)}, u32[]{:S(2)}) collective-permute-start(bf16[128,512]{1,0:T(8,128)(2,1)S(1)} %shard_map.117.refs_0_), channel_id=1, source_target_pairs={{192,0},{0,64},{64,128},{128,192},{193,1},{1,65},{65,129},{129,193... | collective-permute-start | bytes 393224 | tf_op jit(solution)/shard_map/ppermute | solution.py:153
  98.6 7.3 %collective-permute-start.17 = (bf16[128,512]{1,0:T(8,128)(2,1)S(1)}, bf16[128,512]{1,0:T(8,128)(2,1)S(1)}, u32[]{:S(2)}, u32[]{:S(2)}) collective-permute-start(bf16[128,512]{1,0:T(8,128)(2,1)S(1)} %shard_map.117.refs_0_), channel_id=1, source_target_pairs={{128,0},{192,64},{0,128},{64,192},{129,1},{193,65},{1,129},{65,193... | collective-permute-start | bytes 393224 | tf_op jit(solution)/shard_map/ppermute | solution.py:153
  100.8 6.2 %collective-permute-start.16 = (bf16[128,512]{1,0:T(8,128)(2,1)S(1)}, bf16[128,512]{1,0:T(8,128)(2,1)S(1)}, u32[]{:S(2)}, u32[]{:S(2)}) collective-permute-start(bf16[128,512]{1,0:T(8,128)(2,1)S(1)} %shard_map.117.refs_0_), channel_id=1, source_target_pairs={{64,0},{128,64},{192,128},{0,192},{65,1},{129,65},{193,129},{1,193... | collective-permute-start | bytes 393224 | tf_op jit(solution)/shard_map/ppermute | solution.py:153
  101.9 2.2 %copy-start.2 = (bf16[1024,2048]{1,0:T(8,128)(2,1)S(1)}, bf16[1024,2048]{1,0:T(8,128)(2,1)}, u32[]{:S(2)}) copy-start(bf16[1024,2048]{1,0:T(8,128)(2,1)} %refs_3_.3) | copy-start | bytes 12582916

commit v8 on v7

--- a/solution.py
+++ b/solution.py
@@ -117,31 +117,53 @@
     def columns(w_ref, k_ref, s):
         return w_ref[:, pl.ds(pl.multiple_of(lax.rem(k_ref[0] + s, N_PHASE) * cols, cols), cols)]
 
-    def product(*shifts):
+    vmem = pl.BlockSpec(memory_space=pltpu.VMEM)
+    smem = pl.BlockSpec(memory_space=pltpu.SMEM)
+
+    def product(s, acc, block):
         def body(k_ref, *refs):
-            block_refs, w_ref, out_ref = refs[-len(shifts) - 2 : -2], refs[-2], refs[-1]
-            total = sum(dot(r[...], columns(w_ref, k_ref, s), NT) for s, r in zip(shifts, block_refs))
-            if len(refs) > len(shifts) + 2:
-                total = refs[0][...] + total
-            out_ref[...] = total.astype(out_ref.dtype)
-
-        return body
-
-    def run(body, dtype, *args):
-        vmem = pl.BlockSpec(memory_space=pltpu.VMEM)
+            acc_refs, block_ref, w_ref, out_ref = refs[:-3], refs[-3], refs[-2], refs[-1]
+            part = dot(block_ref[...], columns(w_ref, k_ref, s), NT)
+            out_ref[...] = part + acc_refs[0][...] if acc_refs else part
+
+        args = acc + [block, w]
         return pl.pallas_call(
             body,
-            in_specs=[pl.BlockSpec(memory_space=pltpu.SMEM)] + [vmem] * len(args),
+            in_specs=[smem] + [vmem] * len(args),
             out_specs=vmem,
-            out_shape=jax.ShapeDtypeStruct((rows, depth), dtype),
+            out_shape=jax.ShapeDtypeStruct((rows, depth), f32),
             compiler_params=params(),
             cost_estimate=cost,
         )(k, *args)
 
+    def last(k_ref, acc_ref, block_ref, w_ref, out_ref, buf_ref, sem_ref):
+        half = depth // 2
+        start = pl.multiple_of(lax.rem(k_ref[0] + 2, N_PHASE) * cols, cols)
+
+        def store(i):
+            return pltpu.make_async_copy(buf_ref.at[i], out_ref.at[:, pl.ds(i * half, half)], sem_ref.at[i])
+
+        for i in range(2):
+            part = slice(i * half, (i + 1) * half)
+            total = acc_ref[:, part] + dot(block_ref[...], w_ref[part, pl.ds(start, cols)], NT)
+            buf_ref[i] = total.astype(bf16)
+            store(i).start()
+        for i in range(2):
+            store(i).wait()
+
     blocks = gather_blocks(u)
-    acc = run(product(0), f32, blocks[0], w)
-    acc = run(product(3), f32, acc, blocks[3], w)
-    return run(product(1, 2), bf16, acc, blocks[1], blocks[2], w)
+    acc = product(0, [], blocks[0])
+    acc = product(1, [acc], blocks[1])
+    acc = product(3, [acc], blocks[3])
+    return pl.pallas_call(
+        last,
+        in_specs=[smem] + [vmem] * 3,
+        out_specs=pl.BlockSpec(memory_space=pltpu.HBM),
+        out_shape=jax.ShapeDtypeStruct((rows, depth), bf16),
+        scratch_shapes=[pltpu.VMEM((2, rows, depth // 2), bf16), pltpu.SemaphoreType.DMA((2,))],
+        compiler_params=params(),
+        cost_estimate=cost,
+    )(k, acc, blocks[2], w)
 
 
 def send(block, s):

time: 111 us -> 112 us (level); the launches traced: 109 us -> 111 us
  waiting for transfers between devices: 34.1 us -> 35.9 us
    ppermute x12, waiting for transfers between devices: 6.15 us -> 7.82 us  [gather_blocks(): lax.ppermute(x, 'phase', [((i + s) % N_PHASE, i) for i in range(N_PHASE)])]
    pallas_call x6 -> x8, Pallas kernels: 4.13 us -> 4.41 us  [the longest x6 2.32 us: product(): pl.pallas_call(body, in_specs=[smem] + [vmem] * len(args), out_specs=vmem...]
  transfers between devices with their start and end apart: 20 -> 20, of which waited for: 12 -> 9; matrix products, arithmetic and copies ran while one was open for 3% -> 3% of each run, Pallas kernels for 6% -> 6%
where the time goes in v8:
time: 112 us; the launch traced here: 111 us
  starting transfers between devices  48.4 us (43%)
  waiting for transfers between devices  35.9 us (32%)
  Pallas kernels  14.5 us (13%)
  local copies, waits for them, and re-layouts  10.7 us (10%)
    all_to_all x2, starting transfers between devices, exchange(): lax.all_to_all(blocks, 'dp', split_axis=0, concat_axis=0, tiled=True, axi...  24.1 us
    all_to_all x2, waiting for transfers between devices, exchange(): lax.all_to_all(blocks, 'dp', split_axis=0, concat_axis=0, tiled=True, axi...  24.1 us
    ppermute x12, starting transfers between devices, gather_blocks(): lax.ppermute(x, 'phase', [((i + s) % N_PHASE, i) for i in range(N_PHASE)])  13.7 us
    ppermute x6, starting transfers between devices, send(): lax.ppermute(block, 'phase', [(i, (i + s) % N_PHASE) for i in range(N_PHA...  10.6 us
    ppermute x12, waiting for transfers between devices, gather_blocks(): lax.ppermute(x, 'phase', [((i + s) % N_PHASE, i) for i in range(N_PHASE)])  7.82 us
    unnamed x20, local copies, waits for them, and re-layouts  7.59 us
    pallas_call x2, Pallas kernels, project_sends(): pl.pallas_call(body, in_specs=[pl.BlockSpec(memory_space=pltpu.SMEM), hbm...  4.23 us
    ppermute x6, waiting for transfers between devices, send(): lax.ppermute(block, 'phase', [(i, (i + s) % N_PHASE) for i in range(N_PHA...  4 us
  transfers between devices with their start and end apart: 20, of which 9 were waited for; matrix products, arithmetic and copies ran while one was open for 3% of the time, Pallas kernels for 6%

profile of v8, /device:TPU:1, one launch (start us, length us, event | category | flops | bytes accessed | tf_op | source)
XLA Modules:
  0.0 110.8 jit_solution(2177658000270572161)
XLA Ops:
  0.7 3.0 %shard_map.104 = (bf16[128,512]{1,0:T(8,128)(2,1)}, bf16[128,512]{1,0:T(8,128)(2,1)}, bf16[128,512]{1,0:T(8,128)(2,1)}) custom-call(s32[1]{0:T(128)} %bitcast.k_ref, bf16[128,1024]{1,0:T(8,128)(2,1)} %x_ref.3, bf16[1024,2048]{1,0:T(8,128)(2,1)} %w_ref.11), custom_call_target="tpu_custom_call" | custom-call | flops 1000000000 | bytes 100000 | tf_op jit(solution)/shard_map/pallas_call | solution.py:73
  3.7 3.7 %collective-permute-start = (bf16[128,512]{1,0:T(8,128)(2,1)}, bf16[128,512]{1,0:T(8,128)(2,1)S(1)}, u32[]{:S(2)}, u32[]{:S(2)}) collective-permute-start(bf16[128,512]{1,0:T(8,128)(2,1)} %get-tuple-element.35), channel_id=1, source_target_pairs={{0,128},{64,192},{128,0},{192,64},{1,129},{65,193},{129,1},{193,65... | collective-permute-start | bytes 393224 | tf_op jit(solution)/shard_map/ppermute | solution.py:170
  7.7 2.4 %collective-permute-start.2 = (bf16[128,512]{1,0:T(8,128)(2,1)}, bf16[128,512]{1,0:T(8,128)(2,1)S(1)}, u32[]{:S(2)}, u32[]{:S(2)}) collective-permute-start(bf16[128,512]{1,0:T(8,128)(2,1)} %get-tuple-element.37), channel_id=1, source_target_pairs={{0,192},{64,0},{128,64},{192,128},{1,193},{65,1},{129,65},{193,129... | collective-permute-start | bytes 393224 | tf_op jit(solution)/shard_map/ppermute | solution.py:170
  10.0 2.2 %copy-done.1 = bf16[1024,2048]{1,0:T(8,128)(2,1)S(1)} copy-done((bf16[1024,2048]{1,0:T(8,128)(2,1)S(1)}, bf16[1024,2048]{1,0:T(8,128)(2,1)}, u32[]{:S(2)}) %copy-start.1) | copy-done | bytes 4194328
  13.1 1.7 %collective-permute-done.1.c = bf16[128,512]{1,0:T(8,128)(2,1)S(1)} collective-permute-done((bf16[128,512]{1,0:T(8,128)(2,1)}, bf16[128,512]{1,0:T(8,128)(2,1)S(1)}, u32[]{:S(2)}, u32[]{:S(2)}) %collective-permute-start.1) | collective-permute-done | bytes 131104 | tf_op jit(solution)/shard_map/ppermute | solution.py:170
  14.8 1.3 %shard_map.106 = (f32[128,512]{1,0:T(8,128)S(1)}, bf16[1024,512]{1,0:T(8,128)(2,1)}) custom-call(f32[128,512]{1,0:T(8,128)S(1)} %shard_map.103.a, bf16[128,512]{1,0:T(8,128)(2,1)S(1)} %collective-permute-done.b, bf16[128,512]{1,0:T(8,128)(2,1)S(1)} %collective-permute-done.1.c, bf16[128,512]{1,0:T(8,128)(2,1)S(1)} %collective-permute-done.2.d, ...), custom_call_target="tpu_custom_call" | custom-call | flops 1000000000 | bytes 100000 | tf_op jit(solution)/shard_map/pallas_call | solution.py:222
  16.1 13.0 %all-to-all-start = ((bf16[64,16,512]{2,1,0:T(8,128)(2,1)}), bf16[64,16,512]{2,1,0:T(8,128)(2,1)S(1)}, u32[]{:S(2)}, u32[]{:S(2)}) async-start(bf16[64,16,512]{2,1,0:T(8,128)(2,1)} %bitcast.1), calls=%async_computation | async-start | bytes 2097152 | tf_op jit(solution)/shard_map/all_to_all | solution.py:383
  29.1 2.1 %gather_fusion = s32[448]{0:T(512)S(1)} fusion(s32[1024]{0:T(1024)S(1)} %bitcast.35, s32[1024]{0:T(1024)S(1)} %pad_clamp_fusion), kind=kCustom, calls=%fused_computation | custom fusion | bytes 5376 | tf_op jit(solution)/shard_map/jit(_take)/gather | solution.py:405
  31.6 1.6 %copy-done.4 = bf16[512,2048]{1,0:T(8,128)(2,1)S(1)} copy-done((bf16[512,2048]{1,0:T(8,128)(2,1)S(1)}, bf16[512,2048]{1,0:T(8,128)(2,1)}, u32[]{:S(2)}) %copy-start.4) | copy-done | bytes 2097176
  33.2 1.2 %shard_map.108 = (bf16[64,512]{1,0:T(8,128)(2,1)S(1)}, bf16[64,512]{1,0:T(8,128)(2,1)S(1)}, bf16[64,512]{1,0:T(8,128)(2,1)S(1)}) custom-call(s32[1]{0:T(128)} %bitcast.k_ref, bf16[64,512]{1,0:T(8,128)(2,1)S(1)} %copy-done.6, bf16[512,2048]{1,0:T(8,128)(2,1)S(1)} %copy-done.4), custom_call_target="tpu_custom_call" | custom-call | flops 1000000000 | bytes 100000 | tf_op jit(solution)/shard_map/pallas_call | solution.py:73
  34.5 1.6 %collective-permute-start.3 = (bf16[64,512]{1,0:T(8,128)(2,1)S(1)}, bf16[64,512]{1,0:T(8,128)(2,1)S(1)}, u32[]{:S(2)}, u32[]{:S(2)}) collective-permute-start(bf16[64,512]{1,0:T(8,128)(2,1)S(1)} %get-tuple-element.41), channel_id=1, source_target_pairs={{0,128},{64,192},{128,0},{192,64},{1,129},{65,193},{129,1},{193,65... | collective-permute-start | bytes 196616 | tf_op jit(solution)/shard_map/ppermute | solution.py:170
  36.1 1.7 %collective-permute-start.4 = (bf16[64,512]{1,0:T(8,128)(2,1)S(1)}, bf16[64,512]{1,0:T(8,128)(2,1)S(1)}, u32[]{:S(2)}, u32[]{:S(2)}) collective-permute-start(bf16[64,512]{1,0:T(8,128)(2,1)S(1)} %get-tuple-element.42), channel_id=1, source_target_pairs={{0,64},{64,128},{128,192},{192,0},{1,65},{65,129},{129,193},{193,1... | collective-permute-start | bytes 196616 | tf_op jit(solution)/shard_map/ppermute | solution.py:170
  37.8 1.0 collective-permute-start.5
  39.5 1.6 %collective-permute-done.4.b = bf16[64,512]{1,0:T(8,128)(2,1)S(1)} collective-permute-done((bf16[64,512]{1,0:T(8,128)(2,1)S(1)}, bf16[64,512]{1,0:T(8,128)(2,1)S(1)}, u32[]{:S(2)}, u32[]{:S(2)}) %collective-permute-start.4) | collective-permute-done | bytes 65568 | tf_op jit(solution)/shard_map/ppermute | solution.py:170
  42.4 2.8 %collective-permute-start.7 = (f32[144,128]{1,0:T(8,128)S(1)}, f32[144,128]{1,0:T(8,128)S(1)}, u32[]{:S(2)}, u32[]{:S(2)}) collective-permute-start(f32[144,128]{1,0:T(8,128)S(1)} %shard_map.110.refs_0_), channel_id=1, source_target_pairs={{128,0},{192,64},{0,128},{64,192},{129,1},{193,65},{1,129},{65,193... | collective-permute-start | bytes 221192 | tf_op jit(solution)/shard_map/ppermute | solution.py:175
  45.3 8.1 %all-to-all-done = bf16[64,16,512]{2,1,0:T(8,128)(2,1)S(1)} async-done(((bf16[64,16,512]{2,1,0:T(8,128)(2,1)}), bf16[64,16,512]{2,1,0:T(8,128)(2,1)S(1)}, u32[]{:S(2)}, u32[]{:S(2)}) %all-to-all-start) | async-done | bytes 1048608 | tf_op jit(solution)/shard_map/all_to_all | solution.py:383
  53.4 1.1 shard_map.111.refs_4_
  54.5 1.0 collective-permute-start.11
  55.5 2.9 %collective-permute-start.10 = (f32[8,128]{1,0:T(8,128)S(1)}, f32[8,128]{1,0:T(8,128)S(1)}, u32[]{:S(2)}, u32[]{:S(2)}) collective-permute-start(f32[8,128]{1,0:T(8,128)S(1)} %shard_map.111.refs_4_), channel_id=1, source_target_pairs={{128,0},{192,64},{0,128},{64,192},{129,1},{193,65},{1,129},{65,193... | collective-permute-start | bytes 12296 | tf_op jit(solution)/shard_map/ppermute | solution.py:175
  58.4 1.1 collective-permute-done.10.refs_6_
  59.4 1.7 %collective-permute-done.9.refs_5_ = f32[8,128]{1,0:T(8,128)S(1)} collective-permute-done((f32[8,128]{1,0:T(8,128)S(1)}, f32[8,128]{1,0:T(8,128)S(1)}, u32[]{:S(2)}, u32[]{:S(2)}) %collective-permute-start.9) | collective-permute-done | bytes 4128 | tf_op jit(solution)/shard_map/ppermute | solution.py:175
  61.1 1.7 %shard_map.112 = (bf16[1024,512]{1,0:T(8,128)(2,1)}, bf16[1024,128]{1,0:T(8,128)(2,1)S(1)}, bf16[128,128]{1,0:T(8,128)(2,1)S(1)}, f32[8,128]{1,0:T(8,128)S(1)}, f32[128,128]{1,0:T(8,128)S(1)}) custom-call(f32[144,128]{1,0:T(8,128)S(1)} %shard_map.110.refs_0_, f32[144,128]{1,0:T(8,128)S(1)} %collective-permute-done.6.refs_1_, ...), custom_call_target="tpu_custom_call" | custom-call | flops 1000000000 | bytes 100000 | tf_op jit(solution)/shard_map/pallas_call | solution.py:416
  62.8 11.1 %all-to-all-start.1 = ((bf16[64,16,512]{2,1,0:T(8,128)(2,1)}), bf16[64,16,512]{2,1,0:T(8,128)(2,1)S(1)}, u32[]{:S(2)}, u32[]{:S(2)}) async-start(bf16[64,16,512]{2,1,0:T(8,128)(2,1)} %bitcast.6), calls=%async_computation.1 | async-start | bytes 2097152 | tf_op jit(solution)/shard_map/all_to_all | solution.py:383
  74.3 1.3 %collective-permute-start.14 = (bf16[64,512]{1,0:T(8,128)(2,1)S(1)}, bf16[64,512]{1,0:T(8,128)(2,1)S(1)}, u32[]{:S(2)}, u32[]{:S(2)}) collective-permute-start(bf16[64,512]{1,0:T(8,128)(2,1)S(1)} %get-tuple-element.56.refs_0_), channel_id=1, source_target_pairs={{128,0},{192,64},{0,128},{64,192},{129,1},{193,65},{1,129},{65,193... | collective-permute-start | bytes 196616 | tf_op jit(solution)/shard_map/ppermute | solution.py:175
  76.0 2.3 %collective-permute-start.12 = (bf16[64,512]{1,0:T(8,128)(2,1)S(1)}, bf16[64,512]{1,0:T(8,128)(2,1)S(1)}, u32[]{:S(2)}, u32[]{:S(2)}) collective-permute-start(bf16[64,512]{1,0:T(8,128)(2,1)S(1)} %get-tuple-element.56.refs_0_), channel_id=1, source_target_pairs={{64,0},{128,64},{192,128},{0,192},{65,1},{129,65},{193,129},{1,193... | collective-permute-start | bytes 196616 | tf_op jit(solution)/shard_map/ppermute | solution.py:175
  78.8 1.6 %copy-done.5 = bf16[512,2048]{1,0:T(8,128)(2,1)S(1)} copy-done((bf16[512,2048]{1,0:T(8,128)(2,1)S(1)}, bf16[512,2048]{1,0:T(8,128)(2,1)}, u32[]{:S(2)}) %copy-start.5) | copy-done | bytes 2097176
  81.3 0.9 shard_map.117
  82.3 16.0 %all-to-all-done.1 = bf16[64,16,512]{2,1,0:T(8,128)(2,1)S(1)} async-done(((bf16[64,16,512]{2,1,0:T(8,128)(2,1)}), bf16[64,16,512]{2,1,0:T(8,128)(2,1)S(1)}, u32[]{:S(2)}, u32[]{:S(2)}) %all-to-all-start.1) | async-done | bytes 1048608 | tf_op jit(solution)/shard_map/all_to_all | solution.py:383
  98.6 1.1 collective-permute-start.15
  100.7 2.2 %copy-done.2 = bf16[1024,2048]{1,0:T(8,128)(2,1)S(1)} copy-done((bf16[1024,2048]{1,0:T(8,128)(2,1)S(1)}, bf16[1024,2048]{1,0:T(8,128)(2,1)}, u32[]{:S(2)}) %copy-start.2) | copy-done | bytes 4194328
  103.9 5.1 %collective-permute-done.16.refs_1_ = bf16[128,512]{1,0:T(8,128)(2,1)S(1)} collective-permute-done((bf16[128,512]{1,0:T(8,128)(2,1)S(1)}, bf16[128,512]{1,0:T(8,128)(2,1)S(1)}, u32[]{:S(2)}, u32[]{:S(2)}) %collective-permute-start.16) | collective-permute-done | bytes 131104 | tf_op jit(solution)/shard_map/ppermute | solution.py:175
  109.5 1.2 %shard_map.122 = bf16[128,1024]{1,0:T(8,128)(2,1)} custom-call(s32[1]{0:T(128)} %bitcast.k_ref, f32[128,1024]{1,0:T(8,128)S(1)} %shard_map.121.acc_ref, bf16[128,512]{1,0:T(8,128)(2,1)S(1)} %collective-permute-done.17.block_ref, bf16[1024,2048]{1,0:T(8,128)(2,1)S(1)} %copy-done.2), custom_call_target="tpu_custom_call" | custom-call | flops 1000000000 | bytes 100000 | tf_op jit(solution)/shard_map/pallas_call | solution.py:158
  (64 shorter events, 8.8 us)
Async XLA Ops:
  0.6 28.5 %copy-start = (s32[1,1024]{1,0:T(1,128)S(1)}, s32[1,1024]{1,0:T(1,128)}, u32[]{:S(2)}) copy-start(s32[1,1024]{1,0:T(1,128)} %param.13) | copy-start | bytes 12292
  0.6 9.4 %copy-start.3 = (bf16[128,1024]{1,0:T(8,128)(2,1)S(1)}, bf16[128,1024]{1,0:T(8,128)(2,1)}, u32[]{:S(2)}) copy-start(bf16[128,1024]{1,0:T(8,128)(2,1)} %x_ref.3) | copy-start | bytes 786436
  0.7 11.9 %copy-start.8 = (s32[1,64,16]{1,2,0:T(8,128)S(1)}, s32[1,64,16]{1,2,0:T(8,128)}, u32[]{:S(2)}) copy-start(s32[1,64,16]{1,2,0:T(8,128)} %param.12) | copy-start | bytes 12292
  3.7 9.4 %collective-permute-start = (bf16[128,512]{1,0:T(8,128)(2,1)}, bf16[128,512]{1,0:T(8,128)(2,1)S(1)}, u32[]{:S(2)}, u32[]{:S(2)}) collective-permute-start(bf16[128,512]{1,0:T(8,128)(2,1)} %get-tuple-element.35), channel_id=1, source_target_pairs={{0,128},{64,192},{128,0},{192,64},{1,129},{65,193},{129,1},{193,65... | collective-permute-start | bytes 393224 | tf_op jit(solution)/shard_map/ppermute | solution.py:170
  7.4 7.4 %collective-permute-start.1 = (bf16[128,512]{1,0:T(8,128)(2,1)}, bf16[128,512]{1,0:T(8,128)(2,1)S(1)}, u32[]{:S(2)}, u32[]{:S(2)}) collective-permute-start(bf16[128,512]{1,0:T(8,128)(2,1)} %get-tuple-element.36), channel_id=1, source_target_pairs={{0,64},{64,128},{128,192},{192,0},{1,65},{65,129},{129,193},{193,1... | collective-permute-start | bytes 393224 | tf_op jit(solution)/shard_map/ppermute | solution.py:170
  7.7 7.1 %collective-permute-start.2 = (bf16[128,512]{1,0:T(8,128)(2,1)}, bf16[128,512]{1,0:T(8,128)(2,1)S(1)}, u32[]{:S(2)}, u32[]{:S(2)}) collective-permute-start(bf16[128,512]{1,0:T(8,128)(2,1)} %get-tuple-element.37), channel_id=1, source_target_pairs={{0,192},{64,0},{128,64},{192,128},{1,193},{65,1},{129,65},{193,129... | collective-permute-start | bytes 393224 | tf_op jit(solution)/shard_map/ppermute | solution.py:170
  10.0 2.2 %copy-start.1 = (bf16[1024,2048]{1,0:T(8,128)(2,1)S(1)}, bf16[1024,2048]{1,0:T(8,128)(2,1)}, u32[]{:S(2)}) copy-start(bf16[1024,2048]{1,0:T(8,128)(2,1)} %w_ref.11) | copy-start | bytes 12582916
  12.8 16.2 %copy-start.7 = (s32[64,7]{0,1:T(8,128)S(1)}, s32[64,7]{0,1:T(8,128)}, u32[]{:S(2)}) copy-start(s32[64,7]{0,1:T(8,128)} %param.14) | copy-start | bytes 5380
  13.1 18.3 %copy-start.9 = (f32[64]{0:T(128)S(1)}, f32[64]{0:T(128)}, u32[]{:S(2)}) copy-start(f32[64]{0:T(128)} %param.15) | copy-start | bytes 772
  13.1 18.6 %copy-start.6 = (bf16[64,512]{1,0:T(8,128)(2,1)S(1)}, bf16[64,512]{1,0:T(8,128)(2,1)}, u32[]{:S(2)}) copy-start(bf16[64,512]{1,0:T(8,128)(2,1)} %x_ref.5) | copy-start | bytes 196612
  16.1 37.3 %all-to-all-start = ((bf16[64,16,512]{2,1,0:T(8,128)(2,1)}), bf16[64,16,512]{2,1,0:T(8,128)(2,1)S(1)}, u32[]{:S(2)}, u32[]{:S(2)}) async-start(bf16[64,16,512]{2,1,0:T(8,128)(2,1)} %bitcast.1), calls=%async_computation | async-start | bytes 2097152 | tf_op jit(solution)/shard_map/all_to_all | solution.py:383
  31.6 1.6 %copy-start.4 = (bf16[512,2048]{1,0:T(8,128)(2,1)S(1)}, bf16[512,2048]{1,0:T(8,128)(2,1)}, u32[]{:S(2)}) copy-start(bf16[512,2048]{1,0:T(8,128)(2,1)} %w_ref.10) | copy-start | bytes 6291460
  34.5 5.0 %collective-permute-start.3 = (bf16[64,512]{1,0:T(8,128)(2,1)S(1)}, bf16[64,512]{1,0:T(8,128)(2,1)S(1)}, u32[]{:S(2)}, u32[]{:S(2)}) collective-permute-start(bf16[64,512]{1,0:T(8,128)(2,1)S(1)} %get-tuple-element.41), channel_id=1, source_target_pairs={{0,128},{64,192},{128,0},{192,64},{1,129},{65,193},{129,1},{193,65... | collective-permute-start | bytes 196616 | tf_op jit(solution)/shard_map/ppermute | solution.py:170
  36.1 5.0 %collective-permute-start.4 = (bf16[64,512]{1,0:T(8,128)(2,1)S(1)}, bf16[64,512]{1,0:T(8,128)(2,1)S(1)}, u32[]{:S(2)}, u32[]{:S(2)}) collective-permute-start(bf16[64,512]{1,0:T(8,128)(2,1)S(1)} %get-tuple-element.42), channel_id=1, source_target_pairs={{0,64},{64,128},{128,192},{192,0},{1,65},{65,129},{129,193},{193,1... | collective-permute-start | bytes 196616 | tf_op jit(solution)/shard_map/ppermute | solution.py:170
  37.8 3.5 %collective-permute-start.5 = (bf16[64,512]{1,0:T(8,128)(2,1)S(1)}, bf16[64,512]{1,0:T(8,128)(2,1)S(1)}, u32[]{:S(2)}, u32[]{:S(2)}) collective-permute-start(bf16[64,512]{1,0:T(8,128)(2,1)S(1)} %get-tuple-element.43), channel_id=1, source_target_pairs={{0,192},{64,0},{128,64},{192,128},{1,193},{65,1},{129,65},{193,129... | collective-permute-start | bytes 196616 | tf_op jit(solution)/shard_map/ppermute | solution.py:170
  41.6 16.7 %collective-permute-start.8 = (f32[144,128]{1,0:T(8,128)S(1)}, f32[144,128]{1,0:T(8,128)S(1)}, u32[]{:S(2)}, u32[]{:S(2)}) collective-permute-start(f32[144,128]{1,0:T(8,128)S(1)} %shard_map.110.refs_0_), channel_id=1, source_target_pairs={{192,0},{0,64},{64,128},{128,192},{193,1},{1,65},{65,129},{129,193... | collective-permute-start | bytes 221192 | tf_op jit(solution)/shard_map/ppermute | solution.py:175
  42.4 15.9 %collective-permute-start.7 = (f32[144,128]{1,0:T(8,128)S(1)}, f32[144,128]{1,0:T(8,128)S(1)}, u32[]{:S(2)}, u32[]{:S(2)}) collective-permute-start(f32[144,128]{1,0:T(8,128)S(1)} %shard_map.110.refs_0_), channel_id=1, source_target_pairs={{128,0},{192,64},{0,128},{64,192},{129,1},{193,65},{1,129},{65,193... | collective-permute-start | bytes 221192 | tf_op jit(solution)/shard_map/ppermute | solution.py:175
  45.2 13.2 %collective-permute-start.6 = (f32[144,128]{1,0:T(8,128)S(1)}, f32[144,128]{1,0:T(8,128)S(1)}, u32[]{:S(2)}, u32[]{:S(2)}) collective-permute-start(f32[144,128]{1,0:T(8,128)S(1)} %shard_map.110.refs_0_), channel_id=1, source_target_pairs={{64,0},{128,64},{192,128},{0,192},{65,1},{129,65},{193,129},{1,193... | collective-permute-start | bytes 221192 | tf_op jit(solution)/shard_map/ppermute | solution.py:175
  54.5 3.9 %collective-permute-start.11 = (f32[8,128]{1,0:T(8,128)S(1)}, f32[8,128]{1,0:T(8,128)S(1)}, u32[]{:S(2)}, u32[]{:S(2)}) collective-permute-start(f32[8,128]{1,0:T(8,128)S(1)} %shard_map.111.refs_4_), channel_id=1, source_target_pairs={{192,0},{0,64},{64,128},{128,192},{193,1},{1,65},{65,129},{129,193... | collective-permute-start | bytes 12296 | tf_op jit(solution)/shard_map/ppermute | solution.py:175
  55.5 4.0 %collective-permute-start.10 = (f32[8,128]{1,0:T(8,128)S(1)}, f32[8,128]{1,0:T(8,128)S(1)}, u32[]{:S(2)}, u32[]{:S(2)}) collective-permute-start(f32[8,128]{1,0:T(8,128)S(1)} %shard_map.111.refs_4_), channel_id=1, source_target_pairs={{128,0},{192,64},{0,128},{64,192},{129,1},{193,65},{1,129},{65,193... | collective-permute-start | bytes 12296 | tf_op jit(solution)/shard_map/ppermute | solution.py:175
  58.4 2.8 %collective-permute-start.9 = (f32[8,128]{1,0:T(8,128)S(1)}, f32[8,128]{1,0:T(8,128)S(1)}, u32[]{:S(2)}, u32[]{:S(2)}) collective-permute-start(f32[8,128]{1,0:T(8,128)S(1)} %shard_map.111.refs_4_), channel_id=1, source_target_pairs={{64,0},{128,64},{192,128},{0,192},{65,1},{129,65},{193,129},{1,193... | collective-permute-start | bytes 12296 | tf_op jit(solution)/shard_map/ppermute | solution.py:175
  62.8 35.5 %all-to-all-start.1 = ((bf16[64,16,512]{2,1,0:T(8,128)(2,1)}), bf16[64,16,512]{2,1,0:T(8,128)(2,1)S(1)}, u32[]{:S(2)}, u32[]{:S(2)}) async-start(bf16[64,16,512]{2,1,0:T(8,128)(2,1)} %bitcast.6), calls=%async_computation.1 | async-start | bytes 2097152 | tf_op jit(solution)/shard_map/all_to_all | solution.py:383
  74.3 7.0 %collective-permute-start.14 = (bf16[64,512]{1,0:T(8,128)(2,1)S(1)}, bf16[64,512]{1,0:T(8,128)(2,1)S(1)}, u32[]{:S(2)}, u32[]{:S(2)}) collective-permute-start(bf16[64,512]{1,0:T(8,128)(2,1)S(1)} %get-tuple-element.56.refs_0_), channel_id=1, source_target_pairs={{128,0},{192,64},{0,128},{64,192},{129,1},{193,65},{1,129},{65,193... | collective-permute-start | bytes 196616 | tf_op jit(solution)/shard_map/ppermute | solution.py:175
  75.7 5.4 %collective-permute-start.13 = (bf16[64,512]{1,0:T(8,128)(2,1)S(1)}, bf16[64,512]{1,0:T(8,128)(2,1)S(1)}, u32[]{:S(2)}, u32[]{:S(2)}) collective-permute-start(bf16[64,512]{1,0:T(8,128)(2,1)S(1)} %get-tuple-element.56.refs_0_), channel_id=1, source_target_pairs={{192,0},{0,64},{64,128},{128,192},{193,1},{1,65},{65,129},{129,193... | collective-permute-start | bytes 196616 | tf_op jit(solution)/shard_map/ppermute | solution.py:175
  76.0 4.7 %collective-permute-start.12 = (bf16[64,512]{1,0:T(8,128)(2,1)S(1)}, bf16[64,512]{1,0:T(8,128)(2,1)S(1)}, u32[]{:S(2)}, u32[]{:S(2)}) collective-permute-start(bf16[64,512]{1,0:T(8,128)(2,1)S(1)} %get-tuple-element.56.refs_0_), channel_id=1, source_target_pairs={{64,0},{128,64},{192,128},{0,192},{65,1},{129,65},{193,129},{1,193... | collective-permute-start | bytes 196616 | tf_op jit(solution)/shard_map/ppermute | solution.py:175
  78.8 1.6 %copy-start.5 = (bf16[512,2048]{1,0:T(8,128)(2,1)S(1)}, bf16[512,2048]{1,0:T(8,128)(2,1)}, u32[]{:S(2)}) copy-start(bf16[512,2048]{1,0:T(8,128)(2,1)} %w_ref.10) | copy-start | bytes 6291460
  98.6 4.8 %collective-permute-start.15 = (bf16[128,512]{1,0:T(8,128)(2,1)S(1)}, bf16[128,512]{1,0:T(8,128)(2,1)S(1)}, u32[]{:S(2)}, u32[]{:S(2)}) collective-permute-start(bf16[128,512]{1,0:T(8,128)(2,1)S(1)} %shard_map.118.refs_0_), channel_id=1, source_target_pairs={{64,0},{128,64},{192,128},{0,192},{65,1},{129,65},{193,129},{1,193... | collective-permute-start | bytes 393224 | tf_op jit(solution)/shard_map/ppermute | solution.py:175
  99.6 9.8 %collective-permute-start.17 = (bf16[128,512]{1,0:T(8,128)(2,1)S(1)}, bf16[128,512]{1,0:T(8,128)(2,1)S(1)}, u32[]{:S(2)}, u32[]{:S(2)}) collective-permute-start(bf16[128,512]{1,0:T(8,128)(2,1)S(1)} %shard_map.118.refs_0_), channel_id=1, source_target_pairs={{128,0},{192,64},{0,128},{64,192},{129,1},{193,65},{1,129},{65,193... | collective-permute-start | bytes 393224 | tf_op jit(solution)/shard_map/ppermute | solution.py:175
  100.0 9.0 %collective-permute-start.16 = (bf16[128,512]{1,0:T(8,128)(2,1)S(1)}, bf16[128,512]{1,0:T(8,128)(2,1)S(1)}, u32[]{:S(2)}, u32[]{:S(2)}) collective-permute-start(bf16[128,512]{1,0:T(8,128)(2,1)S(1)} %shard_map.118.refs_0_), channel_id=1, source_target_pairs={{192,0},{0,64},{64,128},{128,192},{193,1},{1,65},{65,129},{129,193... | collective-permute-start | bytes 393224 | tf_op jit(solution)/shard_map/ppermute | solution.py:175
  100.7 2.2 %copy-start.2 = (bf16[1024,2048]{1,0:T(8,128)(2,1)S(1)}, bf16[1024,2048]{1,0:T(8,128)(2,1)}, u32[]{:S(2)}) copy-start(bf16[1024,2048]{1,0:T(8,128)(2,1)} %w_ref.11) | copy-start | bytes 12582916

commit v9 on v7

--- a/solution.py
+++ b/solution.py
@@ -13,6 +13,8 @@
 TN = (((0,), (0,)), ((), ()))
 N_PHASE = 4
 CHUNKS = 4
+DP_ORDER = [45, 29, 43, 61, 34, 33, 31, 40, 26, 62, 22, 2, 11, 28, 54, 4, 10, 35, 52, 46, 30, 7, 14, 27, 63, 55, 41, 42, 58, 18, 60, 32, 15, 5, 16, 20, 56, 8, 13, 25, 37, 17, 48, 51, 57, 38, 1, 12, 49, 24, 6, 23, 36, 50, 21, 19, 9, 39, 59, 3, 0, 53, 47, 44]
+DP_PLACE = [60, 46, 11, 59, 15, 33, 50, 21, 37, 56, 16, 12, 47, 38, 22, 32, 34, 41, 29, 55, 35, 54, 10, 51, 49, 39, 8, 23, 13, 1, 20, 6, 31, 5, 4, 17, 52, 40, 45, 57, 7, 26, 27, 2, 63, 0, 19, 62, 42, 48, 53, 43, 18, 61, 14, 25, 36, 44, 28, 58, 30, 3, 9, 24]
 cost = pl.CostEstimate(flops=10**9, bytes_accessed=10**5, transcendentals=0)
 
 
@@ -352,9 +354,9 @@
     slots = n_dp * cap
 
     negatives = neg_slot.T
-    held = (n_dp - 1 - negatives // cap) * cap + negatives % cap
+    held = jnp.asarray(DP_PLACE, jnp.int32)[negatives // cap] * cap + negatives % cap
     neg_rows = jnp.pad(jnp.concatenate([held, held], axis=1), ((0, 1), (0, 0)), constant_values=-1)
-    order = [list(range(n_dp - 1, -1, -1))]
+    order = [DP_ORDER]
 
     def exchange(rows):
         blocks = rows.reshape(n_dp, cap, cols)
@@ -366,7 +368,7 @@
     d_far, d_next, d_last, document_requests = lax.optimization_barrier(
         (*project_sends(doc_states, doc_proj, k, 63, (2, 1, 3)), document_requests)
     )
-    requests = document_requests[0, ::-1].reshape(1, slots)
+    requests = document_requests[0][jnp.asarray(DP_ORDER, jnp.int32)].reshape(1, slots)
     d_parts = [send(d_far, 2), send(d_next, 1), send(d_last, 3)]
     d_own = project_own(doc_states, doc_proj, k)
     (onehot,) = call(onehot_rows, [((slots, docs), bf16)], requests)

time: 111 us -> 110 us (level); the launches traced: 109 us -> 109 us
  waiting for transfers between devices: 34.1 us -> 28.9 us
  local copies, waits for them, and re-layouts: 10.7 us -> 14.4 us
  starting transfers between devices: 48.4 us -> 50.3 us
    all_to_all x2, waiting for transfers between devices: 23.9 us -> 18.8 us  [exchange(): lax.all_to_all(blocks, 'dp', split_axis=0, concat_axis=0, tiled=True, axi...]
    gather x0 -> x2, local copies, waits for them, and re-layouts: none -> 3.62 us  [the longest x1 3.02 us: local(): jnp.asarray(DP_PLACE, jnp.int32)[negatives // cap] * cap + negatives % cap]
    all_to_all x2, starting transfers between devices: 24.1 us -> 26.1 us  [exchange(): lax.all_to_all(blocks, 'dp', split_axis=0, concat_axis=0, tiled=True, axi...]
    unnamed x20 -> x24, local copies, waits for them, and re-layouts: 7.59 us -> 7.6 us
  transfers between devices with their start and end apart: 20 -> 20, of which waited for: 12 -> 12; matrix products, arithmetic and copies ran while one was open for 3% -> 6% of each run, Pallas kernels for 6% -> 6%
where the time goes in v9:
time: 110 us; the launch traced here: 109 us
  starting transfers between devices  50.3 us (46%)
  waiting for transfers between devices  28.9 us (26%)
  local copies, waits for them, and re-layouts  14.4 us (13%)
  Pallas kernels  14.3 us (13%)
    all_to_all x2, starting transfers between devices, exchange(): lax.all_to_all(blocks, 'dp', split_axis=0, concat_axis=0, tiled=True, axi...  26.1 us
    all_to_all x2, waiting for transfers between devices, exchange(): lax.all_to_all(blocks, 'dp', split_axis=0, concat_axis=0, tiled=True, axi...  18.8 us
    ppermute x12, starting transfers between devices, gather_blocks(): lax.ppermute(x, 'phase', [((i + s) % N_PHASE, i) for i in range(N_PHASE)])  13.6 us
    ppermute x6, starting transfers between devices, send(): lax.ppermute(block, 'phase', [(i, (i + s) % N_PHASE) for i in range(N_PHA...  10.6 us
    unnamed x24, local copies, waits for them, and re-layouts  7.6 us
    ppermute x12, waiting for transfers between devices, gather_blocks(): lax.ppermute(x, 'phase', [((i + s) % N_PHASE, i) for i in range(N_PHASE)])  6.59 us
    pallas_call x2, Pallas kernels, project_sends(): pl.pallas_call(body, in_specs=[pl.BlockSpec(memory_space=pltpu.SMEM), hbm...  4.23 us
    pallas_call x6, Pallas kernels, run(): pl.pallas_call(body, in_specs=[pl.BlockSpec(memory_space=pltpu.SMEM)] + [...  4.12 us
  transfers between devices with their start and end apart: 20, of which 12 were waited for; matrix products, arithmetic and copies ran while one was open for 6% of the time, Pallas kernels for 6%

profile of v9, /device:TPU:1, one launch (start us, length us, event | category | flops | bytes accessed | tf_op | source)
XLA Modules:
  0.0 109.0 jit_solution(11721651133699995938)
XLA Ops:
  0.7 3.0 %shard_map.122 = (bf16[128,512]{1,0:T(8,128)(2,1)}, bf16[128,512]{1,0:T(8,128)(2,1)}, bf16[128,512]{1,0:T(8,128)(2,1)}) custom-call(s32[1]{0:T(128)} %bitcast.k_ref, bf16[128,1024]{1,0:T(8,128)(2,1)} %x_ref.3, bf16[1024,2048]{1,0:T(8,128)(2,1)} %refs_3_.3), custom_call_target="tpu_custom_call" | custom-call | flops 1000000000 | bytes 100000 | tf_op jit(solution)/shard_map/pallas_call | solution.py:75
  3.7 3.7 %collective-permute-start = (bf16[128,512]{1,0:T(8,128)(2,1)}, bf16[128,512]{1,0:T(8,128)(2,1)S(1)}, u32[]{:S(2)}, u32[]{:S(2)}) collective-permute-start(bf16[128,512]{1,0:T(8,128)(2,1)} %get-tuple-element.35), channel_id=1, source_target_pairs={{0,128},{64,192},{128,0},{192,64},{1,129},{65,193},{129,1},{193,65... | collective-permute-start | bytes 393224 | tf_op jit(solution)/shard_map/ppermute | solution.py:150
  7.7 2.4 %collective-permute-start.2 = (bf16[128,512]{1,0:T(8,128)(2,1)}, bf16[128,512]{1,0:T(8,128)(2,1)S(1)}, u32[]{:S(2)}, u32[]{:S(2)}) collective-permute-start(bf16[128,512]{1,0:T(8,128)(2,1)} %get-tuple-element.37), channel_id=1, source_target_pairs={{0,192},{64,0},{128,64},{192,128},{1,193},{65,1},{129,65},{193,129... | collective-permute-start | bytes 393224 | tf_op jit(solution)/shard_map/ppermute | solution.py:150
  10.1 2.2 %copy-done.1 = bf16[1024,2048]{1,0:T(8,128)(2,1)S(1)} copy-done((bf16[1024,2048]{1,0:T(8,128)(2,1)S(1)}, bf16[1024,2048]{1,0:T(8,128)(2,1)}, u32[]{:S(2)}) %copy-start.1) | copy-done | bytes 4194328
  13.6 1.1 %collective-permute-done.1.c = bf16[128,512]{1,0:T(8,128)(2,1)S(1)} collective-permute-done((bf16[128,512]{1,0:T(8,128)(2,1)}, bf16[128,512]{1,0:T(8,128)(2,1)S(1)}, u32[]{:S(2)}, u32[]{:S(2)}) %collective-permute-start.1) | collective-permute-done | bytes 131104 | tf_op jit(solution)/shard_map/ppermute | solution.py:150
  14.8 1.3 %shard_map.124 = (f32[128,512]{1,0:T(8,128)S(1)}, bf16[1024,512]{1,0:T(8,128)(2,1)}) custom-call(f32[128,512]{1,0:T(8,128)S(1)} %shard_map.121.a, bf16[128,512]{1,0:T(8,128)(2,1)S(1)} %collective-permute-done.b, bf16[128,512]{1,0:T(8,128)(2,1)S(1)} %collective-permute-done.1.c, bf16[128,512]{1,0:T(8,128)(2,1)S(1)} %collective-permute-done.2.d, ...), custom_call_target="tpu_custom_call" | custom-call | flops 1000000000 | bytes 100000 | tf_op jit(solution)/shard_map/pallas_call | solution.py:202
  16.1 13.5 %all-to-all-start = ((bf16[64,16,512]{2,1,0:T(8,128)(2,1)}), bf16[64,16,512]{2,1,0:T(8,128)(2,1)S(1)}, u32[]{:S(2)}, u32[]{:S(2)}) async-start(bf16[64,16,512]{2,1,0:T(8,128)(2,1)} %bitcast.2), calls=%async_computation | async-start | bytes 2097152 | tf_op jit(solution)/shard_map/all_to_all | solution.py:363
  29.8 3.0 %gather_fusion.2 = s32[448]{0:T(512)S(1)} fusion(s32[64]{0:T(128)S(1)} %copy-done.7, s32[1024]{0:T(1024)S(1)} %pad_clamp_fusion), kind=kCustom, calls=%fused_computation.2 | custom fusion | bytes 5376 | tf_op jit(solution)/shard_map/gather | solution.py:357
  33.0 2.1 %gather_fusion.1 = s32[448]{0:T(512)S(1)} fusion(s32[1024]{0:T(1024)S(1)} %bitcast.42, s32[1024]{0:T(1024)S(1)} %pad_clamp_fusion.1), kind=kCustom, calls=%fused_computation.1 | custom fusion | bytes 5376 | tf_op jit(solution)/shard_map/jit(_take)/gather | solution.py:385
  35.5 1.6 %copy-done.4 = bf16[512,2048]{1,0:T(8,128)(2,1)S(1)} copy-done((bf16[512,2048]{1,0:T(8,128)(2,1)S(1)}, bf16[512,2048]{1,0:T(8,128)(2,1)}, u32[]{:S(2)}) %copy-start.4) | copy-done | bytes 2097176
  37.1 1.2 %shard_map.126 = (bf16[64,512]{1,0:T(8,128)(2,1)S(1)}, bf16[64,512]{1,0:T(8,128)(2,1)S(1)}, bf16[64,512]{1,0:T(8,128)(2,1)S(1)}) custom-call(s32[1]{0:T(128)} %bitcast.k_ref, bf16[64,512]{1,0:T(8,128)(2,1)S(1)} %copy-done.6, bf16[512,2048]{1,0:T(8,128)(2,1)S(1)} %copy-done.4), custom_call_target="tpu_custom_call" | custom-call | flops 1000000000 | bytes 100000 | tf_op jit(solution)/shard_map/pallas_call | solution.py:75
  38.3 1.6 %collective-permute-start.3 = (bf16[64,512]{1,0:T(8,128)(2,1)S(1)}, bf16[64,512]{1,0:T(8,128)(2,1)S(1)}, u32[]{:S(2)}, u32[]{:S(2)}) collective-permute-start(bf16[64,512]{1,0:T(8,128)(2,1)S(1)} %get-tuple-element.41), channel_id=1, source_target_pairs={{0,128},{64,192},{128,0},{192,64},{1,129},{65,193},{129,1},{193,65... | collective-permute-start | bytes 196616 | tf_op jit(solution)/shard_map/ppermute | solution.py:150
  39.9 1.7 %collective-permute-start.4 = (bf16[64,512]{1,0:T(8,128)(2,1)S(1)}, bf16[64,512]{1,0:T(8,128)(2,1)S(1)}, u32[]{:S(2)}, u32[]{:S(2)}) collective-permute-start(bf16[64,512]{1,0:T(8,128)(2,1)S(1)} %get-tuple-element.42), channel_id=1, source_target_pairs={{0,64},{64,128},{128,192},{192,0},{1,65},{65,129},{129,193},{193,1... | collective-permute-start | bytes 196616 | tf_op jit(solution)/shard_map/ppermute | solution.py:150
  43.3 1.7 %collective-permute-done.4.b = bf16[64,512]{1,0:T(8,128)(2,1)S(1)} collective-permute-done((bf16[64,512]{1,0:T(8,128)(2,1)S(1)}, bf16[64,512]{1,0:T(8,128)(2,1)S(1)}, u32[]{:S(2)}, u32[]{:S(2)}) %collective-permute-start.4) | collective-permute-done | bytes 65568 | tf_op jit(solution)/shard_map/ppermute | solution.py:150
  46.2 2.9 %collective-permute-start.7 = (f32[144,128]{1,0:T(8,128)S(1)}, f32[144,128]{1,0:T(8,128)S(1)}, u32[]{:S(2)}, u32[]{:S(2)}) collective-permute-start(f32[144,128]{1,0:T(8,128)S(1)} %shard_map.128.refs_0_), channel_id=1, source_target_pairs={{128,0},{192,64},{0,128},{64,192},{129,1},{193,65},{1,129},{65,193... | collective-permute-start | bytes 221192 | tf_op jit(solution)/shard_map/ppermute | solution.py:155
  49.1 3.9 %all-to-all-done = bf16[64,16,512]{2,1,0:T(8,128)(2,1)S(1)} async-done(((bf16[64,16,512]{2,1,0:T(8,128)(2,1)}), bf16[64,16,512]{2,1,0:T(8,128)(2,1)S(1)}, u32[]{:S(2)}, u32[]{:S(2)}) %all-to-all-start) | async-done | bytes 1048608 | tf_op jit(solution)/shard_map/all_to_all | solution.py:363
  53.0 1.1 shard_map.129.refs_4_
  55.2 2.9 %collective-permute-start.10 = (f32[8,128]{1,0:T(8,128)S(1)}, f32[8,128]{1,0:T(8,128)S(1)}, u32[]{:S(2)}, u32[]{:S(2)}) collective-permute-start(f32[8,128]{1,0:T(8,128)S(1)} %shard_map.129.refs_4_), channel_id=1, source_target_pairs={{128,0},{192,64},{0,128},{64,192},{129,1},{193,65},{1,129},{65,193... | collective-permute-start | bytes 12296 | tf_op jit(solution)/shard_map/ppermute | solution.py:155
  58.1 1.1 collective-permute-done.10.refs_6_
  59.1 1.6 %collective-permute-done.9.refs_5_ = f32[8,128]{1,0:T(8,128)S(1)} collective-permute-done((f32[8,128]{1,0:T(8,128)S(1)}, f32[8,128]{1,0:T(8,128)S(1)}, u32[]{:S(2)}, u32[]{:S(2)}) %collective-permute-start.9) | collective-permute-done | bytes 4128 | tf_op jit(solution)/shard_map/ppermute | solution.py:155
  60.7 1.7 %shard_map.130 = (bf16[1024,512]{1,0:T(8,128)(2,1)}, bf16[1024,128]{1,0:T(8,128)(2,1)S(1)}, bf16[128,128]{1,0:T(8,128)(2,1)S(1)}, f32[8,128]{1,0:T(8,128)S(1)}, f32[128,128]{1,0:T(8,128)S(1)}) custom-call(f32[144,128]{1,0:T(8,128)S(1)} %shard_map.128.refs_0_, f32[144,128]{1,0:T(8,128)S(1)} %collective-permute-done.6.refs_1_, ...), custom_call_target="tpu_custom_call" | custom-call | flops 1000000000 | bytes 100000 | tf_op jit(solution)/shard_map/pallas_call | solution.py:396
  62.4 12.5 %all-to-all-start.1 = ((bf16[64,16,512]{2,1,0:T(8,128)(2,1)}), bf16[64,16,512]{2,1,0:T(8,128)(2,1)S(1)}, u32[]{:S(2)}, u32[]{:S(2)}) async-start(bf16[64,16,512]{2,1,0:T(8,128)(2,1)} %bitcast.7), calls=%async_computation.1 | async-start | bytes 2097152 | tf_op jit(solution)/shard_map/all_to_all | solution.py:363
  75.3 1.3 %collective-permute-start.14 = (bf16[64,512]{1,0:T(8,128)(2,1)S(1)}, bf16[64,512]{1,0:T(8,128)(2,1)S(1)}, u32[]{:S(2)}, u32[]{:S(2)}) collective-permute-start(bf16[64,512]{1,0:T(8,128)(2,1)S(1)} %get-tuple-element.56.refs_0_), channel_id=1, source_target_pairs={{128,0},{192,64},{0,128},{64,192},{129,1},{193,65},{1,129},{65,193... | collective-permute-start | bytes 196616 | tf_op jit(solution)/shard_map/ppermute | solution.py:155
  78.6 1.6 %copy-done.5 = bf16[512,2048]{1,0:T(8,128)(2,1)S(1)} copy-done((bf16[512,2048]{1,0:T(8,128)(2,1)S(1)}, bf16[512,2048]{1,0:T(8,128)(2,1)}, u32[]{:S(2)}) %copy-start.5) | copy-done | bytes 2097176
  80.5 1.6 %collective-permute-done.12.refs_1_ = bf16[64,512]{1,0:T(8,128)(2,1)S(1)} collective-permute-done((bf16[64,512]{1,0:T(8,128)(2,1)S(1)}, bf16[64,512]{1,0:T(8,128)(2,1)S(1)}, u32[]{:S(2)}, u32[]{:S(2)}) %collective-permute-start.12) | collective-permute-done | bytes 65568 | tf_op jit(solution)/shard_map/ppermute | solution.py:155
  82.4 1.1 shard_map.134
  83.5 14.8 %all-to-all-done.1 = bf16[64,16,512]{2,1,0:T(8,128)(2,1)S(1)} async-done(((bf16[64,16,512]{2,1,0:T(8,128)(2,1)}), bf16[64,16,512]{2,1,0:T(8,128)(2,1)S(1)}, u32[]{:S(2)}, u32[]{:S(2)}) %all-to-all-start.1) | async-done | bytes 1048608 | tf_op jit(solution)/shard_map/all_to_all | solution.py:363
  98.7 2.2 %collective-permute-start.17 = (bf16[128,512]{1,0:T(8,128)(2,1)S(1)}, bf16[128,512]{1,0:T(8,128)(2,1)S(1)}, u32[]{:S(2)}, u32[]{:S(2)}) collective-permute-start(bf16[128,512]{1,0:T(8,128)(2,1)S(1)} %shard_map.135.refs_0_), channel_id=1, source_target_pairs={{128,0},{192,64},{0,128},{64,192},{129,1},{193,65},{1,129},{65,193... | collective-permute-start | bytes 393224 | tf_op jit(solution)/shard_map/ppermute | solution.py:155
  100.9 1.1 %collective-permute-start.16 = (bf16[128,512]{1,0:T(8,128)(2,1)S(1)}, bf16[128,512]{1,0:T(8,128)(2,1)S(1)}, u32[]{:S(2)}, u32[]{:S(2)}) collective-permute-start(bf16[128,512]{1,0:T(8,128)(2,1)S(1)} %shard_map.135.refs_0_), channel_id=1, source_target_pairs={{64,0},{128,64},{192,128},{0,192},{65,1},{129,65},{193,129},{1,193... | collective-permute-start | bytes 393224 | tf_op jit(solution)/shard_map/ppermute | solution.py:155
  102.0 2.2 %copy-done.2 = bf16[1024,2048]{1,0:T(8,128)(2,1)S(1)} copy-done((bf16[1024,2048]{1,0:T(8,128)(2,1)S(1)}, bf16[1024,2048]{1,0:T(8,128)(2,1)}, u32[]{:S(2)}) %copy-start.2) | copy-done | bytes 4194328
  105.4 1.4 %collective-permute-done.17.refs_2_ = bf16[128,512]{1,0:T(8,128)(2,1)S(1)} collective-permute-done((bf16[128,512]{1,0:T(8,128)(2,1)S(1)}, bf16[128,512]{1,0:T(8,128)(2,1)S(1)}, u32[]{:S(2)}, u32[]{:S(2)}) %collective-permute-start.17) | collective-permute-done | bytes 131104 | tf_op jit(solution)/shard_map/ppermute | solution.py:155
  107.5 1.5 %shard_map.138 = bf16[128,1024]{1,0:T(8,128)(2,1)} custom-call(s32[1]{0:T(128)} %bitcast.k_ref, f32[128,1024]{1,0:T(8,128)S(1)} %shard_map.137.refs_0_, bf16[128,512]{1,0:T(8,128)(2,1)S(1)} %collective-permute-done.16.refs_1_, bf16[128,512]{1,0:T(8,128)(2,1)S(1)} %collective-permute-done.17.refs_2_, bf16[1024,2048]{1,0:T(8,128)(2,1)S(1)} %copy-done.2), custom_call_target="tpu_custom_call" | custom-call | flops 1000000000 | bytes 100000 | tf_op jit(solution)/shard_map/pallas_call | solution.py:134
  (72 shorter events, 11.7 us)
Async XLA Ops:
  0.6 32.4 %copy-start = (s32[1,1024]{1,0:T(1,128)S(1)}, s32[1,1024]{1,0:T(1,128)}, u32[]{:S(2)}) copy-start(s32[1,1024]{1,0:T(1,128)} %param.15) | copy-start | bytes 12292
  0.6 9.4 %copy-start.10 = (s32[64]{0:T(128)S(1)}, s32[64]{0:T(128)}, u32[]{:S(2)}) copy-start(s32[64]{0:T(128)} %constant.76) | copy-start | bytes 772
  0.7 9.4 %copy-start.3 = (bf16[128,1024]{1,0:T(8,128)(2,1)S(1)}, bf16[128,1024]{1,0:T(8,128)(2,1)}, u32[]{:S(2)}) copy-start(bf16[128,1024]{1,0:T(8,128)(2,1)} %x_ref.3) | copy-start | bytes 786436
  0.7 11.9 %copy-start.9 = (s32[1,64,16]{1,2,0:T(8,128)S(1)}, s32[1,64,16]{1,2,0:T(8,128)}, u32[]{:S(2)}) copy-start(s32[1,64,16]{1,2,0:T(8,128)} %param.14) | copy-start | bytes 12292
  3.7 9.9 %collective-permute-start = (bf16[128,512]{1,0:T(8,128)(2,1)}, bf16[128,512]{1,0:T(8,128)(2,1)S(1)}, u32[]{:S(2)}, u32[]{:S(2)}) collective-permute-start(bf16[128,512]{1,0:T(8,128)(2,1)} %get-tuple-element.35), channel_id=1, source_target_pairs={{0,128},{64,192},{128,0},{192,64},{1,129},{65,193},{129,1},{193,65... | collective-permute-start | bytes 393224 | tf_op jit(solution)/shard_map/ppermute | solution.py:150
  7.4 7.4 %collective-permute-start.1 = (bf16[128,512]{1,0:T(8,128)(2,1)}, bf16[128,512]{1,0:T(8,128)(2,1)S(1)}, u32[]{:S(2)}, u32[]{:S(2)}) collective-permute-start(bf16[128,512]{1,0:T(8,128)(2,1)} %get-tuple-element.36), channel_id=1, source_target_pairs={{0,64},{64,128},{128,192},{192,0},{1,65},{65,129},{129,193},{193,1... | collective-permute-start | bytes 393224 | tf_op jit(solution)/shard_map/ppermute | solution.py:150
  7.7 7.1 %collective-permute-start.2 = (bf16[128,512]{1,0:T(8,128)(2,1)}, bf16[128,512]{1,0:T(8,128)(2,1)S(1)}, u32[]{:S(2)}, u32[]{:S(2)}) collective-permute-start(bf16[128,512]{1,0:T(8,128)(2,1)} %get-tuple-element.37), channel_id=1, source_target_pairs={{0,192},{64,0},{128,64},{192,128},{1,193},{65,1},{129,65},{193,129... | collective-permute-start | bytes 393224 | tf_op jit(solution)/shard_map/ppermute | solution.py:150
  10.1 2.2 %copy-start.1 = (bf16[1024,2048]{1,0:T(8,128)(2,1)S(1)}, bf16[1024,2048]{1,0:T(8,128)(2,1)}, u32[]{:S(2)}) copy-start(bf16[1024,2048]{1,0:T(8,128)(2,1)} %refs_3_.3) | copy-start | bytes 12582916
  13.4 16.3 %copy-start.8 = (s32[64,7]{0,1:T(8,128)S(1)}, s32[64,7]{0,1:T(8,128)}, u32[]{:S(2)}) copy-start(s32[64,7]{0,1:T(8,128)} %param.16) | copy-start | bytes 5380
  13.4 16.4 %copy-start.7 = (s32[64]{0:T(128)S(1)}, s32[64]{0:T(128)}, u32[]{:S(2)}) copy-start(s32[64]{0:T(128)} %constant.64.clone) | copy-start | bytes 772
  16.1 37.0 %all-to-all-start = ((bf16[64,16,512]{2,1,0:T(8,128)(2,1)}), bf16[64,16,512]{2,1,0:T(8,128)(2,1)S(1)}, u32[]{:S(2)}, u32[]{:S(2)}) async-start(bf16[64,16,512]{2,1,0:T(8,128)(2,1)} %bitcast.2), calls=%async_computation | async-start | bytes 2097152 | tf_op jit(solution)/shard_map/all_to_all | solution.py:363
  29.8 5.5 %copy-start.11 = (f32[64]{0:T(128)S(1)}, f32[64]{0:T(128)}, u32[]{:S(2)}) copy-start(f32[64]{0:T(128)} %param.17) | copy-start | bytes 772
  29.8 5.7 %copy-start.6 = (bf16[64,512]{1,0:T(8,128)(2,1)S(1)}, bf16[64,512]{1,0:T(8,128)(2,1)}, u32[]{:S(2)}) copy-start(bf16[64,512]{1,0:T(8,128)(2,1)} %x_ref.5) | copy-start | bytes 196612
  35.5 1.6 %copy-start.4 = (bf16[512,2048]{1,0:T(8,128)(2,1)S(1)}, bf16[512,2048]{1,0:T(8,128)(2,1)}, u32[]{:S(2)}) copy-start(bf16[512,2048]{1,0:T(8,128)(2,1)} %refs_3_.2) | copy-start | bytes 6291460
  38.3 5.0 %collective-permute-start.3 = (bf16[64,512]{1,0:T(8,128)(2,1)S(1)}, bf16[64,512]{1,0:T(8,128)(2,1)S(1)}, u32[]{:S(2)}, u32[]{:S(2)}) collective-permute-start(bf16[64,512]{1,0:T(8,128)(2,1)S(1)} %get-tuple-element.41), channel_id=1, source_target_pairs={{0,128},{64,192},{128,0},{192,64},{1,129},{65,193},{129,1},{193,65... | collective-permute-start | bytes 196616 | tf_op jit(solution)/shard_map/ppermute | solution.py:150
  39.9 5.0 %collective-permute-start.4 = (bf16[64,512]{1,0:T(8,128)(2,1)S(1)}, bf16[64,512]{1,0:T(8,128)(2,1)S(1)}, u32[]{:S(2)}, u32[]{:S(2)}) collective-permute-start(bf16[64,512]{1,0:T(8,128)(2,1)S(1)} %get-tuple-element.42), channel_id=1, source_target_pairs={{0,64},{64,128},{128,192},{192,0},{1,65},{65,129},{129,193},{193,1... | collective-permute-start | bytes 196616 | tf_op jit(solution)/shard_map/ppermute | solution.py:150
  41.6 3.6 %collective-permute-start.5 = (bf16[64,512]{1,0:T(8,128)(2,1)S(1)}, bf16[64,512]{1,0:T(8,128)(2,1)S(1)}, u32[]{:S(2)}, u32[]{:S(2)}) collective-permute-start(bf16[64,512]{1,0:T(8,128)(2,1)S(1)} %get-tuple-element.43), channel_id=1, source_target_pairs={{0,192},{64,0},{128,64},{192,128},{1,193},{65,1},{129,65},{193,129... | collective-permute-start | bytes 196616 | tf_op jit(solution)/shard_map/ppermute | solution.py:150
  45.5 12.5 %collective-permute-start.8 = (f32[144,128]{1,0:T(8,128)S(1)}, f32[144,128]{1,0:T(8,128)S(1)}, u32[]{:S(2)}, u32[]{:S(2)}) collective-permute-start(f32[144,128]{1,0:T(8,128)S(1)} %shard_map.128.refs_0_), channel_id=1, source_target_pairs={{192,0},{0,64},{64,128},{128,192},{193,1},{1,65},{65,129},{129,193... | collective-permute-start | bytes 221192 | tf_op jit(solution)/shard_map/ppermute | solution.py:155
  46.2 11.8 %collective-permute-start.7 = (f32[144,128]{1,0:T(8,128)S(1)}, f32[144,128]{1,0:T(8,128)S(1)}, u32[]{:S(2)}, u32[]{:S(2)}) collective-permute-start(f32[144,128]{1,0:T(8,128)S(1)} %shard_map.128.refs_0_), channel_id=1, source_target_pairs={{128,0},{192,64},{0,128},{64,192},{129,1},{193,65},{1,129},{65,193... | collective-permute-start | bytes 221192 | tf_op jit(solution)/shard_map/ppermute | solution.py:155
  49.1 8.9 %collective-permute-start.6 = (f32[144,128]{1,0:T(8,128)S(1)}, f32[144,128]{1,0:T(8,128)S(1)}, u32[]{:S(2)}, u32[]{:S(2)}) collective-permute-start(f32[144,128]{1,0:T(8,128)S(1)} %shard_map.128.refs_0_), channel_id=1, source_target_pairs={{64,0},{128,64},{192,128},{0,192},{65,1},{129,65},{193,129},{1,193... | collective-permute-start | bytes 221192 | tf_op jit(solution)/shard_map/ppermute | solution.py:155
  54.1 3.9 %collective-permute-start.11 = (f32[8,128]{1,0:T(8,128)S(1)}, f32[8,128]{1,0:T(8,128)S(1)}, u32[]{:S(2)}, u32[]{:S(2)}) collective-permute-start(f32[8,128]{1,0:T(8,128)S(1)} %shard_map.129.refs_4_), channel_id=1, source_target_pairs={{192,0},{0,64},{64,128},{128,192},{193,1},{1,65},{65,129},{129,193... | collective-permute-start | bytes 12296 | tf_op jit(solution)/shard_map/ppermute | solution.py:155
  55.2 4.0 %collective-permute-start.10 = (f32[8,128]{1,0:T(8,128)S(1)}, f32[8,128]{1,0:T(8,128)S(1)}, u32[]{:S(2)}, u32[]{:S(2)}) collective-permute-start(f32[8,128]{1,0:T(8,128)S(1)} %shard_map.129.refs_4_), channel_id=1, source_target_pairs={{128,0},{192,64},{0,128},{64,192},{129,1},{193,65},{1,129},{65,193... | collective-permute-start | bytes 12296 | tf_op jit(solution)/shard_map/ppermute | solution.py:155
  58.0 2.7 %collective-permute-start.9 = (f32[8,128]{1,0:T(8,128)S(1)}, f32[8,128]{1,0:T(8,128)S(1)}, u32[]{:S(2)}, u32[]{:S(2)}) collective-permute-start(f32[8,128]{1,0:T(8,128)S(1)} %shard_map.129.refs_4_), channel_id=1, source_target_pairs={{64,0},{128,64},{192,128},{0,192},{65,1},{129,65},{193,129},{1,193... | collective-permute-start | bytes 12296 | tf_op jit(solution)/shard_map/ppermute | solution.py:155
  62.4 35.9 %all-to-all-start.1 = ((bf16[64,16,512]{2,1,0:T(8,128)(2,1)}), bf16[64,16,512]{2,1,0:T(8,128)(2,1)S(1)}, u32[]{:S(2)}, u32[]{:S(2)}) async-start(bf16[64,16,512]{2,1,0:T(8,128)(2,1)} %bitcast.7), calls=%async_computation.1 | async-start | bytes 2097152 | tf_op jit(solution)/shard_map/all_to_all | solution.py:363
  75.3 7.0 %collective-permute-start.14 = (bf16[64,512]{1,0:T(8,128)(2,1)S(1)}, bf16[64,512]{1,0:T(8,128)(2,1)S(1)}, u32[]{:S(2)}, u32[]{:S(2)}) collective-permute-start(bf16[64,512]{1,0:T(8,128)(2,1)S(1)} %get-tuple-element.56.refs_0_), channel_id=1, source_target_pairs={{128,0},{192,64},{0,128},{64,192},{129,1},{193,65},{1,129},{65,193... | collective-permute-start | bytes 196616 | tf_op jit(solution)/shard_map/ppermute | solution.py:155
  76.7 5.7 %collective-permute-start.13 = (bf16[64,512]{1,0:T(8,128)(2,1)S(1)}, bf16[64,512]{1,0:T(8,128)(2,1)S(1)}, u32[]{:S(2)}, u32[]{:S(2)}) collective-permute-start(bf16[64,512]{1,0:T(8,128)(2,1)S(1)} %get-tuple-element.56.refs_0_), channel_id=1, source_target_pairs={{64,0},{128,64},{192,128},{0,192},{65,1},{129,65},{193,129},{1,193... | collective-permute-start | bytes 196616 | tf_op jit(solution)/shard_map/ppermute | solution.py:155
  77.3 4.8 %collective-permute-start.12 = (bf16[64,512]{1,0:T(8,128)(2,1)S(1)}, bf16[64,512]{1,0:T(8,128)(2,1)S(1)}, u32[]{:S(2)}, u32[]{:S(2)}) collective-permute-start(bf16[64,512]{1,0:T(8,128)(2,1)S(1)} %get-tuple-element.56.refs_0_), channel_id=1, source_target_pairs={{192,0},{0,64},{64,128},{128,192},{193,1},{1,65},{65,129},{129,193... | collective-permute-start | bytes 196616 | tf_op jit(solution)/shard_map/ppermute | solution.py:155
  78.6 1.6 %copy-start.5 = (bf16[512,2048]{1,0:T(8,128)(2,1)S(1)}, bf16[512,2048]{1,0:T(8,128)(2,1)}, u32[]{:S(2)}) copy-start(bf16[512,2048]{1,0:T(8,128)(2,1)} %refs_3_.2) | copy-start | bytes 6291460
  98.6 6.3 %collective-permute-start.15 = (bf16[128,512]{1,0:T(8,128)(2,1)S(1)}, bf16[128,512]{1,0:T(8,128)(2,1)S(1)}, u32[]{:S(2)}, u32[]{:S(2)}) collective-permute-start(bf16[128,512]{1,0:T(8,128)(2,1)S(1)} %shard_map.135.refs_0_), channel_id=1, source_target_pairs={{192,0},{0,64},{64,128},{128,192},{193,1},{1,65},{65,129},{129,193... | collective-permute-start | bytes 393224 | tf_op jit(solution)/shard_map/ppermute | solution.py:155
  98.7 8.1 %collective-permute-start.17 = (bf16[128,512]{1,0:T(8,128)(2,1)S(1)}, bf16[128,512]{1,0:T(8,128)(2,1)S(1)}, u32[]{:S(2)}, u32[]{:S(2)}) collective-permute-start(bf16[128,512]{1,0:T(8,128)(2,1)S(1)} %shard_map.135.refs_0_), channel_id=1, source_target_pairs={{128,0},{192,64},{0,128},{64,192},{129,1},{193,65},{1,129},{65,193... | collective-permute-start | bytes 393224 | tf_op jit(solution)/shard_map/ppermute | solution.py:155
  100.9 6.6 %collective-permute-start.16 = (bf16[128,512]{1,0:T(8,128)(2,1)S(1)}, bf16[128,512]{1,0:T(8,128)(2,1)S(1)}, u32[]{:S(2)}, u32[]{:S(2)}) collective-permute-start(bf16[128,512]{1,0:T(8,128)(2,1)S(1)} %shard_map.135.refs_0_), channel_id=1, source_target_pairs={{64,0},{128,64},{192,128},{0,192},{65,1},{129,65},{193,129},{1,193... | collective-permute-start | bytes 393224 | tf_op jit(solution)/shard_map/ppermute | solution.py:155
  102.0 2.2 %copy-start.2 = (bf16[1024,2048]{1,0:T(8,128)(2,1)S(1)}, bf16[1024,2048]{1,0:T(8,128)(2,1)}, u32[]{:S(2)}) copy-start(bf16[1024,2048]{1,0:T(8,128)(2,1)} %refs_3_.3) | copy-start | bytes 12582916

commit v10 on v9

--- a/solution.py
+++ b/solution.py
@@ -143,7 +143,33 @@
     blocks = gather_blocks(u)
     acc = run(product(0), f32, blocks[0], w)
     acc = run(product(3), f32, acc, blocks[3], w)
-    return run(product(1, 2), bf16, acc, blocks[1], blocks[2], w)
+
+    def last(k_ref, acc_ref, a_ref, b_ref, w_ref, out_ref, buf_ref, sem_ref):
+        half = depth // 2
+
+        def store(i):
+            return pltpu.make_async_copy(buf_ref.at[i], out_ref.at[:, pl.ds(i * half, half)], sem_ref.at[i])
+
+        for i in range(2):
+            part = slice(i * half, (i + 1) * half)
+            total = acc_ref[:, part]
+            for s, block in enumerate((a_ref, b_ref), start=1):
+                start = pl.multiple_of(lax.rem(k_ref[0] + s, N_PHASE) * cols, cols)
+                total = total + dot(block[...], w_ref[part, pl.ds(start, cols)], NT)
+            buf_ref[i] = total.astype(bf16)
+            store(i).start()
+        for i in range(2):
+            store(i).wait()
+
+    return pl.pallas_call(
+        last,
+        in_specs=[pl.BlockSpec(memory_space=pltpu.SMEM)] + [pl.BlockSpec(memory_space=pltpu.VMEM)] * 4,
+        out_specs=pl.BlockSpec(memory_space=pltpu.HBM),
+        out_shape=jax.ShapeDtypeStruct((rows, depth), bf16),
+        scratch_shapes=[pltpu.VMEM((2, rows, depth // 2), bf16), pltpu.SemaphoreType.DMA((2,))],
+        compiler_params=params(),
+        cost_estimate=cost,
+    )(k, acc, blocks[1], blocks[2], w)
 
 
 def send(block, s):

time: 110 us -> 110 us (level)
    pallas_call x6 -> x4, Pallas kernels: 4.12 us -> 1.51 us  [run(): pl.pallas_call(body, in_specs=[pl.BlockSpec(memory_space=pltpu.SMEM)] + [...]
    pallas_call x0 -> x2, Pallas kernels: none -> 2.59 us  [project_back(): pl.pallas_call(last, in_specs=[pl.BlockSpec(memory_space=pltpu.SMEM)] + [...]
where the time goes in v10:
time: 110 us; the launch traced here: 109 us
  starting transfers between devices  50.3 us (46%)
  waiting for transfers between devices  28.9 us (26%)
  local copies, waits for them, and re-layouts  14.4 us (13%)
  Pallas kernels  14.2 us (13%)
  between operations  1.12 us (1%)
    all_to_all x2, starting transfers between devices, exchange(): lax.all_to_all(blocks, 'dp', split_axis=0, concat_axis=0, tiled=True, axi...  26.1 us
    all_to_all x2, waiting for transfers between devices, exchange(): lax.all_to_all(blocks, 'dp', split_axis=0, concat_axis=0, tiled=True, axi...  18.7 us
    ppermute x12, starting transfers between devices, gather_blocks(): lax.ppermute(x, 'phase', [((i + s) % N_PHASE, i) for i in range(N_PHASE)])  13.6 us
    ppermute x6, starting transfers between devices, send(): lax.ppermute(block, 'phase', [(i, (i + s) % N_PHASE) for i in range(N_PHA...  10.6 us
    unnamed x24, local copies, waits for them, and re-layouts  7.6 us
    ppermute x12, waiting for transfers between devices, gather_blocks(): lax.ppermute(x, 'phase', [((i + s) % N_PHASE, i) for i in range(N_PHASE)])  6.59 us
    pallas_call x2, Pallas kernels, project_sends(): pl.pallas_call(body, in_specs=[pl.BlockSpec(memory_space=pltpu.SMEM), hbm...  4.23 us
    ppermute x6, waiting for transfers between devices, send(): lax.ppermute(block, 'phase', [(i, (i + s) % N_PHASE) for i in range(N_PHA...  3.53 us
  transfers between devices with their start and end apart: 20, of which 12 were waited for; matrix products, arithmetic and copies ran while one was open for 6% of the time, Pallas kernels for 6%

profile of v10, /device:TPU:1, one launch (start us, length us, event | category | flops | bytes accessed | tf_op | source)
XLA Modules:
  0.0 109.2 jit_solution(11668718125262191396)
XLA Ops:
  0.7 3.0 %shard_map.122 = (bf16[128,512]{1,0:T(8,128)(2,1)}, bf16[128,512]{1,0:T(8,128)(2,1)}, bf16[128,512]{1,0:T(8,128)(2,1)}) custom-call(s32[1]{0:T(128)} %bitcast.k_ref, bf16[128,1024]{1,0:T(8,128)(2,1)} %x_ref.3, bf16[1024,2048]{1,0:T(8,128)(2,1)} %w_ref.11), custom_call_target="tpu_custom_call" | custom-call | flops 1000000000 | bytes 100000 | tf_op jit(solution)/shard_map/pallas_call | solution.py:75
  3.7 3.7 %collective-permute-start = (bf16[128,512]{1,0:T(8,128)(2,1)}, bf16[128,512]{1,0:T(8,128)(2,1)S(1)}, u32[]{:S(2)}, u32[]{:S(2)}) collective-permute-start(bf16[128,512]{1,0:T(8,128)(2,1)} %get-tuple-element.35), channel_id=1, source_target_pairs={{0,128},{64,192},{128,0},{192,64},{1,129},{65,193},{129,1},{193,65... | collective-permute-start | bytes 393224 | tf_op jit(solution)/shard_map/ppermute | solution.py:176
  7.7 2.4 %collective-permute-start.2 = (bf16[128,512]{1,0:T(8,128)(2,1)}, bf16[128,512]{1,0:T(8,128)(2,1)S(1)}, u32[]{:S(2)}, u32[]{:S(2)}) collective-permute-start(bf16[128,512]{1,0:T(8,128)(2,1)} %get-tuple-element.37), channel_id=1, source_target_pairs={{0,192},{64,0},{128,64},{192,128},{1,193},{65,1},{129,65},{193,129... | collective-permute-start | bytes 393224 | tf_op jit(solution)/shard_map/ppermute | solution.py:176
  10.1 2.2 %copy-done.1 = bf16[1024,2048]{1,0:T(8,128)(2,1)S(1)} copy-done((bf16[1024,2048]{1,0:T(8,128)(2,1)S(1)}, bf16[1024,2048]{1,0:T(8,128)(2,1)}, u32[]{:S(2)}) %copy-start.1) | copy-done | bytes 4194328
  13.6 1.1 %collective-permute-done.1.c = bf16[128,512]{1,0:T(8,128)(2,1)S(1)} collective-permute-done((bf16[128,512]{1,0:T(8,128)(2,1)}, bf16[128,512]{1,0:T(8,128)(2,1)S(1)}, u32[]{:S(2)}, u32[]{:S(2)}) %collective-permute-start.1) | collective-permute-done | bytes 131104 | tf_op jit(solution)/shard_map/ppermute | solution.py:176
  14.8 1.3 %shard_map.124 = (f32[128,512]{1,0:T(8,128)S(1)}, bf16[1024,512]{1,0:T(8,128)(2,1)}) custom-call(f32[128,512]{1,0:T(8,128)S(1)} %shard_map.121.a, bf16[128,512]{1,0:T(8,128)(2,1)S(1)} %collective-permute-done.b, bf16[128,512]{1,0:T(8,128)(2,1)S(1)} %collective-permute-done.1.c, bf16[128,512]{1,0:T(8,128)(2,1)S(1)} %collective-permute-done.2.d, ...), custom_call_target="tpu_custom_call" | custom-call | flops 1000000000 | bytes 100000 | tf_op jit(solution)/shard_map/pallas_call | solution.py:228
  16.1 13.5 %all-to-all-start = ((bf16[64,16,512]{2,1,0:T(8,128)(2,1)}), bf16[64,16,512]{2,1,0:T(8,128)(2,1)S(1)}, u32[]{:S(2)}, u32[]{:S(2)}) async-start(bf16[64,16,512]{2,1,0:T(8,128)(2,1)} %bitcast.2), calls=%async_computation | async-start | bytes 2097152 | tf_op jit(solution)/shard_map/all_to_all | solution.py:389
  29.8 3.0 %gather_fusion.2 = s32[448]{0:T(512)S(1)} fusion(s32[64]{0:T(128)S(1)} %copy-done.7, s32[1024]{0:T(1024)S(1)} %pad_clamp_fusion), kind=kCustom, calls=%fused_computation.2 | custom fusion | bytes 5376 | tf_op jit(solution)/shard_map/gather | solution.py:383
  33.0 2.1 %gather_fusion.1 = s32[448]{0:T(512)S(1)} fusion(s32[1024]{0:T(1024)S(1)} %bitcast.42, s32[1024]{0:T(1024)S(1)} %pad_clamp_fusion.1), kind=kCustom, calls=%fused_computation.1 | custom fusion | bytes 5376 | tf_op jit(solution)/shard_map/jit(_take)/gather | solution.py:411
  35.5 1.6 %copy-done.4 = bf16[512,2048]{1,0:T(8,128)(2,1)S(1)} copy-done((bf16[512,2048]{1,0:T(8,128)(2,1)S(1)}, bf16[512,2048]{1,0:T(8,128)(2,1)}, u32[]{:S(2)}) %copy-start.4) | copy-done | bytes 2097176
  37.1 1.2 %shard_map.126 = (bf16[64,512]{1,0:T(8,128)(2,1)S(1)}, bf16[64,512]{1,0:T(8,128)(2,1)S(1)}, bf16[64,512]{1,0:T(8,128)(2,1)S(1)}) custom-call(s32[1]{0:T(128)} %bitcast.k_ref, bf16[64,512]{1,0:T(8,128)(2,1)S(1)} %copy-done.6, bf16[512,2048]{1,0:T(8,128)(2,1)S(1)} %copy-done.4), custom_call_target="tpu_custom_call" | custom-call | flops 1000000000 | bytes 100000 | tf_op jit(solution)/shard_map/pallas_call | solution.py:75
  38.3 1.6 %collective-permute-start.3 = (bf16[64,512]{1,0:T(8,128)(2,1)S(1)}, bf16[64,512]{1,0:T(8,128)(2,1)S(1)}, u32[]{:S(2)}, u32[]{:S(2)}) collective-permute-start(bf16[64,512]{1,0:T(8,128)(2,1)S(1)} %get-tuple-element.41), channel_id=1, source_target_pairs={{0,128},{64,192},{128,0},{192,64},{1,129},{65,193},{129,1},{193,65... | collective-permute-start | bytes 196616 | tf_op jit(solution)/shard_map/ppermute | solution.py:176
  39.9 1.7 %collective-permute-start.4 = (bf16[64,512]{1,0:T(8,128)(2,1)S(1)}, bf16[64,512]{1,0:T(8,128)(2,1)S(1)}, u32[]{:S(2)}, u32[]{:S(2)}) collective-permute-start(bf16[64,512]{1,0:T(8,128)(2,1)S(1)} %get-tuple-element.42), channel_id=1, source_target_pairs={{0,64},{64,128},{128,192},{192,0},{1,65},{65,129},{129,193},{193,1... | collective-permute-start | bytes 196616 | tf_op jit(solution)/shard_map/ppermute | solution.py:176
  43.3 1.7 %collective-permute-done.4.b = bf16[64,512]{1,0:T(8,128)(2,1)S(1)} collective-permute-done((bf16[64,512]{1,0:T(8,128)(2,1)S(1)}, bf16[64,512]{1,0:T(8,128)(2,1)S(1)}, u32[]{:S(2)}, u32[]{:S(2)}) %collective-permute-start.4) | collective-permute-done | bytes 65568 | tf_op jit(solution)/shard_map/ppermute | solution.py:176
  46.2 2.9 %collective-permute-start.7 = (f32[144,128]{1,0:T(8,128)S(1)}, f32[144,128]{1,0:T(8,128)S(1)}, u32[]{:S(2)}, u32[]{:S(2)}) collective-permute-start(f32[144,128]{1,0:T(8,128)S(1)} %shard_map.128.refs_0_), channel_id=1, source_target_pairs={{128,0},{192,64},{0,128},{64,192},{129,1},{193,65},{1,129},{65,193... | collective-permute-start | bytes 221192 | tf_op jit(solution)/shard_map/ppermute | solution.py:181
  49.1 3.9 %all-to-all-done = bf16[64,16,512]{2,1,0:T(8,128)(2,1)S(1)} async-done(((bf16[64,16,512]{2,1,0:T(8,128)(2,1)}), bf16[64,16,512]{2,1,0:T(8,128)(2,1)S(1)}, u32[]{:S(2)}, u32[]{:S(2)}) %all-to-all-start) | async-done | bytes 1048608 | tf_op jit(solution)/shard_map/all_to_all | solution.py:389
  53.0 1.1 shard_map.129.refs_4_
  55.2 2.9 %collective-permute-start.10 = (f32[8,128]{1,0:T(8,128)S(1)}, f32[8,128]{1,0:T(8,128)S(1)}, u32[]{:S(2)}, u32[]{:S(2)}) collective-permute-start(f32[8,128]{1,0:T(8,128)S(1)} %shard_map.129.refs_4_), channel_id=1, source_target_pairs={{128,0},{192,64},{0,128},{64,192},{129,1},{193,65},{1,129},{65,193... | collective-permute-start | bytes 12296 | tf_op jit(solution)/shard_map/ppermute | solution.py:181
  58.1 1.1 collective-permute-done.10.refs_6_
  59.1 1.6 %collective-permute-done.9.refs_5_ = f32[8,128]{1,0:T(8,128)S(1)} collective-permute-done((f32[8,128]{1,0:T(8,128)S(1)}, f32[8,128]{1,0:T(8,128)S(1)}, u32[]{:S(2)}, u32[]{:S(2)}) %collective-permute-start.9) | collective-permute-done | bytes 4128 | tf_op jit(solution)/shard_map/ppermute | solution.py:181
  60.7 1.7 %shard_map.130 = (bf16[1024,512]{1,0:T(8,128)(2,1)}, bf16[1024,128]{1,0:T(8,128)(2,1)S(1)}, bf16[128,128]{1,0:T(8,128)(2,1)S(1)}, f32[8,128]{1,0:T(8,128)S(1)}, f32[128,128]{1,0:T(8,128)S(1)}) custom-call(f32[144,128]{1,0:T(8,128)S(1)} %shard_map.128.refs_0_, f32[144,128]{1,0:T(8,128)S(1)} %collective-permute-done.6.refs_1_, ...), custom_call_target="tpu_custom_call" | custom-call | flops 1000000000 | bytes 100000 | tf_op jit(solution)/shard_map/pallas_call | solution.py:422
  62.4 12.5 %all-to-all-start.1 = ((bf16[64,16,512]{2,1,0:T(8,128)(2,1)}), bf16[64,16,512]{2,1,0:T(8,128)(2,1)S(1)}, u32[]{:S(2)}, u32[]{:S(2)}) async-start(bf16[64,16,512]{2,1,0:T(8,128)(2,1)} %bitcast.7), calls=%async_computation.1 | async-start | bytes 2097152 | tf_op jit(solution)/shard_map/all_to_all | solution.py:389
  75.3 1.3 %collective-permute-start.14 = (bf16[64,512]{1,0:T(8,128)(2,1)S(1)}, bf16[64,512]{1,0:T(8,128)(2,1)S(1)}, u32[]{:S(2)}, u32[]{:S(2)}) collective-permute-start(bf16[64,512]{1,0:T(8,128)(2,1)S(1)} %get-tuple-element.56.refs_0_), channel_id=1, source_target_pairs={{128,0},{192,64},{0,128},{64,192},{129,1},{193,65},{1,129},{65,193... | collective-permute-start | bytes 196616 | tf_op jit(solution)/shard_map/ppermute | solution.py:181
  78.6 1.6 %copy-done.5 = bf16[512,2048]{1,0:T(8,128)(2,1)S(1)} copy-done((bf16[512,2048]{1,0:T(8,128)(2,1)S(1)}, bf16[512,2048]{1,0:T(8,128)(2,1)}, u32[]{:S(2)}) %copy-start.5) | copy-done | bytes 2097176
  80.5 1.6 %collective-permute-done.12.refs_1_ = bf16[64,512]{1,0:T(8,128)(2,1)S(1)} collective-permute-done((bf16[64,512]{1,0:T(8,128)(2,1)S(1)}, bf16[64,512]{1,0:T(8,128)(2,1)S(1)}, u32[]{:S(2)}, u32[]{:S(2)}) %collective-permute-start.12) | collective-permute-done | bytes 65568 | tf_op jit(solution)/shard_map/ppermute | solution.py:181
  82.4 1.1 %shard_map.134 = bf16[64,512]{1,0:T(8,128)(2,1)} custom-call(s32[1]{0:T(128)} %bitcast.k_ref, f32[64,512]{1,0:T(8,128)S(1)} %shard_map.133.acc_ref, bf16[64,512]{1,0:T(8,128)(2,1)S(1)} %collective-permute-done.13.a_ref, bf16[64,512]{1,0:T(8,128)(2,1)S(1)} %collective-permute-done.14.b_ref, bf16[512,2048]{1,0:T(8,128)(2,1)S(1)} %copy-done.5), custom_call_target="tpu_custom_call" | custom-call | flops 1000000000 | bytes 100000 | tf_op jit(solution)/shard_map/pallas_call | solution.py:164
  83.5 14.8 %all-to-all-done.1 = bf16[64,16,512]{2,1,0:T(8,128)(2,1)S(1)} async-done(((bf16[64,16,512]{2,1,0:T(8,128)(2,1)}), bf16[64,16,512]{2,1,0:T(8,128)(2,1)S(1)}, u32[]{:S(2)}, u32[]{:S(2)}) %all-to-all-start.1) | async-done | bytes 1048608 | tf_op jit(solution)/shard_map/all_to_all | solution.py:389
  98.7 2.2 %collective-permute-start.17 = (bf16[128,512]{1,0:T(8,128)(2,1)S(1)}, bf16[128,512]{1,0:T(8,128)(2,1)S(1)}, u32[]{:S(2)}, u32[]{:S(2)}) collective-permute-start(bf16[128,512]{1,0:T(8,128)(2,1)S(1)} %shard_map.135.refs_0_), channel_id=1, source_target_pairs={{128,0},{192,64},{0,128},{64,192},{129,1},{193,65},{1,129},{65,193... | collective-permute-start | bytes 393224 | tf_op jit(solution)/shard_map/ppermute | solution.py:181
  100.9 1.1 %collective-permute-start.16 = (bf16[128,512]{1,0:T(8,128)(2,1)S(1)}, bf16[128,512]{1,0:T(8,128)(2,1)S(1)}, u32[]{:S(2)}, u32[]{:S(2)}) collective-permute-start(bf16[128,512]{1,0:T(8,128)(2,1)S(1)} %shard_map.135.refs_0_), channel_id=1, source_target_pairs={{64,0},{128,64},{192,128},{0,192},{65,1},{129,65},{193,129},{1,193... | collective-permute-start | bytes 393224 | tf_op jit(solution)/shard_map/ppermute | solution.py:181
  102.0 2.2 %copy-done.2 = bf16[1024,2048]{1,0:T(8,128)(2,1)S(1)} copy-done((bf16[1024,2048]{1,0:T(8,128)(2,1)S(1)}, bf16[1024,2048]{1,0:T(8,128)(2,1)}, u32[]{:S(2)}) %copy-start.2) | copy-done | bytes 4194328
  105.4 1.4 %collective-permute-done.17.b_ref = bf16[128,512]{1,0:T(8,128)(2,1)S(1)} collective-permute-done((bf16[128,512]{1,0:T(8,128)(2,1)S(1)}, bf16[128,512]{1,0:T(8,128)(2,1)S(1)}, u32[]{:S(2)}, u32[]{:S(2)}) %collective-permute-start.17) | collective-permute-done | bytes 131104 | tf_op jit(solution)/shard_map/ppermute | solution.py:181
  107.5 1.5 %shard_map.138 = bf16[128,1024]{1,0:T(8,128)(2,1)} custom-call(s32[1]{0:T(128)} %bitcast.k_ref, f32[128,1024]{1,0:T(8,128)S(1)} %shard_map.137.acc_ref, bf16[128,512]{1,0:T(8,128)(2,1)S(1)} %collective-permute-done.16.a_ref, bf16[128,512]{1,0:T(8,128)(2,1)S(1)} %collective-permute-done.17.b_ref, bf16[1024,2048]{1,0:T(8,128)(2,1)S(1)} %copy-done.2), custom_call_target="tpu_custom_call" | custom-call | flops 1000000000 | bytes 100000 | tf_op jit(solution)/shard_map/pallas_call | solution.py:164
  (72 shorter events, 11.7 us)
Async XLA Ops:
  0.6 32.4 %copy-start = (s32[1,1024]{1,0:T(1,128)S(1)}, s32[1,1024]{1,0:T(1,128)}, u32[]{:S(2)}) copy-start(s32[1,1024]{1,0:T(1,128)} %param.15) | copy-start | bytes 12292
  0.6 9.4 %copy-start.10 = (s32[64]{0:T(128)S(1)}, s32[64]{0:T(128)}, u32[]{:S(2)}) copy-start(s32[64]{0:T(128)} %constant.76) | copy-start | bytes 772
  0.7 9.4 %copy-start.3 = (bf16[128,1024]{1,0:T(8,128)(2,1)S(1)}, bf16[128,1024]{1,0:T(8,128)(2,1)}, u32[]{:S(2)}) copy-start(bf16[128,1024]{1,0:T(8,128)(2,1)} %x_ref.3) | copy-start | bytes 786436
  0.7 11.9 %copy-start.9 = (s32[1,64,16]{1,2,0:T(8,128)S(1)}, s32[1,64,16]{1,2,0:T(8,128)}, u32[]{:S(2)}) copy-start(s32[1,64,16]{1,2,0:T(8,128)} %param.14) | copy-start | bytes 12292
  3.7 9.9 %collective-permute-start = (bf16[128,512]{1,0:T(8,128)(2,1)}, bf16[128,512]{1,0:T(8,128)(2,1)S(1)}, u32[]{:S(2)}, u32[]{:S(2)}) collective-permute-start(bf16[128,512]{1,0:T(8,128)(2,1)} %get-tuple-element.35), channel_id=1, source_target_pairs={{0,128},{64,192},{128,0},{192,64},{1,129},{65,193},{129,1},{193,65... | collective-permute-start | bytes 393224 | tf_op jit(solution)/shard_map/ppermute | solution.py:176
  7.4 7.4 %collective-permute-start.1 = (bf16[128,512]{1,0:T(8,128)(2,1)}, bf16[128,512]{1,0:T(8,128)(2,1)S(1)}, u32[]{:S(2)}, u32[]{:S(2)}) collective-permute-start(bf16[128,512]{1,0:T(8,128)(2,1)} %get-tuple-element.36), channel_id=1, source_target_pairs={{0,64},{64,128},{128,192},{192,0},{1,65},{65,129},{129,193},{193,1... | collective-permute-start | bytes 393224 | tf_op jit(solution)/shard_map/ppermute | solution.py:176
  7.7 7.1 %collective-permute-start.2 = (bf16[128,512]{1,0:T(8,128)(2,1)}, bf16[128,512]{1,0:T(8,128)(2,1)S(1)}, u32[]{:S(2)}, u32[]{:S(2)}) collective-permute-start(bf16[128,512]{1,0:T(8,128)(2,1)} %get-tuple-element.37), channel_id=1, source_target_pairs={{0,192},{64,0},{128,64},{192,128},{1,193},{65,1},{129,65},{193,129... | collective-permute-start | bytes 393224 | tf_op jit(solution)/shard_map/ppermute | solution.py:176
  10.1 2.2 %copy-start.1 = (bf16[1024,2048]{1,0:T(8,128)(2,1)S(1)}, bf16[1024,2048]{1,0:T(8,128)(2,1)}, u32[]{:S(2)}) copy-start(bf16[1024,2048]{1,0:T(8,128)(2,1)} %w_ref.11) | copy-start | bytes 12582916
  13.4 16.3 %copy-start.8 = (s32[64,7]{0,1:T(8,128)S(1)}, s32[64,7]{0,1:T(8,128)}, u32[]{:S(2)}) copy-start(s32[64,7]{0,1:T(8,128)} %param.16) | copy-start | bytes 5380
  13.4 16.4 %copy-start.7 = (s32[64]{0:T(128)S(1)}, s32[64]{0:T(128)}, u32[]{:S(2)}) copy-start(s32[64]{0:T(128)} %constant.64.clone) | copy-start | bytes 772
  16.1 37.0 %all-to-all-start = ((bf16[64,16,512]{2,1,0:T(8,128)(2,1)}), bf16[64,16,512]{2,1,0:T(8,128)(2,1)S(1)}, u32[]{:S(2)}, u32[]{:S(2)}) async-start(bf16[64,16,512]{2,1,0:T(8,128)(2,1)} %bitcast.2), calls=%async_computation | async-start | bytes 2097152 | tf_op jit(solution)/shard_map/all_to_all | solution.py:389
  29.8 5.5 %copy-start.11 = (f32[64]{0:T(128)S(1)}, f32[64]{0:T(128)}, u32[]{:S(2)}) copy-start(f32[64]{0:T(128)} %param.17) | copy-start | bytes 772
  29.8 5.7 %copy-start.6 = (bf16[64,512]{1,0:T(8,128)(2,1)S(1)}, bf16[64,512]{1,0:T(8,128)(2,1)}, u32[]{:S(2)}) copy-start(bf16[64,512]{1,0:T(8,128)(2,1)} %x_ref.5) | copy-start | bytes 196612
  35.5 1.6 %copy-start.4 = (bf16[512,2048]{1,0:T(8,128)(2,1)S(1)}, bf16[512,2048]{1,0:T(8,128)(2,1)}, u32[]{:S(2)}) copy-start(bf16[512,2048]{1,0:T(8,128)(2,1)} %w_ref.10) | copy-start | bytes 6291460
  38.3 5.0 %collective-permute-start.3 = (bf16[64,512]{1,0:T(8,128)(2,1)S(1)}, bf16[64,512]{1,0:T(8,128)(2,1)S(1)}, u32[]{:S(2)}, u32[]{:S(2)}) collective-permute-start(bf16[64,512]{1,0:T(8,128)(2,1)S(1)} %get-tuple-element.41), channel_id=1, source_target_pairs={{0,128},{64,192},{128,0},{192,64},{1,129},{65,193},{129,1},{193,65... | collective-permute-start | bytes 196616 | tf_op jit(solution)/shard_map/ppermute | solution.py:176
  39.9 5.0 %collective-permute-start.4 = (bf16[64,512]{1,0:T(8,128)(2,1)S(1)}, bf16[64,512]{1,0:T(8,128)(2,1)S(1)}, u32[]{:S(2)}, u32[]{:S(2)}) collective-permute-start(bf16[64,512]{1,0:T(8,128)(2,1)S(1)} %get-tuple-element.42), channel_id=1, source_target_pairs={{0,64},{64,128},{128,192},{192,0},{1,65},{65,129},{129,193},{193,1... | collective-permute-start | bytes 196616 | tf_op jit(solution)/shard_map/ppermute | solution.py:176
  41.6 3.6 %collective-permute-start.5 = (bf16[64,512]{1,0:T(8,128)(2,1)S(1)}, bf16[64,512]{1,0:T(8,128)(2,1)S(1)}, u32[]{:S(2)}, u32[]{:S(2)}) collective-permute-start(bf16[64,512]{1,0:T(8,128)(2,1)S(1)} %get-tuple-element.43), channel_id=1, source_target_pairs={{0,192},{64,0},{128,64},{192,128},{1,193},{65,1},{129,65},{193,129... | collective-permute-start | bytes 196616 | tf_op jit(solution)/shard_map/ppermute | solution.py:176
  45.5 12.5 %collective-permute-start.8 = (f32[144,128]{1,0:T(8,128)S(1)}, f32[144,128]{1,0:T(8,128)S(1)}, u32[]{:S(2)}, u32[]{:S(2)}) collective-permute-start(f32[144,128]{1,0:T(8,128)S(1)} %shard_map.128.refs_0_), channel_id=1, source_target_pairs={{192,0},{0,64},{64,128},{128,192},{193,1},{1,65},{65,129},{129,193... | collective-permute-start | bytes 221192 | tf_op jit(solution)/shard_map/ppermute | solution.py:181
  46.2 11.8 %collective-permute-start.7 = (f32[144,128]{1,0:T(8,128)S(1)}, f32[144,128]{1,0:T(8,128)S(1)}, u32[]{:S(2)}, u32[]{:S(2)}) collective-permute-start(f32[144,128]{1,0:T(8,128)S(1)} %shard_map.128.refs_0_), channel_id=1, source_target_pairs={{128,0},{192,64},{0,128},{64,192},{129,1},{193,65},{1,129},{65,193... | collective-permute-start | bytes 221192 | tf_op jit(solution)/shard_map/ppermute | solution.py:181
  49.1 8.9 %collective-permute-start.6 = (f32[144,128]{1,0:T(8,128)S(1)}, f32[144,128]{1,0:T(8,128)S(1)}, u32[]{:S(2)}, u32[]{:S(2)}) collective-permute-start(f32[144,128]{1,0:T(8,128)S(1)} %shard_map.128.refs_0_), channel_id=1, source_target_pairs={{64,0},{128,64},{192,128},{0,192},{65,1},{129,65},{193,129},{1,193... | collective-permute-start | bytes 221192 | tf_op jit(solution)/shard_map/ppermute | solution.py:181
  54.1 3.9 %collective-permute-start.11 = (f32[8,128]{1,0:T(8,128)S(1)}, f32[8,128]{1,0:T(8,128)S(1)}, u32[]{:S(2)}, u32[]{:S(2)}) collective-permute-start(f32[8,128]{1,0:T(8,128)S(1)} %shard_map.129.refs_4_), channel_id=1, source_target_pairs={{192,0},{0,64},{64,128},{128,192},{193,1},{1,65},{65,129},{129,193... | collective-permute-start | bytes 12296 | tf_op jit(solution)/shard_map/ppermute | solution.py:181
  55.2 4.0 %collective-permute-start.10 = (f32[8,128]{1,0:T(8,128)S(1)}, f32[8,128]{1,0:T(8,128)S(1)}, u32[]{:S(2)}, u32[]{:S(2)}) collective-permute-start(f32[8,128]{1,0:T(8,128)S(1)} %shard_map.129.refs_4_), channel_id=1, source_target_pairs={{128,0},{192,64},{0,128},{64,192},{129,1},{193,65},{1,129},{65,193... | collective-permute-start | bytes 12296 | tf_op jit(solution)/shard_map/ppermute | solution.py:181
  58.0 2.7 %collective-permute-start.9 = (f32[8,128]{1,0:T(8,128)S(1)}, f32[8,128]{1,0:T(8,128)S(1)}, u32[]{:S(2)}, u32[]{:S(2)}) collective-permute-start(f32[8,128]{1,0:T(8,128)S(1)} %shard_map.129.refs_4_), channel_id=1, source_target_pairs={{64,0},{128,64},{192,128},{0,192},{65,1},{129,65},{193,129},{1,193... | collective-permute-start | bytes 12296 | tf_op jit(solution)/shard_map/ppermute | solution.py:181
  62.4 35.9 %all-to-all-start.1 = ((bf16[64,16,512]{2,1,0:T(8,128)(2,1)}), bf16[64,16,512]{2,1,0:T(8,128)(2,1)S(1)}, u32[]{:S(2)}, u32[]{:S(2)}) async-start(bf16[64,16,512]{2,1,0:T(8,128)(2,1)} %bitcast.7), calls=%async_computation.1 | async-start | bytes 2097152 | tf_op jit(solution)/shard_map/all_to_all | solution.py:389
  75.3 7.0 %collective-permute-start.14 = (bf16[64,512]{1,0:T(8,128)(2,1)S(1)}, bf16[64,512]{1,0:T(8,128)(2,1)S(1)}, u32[]{:S(2)}, u32[]{:S(2)}) collective-permute-start(bf16[64,512]{1,0:T(8,128)(2,1)S(1)} %get-tuple-element.56.refs_0_), channel_id=1, source_target_pairs={{128,0},{192,64},{0,128},{64,192},{129,1},{193,65},{1,129},{65,193... | collective-permute-start | bytes 196616 | tf_op jit(solution)/shard_map/ppermute | solution.py:181
  76.7 5.7 %collective-permute-start.13 = (bf16[64,512]{1,0:T(8,128)(2,1)S(1)}, bf16[64,512]{1,0:T(8,128)(2,1)S(1)}, u32[]{:S(2)}, u32[]{:S(2)}) collective-permute-start(bf16[64,512]{1,0:T(8,128)(2,1)S(1)} %get-tuple-element.56.refs_0_), channel_id=1, source_target_pairs={{64,0},{128,64},{192,128},{0,192},{65,1},{129,65},{193,129},{1,193... | collective-permute-start | bytes 196616 | tf_op jit(solution)/shard_map/ppermute | solution.py:181
  77.3 4.8 %collective-permute-start.12 = (bf16[64,512]{1,0:T(8,128)(2,1)S(1)}, bf16[64,512]{1,0:T(8,128)(2,1)S(1)}, u32[]{:S(2)}, u32[]{:S(2)}) collective-permute-start(bf16[64,512]{1,0:T(8,128)(2,1)S(1)} %get-tuple-element.56.refs_0_), channel_id=1, source_target_pairs={{192,0},{0,64},{64,128},{128,192},{193,1},{1,65},{65,129},{129,193... | collective-permute-start | bytes 196616 | tf_op jit(solution)/shard_map/ppermute | solution.py:181
  78.6 1.6 %copy-start.5 = (bf16[512,2048]{1,0:T(8,128)(2,1)S(1)}, bf16[512,2048]{1,0:T(8,128)(2,1)}, u32[]{:S(2)}) copy-start(bf16[512,2048]{1,0:T(8,128)(2,1)} %w_ref.10) | copy-start | bytes 6291460
  98.6 6.3 %collective-permute-start.15 = (bf16[128,512]{1,0:T(8,128)(2,1)S(1)}, bf16[128,512]{1,0:T(8,128)(2,1)S(1)}, u32[]{:S(2)}, u32[]{:S(2)}) collective-permute-start(bf16[128,512]{1,0:T(8,128)(2,1)S(1)} %shard_map.135.refs_0_), channel_id=1, source_target_pairs={{192,0},{0,64},{64,128},{128,192},{193,1},{1,65},{65,129},{129,193... | collective-permute-start | bytes 393224 | tf_op jit(solution)/shard_map/ppermute | solution.py:181
  98.7 8.1 %collective-permute-start.17 = (bf16[128,512]{1,0:T(8,128)(2,1)S(1)}, bf16[128,512]{1,0:T(8,128)(2,1)S(1)}, u32[]{:S(2)}, u32[]{:S(2)}) collective-permute-start(bf16[128,512]{1,0:T(8,128)(2,1)S(1)} %shard_map.135.refs_0_), channel_id=1, source_target_pairs={{128,0},{192,64},{0,128},{64,192},{129,1},{193,65},{1,129},{65,193... | collective-permute-start | bytes 393224 | tf_op jit(solution)/shard_map/ppermute | solution.py:181
  100.9 6.6 %collective-permute-start.16 = (bf16[128,512]{1,0:T(8,128)(2,1)S(1)}, bf16[128,512]{1,0:T(8,128)(2,1)S(1)}, u32[]{:S(2)}, u32[]{:S(2)}) collective-permute-start(bf16[128,512]{1,0:T(8,128)(2,1)S(1)} %shard_map.135.refs_0_), channel_id=1, source_target_pairs={{64,0},{128,64},{192,128},{0,192},{65,1},{129,65},{193,129},{1,193... | collective-permute-start | bytes 393224 | tf_op jit(solution)/shard_map/ppermute | solution.py:181
  102.0 2.2 %copy-start.2 = (bf16[1024,2048]{1,0:T(8,128)(2,1)S(1)}, bf16[1024,2048]{1,0:T(8,128)(2,1)}, u32[]{:S(2)}) copy-start(bf16[1024,2048]{1,0:T(8,128)(2,1)} %w_ref.11) | copy-start | bytes 12582916

commit v11 on v10

--- a/solution.py
+++ b/solution.py
@@ -12,7 +12,7 @@
 NT = (((1,), (1,)), ((), ()))
 TN = (((0,), (0,)), ((), ()))
 N_PHASE = 4
-CHUNKS = 4
+CHUNKS = 8
 DP_ORDER = [45, 29, 43, 61, 34, 33, 31, 40, 26, 62, 22, 2, 11, 28, 54, 4, 10, 35, 52, 46, 30, 7, 14, 27, 63, 55, 41, 42, 58, 18, 60, 32, 15, 5, 16, 20, 56, 8, 13, 25, 37, 17, 48, 51, 57, 38, 1, 12, 49, 24, 6, 23, 36, 50, 21, 19, 9, 39, 59, 3, 0, 53, 47, 44]
 DP_PLACE = [60, 46, 11, 59, 15, 33, 50, 21, 37, 56, 16, 12, 47, 38, 22, 32, 34, 41, 29, 55, 35, 54, 10, 51, 49, 39, 8, 23, 13, 1, 20, 6, 31, 5, 4, 17, 52, 40, 45, 57, 7, 26, 27, 2, 63, 0, 19, 62, 42, 48, 53, 43, 18, 61, 14, 25, 36, 44, 28, 58, 30, 3, 9, 24]
 cost = pl.CostEstimate(flops=10**9, bytes_accessed=10**5, transcendentals=0)

time: 110 us -> 110 us (level)
  no operation moved by 1% of the time
where the time goes in v11:
time: 110 us; the launch traced here: 109 us
  starting transfers between devices  50.3 us (46%)
  waiting for transfers between devices  28.8 us (26%)
  local copies, waits for them, and re-layouts  14.4 us (13%)
  Pallas kernels  14.3 us (13%)
  between operations  1.12 us (1%)
    all_to_all x2, starting transfers between devices, exchange(): lax.all_to_all(blocks, 'dp', split_axis=0, concat_axis=0, tiled=True, axi...  26.1 us
    all_to_all x2, waiting for transfers between devices, exchange(): lax.all_to_all(blocks, 'dp', split_axis=0, concat_axis=0, tiled=True, axi...  18.7 us
    ppermute x12, starting transfers between devices, gather_blocks(): lax.ppermute(x, 'phase', [((i + s) % N_PHASE, i) for i in range(N_PHASE)])  13.6 us
    ppermute x6, starting transfers between devices, send(): lax.ppermute(block, 'phase', [(i, (i + s) % N_PHASE) for i in range(N_PHA...  10.6 us
    unnamed x24, local copies, waits for them, and re-layouts  7.6 us
    ppermute x12, waiting for transfers between devices, gather_blocks(): lax.ppermute(x, 'phase', [((i + s) % N_PHASE, i) for i in range(N_PHASE)])  6.57 us
    pallas_call x2, Pallas kernels, project_sends(): pl.pallas_call(body, in_specs=[pl.BlockSpec(memory_space=pltpu.SMEM), hbm...  4.23 us
    ppermute x6, waiting for transfers between devices, send(): lax.ppermute(block, 'phase', [(i, (i + s) % N_PHASE) for i in range(N_PHA...  3.53 us
  transfers between devices with their start and end apart: 20, of which 12 were waited for; matrix products, arithmetic and copies ran while one was open for 6% of the time, Pallas kernels for 6%

profile of v11, /device:TPU:1, one launch (start us, length us, event | category | flops | bytes accessed | tf_op | source)
XLA Modules:
  0.0 109.2 jit_solution(12114653807291730412)
XLA Ops:
  0.7 3.0 %shard_map.122 = (bf16[128,512]{1,0:T(8,128)(2,1)}, bf16[128,512]{1,0:T(8,128)(2,1)}, bf16[128,512]{1,0:T(8,128)(2,1)}) custom-call(s32[1]{0:T(128)} %bitcast.k_ref, bf16[128,1024]{1,0:T(8,128)(2,1)} %x_ref.3, bf16[1024,2048]{1,0:T(8,128)(2,1)} %w_ref.11), custom_call_target="tpu_custom_call" | custom-call | flops 1000000000 | bytes 100000 | tf_op jit(solution)/shard_map/pallas_call | solution.py:75
  3.7 3.7 %collective-permute-start = (bf16[128,512]{1,0:T(8,128)(2,1)}, bf16[128,512]{1,0:T(8,128)(2,1)S(1)}, u32[]{:S(2)}, u32[]{:S(2)}) collective-permute-start(bf16[128,512]{1,0:T(8,128)(2,1)} %get-tuple-element.35), channel_id=1, source_target_pairs={{0,128},{64,192},{128,0},{192,64},{1,129},{65,193},{129,1},{193,65... | collective-permute-start | bytes 393224 | tf_op jit(solution)/shard_map/ppermute | solution.py:176
  7.7 2.4 %collective-permute-start.2 = (bf16[128,512]{1,0:T(8,128)(2,1)}, bf16[128,512]{1,0:T(8,128)(2,1)S(1)}, u32[]{:S(2)}, u32[]{:S(2)}) collective-permute-start(bf16[128,512]{1,0:T(8,128)(2,1)} %get-tuple-element.37), channel_id=1, source_target_pairs={{0,192},{64,0},{128,64},{192,128},{1,193},{65,1},{129,65},{193,129... | collective-permute-start | bytes 393224 | tf_op jit(solution)/shard_map/ppermute | solution.py:176
  10.1 2.2 %copy-done.1 = bf16[1024,2048]{1,0:T(8,128)(2,1)S(1)} copy-done((bf16[1024,2048]{1,0:T(8,128)(2,1)S(1)}, bf16[1024,2048]{1,0:T(8,128)(2,1)}, u32[]{:S(2)}) %copy-start.1) | copy-done | bytes 4194328
  13.6 1.1 %collective-permute-done.1.c = bf16[128,512]{1,0:T(8,128)(2,1)S(1)} collective-permute-done((bf16[128,512]{1,0:T(8,128)(2,1)}, bf16[128,512]{1,0:T(8,128)(2,1)S(1)}, u32[]{:S(2)}, u32[]{:S(2)}) %collective-permute-start.1) | collective-permute-done | bytes 131104 | tf_op jit(solution)/shard_map/ppermute | solution.py:176
  14.8 1.3 %shard_map.124 = (f32[128,512]{1,0:T(8,128)S(1)}, bf16[1024,512]{1,0:T(8,128)(2,1)}) custom-call(f32[128,512]{1,0:T(8,128)S(1)} %shard_map.121.a, bf16[128,512]{1,0:T(8,128)(2,1)S(1)} %collective-permute-done.b, bf16[128,512]{1,0:T(8,128)(2,1)S(1)} %collective-permute-done.1.c, bf16[128,512]{1,0:T(8,128)(2,1)S(1)} %collective-permute-done.2.d, ...), custom_call_target="tpu_custom_call" | custom-call | flops 1000000000 | bytes 100000 | tf_op jit(solution)/shard_map/pallas_call | solution.py:228
  16.1 13.5 %all-to-all-start = ((bf16[64,16,512]{2,1,0:T(8,128)(2,1)}), bf16[64,16,512]{2,1,0:T(8,128)(2,1)S(1)}, u32[]{:S(2)}, u32[]{:S(2)}) async-start(bf16[64,16,512]{2,1,0:T(8,128)(2,1)} %bitcast.2), calls=%async_computation | async-start | bytes 2097152 | tf_op jit(solution)/shard_map/all_to_all | solution.py:389
  29.8 3.0 %gather_fusion.2 = s32[448]{0:T(512)S(1)} fusion(s32[64]{0:T(128)S(1)} %copy-done.7, s32[1024]{0:T(1024)S(1)} %pad_clamp_fusion), kind=kCustom, calls=%fused_computation.2 | custom fusion | bytes 5376 | tf_op jit(solution)/shard_map/gather | solution.py:383
  33.0 2.1 %gather_fusion.1 = s32[448]{0:T(512)S(1)} fusion(s32[1024]{0:T(1024)S(1)} %bitcast.42, s32[1024]{0:T(1024)S(1)} %pad_clamp_fusion.1), kind=kCustom, calls=%fused_computation.1 | custom fusion | bytes 5376 | tf_op jit(solution)/shard_map/jit(_take)/gather | solution.py:411
  35.5 1.6 %copy-done.4 = bf16[512,2048]{1,0:T(8,128)(2,1)S(1)} copy-done((bf16[512,2048]{1,0:T(8,128)(2,1)S(1)}, bf16[512,2048]{1,0:T(8,128)(2,1)}, u32[]{:S(2)}) %copy-start.4) | copy-done | bytes 2097176
  37.1 1.2 %shard_map.126 = (bf16[64,512]{1,0:T(8,128)(2,1)S(1)}, bf16[64,512]{1,0:T(8,128)(2,1)S(1)}, bf16[64,512]{1,0:T(8,128)(2,1)S(1)}) custom-call(s32[1]{0:T(128)} %bitcast.k_ref, bf16[64,512]{1,0:T(8,128)(2,1)S(1)} %copy-done.6, bf16[512,2048]{1,0:T(8,128)(2,1)S(1)} %copy-done.4), custom_call_target="tpu_custom_call" | custom-call | flops 1000000000 | bytes 100000 | tf_op jit(solution)/shard_map/pallas_call | solution.py:75
  38.3 1.6 %collective-permute-start.3 = (bf16[64,512]{1,0:T(8,128)(2,1)S(1)}, bf16[64,512]{1,0:T(8,128)(2,1)S(1)}, u32[]{:S(2)}, u32[]{:S(2)}) collective-permute-start(bf16[64,512]{1,0:T(8,128)(2,1)S(1)} %get-tuple-element.41), channel_id=1, source_target_pairs={{0,128},{64,192},{128,0},{192,64},{1,129},{65,193},{129,1},{193,65... | collective-permute-start | bytes 196616 | tf_op jit(solution)/shard_map/ppermute | solution.py:176
  39.9 1.7 %collective-permute-start.4 = (bf16[64,512]{1,0:T(8,128)(2,1)S(1)}, bf16[64,512]{1,0:T(8,128)(2,1)S(1)}, u32[]{:S(2)}, u32[]{:S(2)}) collective-permute-start(bf16[64,512]{1,0:T(8,128)(2,1)S(1)} %get-tuple-element.42), channel_id=1, source_target_pairs={{0,64},{64,128},{128,192},{192,0},{1,65},{65,129},{129,193},{193,1... | collective-permute-start | bytes 196616 | tf_op jit(solution)/shard_map/ppermute | solution.py:176
  43.3 1.7 %collective-permute-done.4.b = bf16[64,512]{1,0:T(8,128)(2,1)S(1)} collective-permute-done((bf16[64,512]{1,0:T(8,128)(2,1)S(1)}, bf16[64,512]{1,0:T(8,128)(2,1)S(1)}, u32[]{:S(2)}, u32[]{:S(2)}) %collective-permute-start.4) | collective-permute-done | bytes 65568 | tf_op jit(solution)/shard_map/ppermute | solution.py:176
  46.2 2.9 %collective-permute-start.7 = (f32[144,128]{1,0:T(8,128)S(1)}, f32[144,128]{1,0:T(8,128)S(1)}, u32[]{:S(2)}, u32[]{:S(2)}) collective-permute-start(f32[144,128]{1,0:T(8,128)S(1)} %shard_map.128.refs_0_), channel_id=1, source_target_pairs={{128,0},{192,64},{0,128},{64,192},{129,1},{193,65},{1,129},{65,193... | collective-permute-start | bytes 221192 | tf_op jit(solution)/shard_map/ppermute | solution.py:181
  49.1 3.9 %all-to-all-done = bf16[64,16,512]{2,1,0:T(8,128)(2,1)S(1)} async-done(((bf16[64,16,512]{2,1,0:T(8,128)(2,1)}), bf16[64,16,512]{2,1,0:T(8,128)(2,1)S(1)}, u32[]{:S(2)}, u32[]{:S(2)}) %all-to-all-start) | async-done | bytes 1048608 | tf_op jit(solution)/shard_map/all_to_all | solution.py:389
  53.1 1.1 shard_map.129.refs_4_
  55.2 2.9 %collective-permute-start.10 = (f32[8,128]{1,0:T(8,128)S(1)}, f32[8,128]{1,0:T(8,128)S(1)}, u32[]{:S(2)}, u32[]{:S(2)}) collective-permute-start(f32[8,128]{1,0:T(8,128)S(1)} %shard_map.129.refs_4_), channel_id=1, source_target_pairs={{128,0},{192,64},{0,128},{64,192},{129,1},{193,65},{1,129},{65,193... | collective-permute-start | bytes 12296 | tf_op jit(solution)/shard_map/ppermute | solution.py:181
  58.1 1.1 collective-permute-done.10.refs_6_
  59.1 1.6 %collective-permute-done.9.refs_5_ = f32[8,128]{1,0:T(8,128)S(1)} collective-permute-done((f32[8,128]{1,0:T(8,128)S(1)}, f32[8,128]{1,0:T(8,128)S(1)}, u32[]{:S(2)}, u32[]{:S(2)}) %collective-permute-start.9) | collective-permute-done | bytes 4128 | tf_op jit(solution)/shard_map/ppermute | solution.py:181
  60.7 1.7 %shard_map.130 = (bf16[1024,512]{1,0:T(8,128)(2,1)}, bf16[1024,128]{1,0:T(8,128)(2,1)S(1)}, bf16[128,128]{1,0:T(8,128)(2,1)S(1)}, f32[8,128]{1,0:T(8,128)S(1)}, f32[128,128]{1,0:T(8,128)S(1)}) custom-call(f32[144,128]{1,0:T(8,128)S(1)} %shard_map.128.refs_0_, f32[144,128]{1,0:T(8,128)S(1)} %collective-permute-done.6.refs_1_, ...), custom_call_target="tpu_custom_call" | custom-call | flops 1000000000 | bytes 100000 | tf_op jit(solution)/shard_map/pallas_call | solution.py:422
  62.4 12.5 %all-to-all-start.1 = ((bf16[64,16,512]{2,1,0:T(8,128)(2,1)}), bf16[64,16,512]{2,1,0:T(8,128)(2,1)S(1)}, u32[]{:S(2)}, u32[]{:S(2)}) async-start(bf16[64,16,512]{2,1,0:T(8,128)(2,1)} %bitcast.7), calls=%async_computation.1 | async-start | bytes 2097152 | tf_op jit(solution)/shard_map/all_to_all | solution.py:389
  75.3 1.3 %collective-permute-start.14 = (bf16[64,512]{1,0:T(8,128)(2,1)S(1)}, bf16[64,512]{1,0:T(8,128)(2,1)S(1)}, u32[]{:S(2)}, u32[]{:S(2)}) collective-permute-start(bf16[64,512]{1,0:T(8,128)(2,1)S(1)} %get-tuple-element.56.refs_0_), channel_id=1, source_target_pairs={{128,0},{192,64},{0,128},{64,192},{129,1},{193,65},{1,129},{65,193... | collective-permute-start | bytes 196616 | tf_op jit(solution)/shard_map/ppermute | solution.py:181
  78.6 1.6 %copy-done.5 = bf16[512,2048]{1,0:T(8,128)(2,1)S(1)} copy-done((bf16[512,2048]{1,0:T(8,128)(2,1)S(1)}, bf16[512,2048]{1,0:T(8,128)(2,1)}, u32[]{:S(2)}) %copy-start.5) | copy-done | bytes 2097176
  80.5 1.6 %collective-permute-done.12.refs_1_ = bf16[64,512]{1,0:T(8,128)(2,1)S(1)} collective-permute-done((bf16[64,512]{1,0:T(8,128)(2,1)S(1)}, bf16[64,512]{1,0:T(8,128)(2,1)S(1)}, u32[]{:S(2)}, u32[]{:S(2)}) %collective-permute-start.12) | collective-permute-done | bytes 65568 | tf_op jit(solution)/shard_map/ppermute | solution.py:181
  82.4 1.1 %shard_map.134 = bf16[64,512]{1,0:T(8,128)(2,1)} custom-call(s32[1]{0:T(128)} %bitcast.k_ref, f32[64,512]{1,0:T(8,128)S(1)} %shard_map.133.acc_ref, bf16[64,512]{1,0:T(8,128)(2,1)S(1)} %collective-permute-done.13.a_ref, bf16[64,512]{1,0:T(8,128)(2,1)S(1)} %collective-permute-done.14.b_ref, bf16[512,2048]{1,0:T(8,128)(2,1)S(1)} %copy-done.5), custom_call_target="tpu_custom_call" | custom-call | flops 1000000000 | bytes 100000 | tf_op jit(solution)/shard_map/pallas_call | solution.py:164
  83.5 14.8 %all-to-all-done.1 = bf16[64,16,512]{2,1,0:T(8,128)(2,1)S(1)} async-done(((bf16[64,16,512]{2,1,0:T(8,128)(2,1)}), bf16[64,16,512]{2,1,0:T(8,128)(2,1)S(1)}, u32[]{:S(2)}, u32[]{:S(2)}) %all-to-all-start.1) | async-done | bytes 1048608 | tf_op jit(solution)/shard_map/all_to_all | solution.py:389
  98.7 2.2 %collective-permute-start.17 = (bf16[128,512]{1,0:T(8,128)(2,1)S(1)}, bf16[128,512]{1,0:T(8,128)(2,1)S(1)}, u32[]{:S(2)}, u32[]{:S(2)}) collective-permute-start(bf16[128,512]{1,0:T(8,128)(2,1)S(1)} %shard_map.135.refs_0_), channel_id=1, source_target_pairs={{128,0},{192,64},{0,128},{64,192},{129,1},{193,65},{1,129},{65,193... | collective-permute-start | bytes 393224 | tf_op jit(solution)/shard_map/ppermute | solution.py:181
  100.9 1.1 %collective-permute-start.16 = (bf16[128,512]{1,0:T(8,128)(2,1)S(1)}, bf16[128,512]{1,0:T(8,128)(2,1)S(1)}, u32[]{:S(2)}, u32[]{:S(2)}) collective-permute-start(bf16[128,512]{1,0:T(8,128)(2,1)S(1)} %shard_map.135.refs_0_), channel_id=1, source_target_pairs={{64,0},{128,64},{192,128},{0,192},{65,1},{129,65},{193,129},{1,193... | collective-permute-start | bytes 393224 | tf_op jit(solution)/shard_map/ppermute | solution.py:181
  102.0 2.2 %copy-done.2 = bf16[1024,2048]{1,0:T(8,128)(2,1)S(1)} copy-done((bf16[1024,2048]{1,0:T(8,128)(2,1)S(1)}, bf16[1024,2048]{1,0:T(8,128)(2,1)}, u32[]{:S(2)}) %copy-start.2) | copy-done | bytes 4194328
  105.4 1.4 %collective-permute-done.17.b_ref = bf16[128,512]{1,0:T(8,128)(2,1)S(1)} collective-permute-done((bf16[128,512]{1,0:T(8,128)(2,1)S(1)}, bf16[128,512]{1,0:T(8,128)(2,1)S(1)}, u32[]{:S(2)}, u32[]{:S(2)}) %collective-permute-start.17) | collective-permute-done | bytes 131104 | tf_op jit(solution)/shard_map/ppermute | solution.py:181
  107.5 1.5 %shard_map.138 = bf16[128,1024]{1,0:T(8,128)(2,1)} custom-call(s32[1]{0:T(128)} %bitcast.k_ref, f32[128,1024]{1,0:T(8,128)S(1)} %shard_map.137.acc_ref, bf16[128,512]{1,0:T(8,128)(2,1)S(1)} %collective-permute-done.16.a_ref, bf16[128,512]{1,0:T(8,128)(2,1)S(1)} %collective-permute-done.17.b_ref, bf16[1024,2048]{1,0:T(8,128)(2,1)S(1)} %copy-done.2), custom_call_target="tpu_custom_call" | custom-call | flops 1000000000 | bytes 100000 | tf_op jit(solution)/shard_map/pallas_call | solution.py:164
  (72 shorter events, 11.7 us)
Async XLA Ops:
  0.6 32.4 %copy-start = (s32[1,1024]{1,0:T(1,128)S(1)}, s32[1,1024]{1,0:T(1,128)}, u32[]{:S(2)}) copy-start(s32[1,1024]{1,0:T(1,128)} %param.15) | copy-start | bytes 12292
  0.6 9.4 %copy-start.10 = (s32[64]{0:T(128)S(1)}, s32[64]{0:T(128)}, u32[]{:S(2)}) copy-start(s32[64]{0:T(128)} %constant.76) | copy-start | bytes 772
  0.7 9.4 %copy-start.3 = (bf16[128,1024]{1,0:T(8,128)(2,1)S(1)}, bf16[128,1024]{1,0:T(8,128)(2,1)}, u32[]{:S(2)}) copy-start(bf16[128,1024]{1,0:T(8,128)(2,1)} %x_ref.3) | copy-start | bytes 786436
  0.7 11.9 %copy-start.9 = (s32[1,64,16]{1,2,0:T(8,128)S(1)}, s32[1,64,16]{1,2,0:T(8,128)}, u32[]{:S(2)}) copy-start(s32[1,64,16]{1,2,0:T(8,128)} %param.14) | copy-start | bytes 12292
  3.7 9.9 %collective-permute-start = (bf16[128,512]{1,0:T(8,128)(2,1)}, bf16[128,512]{1,0:T(8,128)(2,1)S(1)}, u32[]{:S(2)}, u32[]{:S(2)}) collective-permute-start(bf16[128,512]{1,0:T(8,128)(2,1)} %get-tuple-element.35), channel_id=1, source_target_pairs={{0,128},{64,192},{128,0},{192,64},{1,129},{65,193},{129,1},{193,65... | collective-permute-start | bytes 393224 | tf_op jit(solution)/shard_map/ppermute | solution.py:176
  7.4 7.4 %collective-permute-start.1 = (bf16[128,512]{1,0:T(8,128)(2,1)}, bf16[128,512]{1,0:T(8,128)(2,1)S(1)}, u32[]{:S(2)}, u32[]{:S(2)}) collective-permute-start(bf16[128,512]{1,0:T(8,128)(2,1)} %get-tuple-element.36), channel_id=1, source_target_pairs={{0,64},{64,128},{128,192},{192,0},{1,65},{65,129},{129,193},{193,1... | collective-permute-start | bytes 393224 | tf_op jit(solution)/shard_map/ppermute | solution.py:176
  7.7 7.1 %collective-permute-start.2 = (bf16[128,512]{1,0:T(8,128)(2,1)}, bf16[128,512]{1,0:T(8,128)(2,1)S(1)}, u32[]{:S(2)}, u32[]{:S(2)}) collective-permute-start(bf16[128,512]{1,0:T(8,128)(2,1)} %get-tuple-element.37), channel_id=1, source_target_pairs={{0,192},{64,0},{128,64},{192,128},{1,193},{65,1},{129,65},{193,129... | collective-permute-start | bytes 393224 | tf_op jit(solution)/shard_map/ppermute | solution.py:176
  10.1 2.2 %copy-start.1 = (bf16[1024,2048]{1,0:T(8,128)(2,1)S(1)}, bf16[1024,2048]{1,0:T(8,128)(2,1)}, u32[]{:S(2)}) copy-start(bf16[1024,2048]{1,0:T(8,128)(2,1)} %w_ref.11) | copy-start | bytes 12582916
  13.4 16.3 %copy-start.8 = (s32[64,7]{0,1:T(8,128)S(1)}, s32[64,7]{0,1:T(8,128)}, u32[]{:S(2)}) copy-start(s32[64,7]{0,1:T(8,128)} %param.16) | copy-start | bytes 5380
  13.4 16.4 %copy-start.7 = (s32[64]{0:T(128)S(1)}, s32[64]{0:T(128)}, u32[]{:S(2)}) copy-start(s32[64]{0:T(128)} %constant.64.clone) | copy-start | bytes 772
  16.1 37.0 %all-to-all-start = ((bf16[64,16,512]{2,1,0:T(8,128)(2,1)}), bf16[64,16,512]{2,1,0:T(8,128)(2,1)S(1)}, u32[]{:S(2)}, u32[]{:S(2)}) async-start(bf16[64,16,512]{2,1,0:T(8,128)(2,1)} %bitcast.2), calls=%async_computation | async-start | bytes 2097152 | tf_op jit(solution)/shard_map/all_to_all | solution.py:389
  29.8 5.5 %copy-start.11 = (f32[64]{0:T(128)S(1)}, f32[64]{0:T(128)}, u32[]{:S(2)}) copy-start(f32[64]{0:T(128)} %param.17) | copy-start | bytes 772
  29.8 5.7 %copy-start.6 = (bf16[64,512]{1,0:T(8,128)(2,1)S(1)}, bf16[64,512]{1,0:T(8,128)(2,1)}, u32[]{:S(2)}) copy-start(bf16[64,512]{1,0:T(8,128)(2,1)} %x_ref.5) | copy-start | bytes 196612
  35.5 1.6 %copy-start.4 = (bf16[512,2048]{1,0:T(8,128)(2,1)S(1)}, bf16[512,2048]{1,0:T(8,128)(2,1)}, u32[]{:S(2)}) copy-start(bf16[512,2048]{1,0:T(8,128)(2,1)} %w_ref.10) | copy-start | bytes 6291460
  38.3 5.0 %collective-permute-start.3 = (bf16[64,512]{1,0:T(8,128)(2,1)S(1)}, bf16[64,512]{1,0:T(8,128)(2,1)S(1)}, u32[]{:S(2)}, u32[]{:S(2)}) collective-permute-start(bf16[64,512]{1,0:T(8,128)(2,1)S(1)} %get-tuple-element.41), channel_id=1, source_target_pairs={{0,128},{64,192},{128,0},{192,64},{1,129},{65,193},{129,1},{193,65... | collective-permute-start | bytes 196616 | tf_op jit(solution)/shard_map/ppermute | solution.py:176
  39.9 5.0 %collective-permute-start.4 = (bf16[64,512]{1,0:T(8,128)(2,1)S(1)}, bf16[64,512]{1,0:T(8,128)(2,1)S(1)}, u32[]{:S(2)}, u32[]{:S(2)}) collective-permute-start(bf16[64,512]{1,0:T(8,128)(2,1)S(1)} %get-tuple-element.42), channel_id=1, source_target_pairs={{0,64},{64,128},{128,192},{192,0},{1,65},{65,129},{129,193},{193,1... | collective-permute-start | bytes 196616 | tf_op jit(solution)/shard_map/ppermute | solution.py:176
  41.6 3.6 %collective-permute-start.5 = (bf16[64,512]{1,0:T(8,128)(2,1)S(1)}, bf16[64,512]{1,0:T(8,128)(2,1)S(1)}, u32[]{:S(2)}, u32[]{:S(2)}) collective-permute-start(bf16[64,512]{1,0:T(8,128)(2,1)S(1)} %get-tuple-element.43), channel_id=1, source_target_pairs={{0,192},{64,0},{128,64},{192,128},{1,193},{65,1},{129,65},{193,129... | collective-permute-start | bytes 196616 | tf_op jit(solution)/shard_map/ppermute | solution.py:176
  45.5 12.5 %collective-permute-start.8 = (f32[144,128]{1,0:T(8,128)S(1)}, f32[144,128]{1,0:T(8,128)S(1)}, u32[]{:S(2)}, u32[]{:S(2)}) collective-permute-start(f32[144,128]{1,0:T(8,128)S(1)} %shard_map.128.refs_0_), channel_id=1, source_target_pairs={{192,0},{0,64},{64,128},{128,192},{193,1},{1,65},{65,129},{129,193... | collective-permute-start | bytes 221192 | tf_op jit(solution)/shard_map/ppermute | solution.py:181
  46.2 11.8 %collective-permute-start.7 = (f32[144,128]{1,0:T(8,128)S(1)}, f32[144,128]{1,0:T(8,128)S(1)}, u32[]{:S(2)}, u32[]{:S(2)}) collective-permute-start(f32[144,128]{1,0:T(8,128)S(1)} %shard_map.128.refs_0_), channel_id=1, source_target_pairs={{128,0},{192,64},{0,128},{64,192},{129,1},{193,65},{1,129},{65,193... | collective-permute-start | bytes 221192 | tf_op jit(solution)/shard_map/ppermute | solution.py:181
  49.1 8.9 %collective-permute-start.6 = (f32[144,128]{1,0:T(8,128)S(1)}, f32[144,128]{1,0:T(8,128)S(1)}, u32[]{:S(2)}, u32[]{:S(2)}) collective-permute-start(f32[144,128]{1,0:T(8,128)S(1)} %shard_map.128.refs_0_), channel_id=1, source_target_pairs={{64,0},{128,64},{192,128},{0,192},{65,1},{129,65},{193,129},{1,193... | collective-permute-start | bytes 221192 | tf_op jit(solution)/shard_map/ppermute | solution.py:181
  54.1 3.9 %collective-permute-start.11 = (f32[8,128]{1,0:T(8,128)S(1)}, f32[8,128]{1,0:T(8,128)S(1)}, u32[]{:S(2)}, u32[]{:S(2)}) collective-permute-start(f32[8,128]{1,0:T(8,128)S(1)} %shard_map.129.refs_4_), channel_id=1, source_target_pairs={{192,0},{0,64},{64,128},{128,192},{193,1},{1,65},{65,129},{129,193... | collective-permute-start | bytes 12296 | tf_op jit(solution)/shard_map/ppermute | solution.py:181
  55.2 4.0 %collective-permute-start.10 = (f32[8,128]{1,0:T(8,128)S(1)}, f32[8,128]{1,0:T(8,128)S(1)}, u32[]{:S(2)}, u32[]{:S(2)}) collective-permute-start(f32[8,128]{1,0:T(8,128)S(1)} %shard_map.129.refs_4_), channel_id=1, source_target_pairs={{128,0},{192,64},{0,128},{64,192},{129,1},{193,65},{1,129},{65,193... | collective-permute-start | bytes 12296 | tf_op jit(solution)/shard_map/ppermute | solution.py:181
  58.0 2.7 %collective-permute-start.9 = (f32[8,128]{1,0:T(8,128)S(1)}, f32[8,128]{1,0:T(8,128)S(1)}, u32[]{:S(2)}, u32[]{:S(2)}) collective-permute-start(f32[8,128]{1,0:T(8,128)S(1)} %shard_map.129.refs_4_), channel_id=1, source_target_pairs={{64,0},{128,64},{192,128},{0,192},{65,1},{129,65},{193,129},{1,193... | collective-permute-start | bytes 12296 | tf_op jit(solution)/shard_map/ppermute | solution.py:181
  62.4 35.9 %all-to-all-start.1 = ((bf16[64,16,512]{2,1,0:T(8,128)(2,1)}), bf16[64,16,512]{2,1,0:T(8,128)(2,1)S(1)}, u32[]{:S(2)}, u32[]{:S(2)}) async-start(bf16[64,16,512]{2,1,0:T(8,128)(2,1)} %bitcast.7), calls=%async_computation.1 | async-start | bytes 2097152 | tf_op jit(solution)/shard_map/all_to_all | solution.py:389
  75.3 7.0 %collective-permute-start.14 = (bf16[64,512]{1,0:T(8,128)(2,1)S(1)}, bf16[64,512]{1,0:T(8,128)(2,1)S(1)}, u32[]{:S(2)}, u32[]{:S(2)}) collective-permute-start(bf16[64,512]{1,0:T(8,128)(2,1)S(1)} %get-tuple-element.56.refs_0_), channel_id=1, source_target_pairs={{128,0},{192,64},{0,128},{64,192},{129,1},{193,65},{1,129},{65,193... | collective-permute-start | bytes 196616 | tf_op jit(solution)/shard_map/ppermute | solution.py:181
  76.6 5.7 %collective-permute-start.13 = (bf16[64,512]{1,0:T(8,128)(2,1)S(1)}, bf16[64,512]{1,0:T(8,128)(2,1)S(1)}, u32[]{:S(2)}, u32[]{:S(2)}) collective-permute-start(bf16[64,512]{1,0:T(8,128)(2,1)S(1)} %get-tuple-element.56.refs_0_), channel_id=1, source_target_pairs={{64,0},{128,64},{192,128},{0,192},{65,1},{129,65},{193,129},{1,193... | collective-permute-start | bytes 196616 | tf_op jit(solution)/shard_map/ppermute | solution.py:181
  77.3 4.8 %collective-permute-start.12 = (bf16[64,512]{1,0:T(8,128)(2,1)S(1)}, bf16[64,512]{1,0:T(8,128)(2,1)S(1)}, u32[]{:S(2)}, u32[]{:S(2)}) collective-permute-start(bf16[64,512]{1,0:T(8,128)(2,1)S(1)} %get-tuple-element.56.refs_0_), channel_id=1, source_target_pairs={{192,0},{0,64},{64,128},{128,192},{193,1},{1,65},{65,129},{129,193... | collective-permute-start | bytes 196616 | tf_op jit(solution)/shard_map/ppermute | solution.py:181
  78.6 1.6 %copy-start.5 = (bf16[512,2048]{1,0:T(8,128)(2,1)S(1)}, bf16[512,2048]{1,0:T(8,128)(2,1)}, u32[]{:S(2)}) copy-start(bf16[512,2048]{1,0:T(8,128)(2,1)} %w_ref.10) | copy-start | bytes 6291460
  98.6 6.3 %collective-permute-start.15 = (bf16[128,512]{1,0:T(8,128)(2,1)S(1)}, bf16[128,512]{1,0:T(8,128)(2,1)S(1)}, u32[]{:S(2)}, u32[]{:S(2)}) collective-permute-start(bf16[128,512]{1,0:T(8,128)(2,1)S(1)} %shard_map.135.refs_0_), channel_id=1, source_target_pairs={{192,0},{0,64},{64,128},{128,192},{193,1},{1,65},{65,129},{129,193... | collective-permute-start | bytes 393224 | tf_op jit(solution)/shard_map/ppermute | solution.py:181
  98.7 8.0 %collective-permute-start.17 = (bf16[128,512]{1,0:T(8,128)(2,1)S(1)}, bf16[128,512]{1,0:T(8,128)(2,1)S(1)}, u32[]{:S(2)}, u32[]{:S(2)}) collective-permute-start(bf16[128,512]{1,0:T(8,128)(2,1)S(1)} %shard_map.135.refs_0_), channel_id=1, source_target_pairs={{128,0},{192,64},{0,128},{64,192},{129,1},{193,65},{1,129},{65,193... | collective-permute-start | bytes 393224 | tf_op jit(solution)/shard_map/ppermute | solution.py:181
  100.9 6.6 %collective-permute-start.16 = (bf16[128,512]{1,0:T(8,128)(2,1)S(1)}, bf16[128,512]{1,0:T(8,128)(2,1)S(1)}, u32[]{:S(2)}, u32[]{:S(2)}) collective-permute-start(bf16[128,512]{1,0:T(8,128)(2,1)S(1)} %shard_map.135.refs_0_), channel_id=1, source_target_pairs={{64,0},{128,64},{192,128},{0,192},{65,1},{129,65},{193,129},{1,193... | collective-permute-start | bytes 393224 | tf_op jit(solution)/shard_map/ppermute | solution.py:181
  102.0 2.2 %copy-start.2 = (bf16[1024,2048]{1,0:T(8,128)(2,1)S(1)}, bf16[1024,2048]{1,0:T(8,128)(2,1)}, u32[]{:S(2)}) copy-start(bf16[1024,2048]{1,0:T(8,128)(2,1)} %w_ref.11) | copy-start | bytes 12582916
